TPU v7x, 32 devices: a whole 2x2x4 slice. The times are simulated.
32 devices in a mesh: ctx: 4 (over z), tp: 8 (over y, x, core).
Axes of the slice: x: 2, y: 2, z: 4, core: 2. Of those that a mesh axis runs over, the one named last changes fastest.
Arguments:
- hidden_in: bfloat16 [2048, 8192], P('ctx', 'tp'), may hold values from -30 to 30
- norm_gain: bfloat16 [8192], P('tp'), may hold values from 0.099609375 to 1.8984375
- w_query: bfloat16 [8192, 4096], P(None, 'tp'), may hold values from -1 to 1
- w_key: bfloat16 [8192, 1024], P(None, 'tp'), may hold values from -1 to 1
- w_value: bfloat16 [8192, 1024], P(None, 'tp'), may hold values from -0.0625 to 0.0625
- sign_bits: int32 [32, 128], P('tp'), may hold values from 0 to 1
- w_out: bfloat16 [4096, 8192], P(None, 'tp'), may hold values from -1 to 1
- teacher: bfloat16 [2048, 8192], P('ctx', 'tp'), may hold values from -30 to 30
Outputs:
- student: bfloat16 [2048, 8192], P('ctx', 'tp')
- row_loss: float32 [2048], P('ctx')
Inputs may be any that keep to these rules, and one draw needn't show every extreme that they name: `sign_bits`: 1 stands for the sign +1 and 0 for -1.
All inputs are finite; a program needn't handle non-finite values.
Results may differ from a plain program's by a relative error of at most 0.012.
The roundings to bfloat16 on the way count: a program that leaves them out, or rounds other values in their place, can miss the bound.
Values may be sent and summed in bfloat16 or wider, within the bound.
No kernel may reach another device: no remote copies, remote signals or barrier semaphores. Data moves between devices by JAX's collectives and lax.ppermute only.
A program may use at most 128 MiB of HBM per device.

v0:
```python
import functools
import math

import jax
import jax.numpy as jnp
from jax import lax
from jax.experimental import pallas as pl
from jax.experimental.pallas import tpu as pltpu
from jax.sharding import PartitionSpec as P

HD = 128
GROUP = 128
EPS_IN = 1e-05
EPS_OUT = 1e-06
CLIP_RATIO = 0.9
FAR_BELOW = -1e30
LOG2E = math.log2(math.e)
HALVES = 2
MIB = 1024 * 1024


def params(mib, **kw):
    return pltpu.CompilerParams(vmem_limit_bytes=mib * MIB, **kw)


def whole(shape):
    zeros = (0,) * len(shape)
    return pl.BlockSpec(shape, lambda *_: zeros)


IN_SMEM = pl.BlockSpec(memory_space=pltpu.SMEM)
IN_VMEM = pl.BlockSpec(memory_space=pltpu.VMEM)
ANYWHERE = pl.BlockSpec(memory_space=pl.ANY)


def cost(flops, moved, trans=0):
    return pl.CostEstimate(flops=int(flops), bytes_accessed=int(moved), transcendentals=int(trans))


def clip_tile(v):
    limit = CLIP_RATIO * jnp.max(jnp.abs(v), axis=-1, keepdims=True)
    return jnp.clip(v, -limit, limit)


def to_lanes(column):
    rows = column.shape[0]
    return jnp.transpose(jnp.broadcast_to(column, (rows, 128)))[:8]


def pre_kernel(h_ref, g_ref, c_ref, s_ref):
    rows, width = h_ref.shape
    total = jnp.zeros((rows, GROUP), jnp.float32)
    for at in range(0, width, GROUP):
        h = h_ref[:, at : at + GROUP].astype(jnp.float32)
        total = total + h * h
        v = h * g_ref[:, at : at + GROUP].astype(jnp.float32)
        c_ref[:, at : at + GROUP] = clip_tile(v).astype(jnp.bfloat16)
    s_ref[...] = to_lanes(jnp.sum(total, axis=-1, keepdims=True))


def pre(hidden, gain, chunk, rows):
    width = hidden.shape[1]
    return pl.pallas_call(
        pre_kernel,
        grid=(1,),
        in_specs=[pl.BlockSpec((rows, width), lambda i: (chunk, 0)), whole((1, width))],
        out_specs=[whole((rows, width)), whole((8, rows))],
        out_shape=[
            jax.ShapeDtypeStruct((rows, width), jnp.bfloat16),
            jax.ShapeDtypeStruct((8, rows), jnp.float32),
        ],
        compiler_params=params(8),
        cost_estimate=cost(8 * rows * width, 4 * rows * width),
        name="pre",
    )(hidden, gain)


def proj_kernel(counts, joined, order_ref, ss_ref, *refs):
    depth = len(counts)
    blocks = refs[: sum(counts)]
    wq_hbm, wk_hbm, wv_hbm, q_ref, kv_ref, lhs, *rest = refs[sum(counts) :]
    nq, nk, nv = wq_hbm.shape[1], wk_hbm.shape[1], wv_hbm.shape[1]
    k_rows = lhs.shape[2]
    if joined:
        w_all, acc, wsem, lsem = rest
    else:
        wq_all, wk_all, wv_all, accq, acck, accv, wsem, lsem = rest

    def weight_copies(k):
        at = pl.ds(pl.multiple_of(order_ref[k] * k_rows, k_rows), k_rows)
        if joined:
            goals = (
                w_all.at[k, :, :nq],
                w_all.at[k, :, nq : nq + nk],
                w_all.at[k, :, nq + nk : nq + nk + nv],
            )
        else:
            goals = (wq_all.at[k], wk_all.at[k], wv_all.at[k])
        return [
            pltpu.make_async_copy(src.at[at], goal, wsem.at[k, i])
            for i, (src, goal) in enumerate(zip((wq_hbm, wk_hbm, wv_hbm), goals))
        ]

    copies = []
    at_block = 0
    for k in range(depth):
        mine = weight_copies(k)
        row = 0
        for p in range(counts[k]):
            block = blocks[at_block]
            at_block += 1
            rows = block.shape[0]
            mine.append(
                pltpu.make_async_copy(block, lhs.at[k, row : row + rows], lsem.at[k, p])
            )
            row += rows
        for copy in mine:
            copy.start()
        copies.append(mine)
    for k in range(depth):
        for copy in copies[k]:
            copy.wait()
        left = lhs[k]
        if joined:
            pairs = ((w_all, acc),)
        else:
            pairs = ((wq_all, accq), (wk_all, acck), (wv_all, accv))
        for w, total in pairs:
            part = jnp.dot(left, w[k], preferred_element_type=jnp.float32)
            if k == 0:
                total[...] = part
            else:
                total[...] += part

    features = k_rows * depth
    inverse = lax.rsqrt(ss_ref[...] * (1.0 / features) + EPS_IN)
    scale = jnp.transpose(inverse)[:, :1]
    if joined:
        q_ref[...] = (acc[:, :nq] * scale).astype(jnp.bfloat16)
        kv_ref[...] = (acc[:, nq:] * scale).astype(jnp.bfloat16)
    else:
        q_ref[...] = (accq[...] * scale).astype(jnp.bfloat16)
        kv_ref[:, :nk] = (acck[...] * scale).astype(jnp.bfloat16)
        kv_ref[:, nk:] = (accv[...] * scale).astype(jnp.bfloat16)


def proj(order, blocks, wq, wk, wv, squares):
    depth = len(blocks)
    counts = [len(b) for b in blocks]
    rows = squares.shape[1]
    part_cols = blocks[0][0].shape[1]
    nq, nk, nv = wq.shape[1], wk.shape[1], wv.shape[1]
    n = nq + nk + nv
    joined = nk % 128 == 0
    sizes = [n] if joined else [nq, nk, nv]
    scratch = [pltpu.VMEM((depth, rows, part_cols), jnp.bfloat16)]
    scratch += [pltpu.VMEM((depth, part_cols, m), jnp.bfloat16) for m in sizes]
    scratch += [pltpu.VMEM((rows, m), jnp.float32) for m in sizes]
    scratch += [pltpu.SemaphoreType.DMA((depth, 3)), pltpu.SemaphoreType.DMA((depth, 2))]
    flat = [p for b in blocks for p in b]
    return pl.pallas_call(
        functools.partial(proj_kernel, counts, joined),
        in_specs=[IN_SMEM, IN_VMEM] + [ANYWHERE] * (len(flat) + 3),
        out_specs=[IN_VMEM, IN_VMEM],
        out_shape=[
            jax.ShapeDtypeStruct((rows, nq), jnp.bfloat16),
            jax.ShapeDtypeStruct((rows, nk + nv), jnp.bfloat16),
        ],
        scratch_shapes=scratch,
        compiler_params=params(24),
        cost_estimate=cost(
            2 * rows * part_cols * depth * n, 2 * part_cols * depth * (rows + n)
        ),
        name="proj",
    )(order, squares, *flat, wq, wk, wv)


def att_kernel(first, heads, kv_heads, hops, pieces, me_ref, q_ref, sign_ref, *refs):
    kvs = refs[: pieces * (hops + 1)]
    o_ref, high, total, accum = refs[pieces * (hops + 1) :]
    rows = q_ref.shape[0]
    part = kvs[0].shape[0]
    group = heads // kv_heads
    scale = HD ** (-0.5) * LOG2E

    def visit(kv_ref, start, fresh):
        masked = start is not None and start + part > first
        scores, turned = [], []
        for kv in range(kv_heads):
            at = (kv_heads + kv) * HD
            turned.append(jnp.transpose(kv_ref[:, at : at + HD]))
        for head in range(heads):
            kv = head // group
            q = q_ref[:, head * HD : (head + 1) * HD]
            k = kv_ref[:, kv * HD : (kv + 1) * HD]
            s = lax.dot_general(
                k, q, (((1,), (1,)), ((), ())), preferred_element_type=jnp.float32
            )
            if masked:
                kpos = start + lax.broadcasted_iota(jnp.int32, s.shape, 0)
                qpos = first + lax.broadcasted_iota(jnp.int32, s.shape, 1)
                s = jnp.where(kpos <= qpos, s, FAR_BELOW)
            scores.append(s)
        for head in range(heads):
            s = scores[head]
            best = jnp.max(s, axis=0, keepdims=True)
            if not fresh:
                before = high[head : head + 1]
                best = jnp.maximum(best, before)
            w = jnp.exp2((s - best) * scale)
            sums = jnp.sum(w, axis=0, keepdims=True)
            mixed = jnp.dot(
                turned[head // group], w.astype(jnp.bfloat16), preferred_element_type=jnp.float32
            )
            if fresh:
                total[head : head + 1] = sums
                accum[head] = mixed
            else:
                decay = jnp.exp2((before - best) * scale)
                total[head : head + 1] = total[head : head + 1] * decay + sums
                accum[head] = accum[head] * decay + mixed
            high[head : head + 1] = best

    near = [p for p in range(pieces) if p * part < first + rows]
    for at, p in enumerate(near):
        visit(kvs[p], p * part, at == 0)
    for hop in range(1, hops + 1):

        @pl.when(me_ref[0] >= hop)
        def _():
            for p in range(pieces):
                visit(kvs[hop * pieces + p], None, False)

    for head in range(heads):
        att = jnp.transpose(accum[head] / total[head : head + 1])
        att = att.astype(jnp.bfloat16).astype(jnp.float32)
        o_ref[:, head * HD : (head + 1) * HD] = (att * sign_ref[head : head + 1, :]).astype(
            jnp.bfloat16
        )


def attend(me, q, first, signs, kvs, pieces, kv_heads):
    rows = q.shape[0]
    heads = q.shape[1] // HD
    hops = len(kvs) // pieces - 1
    keys = sum(kv.shape[0] for kv in kvs)
    return pl.pallas_call(
        functools.partial(att_kernel, first, heads, kv_heads, hops, pieces),
        in_specs=[IN_SMEM] + [IN_VMEM] * (len(kvs) + 2),
        out_specs=IN_VMEM,
        out_shape=jax.ShapeDtypeStruct((rows, heads * HD), jnp.bfloat16),
        scratch_shapes=[
            pltpu.VMEM((max(heads, 8), rows), jnp.float32),
            pltpu.VMEM((max(heads, 8), rows), jnp.float32),
            pltpu.VMEM((heads, HD, rows), jnp.float32),
        ],
        compiler_params=params(20),
        cost_estimate=cost(4 * rows * keys * heads * HD, 4 * keys * HD, rows * keys * heads),
        name="attend",
    )(me, q, signs, *kvs)


def butterfly(tiles):
    count = len(tiles)
    span = 1
    while span < count:
        out = list(tiles)
        for at in range(count):
            if not at & span:
                a, b = tiles[at], tiles[at | span]
                out[at], out[at | span] = a + b, a - b
        tiles = out
        span *= 2
    return tiles


def out_kernel(counts, steps, sign_ref, t_ref, *refs):
    parts = len(counts)
    blocks, at_block = [], 0
    for n in counts:
        blocks.append(refs[at_block : at_block + n])
        at_block += n
    w_hbm, b_ref, s_ref, w_all, mid, rot, acc, wsem = refs[at_block:]
    rows = b_ref.shape[0]
    width = blocks[0][0].shape[1]
    here = width // HD
    heads = here * parts
    factor = heads ** (-0.5)
    depth = w_hbm.shape[0] // steps
    copies = [
        pltpu.make_async_copy(
            w_hbm.at[i * depth : (i + 1) * depth],
            w_all.at[i * depth : (i + 1) * depth],
            wsem.at[i],
        )
        for i in range(steps)
    ]
    for copy in copies:
        copy.start()

    strip = 16
    most = max(counts)
    span = rows // most
    for section in range(most):

        def turn(i, carry):
            at = pl.multiple_of(section * span + i * strip, strip)
            for m in range(parts):
                if len(blocks[m]) == 1:
                    ref, start = blocks[m][0], at
                else:
                    ref, start = blocks[m][section], pl.multiple_of(i * strip, strip)
                tiles = [
                    ref[pl.ds(start, strip), h * HD : (h + 1) * HD].astype(jnp.float32)
                    for h in range(here)
                ]
                for h, v in enumerate(butterfly(tiles)):
                    mid[m * here + h] = v
            for h in range(here):
                tiles = butterfly([mid[m * here + h] for m in range(parts)])
                for m in range(parts):
                    v = tiles[m] * (factor * sign_ref[m])
                    col = (m * here + h) * HD
                    rot[pl.ds(at, strip), col : col + HD] = clip_tile(v).astype(jnp.bfloat16)
            return carry

        lax.fori_loop(0, span // strip, turn, 0)

    for i in range(steps):
        copies[i].wait()
        part = jnp.dot(
            rot[:, i * depth : (i + 1) * depth],
            w_all[i * depth : (i + 1) * depth, :],
            preferred_element_type=jnp.float32,
        )
        if i == 0:
            acc[...] = part
        else:
            acc[...] += part

    b = acc[...]
    t = t_ref[...].astype(jnp.float32)
    b_ref[...] = b
    sums = [jnp.sum(v, axis=-1, keepdims=True) for v in (b * b, b * t, t * t)]
    lane = lax.broadcasted_iota(jnp.int32, (rows, 128), 1)
    wide = jnp.where(lane == 0, sums[0], jnp.where(lane == 1, sums[1], sums[2]))
    s_ref[...] = jnp.transpose(wide)[:8]


def project_out(flips, blocks, w_out, teacher, chunk):
    parts = len(blocks)
    counts = [len(b) for b in blocks]
    rows, width = blocks[0][0].shape
    depth, cols = w_out.shape
    steps = 4
    flat = [p for b in blocks for p in b]
    return pl.pallas_call(
        functools.partial(out_kernel, counts, steps),
        grid=(1,),
        in_specs=[IN_SMEM, pl.BlockSpec((rows, cols), lambda i: (chunk, 0))]
        + [whole(p.shape) for p in flat]
        + [ANYWHERE],
        out_specs=[whole((rows, cols)), whole((8, rows))],
        out_shape=[
            jax.ShapeDtypeStruct((rows, cols), jnp.float32),
            jax.ShapeDtypeStruct((8, rows), jnp.float32),
        ],
        scratch_shapes=[
            pltpu.VMEM((depth, cols), jnp.bfloat16),
            pltpu.VMEM((parts * width // HD, 16, HD), jnp.float32),
            pltpu.VMEM((rows, depth), jnp.bfloat16),
            pltpu.VMEM((rows, cols), jnp.float32),
            pltpu.SemaphoreType.DMA((steps,)),
        ],
        compiler_params=params(24),
        cost_estimate=cost(2 * rows * depth * cols, 2 * depth * (rows + cols) + 6 * rows * cols),
        name="project_out",
    )(flips, teacher, *flat, w_out)


def final_kernel(features, chunks, parts, *refs):
    branches, stats = refs[:chunks], refs[chunks : chunks + parts]
    student_ref, loss_ref = refs[chunks + parts :]
    total = stats[0][...]
    for at in range(1, parts):
        total = total + stats[at][...]
    inverse = lax.rsqrt(total[0:1] * (1.0 / features) + EPS_OUT)
    loss = inverse * inverse * total[0:1] - 2.0 * inverse * total[1:2] + total[2:3]
    loss_ref[...] = jnp.maximum(loss, 0.0) * (1.0 / features)
    column = jnp.transpose(jnp.broadcast_to(inverse, total.shape))[:, :1]
    rows = branches[0].shape[0]
    for at in range(chunks):
        scale = column[at * rows : (at + 1) * rows]
        student_ref[at * rows : (at + 1) * rows, :] = (branches[at][...] * scale).astype(
            jnp.bfloat16
        )


def final(features, branches, stats):
    chunks, parts = len(branches), len(stats)
    part_rows, cols = branches[0].shape
    rows = part_rows * chunks
    return pl.pallas_call(
        functools.partial(final_kernel, features, chunks, parts),
        grid=(1,),
        in_specs=[whole((part_rows, cols))] * chunks + [whole((8, rows))] * parts,
        out_specs=[whole((rows, cols)), whole((1, rows))],
        out_shape=[
            jax.ShapeDtypeStruct((rows, cols), jnp.bfloat16),
            jax.ShapeDtypeStruct((1, rows), jnp.float32),
        ],
        compiler_params=params(16),
        cost_estimate=cost(2 * rows * cols, 6 * rows * cols),
        name="final",
    )(*branches, *stats)


def swap(x, mask):
    count = lax.axis_size("tp")
    return lax.ppermute(x, "tp", [(i, i ^ mask) for i in range(count)])


def send_up(x, distance):
    count = lax.axis_size("ctx")
    return lax.ppermute(x, "ctx", [(i, i + distance) for i in range(count - distance)])


def after(x, *others):
    return lax.optimization_barrier((x,) + others)[0]


def gather(own):
    count = lax.axis_size("tp")
    got = {0: [own]}
    masks = [1 << b for b in range(1, count.bit_length() - 1)]
    if len(masks) >= 2:
        a, b = masks[0], masks[1]
        half = own.shape[0] // 2
        got[a] = [swap(own, a)]
        got[b] = [swap(own, b)]
        got[a | b] = [swap(got[a][0][:half], b), swap(got[b][0][half:], a)]
        masks = masks[2:]
    if count > 1:
        for m in list(got):
            got[m | 1] = [swap(p, 1) for p in got[m]]
    for mask in masks:
        for m in list(got):
            got[m | mask] = [swap(p, mask) for p in got[m]]
    return [got[m] for m in range(count)]


def body(hidden_in, norm_gain, w_query, w_key, w_value, sign_bits, w_out, teacher):
    rows = hidden_in.shape[0]
    half = rows // HALVES
    tp_count = lax.axis_size("tp")
    ctx_count = lax.axis_size("ctx")
    features = hidden_in.shape[1] * tp_count
    tp_at = lax.axis_index("tp")
    ctx_at = jnp.reshape(lax.axis_index("ctx"), (1,)).astype(jnp.int32)
    masks = jnp.arange(tp_count, dtype=jnp.int32)
    order = tp_at ^ masks
    shared = tp_at & masks
    parity = jnp.zeros_like(shared)
    for bit in range(tp_count.bit_length()):
        parity = parity ^ (shared >> bit & 1)
    flips = (1 - 2 * parity).astype(jnp.float32)
    signs = (2 * sign_bits - 1).astype(jnp.float32)
    gain = norm_gain.reshape(1, -1)

    chunks = [pre(hidden_in, gain, i, half) for i in range(HALVES)]
    gathered = []
    for clipped, _ in chunks:
        if gathered:
            clipped = after(clipped, *[b[0] for b in gathered[-1][2:6:2]])
        gathered.append(gather(clipped))
    squares = jnp.concatenate([s for _, s in chunks], axis=1)
    if tp_count > 2:
        squares = after(squares, gathered[0][2][0])
    for bit in range(tp_count.bit_length() - 1):
        squares = squares + swap(squares, 1 << bit)

    kv_cols = w_key.shape[1]
    sharing = HD // kv_cols if kv_cols < HD else 1
    kv_heads = kv_cols * sharing // HD
    queries, kvs = [], []
    for at in range(HALVES):
        part = squares[:, at * half : (at + 1) * half]
        q, kv = proj(order, gathered[at], w_query, w_key, w_value, part)
        if sharing > 1:
            k, v = kv[:, :kv_cols], kv[:, kv_cols:]
            for bit in range(sharing.bit_length() - 1):
                upper = tp_at >> bit & 1 == 1
                k2, v2 = swap(k, 1 << bit), swap(v, 1 << bit)
                k, v = (
                    jnp.where(
                        upper,
                        jnp.concatenate([far, near], axis=1),
                        jnp.concatenate([near, far], axis=1),
                    )
                    for near, far in ((k, k2), (v, v2))
                )
            kv = jnp.concatenate([k, v], axis=1)
        queries.append(q)
        kvs.append([kv] + [send_up(kv, hop) for hop in range(1, ctx_count)])
    kvs = [kvs[p][hop] for hop in range(ctx_count) for p in range(HALVES)]

    branches, stats = [], []
    for at in range(HALVES):
        signed = attend(ctx_at, queries[at], at * half, signs, kvs, HALVES, kv_heads)
        b, s = project_out(flips, gather(signed), w_out, teacher, at)
        branches.append(b)
        stats.append(s)
    stat = jnp.concatenate(stats, axis=1)
    for bit in range(tp_count.bit_length() - 1):
        stat = stat + swap(stat, 1 << bit)
    student, loss = final(features, branches, [stat])
    return student, loss.reshape(rows)


def solution(mesh):
    in_specs = (
        P("ctx", "tp"),
        P("tp"),
        P(None, "tp"),
        P(None, "tp"),
        P(None, "tp"),
        P("tp", None),
        P(None, "tp"),
        P("ctx", "tp"),
    )
    out_specs = (P("ctx", "tp"), P("ctx"))
    return jax.shard_map(body, mesh=mesh, in_specs=in_specs, out_specs=out_specs, check_vma=False)
```

profile of v0, /device:TPU:24, one launch (start us, length us, event | category | flops | bytes accessed | tf_op | source)
XLA Modules:
  0.0 153.9 jit_solution(16704147442598405470)
XLA Ops:
  0.6 0.7 reshape.14.g_ref
  1.3 1.2 copy-done.7
  3.0 1.5 collective-permute-start
  4.5 1.5 collective-permute-start.6
  6.5 10.2 %collective-permute-done.refs_2_ = bf16[256,1024]{1,0:T(8,128)(2,1)S(1)} collective-permute-done((bf16[256,1024]{1,0:T(8,128)(2,1)S(1)}, bf16[256,1024]{1,0:T(8,128)(2,1)S(1)}, u32[]{:S(2)}, u32[]{:S(2)}) %collective-permute-start) | collective-permute-done | bytes 524320 | tf_op jit(solution)/shard_map/ppermute | solution.py:420
  16.7 1.6 %collective-permute-start.8 = (bf16[128,1024]{1,0:T(8,128)(2,1)S(1)}, bf16[128,1024]{1,0:T(8,128)(2,1)S(1)}, u32[]{:S(2)}, u32[]{:S(2)}) collective-permute-start(bf16[128,1024]{1,0:T(8,128)(2,1)S(1)} %slice.41), channel_id=1, source_target_pairs={{0,4},{1,5},{2,6},{3,7},{4,0},{5,1},{6,2},{7,3},{8,12},{9,13},{10,... | collective-permute-start | bytes 786440 | tf_op jit(solution)/shard_map/ppermute | solution.py:420
  18.3 1.5 collective-permute-start.13
  19.8 0.5 collective-permute-start.15
  20.3 1.2 collective-permute-done.1
  21.7 1.2 collective-permute-start.2
  22.9 8.3 %collective-permute-done.2 = f32[8,512]{1,0:T(8,128)S(1)} collective-permute-done((f32[8,512]{1,0:T(8,128)S(1)}, f32[8,512]{1,0:T(8,128)S(1)}, u32[]{:S(2)}, u32[]{:S(2)}) %collective-permute-start.2) | collective-permute-done | bytes 16416 | tf_op jit(solution)/shard_map/ppermute | solution.py:420
  31.2 1.5 collective-permute-start.9
  32.7 7.3 %collective-permute-done.9.refs_7_ = bf16[128,1024]{1,0:T(8,128)(2,1)} collective-permute-done((bf16[128,1024]{1,0:T(8,128)(2,1)S(1)}, bf16[128,1024]{1,0:T(8,128)(2,1)}, u32[]{:S(2)}, u32[]{:S(2)}) %collective-permute-start.9) | collective-permute-done | bytes 262176 | tf_op jit(solution)/shard_map/ppermute | solution.py:420
  40.0 0.5 collective-permute-start.11
  40.5 1.1 collective-permute-start.3
  41.7 0.7 slice.44
  42.4 0.7 slice.45
  43.1 1.2 collective-permute-done.3
  44.3 1.1 collective-permute-start.17
  45.4 0.9 collective-permute-start.18
  47.0 4.7 %collective-permute-done.17.refs_6_ = bf16[128,1024]{1,0:T(8,128)(2,1)} collective-permute-done((bf16[128,1024]{1,0:T(8,128)(2,1)}, bf16[128,1024]{1,0:T(8,128)(2,1)}, u32[]{:S(2)}, u32[]{:S(2)}) %collective-permute-start.17) | collective-permute-done | bytes 262176 | tf_op jit(solution)/shard_map/ppermute | solution.py:420
  51.7 0.8 collective-permute-done.18.refs_7_
  52.5 3.4 %copy-done = bf16[8192,512]{1,0:T(8,128)(2,1)S(1)} copy-done((bf16[8192,512]{1,0:T(8,128)(2,1)S(1)}, bf16[8192,512]{1,0:T(8,128)(2,1)}, u32[]{:S(2)}) %copy-start) | copy-done | bytes 8388632
  55.9 1.6 %copy-done.2 = bf16[8192,128]{1,0:T(8,128)(2,1)S(1)} copy-done((bf16[8192,128]{1,0:T(8,128)(2,1)S(1)}, bf16[8192,128]{1,0:T(8,128)(2,1)}, u32[]{:S(2)}) %copy-start.2) | copy-done | bytes 2097176
  57.5 1.6 %copy-done.4 = bf16[8192,128]{1,0:T(8,128)(2,1)S(1)} copy-done((bf16[8192,128]{1,0:T(8,128)(2,1)S(1)}, bf16[8192,128]{1,0:T(8,128)(2,1)}, u32[]{:S(2)}) %copy-start.4) | copy-done | bytes 2097176
  59.1 1.0 copy-done.9
  60.1 7.8 %proj.2 = (bf16[256,512]{1,0:T(8,128)(2,1)S(1)}, bf16[256,256]{1,0:T(8,128)(2,1)S(1)}) custom-call(s32[8]{0:T(128)S(1)} %iota_xor_fusion.order_ref, f32[8,256]{1,0:T(8,128)S(1)} %get-tuple-element.35.ss_ref, bf16[256,1024]{1,0:T(8,128)(2,1)S(1)} %get-tuple-element.20.refs_0_, bf16[256,1024]{1,0:T(8,128)(2,1)S(1)} %copy-done.9, ...), custom_call_target="tpu_custom_call" | custom-call | flops 3221225472 | bytes 16777216 | tf_op jit(solution)/shard_map/proj/pallas_call | solution.py:161
  68.0 0.7 copy-done.12
  68.7 1.3 collective-permute-start.21
  70.0 1.3 collective-permute-start.23
  71.3 1.5 collective-permute-start.25
  72.8 0.7 copy-done.10
  73.5 1.1 copy-done.11
  74.6 7.9 %proj.3 = (bf16[256,512]{1,0:T(8,128)(2,1)S(1)}, bf16[256,256]{1,0:T(8,128)(2,1)S(1)}) custom-call(s32[8]{0:T(128)S(1)} %iota_xor_fusion.order_ref, f32[8,256]{1,0:T(8,128)S(1)} %get-tuple-element.34.ss_ref, bf16[256,1024]{1,0:T(8,128)(2,1)S(1)} %get-tuple-element.25.refs_0_, bf16[256,1024]{1,0:T(8,128)(2,1)S(1)} %collective-permute-done.12.refs_1_, ...), custom_call_target="tpu_custom_call" | custom-call | flops 3221225472 | bytes 16777216 | tf_op jit(solution)/shard_map/proj/pallas_call | solution.py:161
  82.6 1.4 collective-permute-start.22
  84.0 1.3 collective-permute-start.24
  85.3 1.3 collective-permute-start.26
  86.7 3.9 %collective-permute-done.22.refs_3_ = bf16[256,256]{1,0:T(8,128)(2,1)S(1)} collective-permute-done((bf16[256,256]{1,0:T(8,128)(2,1)S(1)}, bf16[256,256]{1,0:T(8,128)(2,1)S(1)}, u32[]{:S(2)}, u32[]{:S(2)}) %collective-permute-start.22) | collective-permute-done | bytes 131104 | tf_op jit(solution)/shard_map/ppermute | solution.py:425
  90.5 9.6 %collective-permute-done.24.refs_5_ = bf16[256,256]{1,0:T(8,128)(2,1)S(1)} collective-permute-done((bf16[256,256]{1,0:T(8,128)(2,1)S(1)}, bf16[256,256]{1,0:T(8,128)(2,1)S(1)}, u32[]{:S(2)}, u32[]{:S(2)}) %collective-permute-start.24) | collective-permute-done | bytes 131104 | tf_op jit(solution)/shard_map/ppermute | solution.py:425
  100.1 4.2 %attend.2.refs_0_ = bf16[256,512]{1,0:T(8,128)(2,1)S(1)} custom-call(s32[1]{0:T(128)} %bitcast.me_ref, bf16[256,512]{1,0:T(8,128)(2,1)S(1)} %copy-done.13, f32[4,128]{1,0:T(4,128)S(1)} %add_convert_fusion.sign_ref, bf16[256,256]{1,0:T(8,128)(2,1)S(1)} %get-tuple-element.23.refs_0_, bf16[256,256]{1,0:T(8,128)(2,1)S(1)} %get-tuple-element.26.refs_1_, ...), custom_call_target="tpu_custom_call" | custom-call | flops 1073741824 | bytes 1048576 | tf_op jit(solution)/shard_map/attend/pallas_call | solution.py:247
  104.4 1.1 collective-permute-start.28
  105.5 1.4 collective-permute-start.30
  106.9 5.0 %attend.3.refs_0_ = bf16[256,512]{1,0:T(8,128)(2,1)S(1)} custom-call(s32[1]{0:T(128)} %bitcast.me_ref, bf16[256,512]{1,0:T(8,128)(2,1)S(1)} %get-tuple-element.28.q_ref, f32[4,128]{1,0:T(4,128)S(1)} %add_convert_fusion.sign_ref, bf16[256,256]{1,0:T(8,128)(2,1)S(1)} %get-tuple-element.23.refs_0_, bf16[256,256]{1,0:T(8,128)(2,1)S(1)} %get-tuple-element.26.refs_1_, ...), custom_call_target="tpu_custom_call" | custom-call | flops 1073741824 | bytes 1048576 | tf_op jit(solution)/shard_map/attend/pallas_call | solution.py:247
  111.8 0.6 collective-permute-start.37
  112.4 1.1 collective-permute-start.39
  113.5 1.0 collective-permute-start.32
  114.6 4.4 %collective-permute-done.37.refs_2_ = bf16[256,512]{1,0:T(8,128)(2,1)S(1)} collective-permute-done((bf16[256,512]{1,0:T(8,128)(2,1)S(1)}, bf16[256,512]{1,0:T(8,128)(2,1)S(1)}, u32[]{:S(2)}, u32[]{:S(2)}) %collective-permute-start.37) | collective-permute-done | bytes 262176 | tf_op jit(solution)/shard_map/ppermute | solution.py:420
  119.0 0.6 collective-permute-start.33
  119.6 2.0 %collective-permute-done.39.refs_4_ = bf16[256,512]{1,0:T(8,128)(2,1)S(1)} collective-permute-done((bf16[256,512]{1,0:T(8,128)(2,1)S(1)}, bf16[256,512]{1,0:T(8,128)(2,1)S(1)}, u32[]{:S(2)}, u32[]{:S(2)}) %collective-permute-start.39) | collective-permute-done | bytes 262176 | tf_op jit(solution)/shard_map/ppermute | solution.py:420
  121.5 1.1 collective-permute-start.41
  122.6 1.7 %collective-permute-done.32.refs_6_ = bf16[128,512]{1,0:T(8,128)(2,1)S(1)} collective-permute-done((bf16[128,512]{1,0:T(8,128)(2,1)S(1)}, bf16[128,512]{1,0:T(8,128)(2,1)S(1)}, u32[]{:S(2)}, u32[]{:S(2)}) %collective-permute-start.32) | collective-permute-done | bytes 131104 | tf_op jit(solution)/shard_map/ppermute | solution.py:420
  124.3 1.5 collective-permute-start.42
  125.8 0.9 collective-permute-done.41.refs_6_
  126.8 2.5 %collective-permute-done.42.refs_7_ = bf16[128,512]{1,0:T(8,128)(2,1)S(1)} collective-permute-done((bf16[128,512]{1,0:T(8,128)(2,1)S(1)}, bf16[128,512]{1,0:T(8,128)(2,1)S(1)}, u32[]{:S(2)}, u32[]{:S(2)}) %collective-permute-start.42) | collective-permute-done | bytes 131104 | tf_op jit(solution)/shard_map/ppermute | solution.py:420
  129.3 0.5 collective-permute-start.38
  130.4 6.7 %project_out.2 = (f32[256,1024]{1,0:T(8,128)S(1)}, f32[8,256]{1,0:T(8,128)S(1)}) custom-call(f32[8]{0:T(128)S(1)} %subtract_convert_fusion.sign_ref, bf16[512,1024]{1,0:T(8,128)(2,1)S(1)} %copy-done.6, bf16[256,512]{1,0:T(8,128)(2,1)S(1)} %attend.2.refs_0_, bf16[256,512]{1,0:T(8,128)(2,1)S(1)} %collective-permute-done.27.refs_1_, ...), custom_call_target="tpu_custom_call" | custom-call | flops 2147483648 | bytes 12058624 | tf_op jit(solution)/shard_map/project_out/pallas_call | solution.py:357
  137.2 6.7 %project_out.3 = (f32[256,1024]{1,0:T(8,128)S(1)}, f32[8,256]{1,0:T(8,128)S(1)}) custom-call(f32[8]{0:T(128)S(1)} %subtract_convert_fusion.sign_ref, bf16[512,1024]{1,0:T(8,128)(2,1)S(1)} %copy-done.6, bf16[256,512]{1,0:T(8,128)(2,1)S(1)} %attend.3.refs_0_, bf16[256,512]{1,0:T(8,128)(2,1)S(1)} %collective-permute-done.36.refs_1_, ...), custom_call_target="tpu_custom_call" | custom-call | flops 2147483648 | bytes 12058624 | tf_op jit(solution)/shard_map/project_out/pallas_call | solution.py:357
  143.8 0.5 collective-permute-start.45
  144.3 0.8 collective-permute-done.45
  145.2 1.5 collective-permute-start.46
  146.7 2.2 %collective-permute-done.46 = f32[8,512]{1,0:T(8,128)S(1)} collective-permute-done((f32[8,512]{1,0:T(8,128)S(1)}, f32[8,512]{1,0:T(8,128)S(1)}, u32[]{:S(2)}, u32[]{:S(2)}) %collective-permute-start.46) | collective-permute-done | bytes 16416 | tf_op jit(solution)/shard_map/ppermute | solution.py:420
  148.9 1.1 collective-permute-start.47
  150.0 2.7 %collective-permute-done.47 = f32[8,512]{1,0:T(8,128)S(1)} collective-permute-done((f32[8,512]{1,0:T(8,128)S(1)}, f32[8,512]{1,0:T(8,128)S(1)}, u32[]{:S(2)}, u32[]{:S(2)}) %collective-permute-start.47) | collective-permute-done | bytes 16416 | tf_op jit(solution)/shard_map/ppermute | solution.py:420
  152.7 1.3 final.1
  (98 shorter events, 2.6 us)
Async XLA Ops:
  1.3 1.2 copy-start.7
  3.0 13.7 %collective-permute-start = (bf16[256,1024]{1,0:T(8,128)(2,1)S(1)}, bf16[256,1024]{1,0:T(8,128)(2,1)S(1)}, u32[]{:S(2)}, u32[]{:S(2)}) collective-permute-start(bf16[256,1024]{1,0:T(8,128)(2,1)S(1)} %get-tuple-element.20.refs_0_), channel_id=1, source_target_pairs={{0,2},{1,3},{2,0},{3,1},{4,6},{5,7},{6,4},{7,5},{8,10},{9,11},{10,... | collective-permute-start | bytes 1572872 | tf_op jit(solution)/shard_map/ppermute | solution.py:420
  4.5 13.8 %collective-permute-start.6 = (bf16[256,1024]{1,0:T(8,128)(2,1)S(1)}, bf16[256,1024]{1,0:T(8,128)(2,1)S(1)}, u32[]{:S(2)}, u32[]{:S(2)}) collective-permute-start(bf16[256,1024]{1,0:T(8,128)(2,1)S(1)} %get-tuple-element.20.refs_0_), channel_id=1, source_target_pairs={{0,4},{1,5},{2,6},{3,7},{4,0},{5,1},{6,2},{7,3},{8,12},{9,13},{10,... | collective-permute-start | bytes 1572872 | tf_op jit(solution)/shard_map/ppermute | solution.py:420
  6.0 15.6 %collective-permute-start.4 = (bf16[256,1024]{1,0:T(8,128)(2,1)S(1)}, bf16[256,1024]{1,0:T(8,128)(2,1)S(1)}, u32[]{:S(2)}, u32[]{:S(2)}) collective-permute-start(bf16[256,1024]{1,0:T(8,128)(2,1)S(1)} %get-tuple-element.20.refs_0_), channel_id=1, source_target_pairs={{0,1},{1,0},{2,3},{3,2},{4,5},{5,4},{6,7},{7,6},{8,9},{9,8},{10,11... | collective-permute-start | bytes 1572872 | tf_op jit(solution)/shard_map/ppermute | solution.py:420
  16.7 14.5 %collective-permute-start.8 = (bf16[128,1024]{1,0:T(8,128)(2,1)S(1)}, bf16[128,1024]{1,0:T(8,128)(2,1)S(1)}, u32[]{:S(2)}, u32[]{:S(2)}) collective-permute-start(bf16[128,1024]{1,0:T(8,128)(2,1)S(1)} %slice.41), channel_id=1, source_target_pairs={{0,4},{1,5},{2,6},{3,7},{4,0},{5,1},{6,2},{7,3},{8,12},{9,13},{10,... | collective-permute-start | bytes 786440 | tf_op jit(solution)/shard_map/ppermute | solution.py:420
  18.3 21.7 %collective-permute-start.13 = (bf16[256,1024]{1,0:T(8,128)(2,1)S(1)}, bf16[256,1024]{1,0:T(8,128)(2,1)S(1)}, u32[]{:S(2)}, u32[]{:S(2)}) collective-permute-start(bf16[256,1024]{1,0:T(8,128)(2,1)S(1)} %get-tuple-element.25.refs_0_), channel_id=1, source_target_pairs={{0,2},{1,3},{2,0},{3,1},{4,6},{5,7},{6,4},{7,5},{8,10},{9,11},{10,... | collective-permute-start | bytes 1572872 | tf_op jit(solution)/shard_map/ppermute | solution.py:420
  19.8 20.7 %collective-permute-start.15 = (bf16[256,1024]{1,0:T(8,128)(2,1)S(1)}, bf16[256,1024]{1,0:T(8,128)(2,1)S(1)}, u32[]{:S(2)}, u32[]{:S(2)}) collective-permute-start(bf16[256,1024]{1,0:T(8,128)(2,1)S(1)} %get-tuple-element.25.refs_0_), channel_id=1, source_target_pairs={{0,4},{1,5},{2,6},{3,7},{4,0},{5,1},{6,2},{7,3},{8,12},{9,13},{10,... | collective-permute-start | bytes 1572872 | tf_op jit(solution)/shard_map/ppermute | solution.py:420
  20.3 1.2 collective-permute-start.1
  21.5 23.9 %collective-permute-start.5 = (bf16[256,1024]{1,0:T(8,128)(2,1)S(1)}, bf16[256,1024]{1,0:T(8,128)(2,1)}, u32[]{:S(2)}, u32[]{:S(2)}) collective-permute-start(bf16[256,1024]{1,0:T(8,128)(2,1)S(1)} %collective-permute-done.refs_2_), channel_id=1, source_target_pairs={{0,1},{1,0},{2,3},{3,2},{4,5},{5,4},{6,7},{7,6},{8,9},{9,8},{10,11... | collective-permute-start | bytes 1572872 | tf_op jit(solution)/shard_map/ppermute | solution.py:420
  21.7 18.9 %copy-start.8 = (bf16[256,1024]{1,0:T(8,128)(2,1)}, bf16[256,1024]{1,0:T(8,128)(2,1)S(1)}, u32[]{:S(2)}) copy-start(bf16[256,1024]{1,0:T(8,128)(2,1)S(1)} %collective-permute-done.4.refs_1_) | copy-start | bytes 1572868
  21.7 9.5 %collective-permute-start.2 = (f32[8,512]{1,0:T(8,128)S(1)}, f32[8,512]{1,0:T(8,128)S(1)}, u32[]{:S(2)}, u32[]{:S(2)}) collective-permute-start(f32[8,512]{1,0:T(8,128)S(1)} %add.19), channel_id=1, source_target_pairs={{0,2},{1,3},{2,0},{3,1},{4,6},{5,7},{6,4},{7,5},{8,10},{9,11},{10,... | collective-permute-start | bytes 49160 | tf_op jit(solution)/shard_map/ppermute | solution.py:420
  31.2 15.2 %collective-permute-start.7 = (bf16[256,1024]{1,0:T(8,128)(2,1)S(1)}, bf16[256,1024]{1,0:T(8,128)(2,1)}, u32[]{:S(2)}, u32[]{:S(2)}) collective-permute-start(bf16[256,1024]{1,0:T(8,128)(2,1)S(1)} %collective-permute-done.6.refs_4_), channel_id=1, source_target_pairs={{0,1},{1,0},{2,3},{3,2},{4,5},{5,4},{6,7},{7,6},{8,9},{9,8},{10,11... | collective-permute-start | bytes 1572872 | tf_op jit(solution)/shard_map/ppermute | solution.py:420
  31.2 8.8 %collective-permute-start.9 = (bf16[128,1024]{1,0:T(8,128)(2,1)S(1)}, bf16[128,1024]{1,0:T(8,128)(2,1)}, u32[]{:S(2)}, u32[]{:S(2)}) collective-permute-start(bf16[128,1024]{1,0:T(8,128)(2,1)S(1)} %slice.42), channel_id=1, source_target_pairs={{0,2},{1,3},{2,0},{3,1},{4,6},{5,7},{6,4},{7,5},{8,10},{9,11},{10,... | collective-permute-start | bytes 786440 | tf_op jit(solution)/shard_map/ppermute | solution.py:420
  40.0 6.4 %collective-permute-start.10 = (bf16[128,1024]{1,0:T(8,128)(2,1)S(1)}, bf16[128,1024]{1,0:T(8,128)(2,1)}, u32[]{:S(2)}, u32[]{:S(2)}) collective-permute-start(bf16[128,1024]{1,0:T(8,128)(2,1)S(1)} %collective-permute-done.8.refs_6_), channel_id=1, source_target_pairs={{0,1},{1,0},{2,3},{3,2},{4,5},{5,4},{6,7},{7,6},{8,9},{9,8},{10,11... | collective-permute-start | bytes 786440 | tf_op jit(solution)/shard_map/ppermute | solution.py:420
  40.0 6.9 %collective-permute-start.11 = (bf16[128,1024]{1,0:T(8,128)(2,1)}, bf16[128,1024]{1,0:T(8,128)(2,1)}, u32[]{:S(2)}, u32[]{:S(2)}) collective-permute-start(bf16[128,1024]{1,0:T(8,128)(2,1)} %collective-permute-done.9.refs_7_), channel_id=1, source_target_pairs={{0,1},{1,0},{2,3},{3,2},{4,5},{5,4},{6,7},{7,6},{8,9},{9,8},{10,11... | collective-permute-start | bytes 786440 | tf_op jit(solution)/shard_map/ppermute | solution.py:420
  40.5 3.8 %collective-permute-start.3 = (f32[8,512]{1,0:T(8,128)S(1)}, f32[8,512]{1,0:T(8,128)S(1)}, u32[]{:S(2)}, u32[]{:S(2)}) collective-permute-start(f32[8,512]{1,0:T(8,128)S(1)} %add.20), channel_id=1, source_target_pairs={{0,4},{1,5},{2,6},{3,7},{4,0},{5,1},{6,2},{7,3},{8,12},{9,13},{10,... | collective-permute-start | bytes 49160 | tf_op jit(solution)/shard_map/ppermute | solution.py:420
  44.3 7.4 %collective-permute-start.17 = (bf16[128,1024]{1,0:T(8,128)(2,1)}, bf16[128,1024]{1,0:T(8,128)(2,1)}, u32[]{:S(2)}, u32[]{:S(2)}) collective-permute-start(bf16[128,1024]{1,0:T(8,128)(2,1)} %slice.44), channel_id=1, source_target_pairs={{0,4},{1,5},{2,6},{3,7},{4,0},{5,1},{6,2},{7,3},{8,12},{9,13},{10,... | collective-permute-start | bytes 786440 | tf_op jit(solution)/shard_map/ppermute | solution.py:420
  45.4 7.1 %collective-permute-start.18 = (bf16[128,1024]{1,0:T(8,128)(2,1)}, bf16[128,1024]{1,0:T(8,128)(2,1)}, u32[]{:S(2)}, u32[]{:S(2)}) collective-permute-start(bf16[128,1024]{1,0:T(8,128)(2,1)} %slice.45), channel_id=1, source_target_pairs={{0,2},{1,3},{2,0},{3,1},{4,6},{5,7},{6,4},{7,5},{8,10},{9,11},{10,... | collective-permute-start | bytes 786440 | tf_op jit(solution)/shard_map/ppermute | solution.py:420
  46.3 22.4 %collective-permute-start.12 = (bf16[256,1024]{1,0:T(8,128)(2,1)S(1)}, bf16[256,1024]{1,0:T(8,128)(2,1)S(1)}, u32[]{:S(2)}, u32[]{:S(2)}) collective-permute-start(bf16[256,1024]{1,0:T(8,128)(2,1)S(1)} %get-tuple-element.25.refs_0_), channel_id=1, source_target_pairs={{0,1},{1,0},{2,3},{3,2},{4,5},{5,4},{6,7},{7,6},{8,9},{9,8},{10,11... | collective-permute-start | bytes 1572872 | tf_op jit(solution)/shard_map/ppermute | solution.py:420
  46.4 23.6 %collective-permute-start.14 = (bf16[256,1024]{1,0:T(8,128)(2,1)S(1)}, bf16[256,1024]{1,0:T(8,128)(2,1)S(1)}, u32[]{:S(2)}, u32[]{:S(2)}) collective-permute-start(bf16[256,1024]{1,0:T(8,128)(2,1)S(1)} %collective-permute-done.13.refs_2_), channel_id=1, source_target_pairs={{0,1},{1,0},{2,3},{3,2},{4,5},{5,4},{6,7},{7,6},{8,9},{9,8},{10,11... | collective-permute-start | bytes 1572872 | tf_op jit(solution)/shard_map/ppermute | solution.py:420
  46.9 24.4 %collective-permute-start.16 = (bf16[256,1024]{1,0:T(8,128)(2,1)S(1)}, bf16[256,1024]{1,0:T(8,128)(2,1)S(1)}, u32[]{:S(2)}, u32[]{:S(2)}) collective-permute-start(bf16[256,1024]{1,0:T(8,128)(2,1)S(1)} %collective-permute-done.15.refs_4_), channel_id=1, source_target_pairs={{0,1},{1,0},{2,3},{3,2},{4,5},{5,4},{6,7},{7,6},{8,9},{9,8},{10,11... | collective-permute-start | bytes 1572872 | tf_op jit(solution)/shard_map/ppermute | solution.py:420
  51.7 21.1 %collective-permute-start.19 = (bf16[128,1024]{1,0:T(8,128)(2,1)}, bf16[128,1024]{1,0:T(8,128)(2,1)S(1)}, u32[]{:S(2)}, u32[]{:S(2)}) collective-permute-start(bf16[128,1024]{1,0:T(8,128)(2,1)} %collective-permute-done.17.refs_6_), channel_id=1, source_target_pairs={{0,1},{1,0},{2,3},{3,2},{4,5},{5,4},{6,7},{7,6},{8,9},{9,8},{10,11... | collective-permute-start | bytes 786440 | tf_op jit(solution)/shard_map/ppermute | solution.py:420
  52.5 20.3 %collective-permute-start.20 = (bf16[128,1024]{1,0:T(8,128)(2,1)}, bf16[128,1024]{1,0:T(8,128)(2,1)S(1)}, u32[]{:S(2)}, u32[]{:S(2)}) collective-permute-start(bf16[128,1024]{1,0:T(8,128)(2,1)} %collective-permute-done.18.refs_7_), channel_id=1, source_target_pairs={{0,1},{1,0},{2,3},{3,2},{4,5},{5,4},{6,7},{7,6},{8,9},{9,8},{10,11... | collective-permute-start | bytes 786440 | tf_op jit(solution)/shard_map/ppermute | solution.py:420
  52.5 3.4 %copy-start = (bf16[8192,512]{1,0:T(8,128)(2,1)S(1)}, bf16[8192,512]{1,0:T(8,128)(2,1)}, u32[]{:S(2)}) copy-start(bf16[8192,512]{1,0:T(8,128)(2,1)} %refs_10_.5) | copy-start | bytes 25165828
  55.9 1.6 %copy-start.2 = (bf16[8192,128]{1,0:T(8,128)(2,1)S(1)}, bf16[8192,128]{1,0:T(8,128)(2,1)}, u32[]{:S(2)}) copy-start(bf16[8192,128]{1,0:T(8,128)(2,1)} %refs_11_.3) | copy-start | bytes 6291460
  57.5 1.6 %copy-start.4 = (bf16[8192,128]{1,0:T(8,128)(2,1)S(1)}, bf16[8192,128]{1,0:T(8,128)(2,1)}, u32[]{:S(2)}) copy-start(bf16[8192,128]{1,0:T(8,128)(2,1)} %refs_12_.3) | copy-start | bytes 6291460
  59.1 1.0 copy-start.9
  60.1 13.4 %copy-start.1 = (bf16[8192,512]{1,0:T(8,128)(2,1)S(1)}, bf16[8192,512]{1,0:T(8,128)(2,1)}, u32[]{:S(2)}) copy-start(bf16[8192,512]{1,0:T(8,128)(2,1)} %refs_10_.5) | copy-start | bytes 25165828
  60.1 13.4 %copy-start.3 = (bf16[8192,128]{1,0:T(8,128)(2,1)S(1)}, bf16[8192,128]{1,0:T(8,128)(2,1)}, u32[]{:S(2)}) copy-start(bf16[8192,128]{1,0:T(8,128)(2,1)} %refs_11_.3) | copy-start | bytes 6291460
  60.1 13.4 %copy-start.5 = (bf16[8192,128]{1,0:T(8,128)(2,1)S(1)}, bf16[8192,128]{1,0:T(8,128)(2,1)}, u32[]{:S(2)}) copy-start(bf16[8192,128]{1,0:T(8,128)(2,1)} %refs_12_.3) | copy-start | bytes 6291460
  68.7 16.6 %collective-permute-start.21 = (bf16[256,256]{1,0:T(8,128)(2,1)S(1)}, bf16[256,256]{1,0:T(8,128)(2,1)S(1)}, u32[]{:S(2)}, u32[]{:S(2)}) collective-permute-start(bf16[256,256]{1,0:T(8,128)(2,1)S(1)} %get-tuple-element.23.refs_0_), channel_id=1, source_target_pairs={{0,8},{8,16},{16,24},{1,9},{9,17},{17,25},{2,10},{10,18},{18,26},{... | collective-permute-start | bytes 393224 | tf_op jit(solution)/shard_map/ppermute | solution.py:425
  70.0 16.7 %collective-permute-start.23 = (bf16[256,256]{1,0:T(8,128)(2,1)S(1)}, bf16[256,256]{1,0:T(8,128)(2,1)S(1)}, u32[]{:S(2)}, u32[]{:S(2)}) collective-permute-start(bf16[256,256]{1,0:T(8,128)(2,1)S(1)} %get-tuple-element.23.refs_0_), channel_id=1, source_target_pairs={{0,16},{8,24},{1,17},{9,25},{2,18},{10,26},{3,19},{11,27},{4,20},{... | collective-permute-start | bytes 393224 | tf_op jit(solution)/shard_map/ppermute | solution.py:425
  71.3 15.4 %collective-permute-start.25 = (bf16[256,256]{1,0:T(8,128)(2,1)S(1)}, bf16[256,256]{1,0:T(8,128)(2,1)S(1)}, u32[]{:S(2)}, u32[]{:S(2)}) collective-permute-start(bf16[256,256]{1,0:T(8,128)(2,1)S(1)} %get-tuple-element.23.refs_0_), channel_id=1, source_target_pairs={{0,24},{1,25},{2,26},{3,27},{4,28},{5,29},{6,30},{7,31}} | collective-permute-start | bytes 393224 | tf_op jit(solution)/shard_map/ppermute | solution.py:425
  72.8 0.7 copy-start.10
  73.5 56.9 %slice-start = ((s8[8388608]{0:T(1024)(128)(4,1)}), s8[4194304]{0:T(1024)(128)(4,1)S(1)}, s32[]{:S(2)}) async-start(s8[8388608]{0:T(1024)(128)(4,1)} %bitcast.2), calls=%async_computation | async-start | bytes 8388608
  73.5 1.1 copy-start.11
  74.6 12.0 %copy-start.14 = (s32[4,128]{1,0:T(4,128)S(1)}, s32[4,128]{1,0:T(4,128)}, u32[]{:S(2)}) copy-start(s32[4,128]{1,0:T(4,128)} %param.13) | copy-start | bytes 6148
  74.6 25.5 %copy-start.13 = (bf16[256,512]{1,0:T(8,128)(2,1)S(1)}, bf16[256,512]{1,0:T(8,128)(2,1)}, u32[]{:S(2)}) copy-start(bf16[256,512]{1,0:T(8,128)(2,1)} %copy-done.12) | copy-start | bytes 786436
  74.6 55.8 %slice-start.1 = ((s8[8388608]{0:T(1024)(128)(4,1)}), s8[4194304]{0:T(1024)(128)(4,1)S(1)}, s32[]{:S(2)}) async-start(s8[8388608]{0:T(1024)(128)(4,1)} %bitcast.2), calls=%async_computation.1 | async-start | bytes 8388608
  82.6 47.9 %copy-start.6 = (bf16[512,1024]{1,0:T(8,128)(2,1)S(1)}, bf16[512,1024]{1,0:T(8,128)(2,1)}, u32[]{:S(2)}) copy-start(bf16[512,1024]{1,0:T(8,128)(2,1)} %t_ref.3) | copy-start | bytes 3145732
  82.6 7.9 %collective-permute-start.22 = (bf16[256,256]{1,0:T(8,128)(2,1)S(1)}, bf16[256,256]{1,0:T(8,128)(2,1)S(1)}, u32[]{:S(2)}, u32[]{:S(2)}) collective-permute-start(bf16[256,256]{1,0:T(8,128)(2,1)S(1)} %get-tuple-element.26.refs_1_), channel_id=1, source_target_pairs={{0,8},{8,16},{16,24},{1,9},{9,17},{17,25},{2,10},{10,18},{18,26},{... | collective-permute-start | bytes 393224 | tf_op jit(solution)/shard_map/ppermute | solution.py:425
  84.0 16.1 %collective-permute-start.24 = (bf16[256,256]{1,0:T(8,128)(2,1)S(1)}, bf16[256,256]{1,0:T(8,128)(2,1)S(1)}, u32[]{:S(2)}, u32[]{:S(2)}) collective-permute-start(bf16[256,256]{1,0:T(8,128)(2,1)S(1)} %get-tuple-element.26.refs_1_), channel_id=1, source_target_pairs={{0,16},{8,24},{1,17},{9,25},{2,18},{10,26},{3,19},{11,27},{4,20},{... | collective-permute-start | bytes 393224 | tf_op jit(solution)/shard_map/ppermute | solution.py:425
  85.3 14.8 %collective-permute-start.26 = (bf16[256,256]{1,0:T(8,128)(2,1)S(1)}, bf16[256,256]{1,0:T(8,128)(2,1)S(1)}, u32[]{:S(2)}, u32[]{:S(2)}) collective-permute-start(bf16[256,256]{1,0:T(8,128)(2,1)S(1)} %get-tuple-element.26.refs_1_), channel_id=1, source_target_pairs={{0,24},{1,25},{2,26},{3,27},{4,28},{5,29},{6,30},{7,31}} | collective-permute-start | bytes 393224 | tf_op jit(solution)/shard_map/ppermute | solution.py:425
  104.4 9.2 %collective-permute-start.28 = (bf16[256,512]{1,0:T(8,128)(2,1)S(1)}, bf16[256,512]{1,0:T(8,128)(2,1)S(1)}, u32[]{:S(2)}, u32[]{:S(2)}) collective-permute-start(bf16[256,512]{1,0:T(8,128)(2,1)S(1)} %attend.2.refs_0_), channel_id=1, source_target_pairs={{0,2},{1,3},{2,0},{3,1},{4,6},{5,7},{6,4},{7,5},{8,10},{9,11},{10,... | collective-permute-start | bytes 786440 | tf_op jit(solution)/shard_map/ppermute | solution.py:420
  105.5 9.1 %collective-permute-start.30 = (bf16[256,512]{1,0:T(8,128)(2,1)S(1)}, bf16[256,512]{1,0:T(8,128)(2,1)S(1)}, u32[]{:S(2)}, u32[]{:S(2)}) collective-permute-start(bf16[256,512]{1,0:T(8,128)(2,1)S(1)} %attend.2.refs_0_), channel_id=1, source_target_pairs={{0,4},{1,5},{2,6},{3,7},{4,0},{5,1},{6,2},{7,3},{8,12},{9,13},{10,... | collective-permute-start | bytes 786440 | tf_op jit(solution)/shard_map/ppermute | solution.py:420
  111.8 7.1 %collective-permute-start.37 = (bf16[256,512]{1,0:T(8,128)(2,1)S(1)}, bf16[256,512]{1,0:T(8,128)(2,1)S(1)}, u32[]{:S(2)}, u32[]{:S(2)}) collective-permute-start(bf16[256,512]{1,0:T(8,128)(2,1)S(1)} %attend.3.refs_0_), channel_id=1, source_target_pairs={{0,2},{1,3},{2,0},{3,1},{4,6},{5,7},{6,4},{7,5},{8,10},{9,11},{10,... | collective-permute-start | bytes 786440 | tf_op jit(solution)/shard_map/ppermute | solution.py:420
  112.4 6.5 %collective-permute-start.27 = (bf16[256,512]{1,0:T(8,128)(2,1)S(1)}, bf16[256,512]{1,0:T(8,128)(2,1)S(1)}, u32[]{:S(2)}, u32[]{:S(2)}) collective-permute-start(bf16[256,512]{1,0:T(8,128)(2,1)S(1)} %attend.2.refs_0_), channel_id=1, source_target_pairs={{0,1},{1,0},{2,3},{3,2},{4,5},{5,4},{6,7},{7,6},{8,9},{9,8},{10,11... | collective-permute-start | bytes 786440 | tf_op jit(solution)/shard_map/ppermute | solution.py:420
  112.4 9.1 %collective-permute-start.39 = (bf16[256,512]{1,0:T(8,128)(2,1)S(1)}, bf16[256,512]{1,0:T(8,128)(2,1)S(1)}, u32[]{:S(2)}, u32[]{:S(2)}) collective-permute-start(bf16[256,512]{1,0:T(8,128)(2,1)S(1)} %attend.3.refs_0_), channel_id=1, source_target_pairs={{0,4},{1,5},{2,6},{3,7},{4,0},{5,1},{6,2},{7,3},{8,12},{9,13},{10,... | collective-permute-start | bytes 786440 | tf_op jit(solution)/shard_map/ppermute | solution.py:420
  113.5 10.8 %collective-permute-start.32 = (bf16[128,512]{1,0:T(8,128)(2,1)S(1)}, bf16[128,512]{1,0:T(8,128)(2,1)S(1)}, u32[]{:S(2)}, u32[]{:S(2)}) collective-permute-start(bf16[128,512]{1,0:T(8,128)(2,1)S(1)} %slice.46), channel_id=1, source_target_pairs={{0,4},{1,5},{2,6},{3,7},{4,0},{5,1},{6,2},{7,3},{8,12},{9,13},{10,... | collective-permute-start | bytes 393224 | tf_op jit(solution)/shard_map/ppermute | solution.py:420
  114.5 14.8 %collective-permute-start.29 = (bf16[256,512]{1,0:T(8,128)(2,1)S(1)}, bf16[256,512]{1,0:T(8,128)(2,1)S(1)}, u32[]{:S(2)}, u32[]{:S(2)}) collective-permute-start(bf16[256,512]{1,0:T(8,128)(2,1)S(1)} %collective-permute-done.28.refs_2_), channel_id=1, source_target_pairs={{0,1},{1,0},{2,3},{3,2},{4,5},{5,4},{6,7},{7,6},{8,9},{9,8},{10,11... | collective-permute-start | bytes 786440 | tf_op jit(solution)/shard_map/ppermute | solution.py:420
  118.9 10.9 %collective-permute-start.31 = (bf16[256,512]{1,0:T(8,128)(2,1)S(1)}, bf16[256,512]{1,0:T(8,128)(2,1)S(1)}, u32[]{:S(2)}, u32[]{:S(2)}) collective-permute-start(bf16[256,512]{1,0:T(8,128)(2,1)S(1)} %collective-permute-done.30.refs_4_), channel_id=1, source_target_pairs={{0,1},{1,0},{2,3},{3,2},{4,5},{5,4},{6,7},{7,6},{8,9},{9,8},{10,11... | collective-permute-start | bytes 786440 | tf_op jit(solution)/shard_map/ppermute | solution.py:420
  119.0 6.9 %collective-permute-start.33 = (bf16[128,512]{1,0:T(8,128)(2,1)S(1)}, bf16[128,512]{1,0:T(8,128)(2,1)S(1)}, u32[]{:S(2)}, u32[]{:S(2)}) collective-permute-start(bf16[128,512]{1,0:T(8,128)(2,1)S(1)} %slice.47), channel_id=1, source_target_pairs={{0,2},{1,3},{2,0},{3,1},{4,6},{5,7},{6,4},{7,5},{8,10},{9,11},{10,... | collective-permute-start | bytes 393224 | tf_op jit(solution)/shard_map/ppermute | solution.py:420
  121.5 5.2 %collective-permute-start.41 = (bf16[128,512]{1,0:T(8,128)(2,1)S(1)}, bf16[128,512]{1,0:T(8,128)(2,1)S(1)}, u32[]{:S(2)}, u32[]{:S(2)}) collective-permute-start(bf16[128,512]{1,0:T(8,128)(2,1)S(1)} %slice.48), channel_id=1, source_target_pairs={{0,4},{1,5},{2,6},{3,7},{4,0},{5,1},{6,2},{7,3},{8,12},{9,13},{10,... | collective-permute-start | bytes 393224 | tf_op jit(solution)/shard_map/ppermute | solution.py:420
  124.3 5.0 %collective-permute-start.42 = (bf16[128,512]{1,0:T(8,128)(2,1)S(1)}, bf16[128,512]{1,0:T(8,128)(2,1)S(1)}, u32[]{:S(2)}, u32[]{:S(2)}) collective-permute-start(bf16[128,512]{1,0:T(8,128)(2,1)S(1)} %slice.49), channel_id=1, source_target_pairs={{0,2},{1,3},{2,0},{3,1},{4,6},{5,7},{6,4},{7,5},{8,10},{9,11},{10,... | collective-permute-start | bytes 393224 | tf_op jit(solution)/shard_map/ppermute | solution.py:420
  125.8 4.1 %collective-permute-start.34 = (bf16[128,512]{1,0:T(8,128)(2,1)S(1)}, bf16[128,512]{1,0:T(8,128)(2,1)S(1)}, u32[]{:S(2)}, u32[]{:S(2)}) collective-permute-start(bf16[128,512]{1,0:T(8,128)(2,1)S(1)} %collective-permute-done.32.refs_6_), channel_id=1, source_target_pairs={{0,1},{1,0},{2,3},{3,2},{4,5},{5,4},{6,7},{7,6},{8,9},{9,8},{10,11... | collective-permute-start | bytes 393224 | tf_op jit(solution)/shard_map/ppermute | solution.py:420
  126.8 3.6 %collective-permute-start.35 = (bf16[128,512]{1,0:T(8,128)(2,1)S(1)}, bf16[128,512]{1,0:T(8,128)(2,1)S(1)}, u32[]{:S(2)}, u32[]{:S(2)}) collective-permute-start(bf16[128,512]{1,0:T(8,128)(2,1)S(1)} %collective-permute-done.33.refs_7_), channel_id=1, source_target_pairs={{0,1},{1,0},{2,3},{3,2},{4,5},{5,4},{6,7},{7,6},{8,9},{9,8},{10,11... | collective-permute-start | bytes 393224 | tf_op jit(solution)/shard_map/ppermute | solution.py:420
  129.3 7.8 %collective-permute-start.36 = (bf16[256,512]{1,0:T(8,128)(2,1)S(1)}, bf16[256,512]{1,0:T(8,128)(2,1)S(1)}, u32[]{:S(2)}, u32[]{:S(2)}) collective-permute-start(bf16[256,512]{1,0:T(8,128)(2,1)S(1)} %attend.3.refs_0_), channel_id=1, source_target_pairs={{0,1},{1,0},{2,3},{3,2},{4,5},{5,4},{6,7},{7,6},{8,9},{9,8},{10,11... | collective-permute-start | bytes 786440 | tf_op jit(solution)/shard_map/ppermute | solution.py:420
  129.3 7.8 %collective-permute-start.38 = (bf16[256,512]{1,0:T(8,128)(2,1)S(1)}, bf16[256,512]{1,0:T(8,128)(2,1)S(1)}, u32[]{:S(2)}, u32[]{:S(2)}) collective-permute-start(bf16[256,512]{1,0:T(8,128)(2,1)S(1)} %collective-permute-done.37.refs_2_), channel_id=1, source_target_pairs={{0,1},{1,0},{2,3},{3,2},{4,5},{5,4},{6,7},{7,6},{8,9},{9,8},{10,11... | collective-permute-start | bytes 786440 | tf_op jit(solution)/shard_map/ppermute | solution.py:420
  129.8 7.3 %collective-permute-start.40 = (bf16[256,512]{1,0:T(8,128)(2,1)S(1)}, bf16[256,512]{1,0:T(8,128)(2,1)S(1)}, u32[]{:S(2)}, u32[]{:S(2)}) collective-permute-start(bf16[256,512]{1,0:T(8,128)(2,1)S(1)} %collective-permute-done.39.refs_4_), channel_id=1, source_target_pairs={{0,1},{1,0},{2,3},{3,2},{4,5},{5,4},{6,7},{7,6},{8,9},{9,8},{10,11... | collective-permute-start | bytes 786440 | tf_op jit(solution)/shard_map/ppermute | solution.py:420
  129.9 7.2 %collective-permute-start.43 = (bf16[128,512]{1,0:T(8,128)(2,1)S(1)}, bf16[128,512]{1,0:T(8,128)(2,1)S(1)}, u32[]{:S(2)}, u32[]{:S(2)}) collective-permute-start(bf16[128,512]{1,0:T(8,128)(2,1)S(1)} %collective-permute-done.41.refs_6_), channel_id=1, source_target_pairs={{0,1},{1,0},{2,3},{3,2},{4,5},{5,4},{6,7},{7,6},{8,9},{9,8},{10,11... | collective-permute-start | bytes 393224 | tf_op jit(solution)/shard_map/ppermute | solution.py:420
  130.3 6.8 %collective-permute-start.44 = (bf16[128,512]{1,0:T(8,128)(2,1)S(1)}, bf16[128,512]{1,0:T(8,128)(2,1)S(1)}, u32[]{:S(2)}, u32[]{:S(2)}) collective-permute-start(bf16[128,512]{1,0:T(8,128)(2,1)S(1)} %collective-permute-done.42.refs_7_), channel_id=1, source_target_pairs={{0,1},{1,0},{2,3},{3,2},{4,5},{5,4},{6,7},{7,6},{8,9},{9,8},{10,11... | collective-permute-start | bytes 393224 | tf_op jit(solution)/shard_map/ppermute | solution.py:420
  143.8 1.3 collective-permute-start.45
  145.2 3.7 %collective-permute-start.46 = (f32[8,512]{1,0:T(8,128)S(1)}, f32[8,512]{1,0:T(8,128)S(1)}, u32[]{:S(2)}, u32[]{:S(2)}) collective-permute-start(f32[8,512]{1,0:T(8,128)S(1)} %add.22), channel_id=1, source_target_pairs={{0,2},{1,3},{2,0},{3,1},{4,6},{5,7},{6,4},{7,5},{8,10},{9,11},{10,... | collective-permute-start | bytes 49160 | tf_op jit(solution)/shard_map/ppermute | solution.py:420
  148.9 3.7 %collective-permute-start.47 = (f32[8,512]{1,0:T(8,128)S(1)}, f32[8,512]{1,0:T(8,128)S(1)}, u32[]{:S(2)}, u32[]{:S(2)}) collective-permute-start(f32[8,512]{1,0:T(8,128)S(1)} %add.23), channel_id=1, source_target_pairs={{0,4},{1,5},{2,6},{3,7},{4,0},{5,1},{6,2},{7,3},{8,12},{9,13},{10,... | collective-permute-start | bytes 49160 | tf_op jit(solution)/shard_map/ppermute | solution.py:420
  (1 other events, 0.7 us)
where the time goes:
time: 154 us
  waiting for transfers between devices  64.5 us (42%)
  Pallas kernels  40.4 us (26%)
  starting transfers between devices  34.4 us (22%)
  local copies, waits for them, and re-layouts  13.6 us (9%)
    ppermute x42, waiting for transfers between devices, swap(): return lax.ppermute(x, 'tp', [(i, i ^ mask) for i in range(count)])  51 us
    ppermute x42, starting transfers between devices, swap(): return lax.ppermute(x, 'tp', [(i, i ^ mask) for i in range(count)])  26.4 us
    pallas_call x2, Pallas kernels, proj(): pl.pallas_call(functools.partial(proj_kernel, counts, joined), in_specs=[...  15.8 us
    ppermute x6, waiting for transfers between devices, send_up(): lax.ppermute(x, 'ctx', [(i, i + distance) for i in range(count - distance)])  13.5 us
    pallas_call x2, Pallas kernels, project_out(): pl.pallas_call(functools.partial(out_kernel, counts, steps), grid=(1,), i...  13.3 us
    unnamed x35, local copies, waits for them, and re-layouts  11.4 us
    pallas_call x2, Pallas kernels, attend(): pl.pallas_call(functools.partial(att_kernel, first, heads, kv_heads, hops...  9.18 us
    ppermute x6, starting transfers between devices, send_up(): lax.ppermute(x, 'ctx', [(i, i + distance) for i in range(count - distance)])  8.05 us
  transfers between devices with their start and end apart: 48, of which 17 were waited for; matrix products, arithmetic and copies ran while one was open for 1% of the time, Pallas kernels for 18%

commit v1 on v0

--- a/solution.py
+++ b/solution.py
@@ -16,6 +16,9 @@
 FAR_BELOW = -1e30
 LOG2E = math.log2(math.e)
 HALVES = 2
+PROJ_MIB = 12
+ATT_MIB = 12
+OUT_MIB = 12
 MIB = 1024 * 1024
 
 
@@ -53,7 +56,7 @@
     for at in range(0, width, GROUP):
         h = h_ref[:, at : at + GROUP].astype(jnp.float32)
         total = total + h * h
-        v = h * g_ref[:, at : at + GROUP].astype(jnp.float32)
+        v = h * g_ref[at // GROUP : at // GROUP + 1, :].astype(jnp.float32)
         c_ref[:, at : at + GROUP] = clip_tile(v).astype(jnp.bfloat16)
     s_ref[...] = to_lanes(jnp.sum(total, axis=-1, keepdims=True))
 
@@ -63,7 +66,7 @@
     return pl.pallas_call(
         pre_kernel,
         grid=(1,),
-        in_specs=[pl.BlockSpec((rows, width), lambda i: (chunk, 0)), whole((1, width))],
+        in_specs=[pl.BlockSpec((rows, width), lambda i: (chunk, 0)), whole(gain.shape)],
         out_specs=[whole((rows, width)), whole((8, rows))],
         out_shape=[
             jax.ShapeDtypeStruct((rows, width), jnp.bfloat16),
@@ -75,73 +78,39 @@
     )(hidden, gain)
 
 
-def proj_kernel(counts, joined, order_ref, ss_ref, *refs):
+def proj_kernel(counts, order_ref, ss_ref, *refs):
     depth = len(counts)
     blocks = refs[: sum(counts)]
-    wq_hbm, wk_hbm, wv_hbm, q_ref, kv_ref, lhs, *rest = refs[sum(counts) :]
-    nq, nk, nv = wq_hbm.shape[1], wk_hbm.shape[1], wv_hbm.shape[1]
-    k_rows = lhs.shape[2]
-    if joined:
-        w_all, acc, wsem, lsem = rest
-    else:
-        wq_all, wk_all, wv_all, accq, acck, accv, wsem, lsem = rest
-
-    def weight_copies(k):
-        at = pl.ds(pl.multiple_of(order_ref[k] * k_rows, k_rows), k_rows)
-        if joined:
-            goals = (
-                w_all.at[k, :, :nq],
-                w_all.at[k, :, nq : nq + nk],
-                w_all.at[k, :, nq + nk : nq + nk + nv],
-            )
-        else:
-            goals = (wq_all.at[k], wk_all.at[k], wv_all.at[k])
-        return [
-            pltpu.make_async_copy(src.at[at], goal, wsem.at[k, i])
-            for i, (src, goal) in enumerate(zip((wq_hbm, wk_hbm, wv_hbm), goals))
-        ]
-
-    copies = []
+    wq_ref, wk_ref, wv_ref, q_ref, kv_ref, accq, acck, accv = refs[sum(counts) :]
+    nk = wk_ref.shape[1]
+    k_rows = blocks[0].shape[1]
     at_block = 0
     for k in range(depth):
-        mine = weight_copies(k)
-        row = 0
-        for p in range(counts[k]):
-            block = blocks[at_block]
-            at_block += 1
-            rows = block.shape[0]
-            mine.append(
-                pltpu.make_async_copy(block, lhs.at[k, row : row + rows], lsem.at[k, p])
+        at = pl.ds(pl.multiple_of(order_ref[k] * k_rows, k_rows), k_rows)
+        mine = [b[...] for b in blocks[at_block : at_block + counts[k]]]
+        at_block += counts[k]
+        left = mine[0] if len(mine) == 1 else jnp.concatenate(mine, axis=0)
+        wq, wk, wv = wq_ref[at, :], wk_ref[at, :], wv_ref[at, :]
+        if nk % 128 == 0:
+            both = jnp.dot(
+                left, jnp.concatenate([wk, wv], axis=1), preferred_element_type=jnp.float32
             )
-            row += rows
-        for copy in mine:
-            copy.start()
-        copies.append(mine)
-    for k in range(depth):
-        for copy in copies[k]:
-            copy.wait()
-        left = lhs[k]
-        if joined:
-            pairs = ((w_all, acc),)
+            parts = (both[:, :nk], both[:, nk:])
         else:
-            pairs = ((wq_all, accq), (wk_all, acck), (wv_all, accv))
-        for w, total in pairs:
-            part = jnp.dot(left, w[k], preferred_element_type=jnp.float32)
+            parts = [jnp.dot(left, w, preferred_element_type=jnp.float32) for w in (wk, wv)]
+        first = jnp.dot(left, wq, preferred_element_type=jnp.float32)
+        for part, acc in zip((first, *parts), (accq, acck, accv)):
             if k == 0:
-                total[...] = part
+                acc[...] = part
             else:
-                total[...] += part
+                acc[...] += part
 
     features = k_rows * depth
     inverse = lax.rsqrt(ss_ref[...] * (1.0 / features) + EPS_IN)
     scale = jnp.transpose(inverse)[:, :1]
-    if joined:
-        q_ref[...] = (acc[:, :nq] * scale).astype(jnp.bfloat16)
-        kv_ref[...] = (acc[:, nq:] * scale).astype(jnp.bfloat16)
-    else:
-        q_ref[...] = (accq[...] * scale).astype(jnp.bfloat16)
-        kv_ref[:, :nk] = (acck[...] * scale).astype(jnp.bfloat16)
-        kv_ref[:, nk:] = (accv[...] * scale).astype(jnp.bfloat16)
+    q_ref[...] = (accq[...] * scale).astype(jnp.bfloat16)
+    kv_ref[:, :nk] = (acck[...] * scale).astype(jnp.bfloat16)
+    kv_ref[:, nk:] = (accv[...] * scale).astype(jnp.bfloat16)
 
 
 def proj(order, blocks, wq, wk, wv, squares):
@@ -151,23 +120,17 @@
     part_cols = blocks[0][0].shape[1]
     nq, nk, nv = wq.shape[1], wk.shape[1], wv.shape[1]
     n = nq + nk + nv
-    joined = nk % 128 == 0
-    sizes = [n] if joined else [nq, nk, nv]
-    scratch = [pltpu.VMEM((depth, rows, part_cols), jnp.bfloat16)]
-    scratch += [pltpu.VMEM((depth, part_cols, m), jnp.bfloat16) for m in sizes]
-    scratch += [pltpu.VMEM((rows, m), jnp.float32) for m in sizes]
-    scratch += [pltpu.SemaphoreType.DMA((depth, 3)), pltpu.SemaphoreType.DMA((depth, 2))]
     flat = [p for b in blocks for p in b]
     return pl.pallas_call(
-        functools.partial(proj_kernel, counts, joined),
-        in_specs=[IN_SMEM, IN_VMEM] + [ANYWHERE] * (len(flat) + 3),
+        functools.partial(proj_kernel, counts),
+        in_specs=[IN_SMEM] + [IN_VMEM] * (len(flat) + 4),
         out_specs=[IN_VMEM, IN_VMEM],
         out_shape=[
             jax.ShapeDtypeStruct((rows, nq), jnp.bfloat16),
             jax.ShapeDtypeStruct((rows, nk + nv), jnp.bfloat16),
         ],
-        scratch_shapes=scratch,
-        compiler_params=params(24),
+        scratch_shapes=[pltpu.VMEM((rows, m), jnp.float32) for m in (nq, nk, nv)],
+        compiler_params=params(PROJ_MIB),
         cost_estimate=cost(
             2 * rows * part_cols * depth * n, 2 * part_cols * depth * (rows + n)
         ),
@@ -175,13 +138,25 @@
     )(order, squares, *flat, wq, wk, wv)
 
 
-def att_kernel(first, heads, kv_heads, hops, pieces, me_ref, q_ref, sign_ref, *refs):
-    kvs = refs[: pieces * (hops + 1)]
-    o_ref, high, total, accum = refs[pieces * (hops + 1) :]
+def att_kernel(first, kv_heads, near, far, begins, ends, me_ref, q_ref, *refs):
+    count = len(near) + len(far)
+    kvs, refs = refs[:count], refs[count:]
+    if not begins:
+        high_in, total_in, accum_in, *refs = refs
+    if ends:
+        sign_ref, o_ref, high, total, accum = refs
+    else:
+        high, total, accum = refs
     rows = q_ref.shape[0]
+    heads = q_ref.shape[1] // HD
     part = kvs[0].shape[0]
     group = heads // kv_heads
     scale = HD ** (-0.5) * LOG2E
+
+    if not begins:
+        high[...] = high_in[...]
+        total[...] = total_in[...]
+        accum[...] = accum_in[...]
 
     def visit(kv_ref, start, fresh):
         masked = start is not None and start + part > first
@@ -221,43 +196,53 @@
                 accum[head] = accum[head] * decay + mixed
             high[head : head + 1] = best
 
-    near = [p for p in range(pieces) if p * part < first + rows]
-    for at, p in enumerate(near):
-        visit(kvs[p], p * part, at == 0)
-    for hop in range(1, hops + 1):
+    for at, start in enumerate(near):
+        visit(kvs[at], start, begins and at == 0)
+    for at, hop in enumerate(far):
 
         @pl.when(me_ref[0] >= hop)
         def _():
-            for p in range(pieces):
-                visit(kvs[hop * pieces + p], None, False)
-
-    for head in range(heads):
-        att = jnp.transpose(accum[head] / total[head : head + 1])
-        att = att.astype(jnp.bfloat16).astype(jnp.float32)
-        o_ref[:, head * HD : (head + 1) * HD] = (att * sign_ref[head : head + 1, :]).astype(
-            jnp.bfloat16
-        )
-
-
-def attend(me, q, first, signs, kvs, pieces, kv_heads):
+            visit(kvs[len(near) + at], None, False)
+
+    if ends:
+        for head in range(heads):
+            att = jnp.transpose(accum[head] / total[head : head + 1])
+            att = att.astype(jnp.bfloat16).astype(jnp.float32)
+            o_ref[:, head * HD : (head + 1) * HD] = (att * sign_ref[head : head + 1, :]).astype(
+                jnp.bfloat16
+            )
+
+
+def attend(me, q, first, kv_heads, near, far, state, signs):
     rows = q.shape[0]
     heads = q.shape[1] // HD
-    hops = len(kvs) // pieces - 1
+    kvs = [kv for _, kv in near + far]
     keys = sum(kv.shape[0] for kv in kvs)
+    shapes = [(max(heads, 8), rows), (max(heads, 8), rows), (heads, HD, rows)]
+    args = [me, q, *kvs]
+    if state is not None:
+        args += list(state)
+    if signs is None:
+        out_shape = [jax.ShapeDtypeStruct(shape, jnp.float32) for shape in shapes]
+        scratch = []
+    else:
+        args.append(signs)
+        out_shape = jax.ShapeDtypeStruct((rows, heads * HD), jnp.bfloat16)
+        scratch = [pltpu.VMEM(shape, jnp.float32) for shape in shapes]
+    near_at, far_at = [n for n, _ in near], [n for n, _ in far]
+    kernel = functools.partial(
+        att_kernel, first, kv_heads, near_at, far_at, state is None, signs is not None
+    )
     return pl.pallas_call(
-        functools.partial(att_kernel, first, heads, kv_heads, hops, pieces),
-        in_specs=[IN_SMEM] + [IN_VMEM] * (len(kvs) + 2),
-        out_specs=IN_VMEM,
-        out_shape=jax.ShapeDtypeStruct((rows, heads * HD), jnp.bfloat16),
-        scratch_shapes=[
-            pltpu.VMEM((max(heads, 8), rows), jnp.float32),
-            pltpu.VMEM((max(heads, 8), rows), jnp.float32),
-            pltpu.VMEM((heads, HD, rows), jnp.float32),
-        ],
-        compiler_params=params(20),
+        kernel,
+        in_specs=[IN_SMEM] + [IN_VMEM] * (len(args) - 1),
+        out_specs=IN_VMEM if signs is not None else [IN_VMEM] * 3,
+        out_shape=out_shape,
+        scratch_shapes=scratch,
+        compiler_params=params(ATT_MIB),
         cost_estimate=cost(4 * rows * keys * heads * HD, 4 * keys * HD, rows * keys * heads),
         name="attend",
-    )(me, q, signs, *kvs)
+    )(*args)
 
 
 def butterfly(tiles):
@@ -274,29 +259,18 @@
     return tiles
 
 
-def out_kernel(counts, steps, sign_ref, t_ref, *refs):
+def out_kernel(counts, steps, chunk, sign_ref, t_ref, *refs):
     parts = len(counts)
     blocks, at_block = [], 0
     for n in counts:
         blocks.append(refs[at_block : at_block + n])
         at_block += n
-    w_hbm, b_ref, s_ref, w_all, mid, rot, acc, wsem = refs[at_block:]
+    w_ref, b_ref, s_ref, mid, rot, acc = refs[at_block:]
     rows = b_ref.shape[0]
     width = blocks[0][0].shape[1]
     here = width // HD
     heads = here * parts
     factor = heads ** (-0.5)
-    depth = w_hbm.shape[0] // steps
-    copies = [
-        pltpu.make_async_copy(
-            w_hbm.at[i * depth : (i + 1) * depth],
-            w_all.at[i * depth : (i + 1) * depth],
-            wsem.at[i],
-        )
-        for i in range(steps)
-    ]
-    for copy in copies:
-        copy.start()
 
     strip = 16
     most = max(counts)
@@ -326,11 +300,11 @@
 
         lax.fori_loop(0, span // strip, turn, 0)
 
+    depth = w_ref.shape[0] // steps
     for i in range(steps):
-        copies[i].wait()
         part = jnp.dot(
             rot[:, i * depth : (i + 1) * depth],
-            w_all[i * depth : (i + 1) * depth, :],
+            w_ref[i * depth : (i + 1) * depth, :],
             preferred_element_type=jnp.float32,
         )
         if i == 0:
@@ -339,7 +313,7 @@
             acc[...] += part
 
     b = acc[...]
-    t = t_ref[...].astype(jnp.float32)
+    t = t_ref[chunk * rows : (chunk + 1) * rows, :].astype(jnp.float32)
     b_ref[...] = b
     sums = [jnp.sum(v, axis=-1, keepdims=True) for v in (b * b, b * t, t * t)]
     lane = lax.broadcasted_iota(jnp.int32, (rows, 128), 1)
@@ -355,24 +329,19 @@
     steps = 4
     flat = [p for b in blocks for p in b]
     return pl.pallas_call(
-        functools.partial(out_kernel, counts, steps),
-        grid=(1,),
-        in_specs=[IN_SMEM, pl.BlockSpec((rows, cols), lambda i: (chunk, 0))]
-        + [whole(p.shape) for p in flat]
-        + [ANYWHERE],
-        out_specs=[whole((rows, cols)), whole((8, rows))],
+        functools.partial(out_kernel, counts, steps, chunk),
+        in_specs=[IN_SMEM] + [IN_VMEM] * (len(flat) + 2),
+        out_specs=[IN_VMEM, IN_VMEM],
         out_shape=[
             jax.ShapeDtypeStruct((rows, cols), jnp.float32),
             jax.ShapeDtypeStruct((8, rows), jnp.float32),
         ],
         scratch_shapes=[
-            pltpu.VMEM((depth, cols), jnp.bfloat16),
             pltpu.VMEM((parts * width // HD, 16, HD), jnp.float32),
             pltpu.VMEM((rows, depth), jnp.bfloat16),
             pltpu.VMEM((rows, cols), jnp.float32),
-            pltpu.SemaphoreType.DMA((steps,)),
         ],
-        compiler_params=params(24),
+        compiler_params=params(OUT_MIB),
         cost_estimate=cost(2 * rows * depth * cols, 2 * depth * (rows + cols) + 6 * rows * cols),
         name="project_out",
     )(flips, teacher, *flat, w_out)
@@ -429,7 +398,7 @@
     return lax.optimization_barrier((x,) + others)[0]
 
 
-def gather(own):
+def gather(own, diagonal_after=None, core_after=None):
     count = lax.axis_size("tp")
     got = {0: [own]}
     masks = [1 << b for b in range(1, count.bit_length() - 1)]
@@ -438,8 +407,15 @@
         half = own.shape[0] // 2
         got[a] = [swap(own, a)]
         got[b] = [swap(own, b)]
-        got[a | b] = [swap(got[a][0][:half], b), swap(got[b][0][half:], a)]
+        via_a, via_b = got[a][0], got[b][0]
+        if diagonal_after is not None:
+            via_a, via_b = after(via_a, diagonal_after), after(via_b, diagonal_after)
+        got[a | b] = [swap(via_a[:half], b), swap(via_b[half:], a)]
         masks = masks[2:]
+    if core_after is not None:
+        for m in got:
+            if m:
+                got[m] = [after(p, core_after) for p in got[m]]
     if count > 1:
         for m in list(got):
             got[m | 1] = [swap(p, 1) for p in got[m]]
@@ -465,27 +441,28 @@
         parity = parity ^ (shared >> bit & 1)
     flips = (1 - 2 * parity).astype(jnp.float32)
     signs = (2 * sign_bits - 1).astype(jnp.float32)
-    gain = norm_gain.reshape(1, -1)
+    gain = norm_gain.reshape(-1, GROUP)
 
     chunks = [pre(hidden_in, gain, i, half) for i in range(HALVES)]
-    gathered = []
-    for clipped, _ in chunks:
-        if gathered:
-            clipped = after(clipped, *[b[0] for b in gathered[-1][2:6:2]])
-        gathered.append(gather(clipped))
+    clipped = [c for c, _ in chunks]
     squares = jnp.concatenate([s for _, s in chunks], axis=1)
-    if tp_count > 2:
-        squares = after(squares, gathered[0][2][0])
-    for bit in range(tp_count.bit_length() - 1):
-        squares = squares + swap(squares, 1 << bit)
 
     kv_cols = w_key.shape[1]
     sharing = HD // kv_cols if kv_cols < HD else 1
     kv_heads = kv_cols * sharing // HD
     queries, kvs = [], []
     for at in range(HALVES):
+        own = clipped[at]
+        if at:
+            own = after(own, *[b[0] for b in blocks[2:6:2]])
+        blocks = gather(own, diagonal_after=queries[-1] if at else None)
+        if not at:
+            if tp_count > 1:
+                squares = after(squares, blocks[1][0])
+            for bit in range(tp_count.bit_length() - 1):
+                squares = squares + swap(squares, 1 << bit)
         part = squares[:, at * half : (at + 1) * half]
-        q, kv = proj(order, gathered[at], w_query, w_key, w_value, part)
+        q, kv = proj(order, blocks, w_query, w_key, w_value, part)
         if sharing > 1:
             k, v = kv[:, :kv_cols], kv[:, kv_cols:]
             for bit in range(sharing.bit_length() - 1):
@@ -502,12 +479,22 @@
             kv = jnp.concatenate([k, v], axis=1)
         queries.append(q)
         kvs.append([kv] + [send_up(kv, hop) for hop in range(1, ctx_count)])
-    kvs = [kvs[p][hop] for hop in range(ctx_count) for p in range(HALVES)]
-
+
+    states = []
+    for at in range(HALVES):
+        near = [(p * half, kvs[p][0]) for p in range(at + 1)]
+        far = [(hop, kvs[p][hop]) for p in range(HALVES - 1) for hop in range(1, ctx_count)]
+        states.append(
+            attend(ctx_at, queries[at], at * half, kv_heads, near, far, None, None)
+        )
     branches, stats = [], []
     for at in range(HALVES):
-        signed = attend(ctx_at, queries[at], at * half, signs, kvs, HALVES, kv_heads)
-        b, s = project_out(flips, gather(signed), w_out, teacher, at)
+        far = [(hop, kvs[HALVES - 1][hop]) for hop in range(1, ctx_count)]
+        signed = attend(
+            ctx_at, queries[at], at * half, kv_heads, [], far, states[at], signs
+        )
+        blocks = gather(signed, core_after=branches[-1] if at else None)
+        b, s = project_out(flips, blocks, w_out, teacher, at)
         branches.append(b)
         stats.append(s)
     stat = jnp.concatenate(stats, axis=1)

time: 154 us -> 144 us (0.935)
  waiting for transfers between devices: 64.5 us -> 56.7 us
  Pallas kernels: 40.4 us -> 33.3 us
  local copies, waits for them, and re-layouts: 13.6 us -> 18 us
    pallas_call x6 -> x8, Pallas kernels: 38.3 us -> 31.2 us  [the longest x2 11.9 us: project_out(): pl.pallas_call(functools.partial(out_kernel, counts, steps, chunk), in_sp...]
    unnamed x35 -> x33, local copies, waits for them, and re-layouts: 11.4 us -> 17.2 us
    ppermute x6, waiting for transfers between devices: 13.5 us -> 9.33 us  [send_up(): lax.ppermute(x, 'ctx', [(i, i + distance) for i in range(count - distance)])]
    ppermute x42, waiting for transfers between devices: 51 us -> 47.3 us  [swap(): return lax.ppermute(x, 'tp', [(i, i ^ mask) for i in range(count)])]
  transfers between devices with their start and end apart: 48 -> 48, of which waited for: 17 -> 19; matrix products, arithmetic and copies ran while one was open for 1% -> 1% of each run, Pallas kernels for 18% -> 16%
where the time goes in v1:
time: 144 us; the launch traced here: 143 us
  waiting for transfers between devices  56.7 us (39%)
  starting transfers between devices  34.1 us (24%)
  Pallas kernels  33.3 us (23%)
  local copies, waits for them, and re-layouts  18 us (12%)
    ppermute x42, waiting for transfers between devices, swap(): return lax.ppermute(x, 'tp', [(i, i ^ mask) for i in range(count)])  47.3 us
    ppermute x42, starting transfers between devices, swap(): return lax.ppermute(x, 'tp', [(i, i ^ mask) for i in range(count)])  26.2 us
    unnamed x33, local copies, waits for them, and re-layouts  17.2 us
    pallas_call x2, Pallas kernels, project_out(): pl.pallas_call(functools.partial(out_kernel, counts, steps, chunk), in_sp...  11.9 us
    pallas_call x4, Pallas kernels, attend(): pl.pallas_call(kernel, in_specs=[IN_SMEM] + [IN_VMEM] * (len(args) - 1),...  10.2 us
    ppermute x6, waiting for transfers between devices, send_up(): lax.ppermute(x, 'ctx', [(i, i + distance) for i in range(count - distance)])  9.33 us
    pallas_call x2, Pallas kernels, proj(): pl.pallas_call(functools.partial(proj_kernel, counts), in_specs=[IN_SMEM]...  9.05 us
    ppermute x6, starting transfers between devices, send_up(): lax.ppermute(x, 'ctx', [(i, i + distance) for i in range(count - distance)])  7.87 us
  transfers between devices with their start and end apart: 48, of which 19 were waited for; matrix products, arithmetic and copies ran while one was open for 1% of the time, Pallas kernels for 16%

profile of v1, /device:TPU:24, one launch (start us, length us, event | category | flops | bytes accessed | tf_op | source)
XLA Modules:
  0.0 143.1 jit_solution(4688443395780122681)
XLA Ops:
  0.6 1.2 copy-done.9
  1.9 0.7 copy-done.11
  3.0 1.5 %collective-permute-start.4 = (bf16[256,1024]{1,0:T(8,128)(2,1)S(1)}, bf16[256,1024]{1,0:T(8,128)(2,1)S(1)}, u32[]{:S(2)}, u32[]{:S(2)}) collective-permute-start(bf16[256,1024]{1,0:T(8,128)(2,1)S(1)} %get-tuple-element.32.refs_0_), channel_id=1, source_target_pairs={{0,2},{1,3},{2,0},{3,1},{4,6},{5,7},{6,4},{7,5},{8,10},{9,11},{10,... | collective-permute-start | bytes 1572872 | tf_op jit(solution)/shard_map/ppermute | solution.py:389
  4.5 1.5 %collective-permute-start.6 = (bf16[256,1024]{1,0:T(8,128)(2,1)S(1)}, bf16[256,1024]{1,0:T(8,128)(2,1)S(1)}, u32[]{:S(2)}, u32[]{:S(2)}) collective-permute-start(bf16[256,1024]{1,0:T(8,128)(2,1)S(1)} %get-tuple-element.32.refs_0_), channel_id=1, source_target_pairs={{0,4},{1,5},{2,6},{3,7},{4,0},{5,1},{6,2},{7,3},{8,12},{9,13},{10,... | collective-permute-start | bytes 1572872 | tf_op jit(solution)/shard_map/ppermute | solution.py:389
  6.0 10.6 %collective-permute-done.4.refs_2_ = bf16[256,1024]{1,0:T(8,128)(2,1)S(1)} collective-permute-done((bf16[256,1024]{1,0:T(8,128)(2,1)S(1)}, bf16[256,1024]{1,0:T(8,128)(2,1)S(1)}, u32[]{:S(2)}, u32[]{:S(2)}) %collective-permute-start.4) | collective-permute-done | bytes 524320 | tf_op jit(solution)/shard_map/ppermute | solution.py:389
  16.7 1.6 %collective-permute-start.8 = (bf16[128,1024]{1,0:T(8,128)(2,1)S(1)}, bf16[128,1024]{1,0:T(8,128)(2,1)S(1)}, u32[]{:S(2)}, u32[]{:S(2)}) collective-permute-start(bf16[128,1024]{1,0:T(8,128)(2,1)S(1)} %slice.41), channel_id=1, source_target_pairs={{0,4},{1,5},{2,6},{3,7},{4,0},{5,1},{6,2},{7,3},{8,12},{9,13},{10,... | collective-permute-start | bytes 786440 | tf_op jit(solution)/shard_map/ppermute | solution.py:389
  18.3 0.7 slice.42
  19.0 1.5 %collective-permute-start.9 = (bf16[128,1024]{1,0:T(8,128)(2,1)}, bf16[128,1024]{1,0:T(8,128)(2,1)}, u32[]{:S(2)}, u32[]{:S(2)}) collective-permute-start(bf16[128,1024]{1,0:T(8,128)(2,1)} %slice.42), channel_id=1, source_target_pairs={{0,2},{1,3},{2,0},{3,1},{4,6},{5,7},{6,4},{7,5},{8,10},{9,11},{10,... | collective-permute-start | bytes 786440 | tf_op jit(solution)/shard_map/ppermute | solution.py:389
  20.5 0.5 collective-permute-start.7
  21.0 2.9 %collective-permute-done.8.refs_6_ = bf16[128,1024]{1,0:T(8,128)(2,1)S(1)} collective-permute-done((bf16[128,1024]{1,0:T(8,128)(2,1)S(1)}, bf16[128,1024]{1,0:T(8,128)(2,1)S(1)}, u32[]{:S(2)}, u32[]{:S(2)}) %collective-permute-start.8) | collective-permute-done | bytes 262176 | tf_op jit(solution)/shard_map/ppermute | solution.py:389
  23.9 1.2 copy-done.10
  25.2 0.7 copy-done.12
  26.3 0.6 collective-permute-start.1
  26.9 0.8 collective-permute-done.1
  27.7 1.5 %collective-permute-start.2 = (f32[8,512]{1,0:T(8,128)S(1)}, f32[8,512]{1,0:T(8,128)S(1)}, u32[]{:S(2)}, u32[]{:S(2)}) collective-permute-start(f32[8,512]{1,0:T(8,128)S(1)} %add.19), channel_id=1, source_target_pairs={{0,2},{1,3},{2,0},{3,1},{4,6},{5,7},{6,4},{7,5},{8,10},{9,11},{10,... | collective-permute-start | bytes 49160 | tf_op jit(solution)/shard_map/ppermute | solution.py:389
  29.2 2.2 %collective-permute-done.2 = f32[8,512]{1,0:T(8,128)S(1)} collective-permute-done((f32[8,512]{1,0:T(8,128)S(1)}, f32[8,512]{1,0:T(8,128)S(1)}, u32[]{:S(2)}, u32[]{:S(2)}) %collective-permute-start.2) | collective-permute-done | bytes 16416 | tf_op jit(solution)/shard_map/ppermute | solution.py:389
  31.4 1.5 %collective-permute-start.3 = (f32[8,512]{1,0:T(8,128)S(1)}, f32[8,512]{1,0:T(8,128)S(1)}, u32[]{:S(2)}, u32[]{:S(2)}) collective-permute-start(f32[8,512]{1,0:T(8,128)S(1)} %add.20), channel_id=1, source_target_pairs={{0,4},{1,5},{2,6},{3,7},{4,0},{5,1},{6,2},{7,3},{8,12},{9,13},{10,... | collective-permute-start | bytes 49160 | tf_op jit(solution)/shard_map/ppermute | solution.py:389
  33.0 2.2 %collective-permute-done.3 = f32[8,512]{1,0:T(8,128)S(1)} collective-permute-done((f32[8,512]{1,0:T(8,128)S(1)}, f32[8,512]{1,0:T(8,128)S(1)}, u32[]{:S(2)}, u32[]{:S(2)}) %collective-permute-start.3) | collective-permute-done | bytes 16416 | tf_op jit(solution)/shard_map/ppermute | solution.py:389
  35.2 1.5 %collective-permute-start.15 = (bf16[256,1024]{1,0:T(8,128)(2,1)S(1)}, bf16[256,1024]{1,0:T(8,128)(2,1)S(1)}, u32[]{:S(2)}, u32[]{:S(2)}) collective-permute-start(bf16[256,1024]{1,0:T(8,128)(2,1)S(1)} %get-tuple-element.36.refs_0_), channel_id=1, source_target_pairs={{0,4},{1,5},{2,6},{3,7},{4,0},{5,1},{6,2},{7,3},{8,12},{9,13},{10,... | collective-permute-start | bytes 1572872 | tf_op jit(solution)/shard_map/ppermute | solution.py:389
  36.7 1.6 %collective-permute-start.13 = (bf16[256,1024]{1,0:T(8,128)(2,1)S(1)}, bf16[256,1024]{1,0:T(8,128)(2,1)S(1)}, u32[]{:S(2)}, u32[]{:S(2)}) collective-permute-start(bf16[256,1024]{1,0:T(8,128)(2,1)S(1)} %get-tuple-element.36.refs_0_), channel_id=1, source_target_pairs={{0,2},{1,3},{2,0},{3,1},{4,6},{5,7},{6,4},{7,5},{8,10},{9,11},{10,... | collective-permute-start | bytes 1572872 | tf_op jit(solution)/shard_map/ppermute | solution.py:389
  38.3 3.4 %copy-done = bf16[8192,512]{1,0:T(8,128)(2,1)S(1)} copy-done((bf16[8192,512]{1,0:T(8,128)(2,1)S(1)}, bf16[8192,512]{1,0:T(8,128)(2,1)}, u32[]{:S(2)}) %copy-start) | copy-done | bytes 8388632
  41.7 1.6 %copy-done.4 = bf16[8192,128]{1,0:T(8,128)(2,1)S(1)} copy-done((bf16[8192,128]{1,0:T(8,128)(2,1)S(1)}, bf16[8192,128]{1,0:T(8,128)(2,1)}, u32[]{:S(2)}) %copy-start.4) | copy-done | bytes 2097176
  43.3 1.6 %copy-done.6 = bf16[8192,128]{1,0:T(8,128)(2,1)S(1)} copy-done((bf16[8192,128]{1,0:T(8,128)(2,1)S(1)}, bf16[8192,128]{1,0:T(8,128)(2,1)}, u32[]{:S(2)}) %copy-start.6) | copy-done | bytes 2097176
  44.9 4.9 %proj.2 = (bf16[256,512]{1,0:T(8,128)(2,1)S(1)}, bf16[256,256]{1,0:T(8,128)(2,1)S(1)}) custom-call(s32[8]{0:T(128)S(1)} %iota_xor_fusion.order_ref, f32[8,256]{1,0:T(8,128)S(1)} %get-tuple-element.59.ss_ref, bf16[256,1024]{1,0:T(8,128)(2,1)S(1)} %get-tuple-element.32.refs_0_, bf16[256,1024]{1,0:T(8,128)(2,1)S(1)} %collective-permute-done.refs_1_, ...), custom_call_target="tpu_custom_call" | custom-call | flops 3221225472 | bytes 16777216 | tf_op jit(solution)/shard_map/proj/pallas_call | solution.py:124
  49.9 0.6 collective-permute-start.18
  51.0 0.6 collective-permute-start.17
  51.6 7.1 %collective-permute-done.18.refs_7_ = bf16[128,1024]{1,0:T(8,128)(2,1)S(1)} collective-permute-done((bf16[128,1024]{1,0:T(8,128)(2,1)S(1)}, bf16[128,1024]{1,0:T(8,128)(2,1)S(1)}, u32[]{:S(2)}, u32[]{:S(2)}) %collective-permute-start.18) | collective-permute-done | bytes 262176 | tf_op jit(solution)/shard_map/ppermute | solution.py:389
  58.6 0.9 collective-permute-done.17.refs_6_
  59.5 1.3 collective-permute-start.24
  60.8 1.3 collective-permute-start.25
  62.1 1.3 collective-permute-start.26
  63.5 4.1 %proj.3 = (bf16[256,512]{1,0:T(8,128)(2,1)S(1)}, bf16[256,256]{1,0:T(8,128)(2,1)S(1)}) custom-call(s32[8]{0:T(128)S(1)} %iota_xor_fusion.order_ref, f32[8,256]{1,0:T(8,128)S(1)} %get-tuple-element.58.ss_ref, bf16[256,1024]{1,0:T(8,128)(2,1)S(1)} %get-tuple-element.36.refs_0_, bf16[256,1024]{1,0:T(8,128)(2,1)S(1)} %collective-permute-done.12.refs_1_, ...), custom_call_target="tpu_custom_call" | custom-call | flops 3221225472 | bytes 16777216 | tf_op jit(solution)/shard_map/proj/pallas_call | solution.py:124
  67.6 1.4 collective-permute-start.21
  69.0 1.3 collective-permute-start.22
  70.4 1.3 collective-permute-start.23
  71.7 4.3 %collective-permute-done.25.refs_2_.refs_3_ = bf16[256,256]{1,0:T(8,128)(2,1)S(1)} collective-permute-done((bf16[256,256]{1,0:T(8,128)(2,1)S(1)}, bf16[256,256]{1,0:T(8,128)(2,1)S(1)}, u32[]{:S(2)}, u32[]{:S(2)}) %collective-permute-start.25) | collective-permute-done | bytes 131104 | tf_op jit(solution)/shard_map/ppermute | solution.py:394
  76.0 2.6 %attend.4 = (f32[8,256]{1,0:T(8,128)S(1)}, f32[8,256]{1,0:T(8,128)S(1)}, f32[4,128,256]{2,1,0:T(8,128)S(1)}) custom-call(s32[1]{0:T(128)} %bitcast.me_ref, bf16[256,512]{1,0:T(8,128)(2,1)S(1)} %copy-done.14, bf16[256,256]{1,0:T(8,128)(2,1)S(1)} %get-tuple-element.40.refs_0_, bf16[256,256]{1,0:T(8,128)(2,1)S(1)} %collective-permute-done.24.refs_1_.refs_2_, ...), custom_call_target="tpu_custom_call" | custom-call | flops 536870912 | bytes 524288 | tf_op jit(solution)/shard_map/attend/pallas_call | solution.py:236
  78.6 3.3 %attend.6 = (f32[8,256]{1,0:T(8,128)S(1)}, f32[8,256]{1,0:T(8,128)S(1)}, f32[4,128,256]{2,1,0:T(8,128)S(1)}) custom-call(s32[1]{0:T(128)} %bitcast.me_ref, bf16[256,512]{1,0:T(8,128)(2,1)S(1)} %get-tuple-element.45.q_ref, bf16[256,256]{1,0:T(8,128)(2,1)S(1)} %get-tuple-element.40.refs_0_, bf16[256,256]{1,0:T(8,128)(2,1)S(1)} %get-tuple-element.39.refs_1_, ...), custom_call_target="tpu_custom_call" | custom-call | flops 671088640 | bytes 655360 | tf_op jit(solution)/shard_map/attend/pallas_call | solution.py:236
  81.9 5.0 %collective-permute-done.22.refs_1_ = bf16[256,256]{1,0:T(8,128)(2,1)S(1)} collective-permute-done((bf16[256,256]{1,0:T(8,128)(2,1)S(1)}, bf16[256,256]{1,0:T(8,128)(2,1)S(1)}, u32[]{:S(2)}, u32[]{:S(2)}) %collective-permute-start.22) | collective-permute-done | bytes 131104 | tf_op jit(solution)/shard_map/ppermute | solution.py:394
  86.9 2.2 %attend.5.refs_0_ = bf16[256,512]{1,0:T(8,128)(2,1)S(1)} custom-call(s32[1]{0:T(128)} %bitcast.me_ref, bf16[256,512]{1,0:T(8,128)(2,1)S(1)} %copy-done.14, bf16[256,256]{1,0:T(8,128)(2,1)S(1)} %collective-permute-done.21.refs_0_, bf16[256,256]{1,0:T(8,128)(2,1)S(1)} %collective-permute-done.22.refs_1_, bf16[256,256]{1,0:T(8,128)(2,1)S(1)} %collective-permute-done.23.refs_2_, ...), custom_call_target="tpu_custom_call" | custom-call | flops 402653184 | bytes 393216 | tf_op jit(solution)/shard_map/attend/pallas_call | solution.py:236
  89.0 1.6 %collective-permute-start.28 = (bf16[256,512]{1,0:T(8,128)(2,1)S(1)}, bf16[256,512]{1,0:T(8,128)(2,1)S(1)}, u32[]{:S(2)}, u32[]{:S(2)}) collective-permute-start(bf16[256,512]{1,0:T(8,128)(2,1)S(1)} %attend.5.refs_0_), channel_id=1, source_target_pairs={{0,2},{1,3},{2,0},{3,1},{4,6},{5,7},{6,4},{7,5},{8,10},{9,11},{10,... | collective-permute-start | bytes 786440 | tf_op jit(solution)/shard_map/ppermute | solution.py:389
  90.6 0.5 collective-permute-start.30
  91.1 2.2 %attend.7.refs_0_ = bf16[256,512]{1,0:T(8,128)(2,1)S(1)} custom-call(s32[1]{0:T(128)} %bitcast.me_ref, bf16[256,512]{1,0:T(8,128)(2,1)S(1)} %get-tuple-element.45.q_ref, bf16[256,256]{1,0:T(8,128)(2,1)S(1)} %collective-permute-done.21.refs_0_, bf16[256,256]{1,0:T(8,128)(2,1)S(1)} %collective-permute-done.22.refs_1_, ...), custom_call_target="tpu_custom_call" | custom-call | flops 402653184 | bytes 393216 | tf_op jit(solution)/shard_map/attend/pallas_call | solution.py:236
  93.3 1.6 %collective-permute-start.39 = (bf16[256,512]{1,0:T(8,128)(2,1)S(1)}, bf16[256,512]{1,0:T(8,128)(2,1)S(1)}, u32[]{:S(2)}, u32[]{:S(2)}) collective-permute-start(bf16[256,512]{1,0:T(8,128)(2,1)S(1)} %attend.7.refs_0_), channel_id=1, source_target_pairs={{0,4},{1,5},{2,6},{3,7},{4,0},{5,1},{6,2},{7,3},{8,12},{9,13},{10,... | collective-permute-start | bytes 786440 | tf_op jit(solution)/shard_map/ppermute | solution.py:389
  94.9 0.5 collective-permute-start.37
  95.4 2.3 %collective-permute-done.28.refs_2_ = bf16[256,512]{1,0:T(8,128)(2,1)S(1)} collective-permute-done((bf16[256,512]{1,0:T(8,128)(2,1)S(1)}, bf16[256,512]{1,0:T(8,128)(2,1)S(1)}, u32[]{:S(2)}, u32[]{:S(2)}) %collective-permute-start.28) | collective-permute-done | bytes 262176 | tf_op jit(solution)/shard_map/ppermute | solution.py:389
  97.8 2.1 %collective-permute-done.30.refs_4_ = bf16[256,512]{1,0:T(8,128)(2,1)S(1)} collective-permute-done((bf16[256,512]{1,0:T(8,128)(2,1)S(1)}, bf16[256,512]{1,0:T(8,128)(2,1)S(1)}, u32[]{:S(2)}, u32[]{:S(2)}) %collective-permute-start.30) | collective-permute-done | bytes 262176 | tf_op jit(solution)/shard_map/ppermute | solution.py:389
  99.9 3.9 %collective-permute-done.39.refs_4_ = bf16[256,512]{1,0:T(8,128)(2,1)S(1)} collective-permute-done((bf16[256,512]{1,0:T(8,128)(2,1)S(1)}, bf16[256,512]{1,0:T(8,128)(2,1)S(1)}, u32[]{:S(2)}, u32[]{:S(2)}) %collective-permute-start.39) | collective-permute-done | bytes 262176 | tf_op jit(solution)/shard_map/ppermute | solution.py:389
  104.4 0.5 collective-permute-start.33
  104.9 3.9 %collective-permute-done.32.refs_6_ = bf16[128,512]{1,0:T(8,128)(2,1)S(1)} collective-permute-done((bf16[128,512]{1,0:T(8,128)(2,1)S(1)}, bf16[128,512]{1,0:T(8,128)(2,1)S(1)}, u32[]{:S(2)}, u32[]{:S(2)}) %collective-permute-start.32) | collective-permute-done | bytes 131104 | tf_op jit(solution)/shard_map/ppermute | solution.py:389
  109.4 0.6 collective-permute-start.36
  110.0 0.5 collective-permute-start.42
  110.5 1.5 %collective-permute-start.41 = (bf16[128,512]{1,0:T(8,128)(2,1)S(1)}, bf16[128,512]{1,0:T(8,128)(2,1)S(1)}, u32[]{:S(2)}, u32[]{:S(2)}) collective-permute-start(bf16[128,512]{1,0:T(8,128)(2,1)S(1)} %slice.46), channel_id=1, source_target_pairs={{0,4},{1,5},{2,6},{3,7},{4,0},{5,1},{6,2},{7,3},{8,12},{9,13},{10,... | collective-permute-start | bytes 393224 | tf_op jit(solution)/shard_map/ppermute | solution.py:389
  112.1 3.4 %copy-done.2 = bf16[4096,1024]{1,0:T(8,128)(2,1)S(1)} copy-done((bf16[4096,1024]{1,0:T(8,128)(2,1)S(1)}, bf16[4096,1024]{1,0:T(8,128)(2,1)}, u32[]{:S(2)}) %copy-start.2) | copy-done | bytes 8388632
  115.4 6.0 %project_out.2 = (f32[256,1024]{1,0:T(8,128)S(1)}, f32[8,256]{1,0:T(8,128)S(1)}) custom-call(f32[8]{0:T(128)S(1)} %subtract_convert_fusion.sign_ref, bf16[512,1024]{1,0:T(8,128)(2,1)S(1)} %copy-done.8, bf16[256,512]{1,0:T(8,128)(2,1)S(1)} %attend.5.refs_0_, bf16[256,512]{1,0:T(8,128)(2,1)S(1)} %collective-permute-done.27.refs_1_, ...), custom_call_target="tpu_custom_call" | custom-call | flops 2147483648 | bytes 12058624 | tf_op jit(solution)/shard_map/project_out/pallas_call | solution.py:331
  122.5 1.1 collective-permute-done.44.refs_9_
  123.8 3.4 %copy-done.3 = bf16[4096,1024]{1,0:T(8,128)(2,1)S(1)} copy-done((bf16[4096,1024]{1,0:T(8,128)(2,1)S(1)}, bf16[4096,1024]{1,0:T(8,128)(2,1)}, u32[]{:S(2)}) %copy-start.3) | copy-done | bytes 8388632
  127.1 6.0 %project_out.3 = (f32[256,1024]{1,0:T(8,128)S(1)}, f32[8,256]{1,0:T(8,128)S(1)}) custom-call(f32[8]{0:T(128)S(1)} %subtract_convert_fusion.sign_ref, bf16[512,1024]{1,0:T(8,128)(2,1)S(1)} %copy-done.8, bf16[256,512]{1,0:T(8,128)(2,1)S(1)} %attend.7.refs_0_, bf16[256,512]{1,0:T(8,128)(2,1)S(1)} %collective-permute-done.36.refs_1_, ...), custom_call_target="tpu_custom_call" | custom-call | flops 2147483648 | bytes 12058624 | tf_op jit(solution)/shard_map/project_out/pallas_call | solution.py:331
  133.3 1.0 collective-permute-done.45
  134.4 1.5 %collective-permute-start.46 = (f32[8,512]{1,0:T(8,128)S(1)}, f32[8,512]{1,0:T(8,128)S(1)}, u32[]{:S(2)}, u32[]{:S(2)}) collective-permute-start(f32[8,512]{1,0:T(8,128)S(1)} %add.22), channel_id=1, source_target_pairs={{0,2},{1,3},{2,0},{3,1},{4,6},{5,7},{6,4},{7,5},{8,10},{9,11},{10,... | collective-permute-start | bytes 49160 | tf_op jit(solution)/shard_map/ppermute | solution.py:389
  135.8 2.2 %collective-permute-done.46 = f32[8,512]{1,0:T(8,128)S(1)} collective-permute-done((f32[8,512]{1,0:T(8,128)S(1)}, f32[8,512]{1,0:T(8,128)S(1)}, u32[]{:S(2)}, u32[]{:S(2)}) %collective-permute-start.46) | collective-permute-done | bytes 16416 | tf_op jit(solution)/shard_map/ppermute | solution.py:389
  138.1 0.5 collective-permute-start.47
  138.6 3.2 %collective-permute-done.47 = f32[8,512]{1,0:T(8,128)S(1)} collective-permute-done((f32[8,512]{1,0:T(8,128)S(1)}, f32[8,512]{1,0:T(8,128)S(1)}, u32[]{:S(2)}, u32[]{:S(2)}) %collective-permute-start.47) | collective-permute-done | bytes 16416 | tf_op jit(solution)/shard_map/ppermute | solution.py:389
  141.8 1.3 final.1
  (96 shorter events, 4.3 us)
Async XLA Ops:
  0.6 1.2 copy-start.9
  1.9 0.7 copy-start.11
  3.0 13.7 %collective-permute-start.4 = (bf16[256,1024]{1,0:T(8,128)(2,1)S(1)}, bf16[256,1024]{1,0:T(8,128)(2,1)S(1)}, u32[]{:S(2)}, u32[]{:S(2)}) collective-permute-start(bf16[256,1024]{1,0:T(8,128)(2,1)S(1)} %get-tuple-element.32.refs_0_), channel_id=1, source_target_pairs={{0,2},{1,3},{2,0},{3,1},{4,6},{5,7},{6,4},{7,5},{8,10},{9,11},{10,... | collective-permute-start | bytes 1572872 | tf_op jit(solution)/shard_map/ppermute | solution.py:389
  4.5 13.8 %collective-permute-start.6 = (bf16[256,1024]{1,0:T(8,128)(2,1)S(1)}, bf16[256,1024]{1,0:T(8,128)(2,1)S(1)}, u32[]{:S(2)}, u32[]{:S(2)}) collective-permute-start(bf16[256,1024]{1,0:T(8,128)(2,1)S(1)} %get-tuple-element.32.refs_0_), channel_id=1, source_target_pairs={{0,4},{1,5},{2,6},{3,7},{4,0},{5,1},{6,2},{7,3},{8,12},{9,13},{10,... | collective-permute-start | bytes 1572872 | tf_op jit(solution)/shard_map/ppermute | solution.py:389
  6.0 20.3 %collective-permute-start = (bf16[256,1024]{1,0:T(8,128)(2,1)S(1)}, bf16[256,1024]{1,0:T(8,128)(2,1)S(1)}, u32[]{:S(2)}, u32[]{:S(2)}) collective-permute-start(bf16[256,1024]{1,0:T(8,128)(2,1)S(1)} %get-tuple-element.32.refs_0_), channel_id=1, source_target_pairs={{0,1},{1,0},{2,3},{3,2},{4,5},{5,4},{6,7},{7,6},{8,9},{9,8},{10,11... | collective-permute-start | bytes 1572872 | tf_op jit(solution)/shard_map/ppermute | solution.py:389
  16.7 7.2 %collective-permute-start.8 = (bf16[128,1024]{1,0:T(8,128)(2,1)S(1)}, bf16[128,1024]{1,0:T(8,128)(2,1)S(1)}, u32[]{:S(2)}, u32[]{:S(2)}) collective-permute-start(bf16[128,1024]{1,0:T(8,128)(2,1)S(1)} %slice.41), channel_id=1, source_target_pairs={{0,4},{1,5},{2,6},{3,7},{4,0},{5,1},{6,2},{7,3},{8,12},{9,13},{10,... | collective-permute-start | bytes 786440 | tf_op jit(solution)/shard_map/ppermute | solution.py:389
  19.0 14.0 %collective-permute-start.9 = (bf16[128,1024]{1,0:T(8,128)(2,1)}, bf16[128,1024]{1,0:T(8,128)(2,1)}, u32[]{:S(2)}, u32[]{:S(2)}) collective-permute-start(bf16[128,1024]{1,0:T(8,128)(2,1)} %slice.42), channel_id=1, source_target_pairs={{0,2},{1,3},{2,0},{3,1},{4,6},{5,7},{6,4},{7,5},{8,10},{9,11},{10,... | collective-permute-start | bytes 786440 | tf_op jit(solution)/shard_map/ppermute | solution.py:389
  20.5 17.8 %collective-permute-start.5 = (bf16[256,1024]{1,0:T(8,128)(2,1)S(1)}, bf16[256,1024]{1,0:T(8,128)(2,1)S(1)}, u32[]{:S(2)}, u32[]{:S(2)}) collective-permute-start(bf16[256,1024]{1,0:T(8,128)(2,1)S(1)} %collective-permute-done.4.refs_2_), channel_id=1, source_target_pairs={{0,1},{1,0},{2,3},{3,2},{4,5},{5,4},{6,7},{7,6},{8,9},{9,8},{10,11... | collective-permute-start | bytes 1572872 | tf_op jit(solution)/shard_map/ppermute | solution.py:389
  20.5 17.8 %collective-permute-start.7 = (bf16[256,1024]{1,0:T(8,128)(2,1)S(1)}, bf16[256,1024]{1,0:T(8,128)(2,1)}, u32[]{:S(2)}, u32[]{:S(2)}) collective-permute-start(bf16[256,1024]{1,0:T(8,128)(2,1)S(1)} %collective-permute-done.6.refs_4_), channel_id=1, source_target_pairs={{0,1},{1,0},{2,3},{3,2},{4,5},{5,4},{6,7},{7,6},{8,9},{9,8},{10,11... | collective-permute-start | bytes 1572872 | tf_op jit(solution)/shard_map/ppermute | solution.py:389
  23.9 12.8 %collective-permute-start.10 = (bf16[128,1024]{1,0:T(8,128)(2,1)S(1)}, bf16[128,1024]{1,0:T(8,128)(2,1)}, u32[]{:S(2)}, u32[]{:S(2)}) collective-permute-start(bf16[128,1024]{1,0:T(8,128)(2,1)S(1)} %collective-permute-done.8.refs_6_), channel_id=1, source_target_pairs={{0,1},{1,0},{2,3},{3,2},{4,5},{5,4},{6,7},{7,6},{8,9},{9,8},{10,11... | collective-permute-start | bytes 786440 | tf_op jit(solution)/shard_map/ppermute | solution.py:389
  23.9 1.2 copy-start.10
  25.2 0.7 copy-start.12
  26.3 1.4 collective-permute-start.1
  27.7 3.7 %collective-permute-start.2 = (f32[8,512]{1,0:T(8,128)S(1)}, f32[8,512]{1,0:T(8,128)S(1)}, u32[]{:S(2)}, u32[]{:S(2)}) collective-permute-start(f32[8,512]{1,0:T(8,128)S(1)} %add.19), channel_id=1, source_target_pairs={{0,2},{1,3},{2,0},{3,1},{4,6},{5,7},{6,4},{7,5},{8,10},{9,11},{10,... | collective-permute-start | bytes 49160 | tf_op jit(solution)/shard_map/ppermute | solution.py:389
  31.4 3.7 %collective-permute-start.3 = (f32[8,512]{1,0:T(8,128)S(1)}, f32[8,512]{1,0:T(8,128)S(1)}, u32[]{:S(2)}, u32[]{:S(2)}) collective-permute-start(f32[8,512]{1,0:T(8,128)S(1)} %add.20), channel_id=1, source_target_pairs={{0,4},{1,5},{2,6},{3,7},{4,0},{5,1},{6,2},{7,3},{8,12},{9,13},{10,... | collective-permute-start | bytes 49160 | tf_op jit(solution)/shard_map/ppermute | solution.py:389
  33.0 5.3 %collective-permute-start.11 = (bf16[128,1024]{1,0:T(8,128)(2,1)}, bf16[128,1024]{1,0:T(8,128)(2,1)S(1)}, u32[]{:S(2)}, u32[]{:S(2)}) collective-permute-start(bf16[128,1024]{1,0:T(8,128)(2,1)} %collective-permute-done.9.refs_7_), channel_id=1, source_target_pairs={{0,1},{1,0},{2,3},{3,2},{4,5},{5,4},{6,7},{7,6},{8,9},{9,8},{10,11... | collective-permute-start | bytes 786440 | tf_op jit(solution)/shard_map/ppermute | solution.py:389
  35.2 14.7 %collective-permute-start.15 = (bf16[256,1024]{1,0:T(8,128)(2,1)S(1)}, bf16[256,1024]{1,0:T(8,128)(2,1)S(1)}, u32[]{:S(2)}, u32[]{:S(2)}) collective-permute-start(bf16[256,1024]{1,0:T(8,128)(2,1)S(1)} %get-tuple-element.36.refs_0_), channel_id=1, source_target_pairs={{0,4},{1,5},{2,6},{3,7},{4,0},{5,1},{6,2},{7,3},{8,12},{9,13},{10,... | collective-permute-start | bytes 1572872 | tf_op jit(solution)/shard_map/ppermute | solution.py:389
  36.7 13.8 %collective-permute-start.13 = (bf16[256,1024]{1,0:T(8,128)(2,1)S(1)}, bf16[256,1024]{1,0:T(8,128)(2,1)S(1)}, u32[]{:S(2)}, u32[]{:S(2)}) collective-permute-start(bf16[256,1024]{1,0:T(8,128)(2,1)S(1)} %get-tuple-element.36.refs_0_), channel_id=1, source_target_pairs={{0,2},{1,3},{2,0},{3,1},{4,6},{5,7},{6,4},{7,5},{8,10},{9,11},{10,... | collective-permute-start | bytes 1572872 | tf_op jit(solution)/shard_map/ppermute | solution.py:389
  38.3 21.2 %collective-permute-start.12 = (bf16[256,1024]{1,0:T(8,128)(2,1)S(1)}, bf16[256,1024]{1,0:T(8,128)(2,1)S(1)}, u32[]{:S(2)}, u32[]{:S(2)}) collective-permute-start(bf16[256,1024]{1,0:T(8,128)(2,1)S(1)} %get-tuple-element.36.refs_0_), channel_id=1, source_target_pairs={{0,1},{1,0},{2,3},{3,2},{4,5},{5,4},{6,7},{7,6},{8,9},{9,8},{10,11... | collective-permute-start | bytes 1572872 | tf_op jit(solution)/shard_map/ppermute | solution.py:389
  38.3 3.4 %copy-start = (bf16[8192,512]{1,0:T(8,128)(2,1)S(1)}, bf16[8192,512]{1,0:T(8,128)(2,1)}, u32[]{:S(2)}) copy-start(bf16[8192,512]{1,0:T(8,128)(2,1)} %refs_10_.5) | copy-start | bytes 25165828
  41.7 1.6 %copy-start.4 = (bf16[8192,128]{1,0:T(8,128)(2,1)S(1)}, bf16[8192,128]{1,0:T(8,128)(2,1)}, u32[]{:S(2)}) copy-start(bf16[8192,128]{1,0:T(8,128)(2,1)} %refs_11_.3) | copy-start | bytes 6291460
  43.3 1.6 %copy-start.6 = (bf16[8192,128]{1,0:T(8,128)(2,1)S(1)}, bf16[8192,128]{1,0:T(8,128)(2,1)}, u32[]{:S(2)}) copy-start(bf16[8192,128]{1,0:T(8,128)(2,1)} %refs_12_.3) | copy-start | bytes 6291460
  44.9 18.6 %copy-start.1 = (bf16[8192,512]{1,0:T(8,128)(2,1)S(1)}, bf16[8192,512]{1,0:T(8,128)(2,1)}, u32[]{:S(2)}) copy-start(bf16[8192,512]{1,0:T(8,128)(2,1)} %refs_10_.5) | copy-start | bytes 25165828
  44.9 18.6 %copy-start.5 = (bf16[8192,128]{1,0:T(8,128)(2,1)S(1)}, bf16[8192,128]{1,0:T(8,128)(2,1)}, u32[]{:S(2)}) copy-start(bf16[8192,128]{1,0:T(8,128)(2,1)} %refs_11_.3) | copy-start | bytes 6291460
  44.9 18.6 %copy-start.7 = (bf16[8192,128]{1,0:T(8,128)(2,1)S(1)}, bf16[8192,128]{1,0:T(8,128)(2,1)}, u32[]{:S(2)}) copy-start(bf16[8192,128]{1,0:T(8,128)(2,1)} %refs_12_.3) | copy-start | bytes 6291460
  49.8 13.6 %copy-start.13 = (bf16[256,512]{1,0:T(8,128)(2,1)}, bf16[256,512]{1,0:T(8,128)(2,1)S(1)}, u32[]{:S(2)}) copy-start(bf16[256,512]{1,0:T(8,128)(2,1)S(1)} %get-tuple-element.34.q_ref) | copy-start | bytes 786436
  49.9 8.8 %collective-permute-start.18 = (bf16[128,1024]{1,0:T(8,128)(2,1)S(1)}, bf16[128,1024]{1,0:T(8,128)(2,1)S(1)}, u32[]{:S(2)}, u32[]{:S(2)}) collective-permute-start(bf16[128,1024]{1,0:T(8,128)(2,1)S(1)} %slice.35), channel_id=1, source_target_pairs={{0,2},{1,3},{2,0},{3,1},{4,6},{5,7},{6,4},{7,5},{8,10},{9,11},{10,... | collective-permute-start | bytes 786440 | tf_op jit(solution)/shard_map/ppermute | solution.py:389
  50.5 10.3 %collective-permute-start.14 = (bf16[256,1024]{1,0:T(8,128)(2,1)S(1)}, bf16[256,1024]{1,0:T(8,128)(2,1)S(1)}, u32[]{:S(2)}, u32[]{:S(2)}) collective-permute-start(bf16[256,1024]{1,0:T(8,128)(2,1)S(1)} %collective-permute-done.13.refs_2_), channel_id=1, source_target_pairs={{0,1},{1,0},{2,3},{3,2},{4,5},{5,4},{6,7},{7,6},{8,9},{9,8},{10,11... | collective-permute-start | bytes 1572872 | tf_op jit(solution)/shard_map/ppermute | solution.py:389
  50.7 11.4 %collective-permute-start.16 = (bf16[256,1024]{1,0:T(8,128)(2,1)S(1)}, bf16[256,1024]{1,0:T(8,128)(2,1)S(1)}, u32[]{:S(2)}, u32[]{:S(2)}) collective-permute-start(bf16[256,1024]{1,0:T(8,128)(2,1)S(1)} %collective-permute-done.15.refs_4_), channel_id=1, source_target_pairs={{0,1},{1,0},{2,3},{3,2},{4,5},{5,4},{6,7},{7,6},{8,9},{9,8},{10,11... | collective-permute-start | bytes 1572872 | tf_op jit(solution)/shard_map/ppermute | solution.py:389
  51.0 8.5 %collective-permute-start.17 = (bf16[128,1024]{1,0:T(8,128)(2,1)S(1)}, bf16[128,1024]{1,0:T(8,128)(2,1)S(1)}, u32[]{:S(2)}, u32[]{:S(2)}) collective-permute-start(bf16[128,1024]{1,0:T(8,128)(2,1)S(1)} %slice.34), channel_id=1, source_target_pairs={{0,4},{1,5},{2,6},{3,7},{4,0},{5,1},{6,2},{7,3},{8,12},{9,13},{10,... | collective-permute-start | bytes 786440 | tf_op jit(solution)/shard_map/ppermute | solution.py:389
  58.6 4.8 %collective-permute-start.20 = (bf16[128,1024]{1,0:T(8,128)(2,1)S(1)}, bf16[128,1024]{1,0:T(8,128)(2,1)S(1)}, u32[]{:S(2)}, u32[]{:S(2)}) collective-permute-start(bf16[128,1024]{1,0:T(8,128)(2,1)S(1)} %collective-permute-done.18.refs_7_), channel_id=1, source_target_pairs={{0,1},{1,0},{2,3},{3,2},{4,5},{5,4},{6,7},{7,6},{8,9},{9,8},{10,11... | collective-permute-start | bytes 786440 | tf_op jit(solution)/shard_map/ppermute | solution.py:389
  59.5 3.9 %collective-permute-start.19 = (bf16[128,1024]{1,0:T(8,128)(2,1)S(1)}, bf16[128,1024]{1,0:T(8,128)(2,1)S(1)}, u32[]{:S(2)}, u32[]{:S(2)}) collective-permute-start(bf16[128,1024]{1,0:T(8,128)(2,1)S(1)} %collective-permute-done.17.refs_6_), channel_id=1, source_target_pairs={{0,1},{1,0},{2,3},{3,2},{4,5},{5,4},{6,7},{7,6},{8,9},{9,8},{10,11... | collective-permute-start | bytes 786440 | tf_op jit(solution)/shard_map/ppermute | solution.py:389
  59.5 10.9 %collective-permute-start.24 = (bf16[256,256]{1,0:T(8,128)(2,1)S(1)}, bf16[256,256]{1,0:T(8,128)(2,1)S(1)}, u32[]{:S(2)}, u32[]{:S(2)}) collective-permute-start(bf16[256,256]{1,0:T(8,128)(2,1)S(1)} %get-tuple-element.40.refs_0_), channel_id=1, source_target_pairs={{0,8},{8,16},{16,24},{1,9},{9,17},{17,25},{2,10},{10,18},{18,26},{... | collective-permute-start | bytes 393224 | tf_op jit(solution)/shard_map/ppermute | solution.py:394
  60.8 15.2 %collective-permute-start.25 = (bf16[256,256]{1,0:T(8,128)(2,1)S(1)}, bf16[256,256]{1,0:T(8,128)(2,1)S(1)}, u32[]{:S(2)}, u32[]{:S(2)}) collective-permute-start(bf16[256,256]{1,0:T(8,128)(2,1)S(1)} %get-tuple-element.40.refs_0_), channel_id=1, source_target_pairs={{0,16},{8,24},{1,17},{9,25},{2,18},{10,26},{3,19},{11,27},{4,20},{... | collective-permute-start | bytes 393224 | tf_op jit(solution)/shard_map/ppermute | solution.py:394
  62.1 13.9 %collective-permute-start.26 = (bf16[256,256]{1,0:T(8,128)(2,1)S(1)}, bf16[256,256]{1,0:T(8,128)(2,1)S(1)}, u32[]{:S(2)}, u32[]{:S(2)}) collective-permute-start(bf16[256,256]{1,0:T(8,128)(2,1)S(1)} %get-tuple-element.40.refs_0_), channel_id=1, source_target_pairs={{0,24},{1,25},{2,26},{3,27},{4,28},{5,29},{6,30},{7,31}} | collective-permute-start | bytes 393224 | tf_op jit(solution)/shard_map/ppermute | solution.py:394
  63.5 8.2 %copy-start.15 = (s32[4,128]{1,0:T(4,128)S(1)}, s32[4,128]{1,0:T(4,128)}, u32[]{:S(2)}) copy-start(s32[4,128]{1,0:T(4,128)} %param.13) | copy-start | bytes 6148
  63.5 12.6 %copy-start.14 = (bf16[256,512]{1,0:T(8,128)(2,1)S(1)}, bf16[256,512]{1,0:T(8,128)(2,1)}, u32[]{:S(2)}) copy-start(bf16[256,512]{1,0:T(8,128)(2,1)} %copy-done.13) | copy-start | bytes 786436
  67.6 44.5 %copy-start.8 = (bf16[512,1024]{1,0:T(8,128)(2,1)S(1)}, bf16[512,1024]{1,0:T(8,128)(2,1)}, u32[]{:S(2)}) copy-start(bf16[512,1024]{1,0:T(8,128)(2,1)} %t_ref.3) | copy-start | bytes 3145732
  67.6 14.3 %collective-permute-start.21 = (bf16[256,256]{1,0:T(8,128)(2,1)S(1)}, bf16[256,256]{1,0:T(8,128)(2,1)S(1)}, u32[]{:S(2)}, u32[]{:S(2)}) collective-permute-start(bf16[256,256]{1,0:T(8,128)(2,1)S(1)} %get-tuple-element.39.refs_1_), channel_id=1, source_target_pairs={{0,8},{8,16},{16,24},{1,9},{9,17},{17,25},{2,10},{10,18},{18,26},{... | collective-permute-start | bytes 393224 | tf_op jit(solution)/shard_map/ppermute | solution.py:394
  69.0 17.8 %collective-permute-start.22 = (bf16[256,256]{1,0:T(8,128)(2,1)S(1)}, bf16[256,256]{1,0:T(8,128)(2,1)S(1)}, u32[]{:S(2)}, u32[]{:S(2)}) collective-permute-start(bf16[256,256]{1,0:T(8,128)(2,1)S(1)} %get-tuple-element.39.refs_1_), channel_id=1, source_target_pairs={{0,16},{8,24},{1,17},{9,25},{2,18},{10,26},{3,19},{11,27},{4,20},{... | collective-permute-start | bytes 393224 | tf_op jit(solution)/shard_map/ppermute | solution.py:394
  70.4 16.5 %collective-permute-start.23 = (bf16[256,256]{1,0:T(8,128)(2,1)S(1)}, bf16[256,256]{1,0:T(8,128)(2,1)S(1)}, u32[]{:S(2)}, u32[]{:S(2)}) collective-permute-start(bf16[256,256]{1,0:T(8,128)(2,1)S(1)} %get-tuple-element.39.refs_1_), channel_id=1, source_target_pairs={{0,24},{1,25},{2,26},{3,27},{4,28},{5,29},{6,30},{7,31}} | collective-permute-start | bytes 393224 | tf_op jit(solution)/shard_map/ppermute | solution.py:394
  89.0 8.6 %collective-permute-start.28 = (bf16[256,512]{1,0:T(8,128)(2,1)S(1)}, bf16[256,512]{1,0:T(8,128)(2,1)S(1)}, u32[]{:S(2)}, u32[]{:S(2)}) collective-permute-start(bf16[256,512]{1,0:T(8,128)(2,1)S(1)} %attend.5.refs_0_), channel_id=1, source_target_pairs={{0,2},{1,3},{2,0},{3,1},{4,6},{5,7},{6,4},{7,5},{8,10},{9,11},{10,... | collective-permute-start | bytes 786440 | tf_op jit(solution)/shard_map/ppermute | solution.py:389
  90.6 9.2 %collective-permute-start.30 = (bf16[256,512]{1,0:T(8,128)(2,1)S(1)}, bf16[256,512]{1,0:T(8,128)(2,1)S(1)}, u32[]{:S(2)}, u32[]{:S(2)}) collective-permute-start(bf16[256,512]{1,0:T(8,128)(2,1)S(1)} %attend.5.refs_0_), channel_id=1, source_target_pairs={{0,4},{1,5},{2,6},{3,7},{4,0},{5,1},{6,2},{7,3},{8,12},{9,13},{10,... | collective-permute-start | bytes 786440 | tf_op jit(solution)/shard_map/ppermute | solution.py:389
  93.3 10.6 %collective-permute-start.39 = (bf16[256,512]{1,0:T(8,128)(2,1)S(1)}, bf16[256,512]{1,0:T(8,128)(2,1)S(1)}, u32[]{:S(2)}, u32[]{:S(2)}) collective-permute-start(bf16[256,512]{1,0:T(8,128)(2,1)S(1)} %attend.7.refs_0_), channel_id=1, source_target_pairs={{0,4},{1,5},{2,6},{3,7},{4,0},{5,1},{6,2},{7,3},{8,12},{9,13},{10,... | collective-permute-start | bytes 786440 | tf_op jit(solution)/shard_map/ppermute | solution.py:389
  94.9 9.5 %collective-permute-start.37 = (bf16[256,512]{1,0:T(8,128)(2,1)S(1)}, bf16[256,512]{1,0:T(8,128)(2,1)S(1)}, u32[]{:S(2)}, u32[]{:S(2)}) collective-permute-start(bf16[256,512]{1,0:T(8,128)(2,1)S(1)} %attend.7.refs_0_), channel_id=1, source_target_pairs={{0,2},{1,3},{2,0},{3,1},{4,6},{5,7},{6,4},{7,5},{8,10},{9,11},{10,... | collective-permute-start | bytes 786440 | tf_op jit(solution)/shard_map/ppermute | solution.py:389
  95.4 14.0 %collective-permute-start.27 = (bf16[256,512]{1,0:T(8,128)(2,1)S(1)}, bf16[256,512]{1,0:T(8,128)(2,1)S(1)}, u32[]{:S(2)}, u32[]{:S(2)}) collective-permute-start(bf16[256,512]{1,0:T(8,128)(2,1)S(1)} %attend.5.refs_0_), channel_id=1, source_target_pairs={{0,1},{1,0},{2,3},{3,2},{4,5},{5,4},{6,7},{7,6},{8,9},{9,8},{10,11... | collective-permute-start | bytes 786440 | tf_op jit(solution)/shard_map/ppermute | solution.py:389
  97.7 12.3 %collective-permute-start.29 = (bf16[256,512]{1,0:T(8,128)(2,1)S(1)}, bf16[256,512]{1,0:T(8,128)(2,1)S(1)}, u32[]{:S(2)}, u32[]{:S(2)}) collective-permute-start(bf16[256,512]{1,0:T(8,128)(2,1)S(1)} %collective-permute-done.28.refs_2_), channel_id=1, source_target_pairs={{0,1},{1,0},{2,3},{3,2},{4,5},{5,4},{6,7},{7,6},{8,9},{9,8},{10,11... | collective-permute-start | bytes 786440 | tf_op jit(solution)/shard_map/ppermute | solution.py:389
  99.9 10.7 %collective-permute-start.31 = (bf16[256,512]{1,0:T(8,128)(2,1)S(1)}, bf16[256,512]{1,0:T(8,128)(2,1)S(1)}, u32[]{:S(2)}, u32[]{:S(2)}) collective-permute-start(bf16[256,512]{1,0:T(8,128)(2,1)S(1)} %collective-permute-done.30.refs_4_), channel_id=1, source_target_pairs={{0,1},{1,0},{2,3},{3,2},{4,5},{5,4},{6,7},{7,6},{8,9},{9,8},{10,11... | collective-permute-start | bytes 786440 | tf_op jit(solution)/shard_map/ppermute | solution.py:389
  103.9 5.0 %collective-permute-start.32 = (bf16[128,512]{1,0:T(8,128)(2,1)S(1)}, bf16[128,512]{1,0:T(8,128)(2,1)S(1)}, u32[]{:S(2)}, u32[]{:S(2)}) collective-permute-start(bf16[128,512]{1,0:T(8,128)(2,1)S(1)} %slice.44), channel_id=1, source_target_pairs={{0,4},{1,5},{2,6},{3,7},{4,0},{5,1},{6,2},{7,3},{8,12},{9,13},{10,... | collective-permute-start | bytes 393224 | tf_op jit(solution)/shard_map/ppermute | solution.py:389
  104.4 5.0 %collective-permute-start.33 = (bf16[128,512]{1,0:T(8,128)(2,1)S(1)}, bf16[128,512]{1,0:T(8,128)(2,1)S(1)}, u32[]{:S(2)}, u32[]{:S(2)}) collective-permute-start(bf16[128,512]{1,0:T(8,128)(2,1)S(1)} %slice.45), channel_id=1, source_target_pairs={{0,2},{1,3},{2,0},{3,1},{4,6},{5,7},{6,4},{7,5},{8,10},{9,11},{10,... | collective-permute-start | bytes 393224 | tf_op jit(solution)/shard_map/ppermute | solution.py:389
  108.9 3.2 %collective-permute-start.34 = (bf16[128,512]{1,0:T(8,128)(2,1)S(1)}, bf16[128,512]{1,0:T(8,128)(2,1)S(1)}, u32[]{:S(2)}, u32[]{:S(2)}) collective-permute-start(bf16[128,512]{1,0:T(8,128)(2,1)S(1)} %collective-permute-done.32.refs_6_), channel_id=1, source_target_pairs={{0,1},{1,0},{2,3},{3,2},{4,5},{5,4},{6,7},{7,6},{8,9},{9,8},{10,11... | collective-permute-start | bytes 393224 | tf_op jit(solution)/shard_map/ppermute | solution.py:389
  109.4 2.7 %collective-permute-start.35 = (bf16[128,512]{1,0:T(8,128)(2,1)S(1)}, bf16[128,512]{1,0:T(8,128)(2,1)S(1)}, u32[]{:S(2)}, u32[]{:S(2)}) collective-permute-start(bf16[128,512]{1,0:T(8,128)(2,1)S(1)} %collective-permute-done.33.refs_7_), channel_id=1, source_target_pairs={{0,1},{1,0},{2,3},{3,2},{4,5},{5,4},{6,7},{7,6},{8,9},{9,8},{10,11... | collective-permute-start | bytes 393224 | tf_op jit(solution)/shard_map/ppermute | solution.py:389
  109.4 13.1 %collective-permute-start.36 = (bf16[256,512]{1,0:T(8,128)(2,1)S(1)}, bf16[256,512]{1,0:T(8,128)(2,1)S(1)}, u32[]{:S(2)}, u32[]{:S(2)}) collective-permute-start(bf16[256,512]{1,0:T(8,128)(2,1)S(1)} %attend.7.refs_0_), channel_id=1, source_target_pairs={{0,1},{1,0},{2,3},{3,2},{4,5},{5,4},{6,7},{7,6},{8,9},{9,8},{10,11... | collective-permute-start | bytes 786440 | tf_op jit(solution)/shard_map/ppermute | solution.py:389
  110.0 12.0 %collective-permute-start.42 = (bf16[128,512]{1,0:T(8,128)(2,1)S(1)}, bf16[128,512]{1,0:T(8,128)(2,1)S(1)}, u32[]{:S(2)}, u32[]{:S(2)}) collective-permute-start(bf16[128,512]{1,0:T(8,128)(2,1)S(1)} %slice.47), channel_id=1, source_target_pairs={{0,2},{1,3},{2,0},{3,1},{4,6},{5,7},{6,4},{7,5},{8,10},{9,11},{10,... | collective-permute-start | bytes 393224 | tf_op jit(solution)/shard_map/ppermute | solution.py:389
  110.5 11.5 %collective-permute-start.41 = (bf16[128,512]{1,0:T(8,128)(2,1)S(1)}, bf16[128,512]{1,0:T(8,128)(2,1)S(1)}, u32[]{:S(2)}, u32[]{:S(2)}) collective-permute-start(bf16[128,512]{1,0:T(8,128)(2,1)S(1)} %slice.46), channel_id=1, source_target_pairs={{0,4},{1,5},{2,6},{3,7},{4,0},{5,1},{6,2},{7,3},{8,12},{9,13},{10,... | collective-permute-start | bytes 393224 | tf_op jit(solution)/shard_map/ppermute | solution.py:389
  112.1 3.4 %copy-start.2 = (bf16[4096,1024]{1,0:T(8,128)(2,1)S(1)}, bf16[4096,1024]{1,0:T(8,128)(2,1)}, u32[]{:S(2)}) copy-start(bf16[4096,1024]{1,0:T(8,128)(2,1)} %refs_10_.7) | copy-start | bytes 25165828
  121.4 2.3 %collective-permute-start.40 = (bf16[256,512]{1,0:T(8,128)(2,1)S(1)}, bf16[256,512]{1,0:T(8,128)(2,1)S(1)}, u32[]{:S(2)}, u32[]{:S(2)}) collective-permute-start(bf16[256,512]{1,0:T(8,128)(2,1)S(1)} %collective-permute-done.39.refs_4_), channel_id=1, source_target_pairs={{0,1},{1,0},{2,3},{3,2},{4,5},{5,4},{6,7},{7,6},{8,9},{9,8},{10,11... | collective-permute-start | bytes 786440 | tf_op jit(solution)/shard_map/ppermute | solution.py:389
  121.5 2.3 %collective-permute-start.38 = (bf16[256,512]{1,0:T(8,128)(2,1)S(1)}, bf16[256,512]{1,0:T(8,128)(2,1)S(1)}, u32[]{:S(2)}, u32[]{:S(2)}) collective-permute-start(bf16[256,512]{1,0:T(8,128)(2,1)S(1)} %collective-permute-done.37.refs_2_), channel_id=1, source_target_pairs={{0,1},{1,0},{2,3},{3,2},{4,5},{5,4},{6,7},{7,6},{8,9},{9,8},{10,11... | collective-permute-start | bytes 786440 | tf_op jit(solution)/shard_map/ppermute | solution.py:389
  122.0 1.6 %collective-permute-start.44 = (bf16[128,512]{1,0:T(8,128)(2,1)S(1)}, bf16[128,512]{1,0:T(8,128)(2,1)S(1)}, u32[]{:S(2)}, u32[]{:S(2)}) collective-permute-start(bf16[128,512]{1,0:T(8,128)(2,1)S(1)} %collective-permute-done.42.refs_7_), channel_id=1, source_target_pairs={{0,1},{1,0},{2,3},{3,2},{4,5},{5,4},{6,7},{7,6},{8,9},{9,8},{10,11... | collective-permute-start | bytes 393224 | tf_op jit(solution)/shard_map/ppermute | solution.py:389
  122.1 1.7 %collective-permute-start.43 = (bf16[128,512]{1,0:T(8,128)(2,1)S(1)}, bf16[128,512]{1,0:T(8,128)(2,1)S(1)}, u32[]{:S(2)}, u32[]{:S(2)}) collective-permute-start(bf16[128,512]{1,0:T(8,128)(2,1)S(1)} %collective-permute-done.41.refs_6_), channel_id=1, source_target_pairs={{0,1},{1,0},{2,3},{3,2},{4,5},{5,4},{6,7},{7,6},{8,9},{9,8},{10,11... | collective-permute-start | bytes 393224 | tf_op jit(solution)/shard_map/ppermute | solution.py:389
  123.8 3.4 %copy-start.3 = (bf16[4096,1024]{1,0:T(8,128)(2,1)S(1)}, bf16[4096,1024]{1,0:T(8,128)(2,1)}, u32[]{:S(2)}) copy-start(bf16[4096,1024]{1,0:T(8,128)(2,1)} %refs_10_.7) | copy-start | bytes 25165828
  133.1 1.2 collective-permute-start.45
  134.4 3.7 %collective-permute-start.46 = (f32[8,512]{1,0:T(8,128)S(1)}, f32[8,512]{1,0:T(8,128)S(1)}, u32[]{:S(2)}, u32[]{:S(2)}) collective-permute-start(f32[8,512]{1,0:T(8,128)S(1)} %add.22), channel_id=1, source_target_pairs={{0,2},{1,3},{2,0},{3,1},{4,6},{5,7},{6,4},{7,5},{8,10},{9,11},{10,... | collective-permute-start | bytes 49160 | tf_op jit(solution)/shard_map/ppermute | solution.py:389
  138.1 3.7 %collective-permute-start.47 = (f32[8,512]{1,0:T(8,128)S(1)}, f32[8,512]{1,0:T(8,128)S(1)}, u32[]{:S(2)}, u32[]{:S(2)}) collective-permute-start(f32[8,512]{1,0:T(8,128)S(1)} %add.23), channel_id=1, source_target_pairs={{0,4},{1,5},{2,6},{3,7},{4,0},{5,1},{6,2},{7,3},{8,12},{9,13},{10,... | collective-permute-start | bytes 49160 | tf_op jit(solution)/shard_map/ppermute | solution.py:389

commit v2 on v1

--- a/solution.py
+++ b/solution.py
@@ -16,6 +16,9 @@
 FAR_BELOW = -1e30
 LOG2E = math.log2(math.e)
 HALVES = 2
+EXTRA = 16
+LOAD_PARTS = 4
+LOAD_MIB = 38
 PROJ_MIB = 12
 ATT_MIB = 12
 OUT_MIB = 12
@@ -34,6 +37,7 @@
 IN_SMEM = pl.BlockSpec(memory_space=pltpu.SMEM)
 IN_VMEM = pl.BlockSpec(memory_space=pltpu.VMEM)
 ANYWHERE = pl.BlockSpec(memory_space=pl.ANY)
+IN_HBM = pl.BlockSpec(memory_space=pltpu.HBM)
 
 
 def cost(flops, moved, trans=0):
@@ -45,32 +49,54 @@
     return jnp.clip(v, -limit, limit)
 
 
-def to_lanes(column):
-    rows = column.shape[0]
-    return jnp.transpose(jnp.broadcast_to(column, (rows, 128)))[:8]
-
-
-def pre_kernel(h_ref, g_ref, c_ref, s_ref):
-    rows, width = h_ref.shape
-    total = jnp.zeros((rows, GROUP), jnp.float32)
-    for at in range(0, width, GROUP):
-        h = h_ref[:, at : at + GROUP].astype(jnp.float32)
-        total = total + h * h
-        v = h * g_ref[at // GROUP : at // GROUP + 1, :].astype(jnp.float32)
-        c_ref[:, at : at + GROUP] = clip_tile(v).astype(jnp.bfloat16)
-    s_ref[...] = to_lanes(jnp.sum(total, axis=-1, keepdims=True))
-
-
-def pre(hidden, gain, chunk, rows):
-    width = hidden.shape[1]
+def pre_kernel(h_hbm, g_hbm, *refs):
+    outs, (h_all, g_ref, sem) = refs[:HALVES], refs[HALVES:]
+    rows, width = h_all.shape
+    steps = sem.shape[0] - 1
+    part = rows // steps
+    copies = [pltpu.make_async_copy(g_hbm, g_ref, sem.at[steps])]
+    for i in range(steps):
+        at = slice(i * part, (i + 1) * part)
+        copies.append(pltpu.make_async_copy(h_hbm.at[at], h_all.at[at], sem.at[i]))
+    for copy in copies:
+        copy.start()
+    copies[0].wait()
+    for i in range(steps):
+        copies[i + 1].wait()
+        total = jnp.zeros((part, GROUP), jnp.float32)
+        row = i * part % (rows // HALVES)
+        c_ref = outs[i * part // (rows // HALVES)]
+        for at in range(0, width, GROUP):
+            h = h_all[i * part : (i + 1) * part, at : at + GROUP].astype(jnp.float32)
+            total = total + h * h
+            v = h * g_ref[at // GROUP : at // GROUP + 1, :].astype(jnp.float32)
+            c_ref[row : row + part, at : at + GROUP] = clip_tile(v).astype(jnp.bfloat16)
+        sums = jnp.sum(total, axis=-1, keepdims=True)
+        sums = jnp.transpose(jnp.broadcast_to(sums, (part, 128)))[:EXTRA]
+        row = lax.broadcasted_iota(jnp.int32, sums.shape, 0)
+        left = sums
+        for place in range(3):
+            piece = left.astype(jnp.bfloat16).astype(jnp.float32)
+            left = left - piece
+            sums = jnp.where(row == place, piece, sums)
+        outs[0][rows // HALVES :, i * part : (i + 1) * part] = sums.astype(jnp.bfloat16)
+
+
+def pre(hidden, gain):
+    rows, width = hidden.shape
+    steps = HALVES * 2
     return pl.pallas_call(
         pre_kernel,
-        grid=(1,),
-        in_specs=[pl.BlockSpec((rows, width), lambda i: (chunk, 0)), whole(gain.shape)],
-        out_specs=[whole((rows, width)), whole((8, rows))],
+        in_specs=[IN_HBM] * 2,
+        out_specs=[IN_VMEM] * HALVES,
         out_shape=[
-            jax.ShapeDtypeStruct((rows, width), jnp.bfloat16),
-            jax.ShapeDtypeStruct((8, rows), jnp.float32),
+            pltpu.VMEM((rows // HALVES + (0 if i else EXTRA), width), jnp.bfloat16)
+            for i in range(HALVES)
+        ],
+        scratch_shapes=[
+            pltpu.VMEM((rows, width), jnp.bfloat16),
+            pltpu.VMEM(gain.shape, jnp.bfloat16),
+            pltpu.SemaphoreType.DMA((steps + 1,)),
         ],
         compiler_params=params(8),
         cost_estimate=cost(8 * rows * width, 4 * rows * width),
@@ -78,10 +104,47 @@
     )(hidden, gain)
 
 
-def proj_kernel(counts, order_ref, ss_ref, *refs):
+def load_kernel(count, token_ref, *refs):
+    sources, goals, sem = refs[:count], refs[count : 2 * count], refs[-1]
+    copies = []
+    for i in range(count):
+        depth = sources[i].shape[0] // LOAD_PARTS
+        for p in range(LOAD_PARTS):
+            at = slice(p * depth, (p + 1) * depth)
+            copies.append(
+                pltpu.make_async_copy(sources[i].at[at], goals[i].at[at], sem.at[i, p])
+            )
+    for copy in copies:
+        copy.start()
+    for copy in copies:
+        copy.wait()
+
+
+def load(token, *weights):
+    count = len(weights)
+    return pl.pallas_call(
+        functools.partial(load_kernel, count),
+        in_specs=[ANYWHERE] + [IN_HBM] * count,
+        out_specs=[IN_VMEM] * count,
+        out_shape=[pltpu.VMEM(w.shape, w.dtype) for w in weights],
+        scratch_shapes=[pltpu.SemaphoreType.DMA((count, LOAD_PARTS))],
+        compiler_params=params(LOAD_MIB),
+        cost_estimate=cost(0, 2 * sum(w.size * 2 for w in weights)),
+        name="load",
+    )(token, *weights)
+
+
+def proj_kernel(counts, chunk, order_ref, *refs):
     depth = len(counts)
     blocks = refs[: sum(counts)]
-    wq_ref, wk_ref, wv_ref, q_ref, kv_ref, accq, acck, accv = refs[sum(counts) :]
+    refs = refs[sum(counts) :]
+    if chunk:
+        wq_ref, wk_ref, wv_ref, ss_ref, q_ref, kv_ref, accq, acck, accv = refs
+        squares = ss_ref[...]
+    else:
+        wq_ref, wk_ref, wv_ref, q_ref, kv_ref, ss_ref, accq, acck, accv = refs
+        squares = jnp.zeros((1, ss_ref.shape[1]), jnp.float32)
+    rows = q_ref.shape[0]
     nk = wk_ref.shape[1]
     k_rows = blocks[0].shape[1]
     at_block = 0
@@ -89,6 +152,11 @@
         at = pl.ds(pl.multiple_of(order_ref[k] * k_rows, k_rows), k_rows)
         mine = [b[...] for b in blocks[at_block : at_block + counts[k]]]
         at_block += counts[k]
+        if not chunk:
+            body_rows = mine[-1].shape[0] - EXTRA
+            tail = mine[-1][body_rows:, : ss_ref.shape[1]].astype(jnp.float32)
+            squares = squares + (tail[0:1] + tail[1:2] + tail[2:3])
+            mine[-1] = mine[-1][:body_rows]
         left = mine[0] if len(mine) == 1 else jnp.concatenate(mine, axis=0)
         wq, wk, wv = wq_ref[at, :], wk_ref[at, :], wv_ref[at, :]
         if nk % 128 == 0:
@@ -106,36 +174,45 @@
                 acc[...] += part
 
     features = k_rows * depth
-    inverse = lax.rsqrt(ss_ref[...] * (1.0 / features) + EPS_IN)
+    if not chunk:
+        squares = jnp.broadcast_to(squares, ss_ref.shape)
+        ss_ref[...] = squares
+    squares = squares[:, chunk * rows : (chunk + 1) * rows]
+    inverse = lax.rsqrt(squares * (1.0 / features) + EPS_IN)
     scale = jnp.transpose(inverse)[:, :1]
     q_ref[...] = (accq[...] * scale).astype(jnp.bfloat16)
     kv_ref[:, :nk] = (acck[...] * scale).astype(jnp.bfloat16)
     kv_ref[:, nk:] = (accv[...] * scale).astype(jnp.bfloat16)
 
 
-def proj(order, blocks, wq, wk, wv, squares):
+def proj(order, blocks, chunk, rows, squares, wq, wk, wv):
     depth = len(blocks)
     counts = [len(b) for b in blocks]
-    rows = squares.shape[1]
     part_cols = blocks[0][0].shape[1]
     nq, nk, nv = wq.shape[1], wk.shape[1], wv.shape[1]
     n = nq + nk + nv
     flat = [p for b in blocks for p in b]
+    args = [order, *flat, wq, wk, wv]
+    out_shape = [
+        jax.ShapeDtypeStruct((rows, nq), jnp.bfloat16),
+        jax.ShapeDtypeStruct((rows, nk + nv), jnp.bfloat16),
+    ]
+    if chunk:
+        args.append(squares)
+    else:
+        out_shape.append(jax.ShapeDtypeStruct((8, rows * HALVES), jnp.float32))
     return pl.pallas_call(
-        functools.partial(proj_kernel, counts),
-        in_specs=[IN_SMEM] + [IN_VMEM] * (len(flat) + 4),
-        out_specs=[IN_VMEM, IN_VMEM],
-        out_shape=[
-            jax.ShapeDtypeStruct((rows, nq), jnp.bfloat16),
-            jax.ShapeDtypeStruct((rows, nk + nv), jnp.bfloat16),
-        ],
+        functools.partial(proj_kernel, counts, chunk),
+        in_specs=[IN_SMEM] + [IN_VMEM] * (len(args) - 1),
+        out_specs=[IN_VMEM] * len(out_shape),
+        out_shape=out_shape,
         scratch_shapes=[pltpu.VMEM((rows, m), jnp.float32) for m in (nq, nk, nv)],
         compiler_params=params(PROJ_MIB),
         cost_estimate=cost(
             2 * rows * part_cols * depth * n, 2 * part_cols * depth * (rows + n)
         ),
         name="proj",
-    )(order, squares, *flat, wq, wk, wv)
+    )(*args)
 
 
 def att_kernel(first, kv_heads, near, far, begins, ends, me_ref, q_ref, *refs):
@@ -398,27 +475,30 @@
     return lax.optimization_barrier((x,) + others)[0]
 
 
-def gather(own, diagonal_after=None, core_after=None):
+def gather(own, core_after=None, beside=None):
     count = lax.axis_size("tp")
     got = {0: [own]}
     masks = [1 << b for b in range(1, count.bit_length() - 1)]
     if len(masks) >= 2:
         a, b = masks[0], masks[1]
-        half = own.shape[0] // 2
+        half = own.shape[0] // (2 * EXTRA) * EXTRA
         got[a] = [swap(own, a)]
         got[b] = [swap(own, b)]
         via_a, via_b = got[a][0], got[b][0]
-        if diagonal_after is not None:
-            via_a, via_b = after(via_a, diagonal_after), after(via_b, diagonal_after)
+        got[1] = [swap(own, 1)]
+        if beside is not None:
+            first = beside(got[1][0])
+            via_a, via_b = after(via_a, first), after(via_b, first)
         got[a | b] = [swap(via_a[:half], b), swap(via_b[half:], a)]
         masks = masks[2:]
     if core_after is not None:
         for m in got:
-            if m:
+            if m > 1:
                 got[m] = [after(p, core_after) for p in got[m]]
     if count > 1:
         for m in list(got):
-            got[m | 1] = [swap(p, 1) for p in got[m]]
+            if m | 1 not in got:
+                got[m | 1] = [swap(p, 1) for p in got[m]]
     for mask in masks:
         for m in list(got):
             got[m | mask] = [swap(p, mask) for p in got[m]]
@@ -443,9 +523,8 @@
     signs = (2 * sign_bits - 1).astype(jnp.float32)
     gain = norm_gain.reshape(-1, GROUP)
 
-    chunks = [pre(hidden_in, gain, i, half) for i in range(HALVES)]
-    clipped = [c for c, _ in chunks]
-    squares = jnp.concatenate([s for _, s in chunks], axis=1)
+    clipped = pre(hidden_in, gain)
+    squares = None
 
     kv_cols = w_key.shape[1]
     sharing = HD // kv_cols if kv_cols < HD else 1
@@ -454,15 +533,25 @@
     for at in range(HALVES):
         own = clipped[at]
         if at:
-            own = after(own, *[b[0] for b in blocks[2:6:2]])
-        blocks = gather(own, diagonal_after=queries[-1] if at else None)
-        if not at:
-            if tp_count > 1:
-                squares = after(squares, blocks[1][0])
-            for bit in range(tp_count.bit_length() - 1):
-                squares = squares + swap(squares, 1 << bit)
-        part = squares[:, at * half : (at + 1) * half]
-        q, kv = proj(order, blocks, w_query, w_key, w_value, part)
+            own = after(own, *[b[0] for b in blocks[2:6:2]], loaded[1])
+        if at:
+            blocks = gather(own, core_after=queries[-1])
+        else:
+            loaded = []
+
+            def bring(token):
+                loaded.extend(load(token, w_query, w_key, w_value, w_out))
+                return loaded[1]
+
+            blocks = gather(own, beside=bring)
+            if not loaded:
+                bring(own)
+        part = squares
+        if at and ctx_count > 1:
+            part = after(part, kvs[0][1])
+        q, kv, *rest = proj(order, blocks, at, half, part, *loaded[:3])
+        if rest:
+            squares = rest[0]
         if sharing > 1:
             k, v = kv[:, :kv_cols], kv[:, kv_cols:]
             for bit in range(sharing.bit_length() - 1):
@@ -493,8 +582,10 @@
         signed = attend(
             ctx_at, queries[at], at * half, kv_heads, [], far, states[at], signs
         )
-        blocks = gather(signed, core_after=branches[-1] if at else None)
-        b, s = project_out(flips, blocks, w_out, teacher, at)
+        if at:
+            signed = after(signed, *[b[0] for b in blocks[2:6:2]])
+        blocks = gather(signed, branches[-1] if at else None)
+        b, s = project_out(flips, blocks, loaded[3], teacher, at)
         branches.append(b)
         stats.append(s)
     stat = jnp.concatenate(stats, axis=1)

time: 144 us -> 150 us (1.042)
  Pallas kernels: 33.3 us -> 45.2 us
  waiting for transfers between devices: 56.7 us -> 48.9 us
  local copies, waits for them, and re-layouts: 18 us -> 24.6 us
  starting transfers between devices: 34.1 us -> 29.9 us
    ppermute x42 -> x39, waiting for transfers between devices: 47.3 us -> 32.6 us  [swap(): return lax.ppermute(x, 'tp', [(i, i ^ mask) for i in range(count)])]
    pallas_call x4, Pallas kernels: 9.92 us -> 20.1 us  [the longest x2 11 us: proj(): pl.pallas_call(functools.partial(proj_kernel, counts, chunk), in_specs=[I...]
    ppermute x6, waiting for transfers between devices: 9.33 us -> 16.3 us  [send_up(): lax.ppermute(x, 'ctx', [(i, i + distance) for i in range(count - distance)])]
    unnamed x33 -> x35, local copies, waits for them, and re-layouts: 17.2 us -> 22.6 us
    ppermute x42 -> x39, starting transfers between devices: 26.2 us -> 21.9 us  [swap(): return lax.ppermute(x, 'tp', [(i, i ^ mask) for i in range(count)])]
    pallas_call x4, Pallas kernels: 10.2 us -> 12 us  [attend(): pl.pallas_call(kernel, in_specs=[IN_SMEM] + [IN_VMEM] * (len(args) - 1),...]
  transfers between devices with their start and end apart: 48 -> 45, of which waited for: 19 -> 17; matrix products, arithmetic and copies ran while one was open for 1% -> 1% of each run, Pallas kernels for 16% -> 23%
where the time goes in v2:
time: 150 us
  waiting for transfers between devices  48.9 us (33%)
  Pallas kernels  45.2 us (30%)
  starting transfers between devices  29.9 us (20%)
  local copies, waits for them, and re-layouts  24.6 us (16%)
    ppermute x39, waiting for transfers between devices, swap(): return lax.ppermute(x, 'tp', [(i, i ^ mask) for i in range(count)])  32.6 us
    unnamed x35, local copies, waits for them, and re-layouts  22.6 us
    ppermute x39, starting transfers between devices, swap(): return lax.ppermute(x, 'tp', [(i, i ^ mask) for i in range(count)])  21.9 us
    ppermute x6, waiting for transfers between devices, send_up(): lax.ppermute(x, 'ctx', [(i, i + distance) for i in range(count - distance)])  16.3 us
    pallas_call x4, Pallas kernels, attend(): pl.pallas_call(kernel, in_specs=[IN_SMEM] + [IN_VMEM] * (len(args) - 1),...  12 us
    pallas_call x2, Pallas kernels, project_out(): pl.pallas_call(functools.partial(out_kernel, counts, steps, chunk), in_sp...  11.8 us
    pallas_call x2, Pallas kernels, proj(): pl.pallas_call(functools.partial(proj_kernel, counts, chunk), in_specs=[I...  11 us
    ppermute x6, starting transfers between devices, send_up(): lax.ppermute(x, 'ctx', [(i, i + distance) for i in range(count - distance)])  7.99 us
  transfers between devices with their start and end apart: 45, of which 17 were waited for; matrix products, arithmetic and copies ran while one was open for 1% of the time, Pallas kernels for 23%

profile of v2, /device:TPU:24, one launch (start us, length us, event | category | flops | bytes accessed | tf_op | source)
XLA Modules:
  0.0 149.6 jit_solution(1572200701950715545)
XLA Ops:
  0.6 1.2 copy-done.10
  1.9 0.7 copy-done.13
  2.5 2.0 %pre.1 = (bf16[272,1024]{1,0:T(8,128)(2,1)S(1)}, bf16[256,1024]{1,0:T(8,128)(2,1)}) custom-call(bf16[512,1024]{1,0:T(8,128)(2,1)S(1)} %copy-done.10, bf16[8,128]{1,0:T(8,128)(2,1)S(1)} %bitcast.3), custom_call_target="tpu_custom_call" | custom-call | flops 4194304 | bytes 2097152 | tf_op jit(solution)/shard_map/pre/pallas_call | solution.py:88
  4.6 1.6 %collective-permute-start.1 = (bf16[272,1024]{1,0:T(8,128)(2,1)S(1)}, bf16[272,1024]{1,0:T(8,128)(2,1)}, u32[]{:S(2)}, u32[]{:S(2)}) collective-permute-start(bf16[272,1024]{1,0:T(8,128)(2,1)S(1)} %get-tuple-element.38.refs_0_), channel_id=1, source_target_pairs={{0,2},{1,3},{2,0},{3,1},{4,6},{5,7},{6,4},{7,5},{8,10},{9,11},{10,... | collective-permute-start | bytes 1671176 | tf_op jit(solution)/shard_map/ppermute | solution.py:466
  6.2 1.5 %collective-permute-start.3 = (bf16[272,1024]{1,0:T(8,128)(2,1)S(1)}, bf16[272,1024]{1,0:T(8,128)(2,1)S(1)}, u32[]{:S(2)}, u32[]{:S(2)}) collective-permute-start(bf16[272,1024]{1,0:T(8,128)(2,1)S(1)} %get-tuple-element.38.refs_0_), channel_id=1, source_target_pairs={{0,4},{1,5},{2,6},{3,7},{4,0},{5,1},{6,2},{7,3},{8,12},{9,13},{10,... | collective-permute-start | bytes 1671176 | tf_op jit(solution)/shard_map/ppermute | solution.py:466
  7.7 0.8 copy-done.11
  8.5 0.8 copy-done.8
  9.3 7.2 %load.1 = (bf16[8192,512]{1,0:T(8,128)(2,1)S(1)}, bf16[8192,128]{1,0:T(8,128)(2,1)S(1)}, bf16[8192,128]{1,0:T(8,128)(2,1)S(1)}, bf16[4096,1024]{1,0:T(8,128)(2,1)S(1)}) custom-call(bf16[272,1024]{1,0:T(8,128)(2,1)} %copy-done.8, bf16[8192,512]{1,0:T(8,128)(2,1)} %refs_0_.1, bf16[8192,128]{1,0:T(8,128)(2,1)} %refs_1_.1, bf16[8192,128]{1,0:T(8,128)(2,1)} %refs_2_.1, ...), custom_call_target="tpu_custom_call" | custom-call | bytes 41943040 | tf_op jit(solution)/shard_map/load/pallas_call | solution.py:125
  16.5 3.3 %copy-done = bf16[8192,512]{1,0:T(8,128)(2,1)} copy-done((bf16[8192,512]{1,0:T(8,128)(2,1)}, bf16[8192,512]{1,0:T(8,128)(2,1)S(1)}, u32[]{:S(2)}) %copy-start) | copy-done | bytes 8388632
  19.8 3.3 %copy-done.3 = bf16[4096,1024]{1,0:T(8,128)(2,1)} copy-done((bf16[4096,1024]{1,0:T(8,128)(2,1)}, bf16[4096,1024]{1,0:T(8,128)(2,1)S(1)}, u32[]{:S(2)}) %copy-start.3) | copy-done | bytes 8388632
  23.1 1.3 copy-done.5
  24.4 1.0 slice.24
  25.4 0.6 collective-permute-start.5
  26.0 1.5 %collective-permute-start.12 = (bf16[256,1024]{1,0:T(8,128)(2,1)}, bf16[256,1024]{1,0:T(8,128)(2,1)S(1)}, u32[]{:S(2)}, u32[]{:S(2)}) collective-permute-start(bf16[256,1024]{1,0:T(8,128)(2,1)} %get-tuple-element.46.refs_0_), channel_id=1, source_target_pairs={{0,4},{1,5},{2,6},{3,7},{4,0},{5,1},{6,2},{7,3},{8,12},{9,13},{10,... | collective-permute-start | bytes 1572872 | tf_op jit(solution)/shard_map/ppermute | solution.py:466
  27.5 0.6 collective-permute-start.6
  28.6 6.1 %collective-permute-done.5.refs_6_ = bf16[128,1024]{1,0:T(8,128)(2,1)} collective-permute-done((bf16[128,1024]{1,0:T(8,128)(2,1)S(1)}, bf16[128,1024]{1,0:T(8,128)(2,1)}, u32[]{:S(2)}, u32[]{:S(2)}) %collective-permute-start.5) | collective-permute-done | bytes 262176 | tf_op jit(solution)/shard_map/ppermute | solution.py:466
  35.3 0.8 collective-permute-done.6.refs_7_
  36.1 8.7 %collective-permute-done.12.refs_4_ = bf16[256,1024]{1,0:T(8,128)(2,1)S(1)} collective-permute-done((bf16[256,1024]{1,0:T(8,128)(2,1)}, bf16[256,1024]{1,0:T(8,128)(2,1)S(1)}, u32[]{:S(2)}, u32[]{:S(2)}) %collective-permute-start.12) | collective-permute-done | bytes 524320 | tf_op jit(solution)/shard_map/ppermute | solution.py:466
  44.8 2.3 %collective-permute-done.10.refs_2_ = bf16[256,1024]{1,0:T(8,128)(2,1)} collective-permute-done((bf16[256,1024]{1,0:T(8,128)(2,1)}, bf16[256,1024]{1,0:T(8,128)(2,1)}, u32[]{:S(2)}, u32[]{:S(2)}) %collective-permute-start.10) | collective-permute-done | bytes 524320 | tf_op jit(solution)/shard_map/ppermute | solution.py:466
  47.2 1.0 slice.32
  48.1 0.6 collective-permute-start.15
  48.7 0.8 collective-permute-start.14
  49.6 3.4 %copy-done.1 = bf16[8192,512]{1,0:T(8,128)(2,1)S(1)} copy-done((bf16[8192,512]{1,0:T(8,128)(2,1)S(1)}, bf16[8192,512]{1,0:T(8,128)(2,1)}, u32[]{:S(2)}) %copy-start.1) | copy-done | bytes 8388632
  53.0 1.6 %copy-done.6 = bf16[8192,128]{1,0:T(8,128)(2,1)S(1)} copy-done((bf16[8192,128]{1,0:T(8,128)(2,1)S(1)}, bf16[8192,128]{1,0:T(8,128)(2,1)}, u32[]{:S(2)}) %copy-start.6) | copy-done | bytes 2097176
  54.5 1.1 copy-done.9
  55.6 1.1 copy-done.12
  56.7 5.7 %proj.2 = (bf16[256,512]{1,0:T(8,128)(2,1)S(1)}, bf16[256,256]{1,0:T(8,128)(2,1)}, f32[8,512]{1,0:T(8,128)S(1)}) custom-call(s32[8]{0:T(128)S(1)} %iota_xor_fusion.order_ref, bf16[272,1024]{1,0:T(8,128)(2,1)S(1)} %copy-done.12, bf16[272,1024]{1,0:T(8,128)(2,1)S(1)} %copy-done.9, bf16[272,1024]{1,0:T(8,128)(2,1)} %collective-permute-done.1.refs_2_, ...), custom_call_target="tpu_custom_call" | custom-call | flops 3221225472 | bytes 16777216 | tf_op jit(solution)/shard_map/proj/pallas_call | solution.py:204
  62.4 0.7 copy-done.14
  63.6 1.3 collective-permute-start.18
  65.0 6.1 %collective-permute-done.18.refs_1_.refs_2_ = bf16[256,256]{1,0:T(8,128)(2,1)S(1)} collective-permute-done((bf16[256,256]{1,0:T(8,128)(2,1)}, bf16[256,256]{1,0:T(8,128)(2,1)S(1)}, u32[]{:S(2)}, u32[]{:S(2)}) %collective-permute-start.18) | collective-permute-done | bytes 131104 | tf_op jit(solution)/shard_map/ppermute | solution.py:471
  71.1 1.4 collective-permute-start.22
  72.5 1.3 collective-permute-start.23
  73.9 5.3 %proj.3 = (bf16[256,512]{1,0:T(8,128)(2,1)S(1)}, bf16[256,256]{1,0:T(8,128)(2,1)}) custom-call(s32[8]{0:T(128)S(1)} %iota_xor_fusion.order_ref, bf16[256,1024]{1,0:T(8,128)(2,1)} %get-tuple-element.46.refs_0_, bf16[256,1024]{1,0:T(8,128)(2,1)S(1)} %collective-permute-done.9.refs_1_, bf16[256,1024]{1,0:T(8,128)(2,1)} %collective-permute-done.10.refs_2_, ...), custom_call_target="tpu_custom_call" | custom-call | flops 3221225472 | bytes 16777216 | tf_op jit(solution)/shard_map/proj/pallas_call | solution.py:204
  79.1 1.4 collective-permute-start.19
  80.6 1.3 collective-permute-start.20
  81.9 1.3 collective-permute-start.21
  83.2 2.6 %collective-permute-done.22.refs_2_.refs_3_ = bf16[256,256]{1,0:T(8,128)(2,1)S(1)} collective-permute-done((bf16[256,256]{1,0:T(8,128)(2,1)}, bf16[256,256]{1,0:T(8,128)(2,1)S(1)}, u32[]{:S(2)}, u32[]{:S(2)}) %collective-permute-start.22) | collective-permute-done | bytes 131104 | tf_op jit(solution)/shard_map/ppermute | solution.py:471
  85.8 3.5 %attend.4 = (f32[8,256]{1,0:T(8,128)S(1)}, f32[8,256]{1,0:T(8,128)S(1)}, f32[4,128,256]{2,1,0:T(8,128)S(1)}) custom-call(s32[1]{0:T(128)} %bitcast.me_ref, bf16[256,512]{1,0:T(8,128)(2,1)S(1)} %copy-done.15, bf16[256,256]{1,0:T(8,128)(2,1)} %get-tuple-element.52.refs_0_, bf16[256,256]{1,0:T(8,128)(2,1)S(1)} %collective-permute-done.18.refs_1_.refs_2_, ...), custom_call_target="tpu_custom_call" | custom-call | flops 536870912 | bytes 524288 | tf_op jit(solution)/shard_map/attend/pallas_call | solution.py:313
  89.2 7.6 %collective-permute-done.20.refs_1_ = bf16[256,256]{1,0:T(8,128)(2,1)S(1)} collective-permute-done((bf16[256,256]{1,0:T(8,128)(2,1)}, bf16[256,256]{1,0:T(8,128)(2,1)S(1)}, u32[]{:S(2)}, u32[]{:S(2)}) %collective-permute-start.20) | collective-permute-done | bytes 131104 | tf_op jit(solution)/shard_map/ppermute | solution.py:471
  96.9 2.3 %attend.5.refs_0_ = bf16[256,512]{1,0:T(8,128)(2,1)S(1)} custom-call(s32[1]{0:T(128)} %bitcast.me_ref, bf16[256,512]{1,0:T(8,128)(2,1)S(1)} %copy-done.15, bf16[256,256]{1,0:T(8,128)(2,1)S(1)} %collective-permute-done.19.refs_0_, bf16[256,256]{1,0:T(8,128)(2,1)S(1)} %collective-permute-done.20.refs_1_, bf16[256,256]{1,0:T(8,128)(2,1)S(1)} %collective-permute-done.21.refs_2_, ...), custom_call_target="tpu_custom_call" | custom-call | flops 402653184 | bytes 393216 | tf_op jit(solution)/shard_map/attend/pallas_call | solution.py:313
  99.2 1.2 collective-permute-start.25
  100.5 1.5 %collective-permute-start.27 = (bf16[256,512]{1,0:T(8,128)(2,1)S(1)}, bf16[256,512]{1,0:T(8,128)(2,1)S(1)}, u32[]{:S(2)}, u32[]{:S(2)}) collective-permute-start(bf16[256,512]{1,0:T(8,128)(2,1)S(1)} %attend.5.refs_0_), channel_id=1, source_target_pairs={{0,4},{1,5},{2,6},{3,7},{4,0},{5,1},{6,2},{7,3},{8,12},{9,13},{10,... | collective-permute-start | bytes 786440 | tf_op jit(solution)/shard_map/ppermute | solution.py:466
  102.0 4.0 %attend.6 = (f32[8,256]{1,0:T(8,128)S(1)}, f32[8,256]{1,0:T(8,128)S(1)}, f32[4,128,256]{2,1,0:T(8,128)S(1)}) custom-call(s32[1]{0:T(128)} %bitcast.me_ref, bf16[256,512]{1,0:T(8,128)(2,1)S(1)} %get-tuple-element.60.q_ref, bf16[256,256]{1,0:T(8,128)(2,1)} %get-tuple-element.52.refs_0_, bf16[256,256]{1,0:T(8,128)(2,1)} %get-tuple-element.54.refs_1_, ...), custom_call_target="tpu_custom_call" | custom-call | flops 671088640 | bytes 655360 | tf_op jit(solution)/shard_map/attend/pallas_call | solution.py:313
  106.0 2.2 %attend.7.refs_0_ = bf16[256,512]{1,0:T(8,128)(2,1)S(1)} custom-call(s32[1]{0:T(128)} %bitcast.me_ref, bf16[256,512]{1,0:T(8,128)(2,1)S(1)} %get-tuple-element.60.q_ref, bf16[256,256]{1,0:T(8,128)(2,1)S(1)} %collective-permute-done.19.refs_0_, bf16[256,256]{1,0:T(8,128)(2,1)S(1)} %collective-permute-done.20.refs_1_, ...), custom_call_target="tpu_custom_call" | custom-call | flops 402653184 | bytes 393216 | tf_op jit(solution)/shard_map/attend/pallas_call | solution.py:313
  108.3 1.6 %collective-permute-start.29 = (bf16[128,512]{1,0:T(8,128)(2,1)S(1)}, bf16[128,512]{1,0:T(8,128)(2,1)S(1)}, u32[]{:S(2)}, u32[]{:S(2)}) collective-permute-start(bf16[128,512]{1,0:T(8,128)(2,1)S(1)} %slice.34), channel_id=1, source_target_pairs={{0,4},{1,5},{2,6},{3,7},{4,0},{5,1},{6,2},{7,3},{8,12},{9,13},{10,... | collective-permute-start | bytes 393224 | tf_op jit(solution)/shard_map/ppermute | solution.py:466
  109.9 0.6 collective-permute-start.30
  110.4 0.8 collective-permute-start.36
  111.3 1.2 collective-permute-start.34
  112.5 2.3 %collective-permute-done.29.refs_6_ = bf16[128,512]{1,0:T(8,128)(2,1)S(1)} collective-permute-done((bf16[128,512]{1,0:T(8,128)(2,1)S(1)}, bf16[128,512]{1,0:T(8,128)(2,1)S(1)}, u32[]{:S(2)}, u32[]{:S(2)}) %collective-permute-start.29) | collective-permute-done | bytes 131104 | tf_op jit(solution)/shard_map/ppermute | solution.py:466
  114.8 1.6 %collective-permute-done.30.refs_7_ = bf16[128,512]{1,0:T(8,128)(2,1)S(1)} collective-permute-done((bf16[128,512]{1,0:T(8,128)(2,1)S(1)}, bf16[128,512]{1,0:T(8,128)(2,1)S(1)}, u32[]{:S(2)}, u32[]{:S(2)}) %collective-permute-start.30) | collective-permute-done | bytes 131104 | tf_op jit(solution)/shard_map/ppermute | solution.py:466
  116.4 2.2 %collective-permute-done.36.refs_4_ = bf16[256,512]{1,0:T(8,128)(2,1)S(1)} collective-permute-done((bf16[256,512]{1,0:T(8,128)(2,1)S(1)}, bf16[256,512]{1,0:T(8,128)(2,1)S(1)}, u32[]{:S(2)}, u32[]{:S(2)}) %collective-permute-start.36) | collective-permute-done | bytes 262176 | tf_op jit(solution)/shard_map/ppermute | solution.py:466
  118.6 0.7 collective-permute-done.34.refs_2_
  120.0 1.2 collective-permute-start.39
  121.1 0.9 collective-permute-start.38
  122.1 3.4 %copy-done.4 = bf16[4096,1024]{1,0:T(8,128)(2,1)S(1)} copy-done((bf16[4096,1024]{1,0:T(8,128)(2,1)S(1)}, bf16[4096,1024]{1,0:T(8,128)(2,1)}, u32[]{:S(2)}) %copy-start.4) | copy-done | bytes 8388632
  125.4 5.9 %project_out.2 = (f32[256,1024]{1,0:T(8,128)S(1)}, f32[8,256]{1,0:T(8,128)S(1)}) custom-call(f32[8]{0:T(128)S(1)} %subtract_convert_fusion.sign_ref, bf16[512,1024]{1,0:T(8,128)(2,1)S(1)} %copy-done.7, bf16[256,512]{1,0:T(8,128)(2,1)S(1)} %attend.5.refs_0_, bf16[256,512]{1,0:T(8,128)(2,1)S(1)} %collective-permute-done.24.refs_1_, ...), custom_call_target="tpu_custom_call" | custom-call | flops 2147483648 | bytes 12058624 | tf_op jit(solution)/shard_map/project_out/pallas_call | solution.py:408
  132.4 1.1 collective-permute-done.41.refs_9_
  133.7 5.9 %project_out.3 = (f32[256,1024]{1,0:T(8,128)S(1)}, f32[8,256]{1,0:T(8,128)S(1)}) custom-call(f32[8]{0:T(128)S(1)} %subtract_convert_fusion.sign_ref, bf16[512,1024]{1,0:T(8,128)(2,1)S(1)} %copy-done.7, bf16[256,512]{1,0:T(8,128)(2,1)S(1)} %attend.7.refs_0_, bf16[256,512]{1,0:T(8,128)(2,1)S(1)} %collective-permute-done.33.refs_1_, ...), custom_call_target="tpu_custom_call" | custom-call | flops 2147483648 | bytes 12058624 | tf_op jit(solution)/shard_map/project_out/pallas_call | solution.py:408
  139.7 1.1 collective-permute-done.42
  140.8 1.0 collective-permute-start.43
  141.8 2.7 %collective-permute-done.43 = f32[8,512]{1,0:T(8,128)S(1)} collective-permute-done((f32[8,512]{1,0:T(8,128)S(1)}, f32[8,512]{1,0:T(8,128)S(1)}, u32[]{:S(2)}, u32[]{:S(2)}) %collective-permute-start.43) | collective-permute-done | bytes 16416 | tf_op jit(solution)/shard_map/ppermute | solution.py:466
  144.5 1.1 collective-permute-start.44
  145.7 2.6 %collective-permute-done.44 = f32[8,512]{1,0:T(8,128)S(1)} collective-permute-done((f32[8,512]{1,0:T(8,128)S(1)}, f32[8,512]{1,0:T(8,128)S(1)}, u32[]{:S(2)}, u32[]{:S(2)}) %collective-permute-start.44) | collective-permute-done | bytes 16416 | tf_op jit(solution)/shard_map/ppermute | solution.py:466
  148.3 1.3 final.1
  (87 shorter events, 4.0 us)
Async XLA Ops:
  0.6 1.2 copy-start.10
  1.9 0.7 copy-start.13
  4.5 4.0 %collective-permute-start = (bf16[272,1024]{1,0:T(8,128)(2,1)S(1)}, bf16[272,1024]{1,0:T(8,128)(2,1)S(1)}, u32[]{:S(2)}, u32[]{:S(2)}) collective-permute-start(bf16[272,1024]{1,0:T(8,128)(2,1)S(1)} %get-tuple-element.38.refs_0_), channel_id=1, source_target_pairs={{0,1},{1,0},{2,3},{3,2},{4,5},{5,4},{6,7},{7,6},{8,9},{9,8},{10,11... | collective-permute-start | bytes 1671176 | tf_op jit(solution)/shard_map/ppermute | solution.py:466
  4.6 19.8 %collective-permute-start.1 = (bf16[272,1024]{1,0:T(8,128)(2,1)S(1)}, bf16[272,1024]{1,0:T(8,128)(2,1)}, u32[]{:S(2)}, u32[]{:S(2)}) collective-permute-start(bf16[272,1024]{1,0:T(8,128)(2,1)S(1)} %get-tuple-element.38.refs_0_), channel_id=1, source_target_pairs={{0,2},{1,3},{2,0},{3,1},{4,6},{5,7},{6,4},{7,5},{8,10},{9,11},{10,... | collective-permute-start | bytes 1671176 | tf_op jit(solution)/shard_map/ppermute | solution.py:466
  6.2 19.8 %collective-permute-start.3 = (bf16[272,1024]{1,0:T(8,128)(2,1)S(1)}, bf16[272,1024]{1,0:T(8,128)(2,1)S(1)}, u32[]{:S(2)}, u32[]{:S(2)}) collective-permute-start(bf16[272,1024]{1,0:T(8,128)(2,1)S(1)} %get-tuple-element.38.refs_0_), channel_id=1, source_target_pairs={{0,4},{1,5},{2,6},{3,7},{4,0},{5,1},{6,2},{7,3},{8,12},{9,13},{10,... | collective-permute-start | bytes 1671176 | tf_op jit(solution)/shard_map/ppermute | solution.py:466
  7.7 0.8 copy-start.11
  8.5 0.8 copy-start.8
  16.5 3.3 %copy-start = (bf16[8192,512]{1,0:T(8,128)(2,1)}, bf16[8192,512]{1,0:T(8,128)(2,1)S(1)}, u32[]{:S(2)}) copy-start(bf16[8192,512]{1,0:T(8,128)(2,1)S(1)} %get-tuple-element.42.refs_10_) | copy-start | bytes 25165828
  19.8 3.3 %copy-start.3 = (bf16[4096,1024]{1,0:T(8,128)(2,1)}, bf16[4096,1024]{1,0:T(8,128)(2,1)S(1)}, u32[]{:S(2)}) copy-start(bf16[4096,1024]{1,0:T(8,128)(2,1)S(1)} %get-tuple-element.58.refs_10_) | copy-start | bytes 25165828
  23.1 1.3 copy-start.5
  25.4 9.4 %collective-permute-start.5 = (bf16[128,1024]{1,0:T(8,128)(2,1)S(1)}, bf16[128,1024]{1,0:T(8,128)(2,1)}, u32[]{:S(2)}, u32[]{:S(2)}) collective-permute-start(bf16[128,1024]{1,0:T(8,128)(2,1)S(1)} %slice.24), channel_id=1, source_target_pairs={{0,4},{1,5},{2,6},{3,7},{4,0},{5,1},{6,2},{7,3},{8,12},{9,13},{10,... | collective-permute-start | bytes 786440 | tf_op jit(solution)/shard_map/ppermute | solution.py:466
  26.0 18.8 %collective-permute-start.12 = (bf16[256,1024]{1,0:T(8,128)(2,1)}, bf16[256,1024]{1,0:T(8,128)(2,1)S(1)}, u32[]{:S(2)}, u32[]{:S(2)}) collective-permute-start(bf16[256,1024]{1,0:T(8,128)(2,1)} %get-tuple-element.46.refs_0_), channel_id=1, source_target_pairs={{0,4},{1,5},{2,6},{3,7},{4,0},{5,1},{6,2},{7,3},{8,12},{9,13},{10,... | collective-permute-start | bytes 1572872 | tf_op jit(solution)/shard_map/ppermute | solution.py:466
  27.5 8.6 %collective-permute-start.6 = (bf16[144,1024]{1,0:T(8,128)(2,1)S(1)}, bf16[144,1024]{1,0:T(8,128)(2,1)S(1)}, u32[]{:S(2)}, u32[]{:S(2)}) collective-permute-start(bf16[144,1024]{1,0:T(8,128)(2,1)S(1)} %slice.25), channel_id=1, source_target_pairs={{0,2},{1,3},{2,0},{3,1},{4,6},{5,7},{6,4},{7,5},{8,10},{9,11},{10,... | collective-permute-start | bytes 884744 | tf_op jit(solution)/shard_map/ppermute | solution.py:466
  28.1 20.6 %collective-permute-start.2 = (bf16[272,1024]{1,0:T(8,128)(2,1)}, bf16[272,1024]{1,0:T(8,128)(2,1)}, u32[]{:S(2)}, u32[]{:S(2)}) collective-permute-start(bf16[272,1024]{1,0:T(8,128)(2,1)} %collective-permute-done.1.refs_2_), channel_id=1, source_target_pairs={{0,1},{1,0},{2,3},{3,2},{4,5},{5,4},{6,7},{7,6},{8,9},{9,8},{10,11... | collective-permute-start | bytes 1671176 | tf_op jit(solution)/shard_map/ppermute | solution.py:466
  28.1 21.5 %collective-permute-start.4 = (bf16[272,1024]{1,0:T(8,128)(2,1)S(1)}, bf16[272,1024]{1,0:T(8,128)(2,1)}, u32[]{:S(2)}, u32[]{:S(2)}) collective-permute-start(bf16[272,1024]{1,0:T(8,128)(2,1)S(1)} %collective-permute-done.3.refs_4_), channel_id=1, source_target_pairs={{0,1},{1,0},{2,3},{3,2},{4,5},{5,4},{6,7},{7,6},{8,9},{9,8},{10,11... | collective-permute-start | bytes 1671176 | tf_op jit(solution)/shard_map/ppermute | solution.py:466
  34.7 12.4 %collective-permute-start.10 = (bf16[256,1024]{1,0:T(8,128)(2,1)}, bf16[256,1024]{1,0:T(8,128)(2,1)}, u32[]{:S(2)}, u32[]{:S(2)}) collective-permute-start(bf16[256,1024]{1,0:T(8,128)(2,1)} %get-tuple-element.46.refs_0_), channel_id=1, source_target_pairs={{0,2},{1,3},{2,0},{3,1},{4,6},{5,7},{6,4},{7,5},{8,10},{9,11},{10,... | collective-permute-start | bytes 1572872 | tf_op jit(solution)/shard_map/ppermute | solution.py:466
  36.1 13.5 %collective-permute-start.8 = (bf16[144,1024]{1,0:T(8,128)(2,1)S(1)}, bf16[144,1024]{1,0:T(8,128)(2,1)}, u32[]{:S(2)}, u32[]{:S(2)}) collective-permute-start(bf16[144,1024]{1,0:T(8,128)(2,1)S(1)} %collective-permute-done.6.refs_7_), channel_id=1, source_target_pairs={{0,1},{1,0},{2,3},{3,2},{4,5},{5,4},{6,7},{7,6},{8,9},{9,8},{10,11... | collective-permute-start | bytes 884744 | tf_op jit(solution)/shard_map/ppermute | solution.py:466
  44.8 3.3 %collective-permute-start.7 = (bf16[128,1024]{1,0:T(8,128)(2,1)}, bf16[128,1024]{1,0:T(8,128)(2,1)}, u32[]{:S(2)}, u32[]{:S(2)}) collective-permute-start(bf16[128,1024]{1,0:T(8,128)(2,1)} %collective-permute-done.5.refs_6_), channel_id=1, source_target_pairs={{0,1},{1,0},{2,3},{3,2},{4,5},{5,4},{6,7},{7,6},{8,9},{9,8},{10,11... | collective-permute-start | bytes 786440 | tf_op jit(solution)/shard_map/ppermute | solution.py:466
  47.2 23.9 %collective-permute-start.9 = (bf16[256,1024]{1,0:T(8,128)(2,1)}, bf16[256,1024]{1,0:T(8,128)(2,1)S(1)}, u32[]{:S(2)}, u32[]{:S(2)}) collective-permute-start(bf16[256,1024]{1,0:T(8,128)(2,1)} %get-tuple-element.46.refs_0_), channel_id=1, source_target_pairs={{0,1},{1,0},{2,3},{3,2},{4,5},{5,4},{6,7},{7,6},{8,9},{9,8},{10,11... | collective-permute-start | bytes 1572872 | tf_op jit(solution)/shard_map/ppermute | solution.py:466
  48.1 15.5 %collective-permute-start.15 = (bf16[128,1024]{1,0:T(8,128)(2,1)S(1)}, bf16[128,1024]{1,0:T(8,128)(2,1)S(1)}, u32[]{:S(2)}, u32[]{:S(2)}) collective-permute-start(bf16[128,1024]{1,0:T(8,128)(2,1)S(1)} %slice.33), channel_id=1, source_target_pairs={{0,2},{1,3},{2,0},{3,1},{4,6},{5,7},{6,4},{7,5},{8,10},{9,11},{10,... | collective-permute-start | bytes 786440 | tf_op jit(solution)/shard_map/ppermute | solution.py:466
  48.7 16.1 %collective-permute-start.14 = (bf16[128,1024]{1,0:T(8,128)(2,1)S(1)}, bf16[128,1024]{1,0:T(8,128)(2,1)S(1)}, u32[]{:S(2)}, u32[]{:S(2)}) collective-permute-start(bf16[128,1024]{1,0:T(8,128)(2,1)S(1)} %slice.32), channel_id=1, source_target_pairs={{0,4},{1,5},{2,6},{3,7},{4,0},{5,1},{6,2},{7,3},{8,12},{9,13},{10,... | collective-permute-start | bytes 786440 | tf_op jit(solution)/shard_map/ppermute | solution.py:466
  49.6 3.4 %copy-start.1 = (bf16[8192,512]{1,0:T(8,128)(2,1)S(1)}, bf16[8192,512]{1,0:T(8,128)(2,1)}, u32[]{:S(2)}) copy-start(bf16[8192,512]{1,0:T(8,128)(2,1)} %copy-done) | copy-start | bytes 25165828
  53.0 1.6 %copy-start.6 = (bf16[8192,128]{1,0:T(8,128)(2,1)S(1)}, bf16[8192,128]{1,0:T(8,128)(2,1)}, u32[]{:S(2)}) copy-start(bf16[8192,128]{1,0:T(8,128)(2,1)} %copy-done.5) | copy-start | bytes 6291460
  54.5 1.1 copy-start.9
  55.6 1.1 copy-start.12
  56.7 17.2 %copy-start.2 = (bf16[8192,512]{1,0:T(8,128)(2,1)S(1)}, bf16[8192,512]{1,0:T(8,128)(2,1)}, u32[]{:S(2)}) copy-start(bf16[8192,512]{1,0:T(8,128)(2,1)} %copy-done) | copy-start | bytes 25165828
  62.4 0.7 copy-start.14
  63.1 10.8 %collective-permute-start.13 = (bf16[256,1024]{1,0:T(8,128)(2,1)S(1)}, bf16[256,1024]{1,0:T(8,128)(2,1)S(1)}, u32[]{:S(2)}, u32[]{:S(2)}) collective-permute-start(bf16[256,1024]{1,0:T(8,128)(2,1)S(1)} %collective-permute-done.12.refs_4_), channel_id=1, source_target_pairs={{0,1},{1,0},{2,3},{3,2},{4,5},{5,4},{6,7},{7,6},{8,9},{9,8},{10,11... | collective-permute-start | bytes 1572872 | tf_op jit(solution)/shard_map/ppermute | solution.py:466
  63.1 10.8 %collective-permute-start.11 = (bf16[256,1024]{1,0:T(8,128)(2,1)}, bf16[256,1024]{1,0:T(8,128)(2,1)S(1)}, u32[]{:S(2)}, u32[]{:S(2)}) collective-permute-start(bf16[256,1024]{1,0:T(8,128)(2,1)} %collective-permute-done.10.refs_2_), channel_id=1, source_target_pairs={{0,1},{1,0},{2,3},{3,2},{4,5},{5,4},{6,7},{7,6},{8,9},{9,8},{10,11... | collective-permute-start | bytes 1572872 | tf_op jit(solution)/shard_map/ppermute | solution.py:466
  63.6 7.5 %collective-permute-start.18 = (bf16[256,256]{1,0:T(8,128)(2,1)}, bf16[256,256]{1,0:T(8,128)(2,1)S(1)}, u32[]{:S(2)}, u32[]{:S(2)}) collective-permute-start(bf16[256,256]{1,0:T(8,128)(2,1)} %get-tuple-element.52.refs_0_), channel_id=1, source_target_pairs={{0,8},{8,16},{16,24},{1,9},{9,17},{17,25},{2,10},{10,18},{18,26},{... | collective-permute-start | bytes 393224 | tf_op jit(solution)/shard_map/ppermute | solution.py:471
  64.9 7.6 %collective-permute-start.17 = (bf16[128,1024]{1,0:T(8,128)(2,1)S(1)}, bf16[128,1024]{1,0:T(8,128)(2,1)S(1)}, u32[]{:S(2)}, u32[]{:S(2)}) collective-permute-start(bf16[128,1024]{1,0:T(8,128)(2,1)S(1)} %collective-permute-done.15.refs_7_), channel_id=1, source_target_pairs={{0,1},{1,0},{2,3},{3,2},{4,5},{5,4},{6,7},{7,6},{8,9},{9,8},{10,11... | collective-permute-start | bytes 786440 | tf_op jit(solution)/shard_map/ppermute | solution.py:466
  71.1 2.8 %collective-permute-start.16 = (bf16[128,1024]{1,0:T(8,128)(2,1)S(1)}, bf16[128,1024]{1,0:T(8,128)(2,1)S(1)}, u32[]{:S(2)}, u32[]{:S(2)}) collective-permute-start(bf16[128,1024]{1,0:T(8,128)(2,1)S(1)} %collective-permute-done.14.refs_6_), channel_id=1, source_target_pairs={{0,1},{1,0},{2,3},{3,2},{4,5},{5,4},{6,7},{7,6},{8,9},{9,8},{10,11... | collective-permute-start | bytes 786440 | tf_op jit(solution)/shard_map/ppermute | solution.py:466
  71.1 12.1 %copy-start.16 = (s32[4,128]{1,0:T(4,128)S(1)}, s32[4,128]{1,0:T(4,128)}, u32[]{:S(2)}) copy-start(s32[4,128]{1,0:T(4,128)} %param.13) | copy-start | bytes 6148
  71.1 14.7 %copy-start.15 = (bf16[256,512]{1,0:T(8,128)(2,1)S(1)}, bf16[256,512]{1,0:T(8,128)(2,1)}, u32[]{:S(2)}) copy-start(bf16[256,512]{1,0:T(8,128)(2,1)} %copy-done.14) | copy-start | bytes 786436
  71.1 14.6 %collective-permute-start.22 = (bf16[256,256]{1,0:T(8,128)(2,1)}, bf16[256,256]{1,0:T(8,128)(2,1)S(1)}, u32[]{:S(2)}, u32[]{:S(2)}) collective-permute-start(bf16[256,256]{1,0:T(8,128)(2,1)} %get-tuple-element.52.refs_0_), channel_id=1, source_target_pairs={{0,16},{8,24},{1,17},{9,25},{2,18},{10,26},{3,19},{11,27},{4,20},{... | collective-permute-start | bytes 393224 | tf_op jit(solution)/shard_map/ppermute | solution.py:471
  72.5 13.2 %collective-permute-start.23 = (bf16[256,256]{1,0:T(8,128)(2,1)}, bf16[256,256]{1,0:T(8,128)(2,1)S(1)}, u32[]{:S(2)}, u32[]{:S(2)}) collective-permute-start(bf16[256,256]{1,0:T(8,128)(2,1)} %get-tuple-element.52.refs_0_), channel_id=1, source_target_pairs={{0,24},{1,25},{2,26},{3,27},{4,28},{5,29},{6,30},{7,31}} | collective-permute-start | bytes 393224 | tf_op jit(solution)/shard_map/ppermute | solution.py:471
  79.1 42.9 %copy-start.7 = (bf16[512,1024]{1,0:T(8,128)(2,1)S(1)}, bf16[512,1024]{1,0:T(8,128)(2,1)}, u32[]{:S(2)}) copy-start(bf16[512,1024]{1,0:T(8,128)(2,1)} %t_ref.3) | copy-start | bytes 3145732
  79.1 10.1 %collective-permute-start.19 = (bf16[256,256]{1,0:T(8,128)(2,1)}, bf16[256,256]{1,0:T(8,128)(2,1)S(1)}, u32[]{:S(2)}, u32[]{:S(2)}) collective-permute-start(bf16[256,256]{1,0:T(8,128)(2,1)} %get-tuple-element.54.refs_1_), channel_id=1, source_target_pairs={{0,8},{8,16},{16,24},{1,9},{9,17},{17,25},{2,10},{10,18},{18,26},{... | collective-permute-start | bytes 393224 | tf_op jit(solution)/shard_map/ppermute | solution.py:471
  80.6 16.3 %collective-permute-start.20 = (bf16[256,256]{1,0:T(8,128)(2,1)}, bf16[256,256]{1,0:T(8,128)(2,1)S(1)}, u32[]{:S(2)}, u32[]{:S(2)}) collective-permute-start(bf16[256,256]{1,0:T(8,128)(2,1)} %get-tuple-element.54.refs_1_), channel_id=1, source_target_pairs={{0,16},{8,24},{1,17},{9,25},{2,18},{10,26},{3,19},{11,27},{4,20},{... | collective-permute-start | bytes 393224 | tf_op jit(solution)/shard_map/ppermute | solution.py:471
  81.9 15.0 %collective-permute-start.21 = (bf16[256,256]{1,0:T(8,128)(2,1)}, bf16[256,256]{1,0:T(8,128)(2,1)S(1)}, u32[]{:S(2)}, u32[]{:S(2)}) collective-permute-start(bf16[256,256]{1,0:T(8,128)(2,1)} %get-tuple-element.54.refs_1_), channel_id=1, source_target_pairs={{0,24},{1,25},{2,26},{3,27},{4,28},{5,29},{6,30},{7,31}} | collective-permute-start | bytes 393224 | tf_op jit(solution)/shard_map/ppermute | solution.py:471
  99.2 9.0 %collective-permute-start.25 = (bf16[256,512]{1,0:T(8,128)(2,1)S(1)}, bf16[256,512]{1,0:T(8,128)(2,1)S(1)}, u32[]{:S(2)}, u32[]{:S(2)}) collective-permute-start(bf16[256,512]{1,0:T(8,128)(2,1)S(1)} %attend.5.refs_0_), channel_id=1, source_target_pairs={{0,2},{1,3},{2,0},{3,1},{4,6},{5,7},{6,4},{7,5},{8,10},{9,11},{10,... | collective-permute-start | bytes 786440 | tf_op jit(solution)/shard_map/ppermute | solution.py:466
  100.5 7.8 %collective-permute-start.27 = (bf16[256,512]{1,0:T(8,128)(2,1)S(1)}, bf16[256,512]{1,0:T(8,128)(2,1)S(1)}, u32[]{:S(2)}, u32[]{:S(2)}) collective-permute-start(bf16[256,512]{1,0:T(8,128)(2,1)S(1)} %attend.5.refs_0_), channel_id=1, source_target_pairs={{0,4},{1,5},{2,6},{3,7},{4,0},{5,1},{6,2},{7,3},{8,12},{9,13},{10,... | collective-permute-start | bytes 786440 | tf_op jit(solution)/shard_map/ppermute | solution.py:466
  108.3 6.5 %collective-permute-start.29 = (bf16[128,512]{1,0:T(8,128)(2,1)S(1)}, bf16[128,512]{1,0:T(8,128)(2,1)S(1)}, u32[]{:S(2)}, u32[]{:S(2)}) collective-permute-start(bf16[128,512]{1,0:T(8,128)(2,1)S(1)} %slice.34), channel_id=1, source_target_pairs={{0,4},{1,5},{2,6},{3,7},{4,0},{5,1},{6,2},{7,3},{8,12},{9,13},{10,... | collective-permute-start | bytes 393224 | tf_op jit(solution)/shard_map/ppermute | solution.py:466
  109.9 6.5 %collective-permute-start.30 = (bf16[128,512]{1,0:T(8,128)(2,1)S(1)}, bf16[128,512]{1,0:T(8,128)(2,1)S(1)}, u32[]{:S(2)}, u32[]{:S(2)}) collective-permute-start(bf16[128,512]{1,0:T(8,128)(2,1)S(1)} %slice.35), channel_id=1, source_target_pairs={{0,2},{1,3},{2,0},{3,1},{4,6},{5,7},{6,4},{7,5},{8,10},{9,11},{10,... | collective-permute-start | bytes 393224 | tf_op jit(solution)/shard_map/ppermute | solution.py:466
  110.4 8.1 %collective-permute-start.36 = (bf16[256,512]{1,0:T(8,128)(2,1)S(1)}, bf16[256,512]{1,0:T(8,128)(2,1)S(1)}, u32[]{:S(2)}, u32[]{:S(2)}) collective-permute-start(bf16[256,512]{1,0:T(8,128)(2,1)S(1)} %attend.7.refs_0_), channel_id=1, source_target_pairs={{0,4},{1,5},{2,6},{3,7},{4,0},{5,1},{6,2},{7,3},{8,12},{9,13},{10,... | collective-permute-start | bytes 786440 | tf_op jit(solution)/shard_map/ppermute | solution.py:466
  111.3 8.0 %collective-permute-start.34 = (bf16[256,512]{1,0:T(8,128)(2,1)S(1)}, bf16[256,512]{1,0:T(8,128)(2,1)S(1)}, u32[]{:S(2)}, u32[]{:S(2)}) collective-permute-start(bf16[256,512]{1,0:T(8,128)(2,1)S(1)} %attend.7.refs_0_), channel_id=1, source_target_pairs={{0,2},{1,3},{2,0},{3,1},{4,6},{5,7},{6,4},{7,5},{8,10},{9,11},{10,... | collective-permute-start | bytes 786440 | tf_op jit(solution)/shard_map/ppermute | solution.py:466
  112.5 6.9 %collective-permute-start.24 = (bf16[256,512]{1,0:T(8,128)(2,1)S(1)}, bf16[256,512]{1,0:T(8,128)(2,1)S(1)}, u32[]{:S(2)}, u32[]{:S(2)}) collective-permute-start(bf16[256,512]{1,0:T(8,128)(2,1)S(1)} %attend.5.refs_0_), channel_id=1, source_target_pairs={{0,1},{1,0},{2,3},{3,2},{4,5},{5,4},{6,7},{7,6},{8,9},{9,8},{10,11... | collective-permute-start | bytes 786440 | tf_op jit(solution)/shard_map/ppermute | solution.py:466
  114.8 5.2 %collective-permute-start.26 = (bf16[256,512]{1,0:T(8,128)(2,1)S(1)}, bf16[256,512]{1,0:T(8,128)(2,1)S(1)}, u32[]{:S(2)}, u32[]{:S(2)}) collective-permute-start(bf16[256,512]{1,0:T(8,128)(2,1)S(1)} %collective-permute-done.25.refs_2_), channel_id=1, source_target_pairs={{0,1},{1,0},{2,3},{3,2},{4,5},{5,4},{6,7},{7,6},{8,9},{9,8},{10,11... | collective-permute-start | bytes 786440 | tf_op jit(solution)/shard_map/ppermute | solution.py:466
  116.4 4.8 %collective-permute-start.28 = (bf16[256,512]{1,0:T(8,128)(2,1)S(1)}, bf16[256,512]{1,0:T(8,128)(2,1)S(1)}, u32[]{:S(2)}, u32[]{:S(2)}) collective-permute-start(bf16[256,512]{1,0:T(8,128)(2,1)S(1)} %collective-permute-done.27.refs_4_), channel_id=1, source_target_pairs={{0,1},{1,0},{2,3},{3,2},{4,5},{5,4},{6,7},{7,6},{8,9},{9,8},{10,11... | collective-permute-start | bytes 786440 | tf_op jit(solution)/shard_map/ppermute | solution.py:466
  118.6 3.5 %collective-permute-start.31 = (bf16[128,512]{1,0:T(8,128)(2,1)S(1)}, bf16[128,512]{1,0:T(8,128)(2,1)S(1)}, u32[]{:S(2)}, u32[]{:S(2)}) collective-permute-start(bf16[128,512]{1,0:T(8,128)(2,1)S(1)} %collective-permute-done.29.refs_6_), channel_id=1, source_target_pairs={{0,1},{1,0},{2,3},{3,2},{4,5},{5,4},{6,7},{7,6},{8,9},{9,8},{10,11... | collective-permute-start | bytes 393224 | tf_op jit(solution)/shard_map/ppermute | solution.py:466
  119.3 2.7 %collective-permute-start.32 = (bf16[128,512]{1,0:T(8,128)(2,1)S(1)}, bf16[128,512]{1,0:T(8,128)(2,1)S(1)}, u32[]{:S(2)}, u32[]{:S(2)}) collective-permute-start(bf16[128,512]{1,0:T(8,128)(2,1)S(1)} %collective-permute-done.30.refs_7_), channel_id=1, source_target_pairs={{0,1},{1,0},{2,3},{3,2},{4,5},{5,4},{6,7},{7,6},{8,9},{9,8},{10,11... | collective-permute-start | bytes 393224 | tf_op jit(solution)/shard_map/ppermute | solution.py:466
  119.4 13.0 %collective-permute-start.33 = (bf16[256,512]{1,0:T(8,128)(2,1)S(1)}, bf16[256,512]{1,0:T(8,128)(2,1)S(1)}, u32[]{:S(2)}, u32[]{:S(2)}) collective-permute-start(bf16[256,512]{1,0:T(8,128)(2,1)S(1)} %attend.7.refs_0_), channel_id=1, source_target_pairs={{0,1},{1,0},{2,3},{3,2},{4,5},{5,4},{6,7},{7,6},{8,9},{9,8},{10,11... | collective-permute-start | bytes 786440 | tf_op jit(solution)/shard_map/ppermute | solution.py:466
  120.0 11.9 %collective-permute-start.39 = (bf16[128,512]{1,0:T(8,128)(2,1)S(1)}, bf16[128,512]{1,0:T(8,128)(2,1)S(1)}, u32[]{:S(2)}, u32[]{:S(2)}) collective-permute-start(bf16[128,512]{1,0:T(8,128)(2,1)S(1)} %slice.37), channel_id=1, source_target_pairs={{0,2},{1,3},{2,0},{3,1},{4,6},{5,7},{6,4},{7,5},{8,10},{9,11},{10,... | collective-permute-start | bytes 393224 | tf_op jit(solution)/shard_map/ppermute | solution.py:466
  121.1 10.8 %collective-permute-start.38 = (bf16[128,512]{1,0:T(8,128)(2,1)S(1)}, bf16[128,512]{1,0:T(8,128)(2,1)S(1)}, u32[]{:S(2)}, u32[]{:S(2)}) collective-permute-start(bf16[128,512]{1,0:T(8,128)(2,1)S(1)} %slice.36), channel_id=1, source_target_pairs={{0,4},{1,5},{2,6},{3,7},{4,0},{5,1},{6,2},{7,3},{8,12},{9,13},{10,... | collective-permute-start | bytes 393224 | tf_op jit(solution)/shard_map/ppermute | solution.py:466
  122.1 3.4 %copy-start.4 = (bf16[4096,1024]{1,0:T(8,128)(2,1)S(1)}, bf16[4096,1024]{1,0:T(8,128)(2,1)}, u32[]{:S(2)}) copy-start(bf16[4096,1024]{1,0:T(8,128)(2,1)} %copy-done.3) | copy-start | bytes 25165828
  131.3 2.3 %collective-permute-start.37 = (bf16[256,512]{1,0:T(8,128)(2,1)S(1)}, bf16[256,512]{1,0:T(8,128)(2,1)S(1)}, u32[]{:S(2)}, u32[]{:S(2)}) collective-permute-start(bf16[256,512]{1,0:T(8,128)(2,1)S(1)} %collective-permute-done.36.refs_4_), channel_id=1, source_target_pairs={{0,1},{1,0},{2,3},{3,2},{4,5},{5,4},{6,7},{7,6},{8,9},{9,8},{10,11... | collective-permute-start | bytes 786440 | tf_op jit(solution)/shard_map/ppermute | solution.py:466
  131.4 2.3 %collective-permute-start.35 = (bf16[256,512]{1,0:T(8,128)(2,1)S(1)}, bf16[256,512]{1,0:T(8,128)(2,1)S(1)}, u32[]{:S(2)}, u32[]{:S(2)}) collective-permute-start(bf16[256,512]{1,0:T(8,128)(2,1)S(1)} %collective-permute-done.34.refs_2_), channel_id=1, source_target_pairs={{0,1},{1,0},{2,3},{3,2},{4,5},{5,4},{6,7},{7,6},{8,9},{9,8},{10,11... | collective-permute-start | bytes 786440 | tf_op jit(solution)/shard_map/ppermute | solution.py:466
  131.9 1.6 %collective-permute-start.41 = (bf16[128,512]{1,0:T(8,128)(2,1)S(1)}, bf16[128,512]{1,0:T(8,128)(2,1)S(1)}, u32[]{:S(2)}, u32[]{:S(2)}) collective-permute-start(bf16[128,512]{1,0:T(8,128)(2,1)S(1)} %collective-permute-done.39.refs_7_), channel_id=1, source_target_pairs={{0,1},{1,0},{2,3},{3,2},{4,5},{5,4},{6,7},{7,6},{8,9},{9,8},{10,11... | collective-permute-start | bytes 393224 | tf_op jit(solution)/shard_map/ppermute | solution.py:466
  132.0 1.7 %collective-permute-start.40 = (bf16[128,512]{1,0:T(8,128)(2,1)S(1)}, bf16[128,512]{1,0:T(8,128)(2,1)S(1)}, u32[]{:S(2)}, u32[]{:S(2)}) collective-permute-start(bf16[128,512]{1,0:T(8,128)(2,1)S(1)} %collective-permute-done.38.refs_6_), channel_id=1, source_target_pairs={{0,1},{1,0},{2,3},{3,2},{4,5},{5,4},{6,7},{7,6},{8,9},{9,8},{10,11... | collective-permute-start | bytes 393224 | tf_op jit(solution)/shard_map/ppermute | solution.py:466
  139.6 1.2 collective-permute-start.42
  140.8 3.7 %collective-permute-start.43 = (f32[8,512]{1,0:T(8,128)S(1)}, f32[8,512]{1,0:T(8,128)S(1)}, u32[]{:S(2)}, u32[]{:S(2)}) collective-permute-start(f32[8,512]{1,0:T(8,128)S(1)} %add.10), channel_id=1, source_target_pairs={{0,2},{1,3},{2,0},{3,1},{4,6},{5,7},{6,4},{7,5},{8,10},{9,11},{10,... | collective-permute-start | bytes 49160 | tf_op jit(solution)/shard_map/ppermute | solution.py:466
  144.5 3.7 %collective-permute-start.44 = (f32[8,512]{1,0:T(8,128)S(1)}, f32[8,512]{1,0:T(8,128)S(1)}, u32[]{:S(2)}, u32[]{:S(2)}) collective-permute-start(f32[8,512]{1,0:T(8,128)S(1)} %add.11), channel_id=1, source_target_pairs={{0,4},{1,5},{2,6},{3,7},{4,0},{5,1},{6,2},{7,3},{8,12},{9,13},{10,... | collective-permute-start | bytes 49160 | tf_op jit(solution)/shard_map/ppermute | solution.py:466

commit v3 on v2

--- a/solution.py
+++ b/solution.py
@@ -98,13 +98,13 @@
             pltpu.VMEM(gain.shape, jnp.bfloat16),
             pltpu.SemaphoreType.DMA((steps + 1,)),
         ],
-        compiler_params=params(8),
+        compiler_params=params(62),
         cost_estimate=cost(8 * rows * width, 4 * rows * width),
         name="pre",
     )(hidden, gain)
 
 
-def load_kernel(count, token_ref, *refs):
+def load_kernel(count, *refs):
     sources, goals, sem = refs[:count], refs[count : 2 * count], refs[-1]
     copies = []
     for i in range(count):
@@ -120,18 +120,18 @@
         copy.wait()
 
 
-def load(token, *weights):
+def load(*weights):
     count = len(weights)
     return pl.pallas_call(
         functools.partial(load_kernel, count),
-        in_specs=[ANYWHERE] + [IN_HBM] * count,
+        in_specs=[IN_HBM] * count,
         out_specs=[IN_VMEM] * count,
         out_shape=[pltpu.VMEM(w.shape, w.dtype) for w in weights],
         scratch_shapes=[pltpu.SemaphoreType.DMA((count, LOAD_PARTS))],
         compiler_params=params(LOAD_MIB),
         cost_estimate=cost(0, 2 * sum(w.size * 2 for w in weights)),
         name="load",
-    )(token, *weights)
+    )(*weights)
 
 
 def proj_kernel(counts, chunk, order_ref, *refs):
@@ -523,6 +523,9 @@
     signs = (2 * sign_bits - 1).astype(jnp.float32)
     gain = norm_gain.reshape(-1, GROUP)
 
+    gain, order, ctx_at, flips, signs = lax.optimization_barrier(
+        (gain, order, ctx_at, flips, signs)
+    )
     clipped = pre(hidden_in, gain)
     squares = None
 
@@ -540,7 +543,8 @@
             loaded = []
 
             def bring(token):
-                loaded.extend(load(token, w_query, w_key, w_value, w_out))
+                first = after(w_query, token, order, ctx_at, flips, signs)
+                loaded.extend(load(first, w_key, w_value, w_out))
                 return loaded[1]
 
             blocks = gather(own, beside=bring)

time: 150 us -> 131 us (0.87); the launches traced: 150 us -> 129 us
  local copies, waits for them, and re-layouts: 24.6 us -> 0.13 us
  Pallas kernels: 45.2 us -> 40.5 us
  waiting for transfers between devices: 48.9 us -> 53.3 us
  starting transfers between devices: 29.9 us -> 33.1 us
    unnamed x35 -> x3, local copies, waits for them, and re-layouts: 22.6 us -> 0.01 us
    ppermute x39, waiting for transfers between devices: 32.6 us -> 37.3 us  [swap(): return lax.ppermute(x, 'tp', [(i, i ^ mask) for i in range(count)])]
    ppermute x39, starting transfers between devices: 21.9 us -> 25.2 us  [swap(): return lax.ppermute(x, 'tp', [(i, i ^ mask) for i in range(count)])]
    pallas_call x2, Pallas kernels: 11 us -> 8.04 us  [proj(): pl.pallas_call(functools.partial(proj_kernel, counts, chunk), in_specs=[I...]
    slice x8, local copies, waits for them, and re-layouts: 2.01 us -> 0.11 us  [gather(): got[a | b] = [swap(via_a[:half], b), swap(via_b[half:], a)]]
    pallas_call x4, Pallas kernels: 12 us -> 10.1 us  [attend(): pl.pallas_call(kernel, in_specs=[IN_SMEM] + [IN_VMEM] * (len(args) - 1),...]
  transfers between devices with their start and end apart: 45 -> 45, of which waited for: 17 -> 18; matrix products, arithmetic and copies ran while one was open for 1% -> 0% of each run, Pallas kernels for 23% -> 22%
where the time goes in v3:
time: 131 us; the launch traced here: 129 us
  waiting for transfers between devices  53.3 us (41%)
  Pallas kernels  40.5 us (31%)
  starting transfers between devices  33.1 us (25%)
    ppermute x39, waiting for transfers between devices, swap(): return lax.ppermute(x, 'tp', [(i, i ^ mask) for i in range(count)])  37.3 us
    ppermute x39, starting transfers between devices, swap(): return lax.ppermute(x, 'tp', [(i, i ^ mask) for i in range(count)])  25.2 us
    ppermute x6, waiting for transfers between devices, send_up(): lax.ppermute(x, 'ctx', [(i, i + distance) for i in range(count - distance)])  16 us
    pallas_call x2, Pallas kernels, project_out(): pl.pallas_call(functools.partial(out_kernel, counts, steps, chunk), in_sp...  11.8 us
    pallas_call x4, Pallas kernels, attend(): pl.pallas_call(kernel, in_specs=[IN_SMEM] + [IN_VMEM] * (len(args) - 1),...  10.1 us
    pallas_call x2, Pallas kernels, proj(): pl.pallas_call(functools.partial(proj_kernel, counts, chunk), in_specs=[I...  8.04 us
    ppermute x6, starting transfers between devices, send_up(): lax.ppermute(x, 'ctx', [(i, i + distance) for i in range(count - distance)])  7.86 us
    pallas_call x1, Pallas kernels, load(): pl.pallas_call(functools.partial(load_kernel, count), in_specs=[IN_HBM] *...  7.19 us
  transfers between devices with their start and end apart: 45, of which 18 were waited for; matrix products, arithmetic and copies ran while one was open for 0% of the time, Pallas kernels for 22%

profile of v3, /device:TPU:24, one launch (start us, length us, event | category | flops | bytes accessed | tf_op | source)
XLA Modules:
  0.0 128.7 jit_solution(16972178669592970352)
XLA Ops:
  0.6 0.7 add_convert_fusion.refs_6_
  1.3 2.1 %pre.1 = (bf16[272,1024]{1,0:T(8,128)(2,1)S(1)}, bf16[256,1024]{1,0:T(8,128)(2,1)S(1)}) custom-call(bf16[512,1024]{1,0:T(8,128)(2,1)} %h_hbm.1, bf16[8,128]{1,0:T(8,128)(2,1)} %bitcast.3), custom_call_target="tpu_custom_call" | custom-call | flops 4194304 | bytes 2097152 | tf_op jit(solution)/shard_map/pre/pallas_call | solution.py:88
  3.4 0.1 collective-permute-start
  3.5 1.6 %collective-permute-start.1 = (bf16[272,1024]{1,0:T(8,128)(2,1)S(1)}, bf16[272,1024]{1,0:T(8,128)(2,1)S(1)}, u32[]{:S(2)}, u32[]{:S(2)}) collective-permute-start(bf16[272,1024]{1,0:T(8,128)(2,1)S(1)} %get-tuple-element.48.refs_0_), channel_id=1, source_target_pairs={{0,2},{1,3},{2,0},{3,1},{4,6},{5,7},{6,4},{7,5},{8,10},{9,11},{10,... | collective-permute-start | bytes 1671176 | tf_op jit(solution)/shard_map/ppermute | solution.py:466
  5.0 1.5 %collective-permute-start.3 = (bf16[272,1024]{1,0:T(8,128)(2,1)S(1)}, bf16[272,1024]{1,0:T(8,128)(2,1)S(1)}, u32[]{:S(2)}, u32[]{:S(2)}) collective-permute-start(bf16[272,1024]{1,0:T(8,128)(2,1)S(1)} %get-tuple-element.48.refs_0_), channel_id=1, source_target_pairs={{0,4},{1,5},{2,6},{3,7},{4,0},{5,1},{6,2},{7,3},{8,12},{9,13},{10,... | collective-permute-start | bytes 1671176 | tf_op jit(solution)/shard_map/ppermute | solution.py:466
  6.6 7.2 %load.1 = (bf16[8192,512]{1,0:T(8,128)(2,1)S(1)}, bf16[8192,128]{1,0:T(8,128)(2,1)S(1)}, bf16[8192,128]{1,0:T(8,128)(2,1)S(1)}, bf16[4096,1024]{1,0:T(8,128)(2,1)S(1)}) custom-call(bf16[8192,512]{1,0:T(8,128)(2,1)} %refs_0_, bf16[8192,128]{1,0:T(8,128)(2,1)} %refs_1_.1, bf16[8192,128]{1,0:T(8,128)(2,1)} %refs_2_.1, bf16[4096,1024]{1,0:T(8,128)(2,1)} %refs_3_.1), custom_call_target="tpu_custom_call" | custom-call | bytes 41943040 | tf_op jit(solution)/shard_map/load/pallas_call | solution.py:125
  13.8 4.8 %collective-permute-done.1.refs_2_ = bf16[272,1024]{1,0:T(8,128)(2,1)S(1)} collective-permute-done((bf16[272,1024]{1,0:T(8,128)(2,1)S(1)}, bf16[272,1024]{1,0:T(8,128)(2,1)S(1)}, u32[]{:S(2)}, u32[]{:S(2)}) %collective-permute-start.1) | collective-permute-done | bytes 557088 | tf_op jit(solution)/shard_map/ppermute | solution.py:466
  18.5 1.6 %collective-permute-start.5 = (bf16[128,1024]{1,0:T(8,128)(2,1)S(1)}, bf16[128,1024]{1,0:T(8,128)(2,1)S(1)}, u32[]{:S(2)}, u32[]{:S(2)}) collective-permute-start(bf16[128,1024]{1,0:T(8,128)(2,1)S(1)} %slice.24), channel_id=1, source_target_pairs={{0,4},{1,5},{2,6},{3,7},{4,0},{5,1},{6,2},{7,3},{8,12},{9,13},{10,... | collective-permute-start | bytes 786440 | tf_op jit(solution)/shard_map/ppermute | solution.py:466
  20.1 1.1 collective-permute-start.12
  21.3 0.9 collective-permute-start.6
  22.2 0.5 collective-permute-start.2
  22.7 5.1 %collective-permute-done.5.refs_6_ = bf16[128,1024]{1,0:T(8,128)(2,1)S(1)} collective-permute-done((bf16[128,1024]{1,0:T(8,128)(2,1)S(1)}, bf16[128,1024]{1,0:T(8,128)(2,1)S(1)}, u32[]{:S(2)}, u32[]{:S(2)}) %collective-permute-start.5) | collective-permute-done | bytes 262176 | tf_op jit(solution)/shard_map/ppermute | solution.py:466
  27.8 1.5 %collective-permute-start.10 = (bf16[256,1024]{1,0:T(8,128)(2,1)S(1)}, bf16[256,1024]{1,0:T(8,128)(2,1)S(1)}, u32[]{:S(2)}, u32[]{:S(2)}) collective-permute-start(bf16[256,1024]{1,0:T(8,128)(2,1)S(1)} %get-tuple-element.58.refs_0_), channel_id=1, source_target_pairs={{0,2},{1,3},{2,0},{3,1},{4,6},{5,7},{6,4},{7,5},{8,10},{9,11},{10,... | collective-permute-start | bytes 1572872 | tf_op jit(solution)/shard_map/ppermute | solution.py:466
  29.3 1.4 %collective-permute-done.6.refs_7_ = bf16[144,1024]{1,0:T(8,128)(2,1)S(1)} collective-permute-done((bf16[144,1024]{1,0:T(8,128)(2,1)S(1)}, bf16[144,1024]{1,0:T(8,128)(2,1)S(1)}, u32[]{:S(2)}, u32[]{:S(2)}) %collective-permute-start.6) | collective-permute-done | bytes 294944 | tf_op jit(solution)/shard_map/ppermute | solution.py:466
  30.7 7.0 %collective-permute-done.12.refs_4_ = bf16[256,1024]{1,0:T(8,128)(2,1)S(1)} collective-permute-done((bf16[256,1024]{1,0:T(8,128)(2,1)S(1)}, bf16[256,1024]{1,0:T(8,128)(2,1)S(1)}, u32[]{:S(2)}, u32[]{:S(2)}) %collective-permute-start.12) | collective-permute-done | bytes 524320 | tf_op jit(solution)/shard_map/ppermute | solution.py:466
  37.7 2.8 %collective-permute-done.10.refs_2_ = bf16[256,1024]{1,0:T(8,128)(2,1)S(1)} collective-permute-done((bf16[256,1024]{1,0:T(8,128)(2,1)S(1)}, bf16[256,1024]{1,0:T(8,128)(2,1)S(1)}, u32[]{:S(2)}, u32[]{:S(2)}) %collective-permute-start.10) | collective-permute-done | bytes 524320 | tf_op jit(solution)/shard_map/ppermute | solution.py:466
  40.6 1.0 collective-permute-start.15
  41.6 1.5 %collective-permute-start.14 = (bf16[128,1024]{1,0:T(8,128)(2,1)S(1)}, bf16[128,1024]{1,0:T(8,128)(2,1)S(1)}, u32[]{:S(2)}, u32[]{:S(2)}) collective-permute-start(bf16[128,1024]{1,0:T(8,128)(2,1)S(1)} %slice.32), channel_id=1, source_target_pairs={{0,4},{1,5},{2,6},{3,7},{4,0},{5,1},{6,2},{7,3},{8,12},{9,13},{10,... | collective-permute-start | bytes 786440 | tf_op jit(solution)/shard_map/ppermute | solution.py:466
  43.1 4.0 %proj.2 = (bf16[256,512]{1,0:T(8,128)(2,1)S(1)}, bf16[256,256]{1,0:T(8,128)(2,1)S(1)}, f32[8,512]{1,0:T(8,128)S(1)}) custom-call(s32[8]{0:T(128)S(1)} %get-tuple-element.46.order_ref, bf16[272,1024]{1,0:T(8,128)(2,1)S(1)} %get-tuple-element.48.refs_0_, bf16[272,1024]{1,0:T(8,128)(2,1)S(1)} %collective-permute-done.refs_1_, ...), custom_call_target="tpu_custom_call" | custom-call | flops 3221225472 | bytes 16777216 | tf_op jit(solution)/shard_map/proj/pallas_call | solution.py:204
  47.1 0.1 collective-permute-start.13
  47.2 0.5 collective-permute-start.11
  47.7 1.7 %collective-permute-done.15.refs_7_ = bf16[128,1024]{1,0:T(8,128)(2,1)S(1)} collective-permute-done((bf16[128,1024]{1,0:T(8,128)(2,1)S(1)}, bf16[128,1024]{1,0:T(8,128)(2,1)S(1)}, u32[]{:S(2)}, u32[]{:S(2)}) %collective-permute-start.15) | collective-permute-done | bytes 262176 | tf_op jit(solution)/shard_map/ppermute | solution.py:466
  49.4 1.3 collective-permute-start.18
  50.7 0.1 collective-permute-start.17
  50.7 5.6 %collective-permute-done.18.refs_1_.refs_2_ = bf16[256,256]{1,0:T(8,128)(2,1)S(1)} collective-permute-done((bf16[256,256]{1,0:T(8,128)(2,1)S(1)}, bf16[256,256]{1,0:T(8,128)(2,1)S(1)}, u32[]{:S(2)}, u32[]{:S(2)}) %collective-permute-start.18) | collective-permute-done | bytes 131104 | tf_op jit(solution)/shard_map/ppermute | solution.py:471
  56.4 1.3 collective-permute-start.23
  57.7 1.3 %collective-permute-start.22 = (bf16[256,256]{1,0:T(8,128)(2,1)S(1)}, bf16[256,256]{1,0:T(8,128)(2,1)S(1)}, u32[]{:S(2)}, u32[]{:S(2)}) collective-permute-start(bf16[256,256]{1,0:T(8,128)(2,1)S(1)} %get-tuple-element.64.refs_0_), channel_id=1, source_target_pairs={{0,16},{8,24},{1,17},{9,25},{2,18},{10,26},{3,19},{11,27},{4,20},{... | collective-permute-start | bytes 393224 | tf_op jit(solution)/shard_map/ppermute | solution.py:471
  59.0 4.0 %proj.3 = (bf16[256,512]{1,0:T(8,128)(2,1)S(1)}, bf16[256,256]{1,0:T(8,128)(2,1)S(1)}) custom-call(s32[8]{0:T(128)S(1)} %get-tuple-element.46.order_ref, bf16[256,1024]{1,0:T(8,128)(2,1)S(1)} %get-tuple-element.58.refs_0_, bf16[256,1024]{1,0:T(8,128)(2,1)S(1)} %collective-permute-done.9.refs_1_, bf16[256,1024]{1,0:T(8,128)(2,1)S(1)} %collective-permute-done.10.refs_2_, ...), custom_call_target="tpu_custom_call" | custom-call | flops 3221225472 | bytes 16777216 | tf_op jit(solution)/shard_map/proj/pallas_call | solution.py:204
  63.1 1.4 %collective-permute-start.21 = (bf16[256,256]{1,0:T(8,128)(2,1)S(1)}, bf16[256,256]{1,0:T(8,128)(2,1)S(1)}, u32[]{:S(2)}, u32[]{:S(2)}) collective-permute-start(bf16[256,256]{1,0:T(8,128)(2,1)S(1)} %get-tuple-element.66.refs_1_), channel_id=1, source_target_pairs={{0,24},{1,25},{2,26},{3,27},{4,28},{5,29},{6,30},{7,31}} | collective-permute-start | bytes 393224 | tf_op jit(solution)/shard_map/ppermute | solution.py:471
  64.5 1.3 %collective-permute-start.20 = (bf16[256,256]{1,0:T(8,128)(2,1)S(1)}, bf16[256,256]{1,0:T(8,128)(2,1)S(1)}, u32[]{:S(2)}, u32[]{:S(2)}) collective-permute-start(bf16[256,256]{1,0:T(8,128)(2,1)S(1)} %get-tuple-element.66.refs_1_), channel_id=1, source_target_pairs={{0,16},{8,24},{1,17},{9,25},{2,18},{10,26},{3,19},{11,27},{4,20},{... | collective-permute-start | bytes 393224 | tf_op jit(solution)/shard_map/ppermute | solution.py:471
  65.8 1.3 %collective-permute-start.19 = (bf16[256,256]{1,0:T(8,128)(2,1)S(1)}, bf16[256,256]{1,0:T(8,128)(2,1)S(1)}, u32[]{:S(2)}, u32[]{:S(2)}) collective-permute-start(bf16[256,256]{1,0:T(8,128)(2,1)S(1)} %get-tuple-element.66.refs_1_), channel_id=1, source_target_pairs={{0,8},{8,16},{16,24},{1,9},{9,17},{17,25},{2,10},{10,18},{18,26},{... | collective-permute-start | bytes 393224 | tf_op jit(solution)/shard_map/ppermute | solution.py:471
  67.1 10.2 %collective-permute-done.22.refs_2_.refs_3_ = bf16[256,256]{1,0:T(8,128)(2,1)S(1)} collective-permute-done((bf16[256,256]{1,0:T(8,128)(2,1)S(1)}, bf16[256,256]{1,0:T(8,128)(2,1)S(1)}, u32[]{:S(2)}, u32[]{:S(2)}) %collective-permute-start.22) | collective-permute-done | bytes 131104 | tf_op jit(solution)/shard_map/ppermute | solution.py:471
  77.3 2.6 %attend.4 = (f32[8,256]{1,0:T(8,128)S(1)}, f32[8,256]{1,0:T(8,128)S(1)}, f32[4,128,256]{2,1,0:T(8,128)S(1)}) custom-call(s32[1]{0:T(128)} %bitcast.1.me_ref, bf16[256,512]{1,0:T(8,128)(2,1)S(1)} %get-tuple-element.56.q_ref, bf16[256,256]{1,0:T(8,128)(2,1)S(1)} %get-tuple-element.64.refs_0_, bf16[256,256]{1,0:T(8,128)(2,1)S(1)} %collective-permute-done.18.refs_1_.refs_2_, ...), custom_call_target="tpu_custom_call" | custom-call | flops 536870912 | bytes 524288 | tf_op jit(solution)/shard_map/attend/pallas_call | solution.py:313
  79.8 0.2 collective-permute-done.20.refs_1_
  80.1 2.3 %attend.5.refs_0_ = bf16[256,512]{1,0:T(8,128)(2,1)S(1)} custom-call(s32[1]{0:T(128)} %bitcast.1.me_ref, bf16[256,512]{1,0:T(8,128)(2,1)S(1)} %get-tuple-element.56.q_ref, bf16[256,256]{1,0:T(8,128)(2,1)S(1)} %collective-permute-done.19.refs_0_, bf16[256,256]{1,0:T(8,128)(2,1)S(1)} %collective-permute-done.20.refs_1_, ...), custom_call_target="tpu_custom_call" | custom-call | flops 402653184 | bytes 393216 | tf_op jit(solution)/shard_map/attend/pallas_call | solution.py:313
  82.4 1.0 collective-permute-start.27
  83.4 1.5 %collective-permute-start.25 = (bf16[256,512]{1,0:T(8,128)(2,1)S(1)}, bf16[256,512]{1,0:T(8,128)(2,1)S(1)}, u32[]{:S(2)}, u32[]{:S(2)}) collective-permute-start(bf16[256,512]{1,0:T(8,128)(2,1)S(1)} %attend.5.refs_0_), channel_id=1, source_target_pairs={{0,2},{1,3},{2,0},{3,1},{4,6},{5,7},{6,4},{7,5},{8,10},{9,11},{10,... | collective-permute-start | bytes 786440 | tf_op jit(solution)/shard_map/ppermute | solution.py:466
  84.9 3.1 %attend.6 = (f32[8,256]{1,0:T(8,128)S(1)}, f32[8,256]{1,0:T(8,128)S(1)}, f32[4,128,256]{2,1,0:T(8,128)S(1)}) custom-call(s32[1]{0:T(128)} %bitcast.1.me_ref, bf16[256,512]{1,0:T(8,128)(2,1)S(1)} %get-tuple-element.72.q_ref, bf16[256,256]{1,0:T(8,128)(2,1)S(1)} %get-tuple-element.64.refs_0_, bf16[256,256]{1,0:T(8,128)(2,1)S(1)} %get-tuple-element.66.refs_1_, ...), custom_call_target="tpu_custom_call" | custom-call | flops 671088640 | bytes 655360 | tf_op jit(solution)/shard_map/attend/pallas_call | solution.py:313
  88.0 2.2 %attend.7.refs_0_ = bf16[256,512]{1,0:T(8,128)(2,1)S(1)} custom-call(s32[1]{0:T(128)} %bitcast.1.me_ref, bf16[256,512]{1,0:T(8,128)(2,1)S(1)} %get-tuple-element.72.q_ref, bf16[256,256]{1,0:T(8,128)(2,1)S(1)} %collective-permute-done.19.refs_0_, bf16[256,256]{1,0:T(8,128)(2,1)S(1)} %collective-permute-done.20.refs_1_, ...), custom_call_target="tpu_custom_call" | custom-call | flops 402653184 | bytes 393216 | tf_op jit(solution)/shard_map/attend/pallas_call | solution.py:313
  90.2 0.6 collective-permute-done.27.refs_4_
  90.8 1.0 collective-permute-start.30
  91.7 1.6 %collective-permute-start.29 = (bf16[128,512]{1,0:T(8,128)(2,1)S(1)}, bf16[128,512]{1,0:T(8,128)(2,1)S(1)}, u32[]{:S(2)}, u32[]{:S(2)}) collective-permute-start(bf16[128,512]{1,0:T(8,128)(2,1)S(1)} %slice.34), channel_id=1, source_target_pairs={{0,4},{1,5},{2,6},{3,7},{4,0},{5,1},{6,2},{7,3},{8,12},{9,13},{10,... | collective-permute-start | bytes 393224 | tf_op jit(solution)/shard_map/ppermute | solution.py:466
  93.3 0.5 collective-permute-start.36
  93.8 1.2 collective-permute-start.34
  95.0 1.9 %collective-permute-done.30.refs_7_ = bf16[128,512]{1,0:T(8,128)(2,1)S(1)} collective-permute-done((bf16[128,512]{1,0:T(8,128)(2,1)S(1)}, bf16[128,512]{1,0:T(8,128)(2,1)S(1)}, u32[]{:S(2)}, u32[]{:S(2)}) %collective-permute-start.30) | collective-permute-done | bytes 131104 | tf_op jit(solution)/shard_map/ppermute | solution.py:466
  96.9 1.4 %collective-permute-done.29.refs_6_ = bf16[128,512]{1,0:T(8,128)(2,1)S(1)} collective-permute-done((bf16[128,512]{1,0:T(8,128)(2,1)S(1)}, bf16[128,512]{1,0:T(8,128)(2,1)S(1)}, u32[]{:S(2)}, u32[]{:S(2)}) %collective-permute-start.29) | collective-permute-done | bytes 131104 | tf_op jit(solution)/shard_map/ppermute | solution.py:466
  98.3 3.5 %collective-permute-done.36.refs_4_ = bf16[256,512]{1,0:T(8,128)(2,1)S(1)} collective-permute-done((bf16[256,512]{1,0:T(8,128)(2,1)S(1)}, bf16[256,512]{1,0:T(8,128)(2,1)S(1)}, u32[]{:S(2)}, u32[]{:S(2)}) %collective-permute-start.36) | collective-permute-done | bytes 262176 | tf_op jit(solution)/shard_map/ppermute | solution.py:466
  101.7 0.5 collective-permute-start.31
  102.4 1.2 collective-permute-start.39
  103.6 0.9 collective-permute-start.38
  104.5 5.9 %project_out.2 = (f32[256,1024]{1,0:T(8,128)S(1)}, f32[8,256]{1,0:T(8,128)S(1)}) custom-call(f32[8]{0:T(128)S(1)} %get-tuple-element.44.sign_ref, bf16[512,1024]{1,0:T(8,128)(2,1)S(1)} %copy-done, bf16[256,512]{1,0:T(8,128)(2,1)S(1)} %attend.5.refs_0_, bf16[256,512]{1,0:T(8,128)(2,1)S(1)} %collective-permute-done.24.refs_1_, ...), custom_call_target="tpu_custom_call" | custom-call | flops 2147483648 | bytes 12058624 | tf_op jit(solution)/shard_map/project_out/pallas_call | solution.py:408
  110.5 0.5 collective-permute-start.37
  111.0 0.1 collective-permute-start.40
  111.1 0.4 collective-permute-start.41
  111.5 1.1 collective-permute-done.40.refs_8_
  112.6 0.2 collective-permute-done.41.refs_9_
  112.8 5.9 %project_out.3 = (f32[256,1024]{1,0:T(8,128)S(1)}, f32[8,256]{1,0:T(8,128)S(1)}) custom-call(f32[8]{0:T(128)S(1)} %get-tuple-element.44.sign_ref, bf16[512,1024]{1,0:T(8,128)(2,1)S(1)} %copy-done, bf16[256,512]{1,0:T(8,128)(2,1)S(1)} %attend.7.refs_0_, bf16[256,512]{1,0:T(8,128)(2,1)S(1)} %collective-permute-done.33.refs_1_, ...), custom_call_target="tpu_custom_call" | custom-call | flops 2147483648 | bytes 12058624 | tf_op jit(solution)/shard_map/project_out/pallas_call | solution.py:408
  118.7 0.2 collective-permute-start.42
  118.8 1.0 collective-permute-done.42
  119.9 1.5 %collective-permute-start.43 = (f32[8,512]{1,0:T(8,128)S(1)}, f32[8,512]{1,0:T(8,128)S(1)}, u32[]{:S(2)}, u32[]{:S(2)}) collective-permute-start(f32[8,512]{1,0:T(8,128)S(1)} %add.10), channel_id=1, source_target_pairs={{0,2},{1,3},{2,0},{3,1},{4,6},{5,7},{6,4},{7,5},{8,10},{9,11},{10,... | collective-permute-start | bytes 49160 | tf_op jit(solution)/shard_map/ppermute | solution.py:466
  121.4 2.2 %collective-permute-done.43 = f32[8,512]{1,0:T(8,128)S(1)} collective-permute-done((f32[8,512]{1,0:T(8,128)S(1)}, f32[8,512]{1,0:T(8,128)S(1)}, u32[]{:S(2)}, u32[]{:S(2)}) %collective-permute-start.43) | collective-permute-done | bytes 16416 | tf_op jit(solution)/shard_map/ppermute | solution.py:466
  123.6 1.1 collective-permute-start.44
  124.7 2.6 %collective-permute-done.44 = f32[8,512]{1,0:T(8,128)S(1)} collective-permute-done((f32[8,512]{1,0:T(8,128)S(1)}, f32[8,512]{1,0:T(8,128)S(1)}, u32[]{:S(2)}, u32[]{:S(2)}) %collective-permute-start.44) | collective-permute-done | bytes 16416 | tf_op jit(solution)/shard_map/ppermute | solution.py:466
  127.4 1.3 final.1
  (54 shorter events, 0.4 us)
Async XLA Ops:
  3.4 3.2 %collective-permute-start = (bf16[272,1024]{1,0:T(8,128)(2,1)S(1)}, bf16[272,1024]{1,0:T(8,128)(2,1)S(1)}, u32[]{:S(2)}, u32[]{:S(2)}) collective-permute-start(bf16[272,1024]{1,0:T(8,128)(2,1)S(1)} %get-tuple-element.48.refs_0_), channel_id=1, source_target_pairs={{0,1},{1,0},{2,3},{3,2},{4,5},{5,4},{6,7},{7,6},{8,9},{9,8},{10,11... | collective-permute-start | bytes 1671176 | tf_op jit(solution)/shard_map/ppermute | solution.py:466
  3.5 15.0 %collective-permute-start.1 = (bf16[272,1024]{1,0:T(8,128)(2,1)S(1)}, bf16[272,1024]{1,0:T(8,128)(2,1)S(1)}, u32[]{:S(2)}, u32[]{:S(2)}) collective-permute-start(bf16[272,1024]{1,0:T(8,128)(2,1)S(1)} %get-tuple-element.48.refs_0_), channel_id=1, source_target_pairs={{0,2},{1,3},{2,0},{3,1},{4,6},{5,7},{6,4},{7,5},{8,10},{9,11},{10,... | collective-permute-start | bytes 1671176 | tf_op jit(solution)/shard_map/ppermute | solution.py:466
  5.0 15.1 %collective-permute-start.3 = (bf16[272,1024]{1,0:T(8,128)(2,1)S(1)}, bf16[272,1024]{1,0:T(8,128)(2,1)S(1)}, u32[]{:S(2)}, u32[]{:S(2)}) collective-permute-start(bf16[272,1024]{1,0:T(8,128)(2,1)S(1)} %get-tuple-element.48.refs_0_), channel_id=1, source_target_pairs={{0,4},{1,5},{2,6},{3,7},{4,0},{5,1},{6,2},{7,3},{8,12},{9,13},{10,... | collective-permute-start | bytes 1671176 | tf_op jit(solution)/shard_map/ppermute | solution.py:466
  18.5 9.3 %collective-permute-start.5 = (bf16[128,1024]{1,0:T(8,128)(2,1)S(1)}, bf16[128,1024]{1,0:T(8,128)(2,1)S(1)}, u32[]{:S(2)}, u32[]{:S(2)}) collective-permute-start(bf16[128,1024]{1,0:T(8,128)(2,1)S(1)} %slice.24), channel_id=1, source_target_pairs={{0,4},{1,5},{2,6},{3,7},{4,0},{5,1},{6,2},{7,3},{8,12},{9,13},{10,... | collective-permute-start | bytes 786440 | tf_op jit(solution)/shard_map/ppermute | solution.py:466
  20.1 17.6 %collective-permute-start.12 = (bf16[256,1024]{1,0:T(8,128)(2,1)S(1)}, bf16[256,1024]{1,0:T(8,128)(2,1)S(1)}, u32[]{:S(2)}, u32[]{:S(2)}) collective-permute-start(bf16[256,1024]{1,0:T(8,128)(2,1)S(1)} %get-tuple-element.58.refs_0_), channel_id=1, source_target_pairs={{0,4},{1,5},{2,6},{3,7},{4,0},{5,1},{6,2},{7,3},{8,12},{9,13},{10,... | collective-permute-start | bytes 1572872 | tf_op jit(solution)/shard_map/ppermute | solution.py:466
  21.3 9.4 %collective-permute-start.6 = (bf16[144,1024]{1,0:T(8,128)(2,1)S(1)}, bf16[144,1024]{1,0:T(8,128)(2,1)S(1)}, u32[]{:S(2)}, u32[]{:S(2)}) collective-permute-start(bf16[144,1024]{1,0:T(8,128)(2,1)S(1)} %slice.25), channel_id=1, source_target_pairs={{0,2},{1,3},{2,0},{3,1},{4,6},{5,7},{6,4},{7,5},{8,10},{9,11},{10,... | collective-permute-start | bytes 884744 | tf_op jit(solution)/shard_map/ppermute | solution.py:466
  22.2 19.4 %collective-permute-start.4 = (bf16[272,1024]{1,0:T(8,128)(2,1)S(1)}, bf16[272,1024]{1,0:T(8,128)(2,1)S(1)}, u32[]{:S(2)}, u32[]{:S(2)}) collective-permute-start(bf16[272,1024]{1,0:T(8,128)(2,1)S(1)} %collective-permute-done.3.refs_4_), channel_id=1, source_target_pairs={{0,1},{1,0},{2,3},{3,2},{4,5},{5,4},{6,7},{7,6},{8,9},{9,8},{10,11... | collective-permute-start | bytes 1671176 | tf_op jit(solution)/shard_map/ppermute | solution.py:466
  22.2 20.9 %collective-permute-start.2 = (bf16[272,1024]{1,0:T(8,128)(2,1)S(1)}, bf16[272,1024]{1,0:T(8,128)(2,1)S(1)}, u32[]{:S(2)}, u32[]{:S(2)}) collective-permute-start(bf16[272,1024]{1,0:T(8,128)(2,1)S(1)} %collective-permute-done.1.refs_2_), channel_id=1, source_target_pairs={{0,1},{1,0},{2,3},{3,2},{4,5},{5,4},{6,7},{7,6},{8,9},{9,8},{10,11... | collective-permute-start | bytes 1671176 | tf_op jit(solution)/shard_map/ppermute | solution.py:466
  27.8 12.7 %collective-permute-start.10 = (bf16[256,1024]{1,0:T(8,128)(2,1)S(1)}, bf16[256,1024]{1,0:T(8,128)(2,1)S(1)}, u32[]{:S(2)}, u32[]{:S(2)}) collective-permute-start(bf16[256,1024]{1,0:T(8,128)(2,1)S(1)} %get-tuple-element.58.refs_0_), channel_id=1, source_target_pairs={{0,2},{1,3},{2,0},{3,1},{4,6},{5,7},{6,4},{7,5},{8,10},{9,11},{10,... | collective-permute-start | bytes 1572872 | tf_op jit(solution)/shard_map/ppermute | solution.py:466
  30.7 12.4 %collective-permute-start.8 = (bf16[144,1024]{1,0:T(8,128)(2,1)S(1)}, bf16[144,1024]{1,0:T(8,128)(2,1)S(1)}, u32[]{:S(2)}, u32[]{:S(2)}) collective-permute-start(bf16[144,1024]{1,0:T(8,128)(2,1)S(1)} %collective-permute-done.6.refs_7_), channel_id=1, source_target_pairs={{0,1},{1,0},{2,3},{3,2},{4,5},{5,4},{6,7},{7,6},{8,9},{9,8},{10,11... | collective-permute-start | bytes 884744 | tf_op jit(solution)/shard_map/ppermute | solution.py:466
  37.7 2.9 %collective-permute-start.7 = (bf16[128,1024]{1,0:T(8,128)(2,1)S(1)}, bf16[128,1024]{1,0:T(8,128)(2,1)S(1)}, u32[]{:S(2)}, u32[]{:S(2)}) collective-permute-start(bf16[128,1024]{1,0:T(8,128)(2,1)S(1)} %collective-permute-done.5.refs_6_), channel_id=1, source_target_pairs={{0,1},{1,0},{2,3},{3,2},{4,5},{5,4},{6,7},{7,6},{8,9},{9,8},{10,11... | collective-permute-start | bytes 786440 | tf_op jit(solution)/shard_map/ppermute | solution.py:466
  40.5 15.8 %collective-permute-start.9 = (bf16[256,1024]{1,0:T(8,128)(2,1)S(1)}, bf16[256,1024]{1,0:T(8,128)(2,1)S(1)}, u32[]{:S(2)}, u32[]{:S(2)}) collective-permute-start(bf16[256,1024]{1,0:T(8,128)(2,1)S(1)} %get-tuple-element.58.refs_0_), channel_id=1, source_target_pairs={{0,1},{1,0},{2,3},{3,2},{4,5},{5,4},{6,7},{7,6},{8,9},{9,8},{10,11... | collective-permute-start | bytes 1572872 | tf_op jit(solution)/shard_map/ppermute | solution.py:466
  40.6 8.8 %collective-permute-start.15 = (bf16[128,1024]{1,0:T(8,128)(2,1)S(1)}, bf16[128,1024]{1,0:T(8,128)(2,1)S(1)}, u32[]{:S(2)}, u32[]{:S(2)}) collective-permute-start(bf16[128,1024]{1,0:T(8,128)(2,1)S(1)} %slice.33), channel_id=1, source_target_pairs={{0,2},{1,3},{2,0},{3,1},{4,6},{5,7},{6,4},{7,5},{8,10},{9,11},{10,... | collective-permute-start | bytes 786440 | tf_op jit(solution)/shard_map/ppermute | solution.py:466
  41.6 9.1 %collective-permute-start.14 = (bf16[128,1024]{1,0:T(8,128)(2,1)S(1)}, bf16[128,1024]{1,0:T(8,128)(2,1)S(1)}, u32[]{:S(2)}, u32[]{:S(2)}) collective-permute-start(bf16[128,1024]{1,0:T(8,128)(2,1)S(1)} %slice.32), channel_id=1, source_target_pairs={{0,4},{1,5},{2,6},{3,7},{4,0},{5,1},{6,2},{7,3},{8,12},{9,13},{10,... | collective-permute-start | bytes 786440 | tf_op jit(solution)/shard_map/ppermute | solution.py:466
  47.1 11.9 %collective-permute-start.13 = (bf16[256,1024]{1,0:T(8,128)(2,1)S(1)}, bf16[256,1024]{1,0:T(8,128)(2,1)S(1)}, u32[]{:S(2)}, u32[]{:S(2)}) collective-permute-start(bf16[256,1024]{1,0:T(8,128)(2,1)S(1)} %collective-permute-done.12.refs_4_), channel_id=1, source_target_pairs={{0,1},{1,0},{2,3},{3,2},{4,5},{5,4},{6,7},{7,6},{8,9},{9,8},{10,11... | collective-permute-start | bytes 1572872 | tf_op jit(solution)/shard_map/ppermute | solution.py:466
  47.2 11.8 %collective-permute-start.11 = (bf16[256,1024]{1,0:T(8,128)(2,1)S(1)}, bf16[256,1024]{1,0:T(8,128)(2,1)S(1)}, u32[]{:S(2)}, u32[]{:S(2)}) collective-permute-start(bf16[256,1024]{1,0:T(8,128)(2,1)S(1)} %collective-permute-done.10.refs_2_), channel_id=1, source_target_pairs={{0,1},{1,0},{2,3},{3,2},{4,5},{5,4},{6,7},{7,6},{8,9},{9,8},{10,11... | collective-permute-start | bytes 1572872 | tf_op jit(solution)/shard_map/ppermute | solution.py:466
  49.4 7.0 %collective-permute-start.18 = (bf16[256,256]{1,0:T(8,128)(2,1)S(1)}, bf16[256,256]{1,0:T(8,128)(2,1)S(1)}, u32[]{:S(2)}, u32[]{:S(2)}) collective-permute-start(bf16[256,256]{1,0:T(8,128)(2,1)S(1)} %get-tuple-element.64.refs_0_), channel_id=1, source_target_pairs={{0,8},{8,16},{16,24},{1,9},{9,17},{17,25},{2,10},{10,18},{18,26},{... | collective-permute-start | bytes 393224 | tf_op jit(solution)/shard_map/ppermute | solution.py:471
  50.7 7.0 %collective-permute-start.17 = (bf16[128,1024]{1,0:T(8,128)(2,1)S(1)}, bf16[128,1024]{1,0:T(8,128)(2,1)S(1)}, u32[]{:S(2)}, u32[]{:S(2)}) collective-permute-start(bf16[128,1024]{1,0:T(8,128)(2,1)S(1)} %collective-permute-done.15.refs_7_), channel_id=1, source_target_pairs={{0,1},{1,0},{2,3},{3,2},{4,5},{5,4},{6,7},{7,6},{8,9},{9,8},{10,11... | collective-permute-start | bytes 786440 | tf_op jit(solution)/shard_map/ppermute | solution.py:466
  56.4 2.6 %collective-permute-start.16 = (bf16[128,1024]{1,0:T(8,128)(2,1)S(1)}, bf16[128,1024]{1,0:T(8,128)(2,1)S(1)}, u32[]{:S(2)}, u32[]{:S(2)}) collective-permute-start(bf16[128,1024]{1,0:T(8,128)(2,1)S(1)} %collective-permute-done.14.refs_6_), channel_id=1, source_target_pairs={{0,1},{1,0},{2,3},{3,2},{4,5},{5,4},{6,7},{7,6},{8,9},{9,8},{10,11... | collective-permute-start | bytes 786440 | tf_op jit(solution)/shard_map/ppermute | solution.py:466
  56.4 10.7 %collective-permute-start.23 = (bf16[256,256]{1,0:T(8,128)(2,1)S(1)}, bf16[256,256]{1,0:T(8,128)(2,1)S(1)}, u32[]{:S(2)}, u32[]{:S(2)}) collective-permute-start(bf16[256,256]{1,0:T(8,128)(2,1)S(1)} %get-tuple-element.64.refs_0_), channel_id=1, source_target_pairs={{0,24},{1,25},{2,26},{3,27},{4,28},{5,29},{6,30},{7,31}} | collective-permute-start | bytes 393224 | tf_op jit(solution)/shard_map/ppermute | solution.py:471
  57.7 19.6 %collective-permute-start.22 = (bf16[256,256]{1,0:T(8,128)(2,1)S(1)}, bf16[256,256]{1,0:T(8,128)(2,1)S(1)}, u32[]{:S(2)}, u32[]{:S(2)}) collective-permute-start(bf16[256,256]{1,0:T(8,128)(2,1)S(1)} %get-tuple-element.64.refs_0_), channel_id=1, source_target_pairs={{0,16},{8,24},{1,17},{9,25},{2,18},{10,26},{3,19},{11,27},{4,20},{... | collective-permute-start | bytes 393224 | tf_op jit(solution)/shard_map/ppermute | solution.py:471
  63.1 41.5 %copy-start = (bf16[512,1024]{1,0:T(8,128)(2,1)S(1)}, bf16[512,1024]{1,0:T(8,128)(2,1)}, u32[]{:S(2)}) copy-start(bf16[512,1024]{1,0:T(8,128)(2,1)} %t_ref.3) | copy-start | bytes 3145732
  63.1 16.8 %collective-permute-start.21 = (bf16[256,256]{1,0:T(8,128)(2,1)S(1)}, bf16[256,256]{1,0:T(8,128)(2,1)S(1)}, u32[]{:S(2)}, u32[]{:S(2)}) collective-permute-start(bf16[256,256]{1,0:T(8,128)(2,1)S(1)} %get-tuple-element.66.refs_1_), channel_id=1, source_target_pairs={{0,24},{1,25},{2,26},{3,27},{4,28},{5,29},{6,30},{7,31}} | collective-permute-start | bytes 393224 | tf_op jit(solution)/shard_map/ppermute | solution.py:471
  64.5 15.6 %collective-permute-start.20 = (bf16[256,256]{1,0:T(8,128)(2,1)S(1)}, bf16[256,256]{1,0:T(8,128)(2,1)S(1)}, u32[]{:S(2)}, u32[]{:S(2)}) collective-permute-start(bf16[256,256]{1,0:T(8,128)(2,1)S(1)} %get-tuple-element.66.refs_1_), channel_id=1, source_target_pairs={{0,16},{8,24},{1,17},{9,25},{2,18},{10,26},{3,19},{11,27},{4,20},{... | collective-permute-start | bytes 393224 | tf_op jit(solution)/shard_map/ppermute | solution.py:471
  65.8 14.3 %collective-permute-start.19 = (bf16[256,256]{1,0:T(8,128)(2,1)S(1)}, bf16[256,256]{1,0:T(8,128)(2,1)S(1)}, u32[]{:S(2)}, u32[]{:S(2)}) collective-permute-start(bf16[256,256]{1,0:T(8,128)(2,1)S(1)} %get-tuple-element.66.refs_1_), channel_id=1, source_target_pairs={{0,8},{8,16},{16,24},{1,9},{9,17},{17,25},{2,10},{10,18},{18,26},{... | collective-permute-start | bytes 393224 | tf_op jit(solution)/shard_map/ppermute | solution.py:471
  82.4 8.3 %collective-permute-start.27 = (bf16[256,512]{1,0:T(8,128)(2,1)S(1)}, bf16[256,512]{1,0:T(8,128)(2,1)S(1)}, u32[]{:S(2)}, u32[]{:S(2)}) collective-permute-start(bf16[256,512]{1,0:T(8,128)(2,1)S(1)} %attend.5.refs_0_), channel_id=1, source_target_pairs={{0,4},{1,5},{2,6},{3,7},{4,0},{5,1},{6,2},{7,3},{8,12},{9,13},{10,... | collective-permute-start | bytes 786440 | tf_op jit(solution)/shard_map/ppermute | solution.py:466
  83.4 8.3 %collective-permute-start.25 = (bf16[256,512]{1,0:T(8,128)(2,1)S(1)}, bf16[256,512]{1,0:T(8,128)(2,1)S(1)}, u32[]{:S(2)}, u32[]{:S(2)}) collective-permute-start(bf16[256,512]{1,0:T(8,128)(2,1)S(1)} %attend.5.refs_0_), channel_id=1, source_target_pairs={{0,2},{1,3},{2,0},{3,1},{4,6},{5,7},{6,4},{7,5},{8,10},{9,11},{10,... | collective-permute-start | bytes 786440 | tf_op jit(solution)/shard_map/ppermute | solution.py:466
  90.8 6.1 %collective-permute-start.30 = (bf16[128,512]{1,0:T(8,128)(2,1)S(1)}, bf16[128,512]{1,0:T(8,128)(2,1)S(1)}, u32[]{:S(2)}, u32[]{:S(2)}) collective-permute-start(bf16[128,512]{1,0:T(8,128)(2,1)S(1)} %slice.35), channel_id=1, source_target_pairs={{0,2},{1,3},{2,0},{3,1},{4,6},{5,7},{6,4},{7,5},{8,10},{9,11},{10,... | collective-permute-start | bytes 393224 | tf_op jit(solution)/shard_map/ppermute | solution.py:466
  91.7 6.5 %collective-permute-start.29 = (bf16[128,512]{1,0:T(8,128)(2,1)S(1)}, bf16[128,512]{1,0:T(8,128)(2,1)S(1)}, u32[]{:S(2)}, u32[]{:S(2)}) collective-permute-start(bf16[128,512]{1,0:T(8,128)(2,1)S(1)} %slice.34), channel_id=1, source_target_pairs={{0,4},{1,5},{2,6},{3,7},{4,0},{5,1},{6,2},{7,3},{8,12},{9,13},{10,... | collective-permute-start | bytes 393224 | tf_op jit(solution)/shard_map/ppermute | solution.py:466
  93.3 8.4 %collective-permute-start.36 = (bf16[256,512]{1,0:T(8,128)(2,1)S(1)}, bf16[256,512]{1,0:T(8,128)(2,1)S(1)}, u32[]{:S(2)}, u32[]{:S(2)}) collective-permute-start(bf16[256,512]{1,0:T(8,128)(2,1)S(1)} %attend.7.refs_0_), channel_id=1, source_target_pairs={{0,4},{1,5},{2,6},{3,7},{4,0},{5,1},{6,2},{7,3},{8,12},{9,13},{10,... | collective-permute-start | bytes 786440 | tf_op jit(solution)/shard_map/ppermute | solution.py:466
  93.8 7.9 %collective-permute-start.34 = (bf16[256,512]{1,0:T(8,128)(2,1)S(1)}, bf16[256,512]{1,0:T(8,128)(2,1)S(1)}, u32[]{:S(2)}, u32[]{:S(2)}) collective-permute-start(bf16[256,512]{1,0:T(8,128)(2,1)S(1)} %attend.7.refs_0_), channel_id=1, source_target_pairs={{0,2},{1,3},{2,0},{3,1},{4,6},{5,7},{6,4},{7,5},{8,10},{9,11},{10,... | collective-permute-start | bytes 786440 | tf_op jit(solution)/shard_map/ppermute | solution.py:466
  95.0 7.3 %collective-permute-start.24 = (bf16[256,512]{1,0:T(8,128)(2,1)S(1)}, bf16[256,512]{1,0:T(8,128)(2,1)S(1)}, u32[]{:S(2)}, u32[]{:S(2)}) collective-permute-start(bf16[256,512]{1,0:T(8,128)(2,1)S(1)} %attend.5.refs_0_), channel_id=1, source_target_pairs={{0,1},{1,0},{2,3},{3,2},{4,5},{5,4},{6,7},{7,6},{8,9},{9,8},{10,11... | collective-permute-start | bytes 786440 | tf_op jit(solution)/shard_map/ppermute | solution.py:466
  96.9 5.5 %collective-permute-start.28 = (bf16[256,512]{1,0:T(8,128)(2,1)S(1)}, bf16[256,512]{1,0:T(8,128)(2,1)S(1)}, u32[]{:S(2)}, u32[]{:S(2)}) collective-permute-start(bf16[256,512]{1,0:T(8,128)(2,1)S(1)} %collective-permute-done.27.refs_4_), channel_id=1, source_target_pairs={{0,1},{1,0},{2,3},{3,2},{4,5},{5,4},{6,7},{7,6},{8,9},{9,8},{10,11... | collective-permute-start | bytes 786440 | tf_op jit(solution)/shard_map/ppermute | solution.py:466
  98.2 5.3 %collective-permute-start.26 = (bf16[256,512]{1,0:T(8,128)(2,1)S(1)}, bf16[256,512]{1,0:T(8,128)(2,1)S(1)}, u32[]{:S(2)}, u32[]{:S(2)}) collective-permute-start(bf16[256,512]{1,0:T(8,128)(2,1)S(1)} %collective-permute-done.25.refs_2_), channel_id=1, source_target_pairs={{0,1},{1,0},{2,3},{3,2},{4,5},{5,4},{6,7},{7,6},{8,9},{9,8},{10,11... | collective-permute-start | bytes 786440 | tf_op jit(solution)/shard_map/ppermute | solution.py:466
  101.7 2.8 %collective-permute-start.32 = (bf16[128,512]{1,0:T(8,128)(2,1)S(1)}, bf16[128,512]{1,0:T(8,128)(2,1)S(1)}, u32[]{:S(2)}, u32[]{:S(2)}) collective-permute-start(bf16[128,512]{1,0:T(8,128)(2,1)S(1)} %collective-permute-done.30.refs_7_), channel_id=1, source_target_pairs={{0,1},{1,0},{2,3},{3,2},{4,5},{5,4},{6,7},{7,6},{8,9},{9,8},{10,11... | collective-permute-start | bytes 393224 | tf_op jit(solution)/shard_map/ppermute | solution.py:466
  101.7 2.8 %collective-permute-start.31 = (bf16[128,512]{1,0:T(8,128)(2,1)S(1)}, bf16[128,512]{1,0:T(8,128)(2,1)S(1)}, u32[]{:S(2)}, u32[]{:S(2)}) collective-permute-start(bf16[128,512]{1,0:T(8,128)(2,1)S(1)} %collective-permute-done.29.refs_6_), channel_id=1, source_target_pairs={{0,1},{1,0},{2,3},{3,2},{4,5},{5,4},{6,7},{7,6},{8,9},{9,8},{10,11... | collective-permute-start | bytes 393224 | tf_op jit(solution)/shard_map/ppermute | solution.py:466
  102.3 9.2 %collective-permute-start.33 = (bf16[256,512]{1,0:T(8,128)(2,1)S(1)}, bf16[256,512]{1,0:T(8,128)(2,1)S(1)}, u32[]{:S(2)}, u32[]{:S(2)}) collective-permute-start(bf16[256,512]{1,0:T(8,128)(2,1)S(1)} %attend.7.refs_0_), channel_id=1, source_target_pairs={{0,1},{1,0},{2,3},{3,2},{4,5},{5,4},{6,7},{7,6},{8,9},{9,8},{10,11... | collective-permute-start | bytes 786440 | tf_op jit(solution)/shard_map/ppermute | solution.py:466
  102.4 8.6 %collective-permute-start.39 = (bf16[128,512]{1,0:T(8,128)(2,1)S(1)}, bf16[128,512]{1,0:T(8,128)(2,1)S(1)}, u32[]{:S(2)}, u32[]{:S(2)}) collective-permute-start(bf16[128,512]{1,0:T(8,128)(2,1)S(1)} %slice.37), channel_id=1, source_target_pairs={{0,2},{1,3},{2,0},{3,1},{4,6},{5,7},{6,4},{7,5},{8,10},{9,11},{10,... | collective-permute-start | bytes 393224 | tf_op jit(solution)/shard_map/ppermute | solution.py:466
  103.6 7.4 %collective-permute-start.38 = (bf16[128,512]{1,0:T(8,128)(2,1)S(1)}, bf16[128,512]{1,0:T(8,128)(2,1)S(1)}, u32[]{:S(2)}, u32[]{:S(2)}) collective-permute-start(bf16[128,512]{1,0:T(8,128)(2,1)S(1)} %slice.36), channel_id=1, source_target_pairs={{0,4},{1,5},{2,6},{3,7},{4,0},{5,1},{6,2},{7,3},{8,12},{9,13},{10,... | collective-permute-start | bytes 393224 | tf_op jit(solution)/shard_map/ppermute | solution.py:466
  110.4 2.3 %collective-permute-start.35 = (bf16[256,512]{1,0:T(8,128)(2,1)S(1)}, bf16[256,512]{1,0:T(8,128)(2,1)S(1)}, u32[]{:S(2)}, u32[]{:S(2)}) collective-permute-start(bf16[256,512]{1,0:T(8,128)(2,1)S(1)} %collective-permute-done.34.refs_2_), channel_id=1, source_target_pairs={{0,1},{1,0},{2,3},{3,2},{4,5},{5,4},{6,7},{7,6},{8,9},{9,8},{10,11... | collective-permute-start | bytes 786440 | tf_op jit(solution)/shard_map/ppermute | solution.py:466
  110.5 2.3 %collective-permute-start.37 = (bf16[256,512]{1,0:T(8,128)(2,1)S(1)}, bf16[256,512]{1,0:T(8,128)(2,1)S(1)}, u32[]{:S(2)}, u32[]{:S(2)}) collective-permute-start(bf16[256,512]{1,0:T(8,128)(2,1)S(1)} %collective-permute-done.36.refs_4_), channel_id=1, source_target_pairs={{0,1},{1,0},{2,3},{3,2},{4,5},{5,4},{6,7},{7,6},{8,9},{9,8},{10,11... | collective-permute-start | bytes 786440 | tf_op jit(solution)/shard_map/ppermute | solution.py:466
  111.0 1.6 %collective-permute-start.40 = (bf16[128,512]{1,0:T(8,128)(2,1)S(1)}, bf16[128,512]{1,0:T(8,128)(2,1)S(1)}, u32[]{:S(2)}, u32[]{:S(2)}) collective-permute-start(bf16[128,512]{1,0:T(8,128)(2,1)S(1)} %collective-permute-done.38.refs_6_), channel_id=1, source_target_pairs={{0,1},{1,0},{2,3},{3,2},{4,5},{5,4},{6,7},{7,6},{8,9},{9,8},{10,11... | collective-permute-start | bytes 393224 | tf_op jit(solution)/shard_map/ppermute | solution.py:466
  111.1 1.7 %collective-permute-start.41 = (bf16[128,512]{1,0:T(8,128)(2,1)S(1)}, bf16[128,512]{1,0:T(8,128)(2,1)S(1)}, u32[]{:S(2)}, u32[]{:S(2)}) collective-permute-start(bf16[128,512]{1,0:T(8,128)(2,1)S(1)} %collective-permute-done.39.refs_7_), channel_id=1, source_target_pairs={{0,1},{1,0},{2,3},{3,2},{4,5},{5,4},{6,7},{7,6},{8,9},{9,8},{10,11... | collective-permute-start | bytes 393224 | tf_op jit(solution)/shard_map/ppermute | solution.py:466
  118.7 1.2 collective-permute-start.42
  119.9 3.7 %collective-permute-start.43 = (f32[8,512]{1,0:T(8,128)S(1)}, f32[8,512]{1,0:T(8,128)S(1)}, u32[]{:S(2)}, u32[]{:S(2)}) collective-permute-start(f32[8,512]{1,0:T(8,128)S(1)} %add.10), channel_id=1, source_target_pairs={{0,2},{1,3},{2,0},{3,1},{4,6},{5,7},{6,4},{7,5},{8,10},{9,11},{10,... | collective-permute-start | bytes 49160 | tf_op jit(solution)/shard_map/ppermute | solution.py:466
  123.6 3.7 %collective-permute-start.44 = (f32[8,512]{1,0:T(8,128)S(1)}, f32[8,512]{1,0:T(8,128)S(1)}, u32[]{:S(2)}, u32[]{:S(2)}) collective-permute-start(f32[8,512]{1,0:T(8,128)S(1)} %add.11), channel_id=1, source_target_pairs={{0,4},{1,5},{2,6},{3,7},{4,0},{5,1},{6,2},{7,3},{8,12},{9,13},{10,... | collective-permute-start | bytes 49160 | tf_op jit(solution)/shard_map/ppermute | solution.py:466

commit v4 on v3

--- a/solution.py
+++ b/solution.py
@@ -466,9 +466,9 @@
     return lax.ppermute(x, "tp", [(i, i ^ mask) for i in range(count)])
 
 
-def send_up(x, distance):
+def send_up(x, distance, first=0):
     count = lax.axis_size("ctx")
-    return lax.ppermute(x, "ctx", [(i, i + distance) for i in range(count - distance)])
+    return lax.ppermute(x, "ctx", [(i, i + distance) for i in range(first, count - distance)])
 
 
 def after(x, *others):
@@ -477,19 +477,21 @@
 
 def gather(own, core_after=None, beside=None):
     count = lax.axis_size("tp")
-    got = {0: [own]}
+    got, direct = {0: [own]}, []
     masks = [1 << b for b in range(1, count.bit_length() - 1)]
     if len(masks) >= 2:
         a, b = masks[0], masks[1]
         half = own.shape[0] // (2 * EXTRA) * EXTRA
         got[a] = [swap(own, a)]
         got[b] = [swap(own, b)]
-        via_a, via_b = got[a][0], got[b][0]
+        direct = via_a, via_b = got[a][0], got[b][0]
         got[1] = [swap(own, 1)]
         if beside is not None:
             first = beside(got[1][0])
             via_a, via_b = after(via_a, first), after(via_b, first)
         got[a | b] = [swap(via_a[:half], b), swap(via_b[half:], a)]
+        first = got[a | b][0]
+        got[a], got[b] = [after(got[a][0], first)], [after(got[b][0], first)]
         masks = masks[2:]
     if core_after is not None:
         for m in got:
@@ -502,7 +504,7 @@
     for mask in masks:
         for m in list(got):
             got[m | mask] = [swap(p, mask) for p in got[m]]
-    return [got[m] for m in range(count)]
+    return [got[m] for m in range(count)], direct
 
 
 def body(hidden_in, norm_gain, w_query, w_key, w_value, sign_bits, w_out, teacher):
@@ -536,9 +538,9 @@
     for at in range(HALVES):
         own = clipped[at]
         if at:
-            own = after(own, *[b[0] for b in blocks[2:6:2]], loaded[1])
+            own = after(own, *neighbours, loaded[1])
         if at:
-            blocks = gather(own, core_after=queries[-1])
+            blocks, neighbours = gather(own, core_after=queries[-1])
         else:
             loaded = []
 
@@ -547,12 +549,10 @@
                 loaded.extend(load(first, w_key, w_value, w_out))
                 return loaded[1]
 
-            blocks = gather(own, beside=bring)
+            blocks, neighbours = gather(own, beside=bring)
             if not loaded:
                 bring(own)
         part = squares
-        if at and ctx_count > 1:
-            part = after(part, kvs[0][1])
         q, kv, *rest = proj(order, blocks, at, half, part, *loaded[:3])
         if rest:
             squares = rest[0]
@@ -571,7 +571,15 @@
                 )
             kv = jnp.concatenate([k, v], axis=1)
         queries.append(q)
-        kvs.append([kv] + [send_up(kv, hop) for hop in range(1, ctx_count)])
+        kvs.append([kv])
+        for hop in range(1, ctx_count):
+            if at == HALVES - 1:
+                kvs[at].append(send_up(kv, hop))
+            elif hop < 2:
+                kvs[at].append(send_up(kvs[at][-1], 1, hop - 1))
+        for near in kvs[:at]:
+            for hop in range(len(near), ctx_count):
+                near.append(send_up(after(near[-1], q), 1, hop - 1))
 
     states = []
     for at in range(HALVES):
@@ -587,8 +595,8 @@
             ctx_at, queries[at], at * half, kv_heads, [], far, states[at], signs
         )
         if at:
-            signed = after(signed, *[b[0] for b in blocks[2:6:2]])
-        blocks = gather(signed, branches[-1] if at else None)
+            signed = after(signed, *neighbours)
+        blocks, neighbours = gather(signed, branches[-1] if at else None)
         b, s = project_out(flips, blocks, loaded[3], teacher, at)
         branches.append(b)
         stats.append(s)

time: 131 us -> 140 us (1.069); the launches traced: 129 us -> 140 us
  waiting for transfers between devices: 53.3 us -> 65.8 us
  starting transfers between devices: 33.1 us -> 31.5 us
    ppermute x39, waiting for transfers between devices: 37.3 us -> 49.3 us  [swap(): return lax.ppermute(x, 'tp', [(i, i ^ mask) for i in range(count)])]
    ppermute x39, starting transfers between devices: 25.2 us -> 23.8 us  [swap(): return lax.ppermute(x, 'tp', [(i, i ^ mask) for i in range(count)])]
  transfers between devices with their start and end apart: 45 -> 45, of which waited for: 18 -> 23; matrix products, arithmetic and copies ran while one was open for 0% -> 0% of each run, Pallas kernels for 22% -> 21%
where the time goes in v4:
time: 140 us
  waiting for transfers between devices  65.8 us (47%)
  Pallas kernels  40.5 us (29%)
  starting transfers between devices  31.5 us (22%)
    ppermute x39, waiting for transfers between devices, swap(): return lax.ppermute(x, 'tp', [(i, i ^ mask) for i in range(count)])  49.3 us
    ppermute x39, starting transfers between devices, swap(): return lax.ppermute(x, 'tp', [(i, i ^ mask) for i in range(count)])  23.8 us
    ppermute x6, waiting for transfers between devices, send_up(): lax.ppermute(x, 'ctx', [(i, i + distance) for i in range(first, count - d...  16.5 us
    pallas_call x2, Pallas kernels, project_out(): pl.pallas_call(functools.partial(out_kernel, counts, steps, chunk), in_sp...  11.8 us
    pallas_call x4, Pallas kernels, attend(): pl.pallas_call(kernel, in_specs=[IN_SMEM] + [IN_VMEM] * (len(args) - 1),...  10.1 us
    pallas_call x2, Pallas kernels, proj(): pl.pallas_call(functools.partial(proj_kernel, counts, chunk), in_specs=[I...  8.04 us
    ppermute x6, starting transfers between devices, send_up(): lax.ppermute(x, 'ctx', [(i, i + distance) for i in range(first, count - d...  7.72 us
    pallas_call x1, Pallas kernels, load(): pl.pallas_call(functools.partial(load_kernel, count), in_specs=[IN_HBM] *...  7.19 us
  transfers between devices with their start and end apart: 45, of which 23 were waited for; matrix products, arithmetic and copies ran while one was open for 0% of the time, Pallas kernels for 21%

profile of v4, /device:TPU:24, one launch (start us, length us, event | category | flops | bytes accessed | tf_op | source)
XLA Modules:
  0.0 139.5 jit_solution(16136202546961644526)
XLA Ops:
  0.7 0.7 add_convert_fusion.refs_6_
  1.3 2.1 %pre.1 = (bf16[272,1024]{1,0:T(8,128)(2,1)S(1)}, bf16[256,1024]{1,0:T(8,128)(2,1)S(1)}) custom-call(bf16[512,1024]{1,0:T(8,128)(2,1)} %h_hbm.1, bf16[8,128]{1,0:T(8,128)(2,1)} %bitcast.3), custom_call_target="tpu_custom_call" | custom-call | flops 4194304 | bytes 2097152 | tf_op jit(solution)/shard_map/pre/pallas_call | solution.py:88
  3.5 1.6 %collective-permute-start.1 = (bf16[272,1024]{1,0:T(8,128)(2,1)S(1)}, bf16[272,1024]{1,0:T(8,128)(2,1)S(1)}, u32[]{:S(2)}, u32[]{:S(2)}) collective-permute-start(bf16[272,1024]{1,0:T(8,128)(2,1)S(1)} %get-tuple-element.57.refs_0_), channel_id=1, source_target_pairs={{0,2},{1,3},{2,0},{3,1},{4,6},{5,7},{6,4},{7,5},{8,10},{9,11},{10,... | collective-permute-start | bytes 1671176 | tf_op jit(solution)/shard_map/ppermute | solution.py:466
  5.0 1.5 %collective-permute-start.4 = (bf16[272,1024]{1,0:T(8,128)(2,1)S(1)}, bf16[272,1024]{1,0:T(8,128)(2,1)S(1)}, u32[]{:S(2)}, u32[]{:S(2)}) collective-permute-start(bf16[272,1024]{1,0:T(8,128)(2,1)S(1)} %get-tuple-element.57.refs_0_), channel_id=1, source_target_pairs={{0,4},{1,5},{2,6},{3,7},{4,0},{5,1},{6,2},{7,3},{8,12},{9,13},{10,... | collective-permute-start | bytes 1671176 | tf_op jit(solution)/shard_map/ppermute | solution.py:466
  6.6 7.2 %load.1 = (bf16[8192,512]{1,0:T(8,128)(2,1)S(1)}, bf16[8192,128]{1,0:T(8,128)(2,1)S(1)}, bf16[8192,128]{1,0:T(8,128)(2,1)S(1)}, bf16[4096,1024]{1,0:T(8,128)(2,1)S(1)}) custom-call(bf16[8192,512]{1,0:T(8,128)(2,1)} %refs_0_, bf16[8192,128]{1,0:T(8,128)(2,1)} %refs_1_.1, bf16[8192,128]{1,0:T(8,128)(2,1)} %refs_2_.1, bf16[4096,1024]{1,0:T(8,128)(2,1)} %refs_3_.1), custom_call_target="tpu_custom_call" | custom-call | bytes 41943040 | tf_op jit(solution)/shard_map/load/pallas_call | solution.py:125
  13.8 4.8 %collective-permute-done.1.refs_2_ = bf16[272,1024]{1,0:T(8,128)(2,1)S(1)} collective-permute-done((bf16[272,1024]{1,0:T(8,128)(2,1)S(1)}, bf16[272,1024]{1,0:T(8,128)(2,1)S(1)}, u32[]{:S(2)}, u32[]{:S(2)}) %collective-permute-start.1) | collective-permute-done | bytes 557088 | tf_op jit(solution)/shard_map/ppermute | solution.py:466
  18.5 1.6 %collective-permute-start.2 = (bf16[128,1024]{1,0:T(8,128)(2,1)S(1)}, bf16[128,1024]{1,0:T(8,128)(2,1)S(1)}, u32[]{:S(2)}, u32[]{:S(2)}) collective-permute-start(bf16[128,1024]{1,0:T(8,128)(2,1)S(1)} %slice.24), channel_id=1, source_target_pairs={{0,4},{1,5},{2,6},{3,7},{4,0},{5,1},{6,2},{7,3},{8,12},{9,13},{10,... | collective-permute-start | bytes 786440 | tf_op jit(solution)/shard_map/ppermute | solution.py:466
  20.1 1.5 %collective-permute-start.10 = (bf16[256,1024]{1,0:T(8,128)(2,1)S(1)}, bf16[256,1024]{1,0:T(8,128)(2,1)S(1)}, u32[]{:S(2)}, u32[]{:S(2)}) collective-permute-start(bf16[256,1024]{1,0:T(8,128)(2,1)S(1)} %get-tuple-element.69.refs_0_), channel_id=1, source_target_pairs={{0,2},{1,3},{2,0},{3,1},{4,6},{5,7},{6,4},{7,5},{8,10},{9,11},{10,... | collective-permute-start | bytes 1572872 | tf_op jit(solution)/shard_map/ppermute | solution.py:466
  21.6 0.5 collective-permute-start.13
  22.2 1.2 collective-permute-start.6
  23.4 4.5 %collective-permute-done.2.refs_6_ = bf16[128,1024]{1,0:T(8,128)(2,1)S(1)} collective-permute-done((bf16[128,1024]{1,0:T(8,128)(2,1)S(1)}, bf16[128,1024]{1,0:T(8,128)(2,1)S(1)}, u32[]{:S(2)}, u32[]{:S(2)}) %collective-permute-start.2) | collective-permute-done | bytes 262176 | tf_op jit(solution)/shard_map/ppermute | solution.py:466
  27.8 0.5 collective-permute-start.3
  28.3 11.3 %collective-permute-done.6.refs_7_ = bf16[144,1024]{1,0:T(8,128)(2,1)S(1)} collective-permute-done((bf16[144,1024]{1,0:T(8,128)(2,1)S(1)}, bf16[144,1024]{1,0:T(8,128)(2,1)S(1)}, u32[]{:S(2)}, u32[]{:S(2)}) %collective-permute-start.6) | collective-permute-done | bytes 294944 | tf_op jit(solution)/shard_map/ppermute | solution.py:466
  39.7 1.1 collective-permute-start.11
  41.1 7.4 %collective-permute-done.11.refs_6_ = bf16[128,1024]{1,0:T(8,128)(2,1)S(1)} collective-permute-done((bf16[128,1024]{1,0:T(8,128)(2,1)S(1)}, bf16[128,1024]{1,0:T(8,128)(2,1)S(1)}, u32[]{:S(2)}, u32[]{:S(2)}) %collective-permute-start.11) | collective-permute-done | bytes 262176 | tf_op jit(solution)/shard_map/ppermute | solution.py:466
  48.5 1.5 %collective-permute-start.15 = (bf16[128,1024]{1,0:T(8,128)(2,1)S(1)}, bf16[128,1024]{1,0:T(8,128)(2,1)S(1)}, u32[]{:S(2)}, u32[]{:S(2)}) collective-permute-start(bf16[128,1024]{1,0:T(8,128)(2,1)S(1)} %slice.33), channel_id=1, source_target_pairs={{0,2},{1,3},{2,0},{3,1},{4,6},{5,7},{6,4},{7,5},{8,10},{9,11},{10,... | collective-permute-start | bytes 786440 | tf_op jit(solution)/shard_map/ppermute | solution.py:466
  50.0 4.0 %proj.2 = (bf16[256,512]{1,0:T(8,128)(2,1)S(1)}, bf16[256,256]{1,0:T(8,128)(2,1)S(1)}, f32[8,512]{1,0:T(8,128)S(1)}) custom-call(s32[8]{0:T(128)S(1)} %get-tuple-element.55.order_ref, bf16[272,1024]{1,0:T(8,128)(2,1)S(1)} %get-tuple-element.57.refs_0_, bf16[272,1024]{1,0:T(8,128)(2,1)S(1)} %collective-permute-done.refs_1_, ...), custom_call_target="tpu_custom_call" | custom-call | flops 3221225472 | bytes 16777216 | tf_op jit(solution)/shard_map/proj/pallas_call | solution.py:204
  54.0 0.3 collective-permute-start.14
  54.3 0.3 collective-permute-start.12
  54.6 2.6 %collective-permute-done.15.refs_7_ = bf16[128,1024]{1,0:T(8,128)(2,1)S(1)} collective-permute-done((bf16[128,1024]{1,0:T(8,128)(2,1)S(1)}, bf16[128,1024]{1,0:T(8,128)(2,1)S(1)}, u32[]{:S(2)}, u32[]{:S(2)}) %collective-permute-start.15) | collective-permute-done | bytes 262176 | tf_op jit(solution)/shard_map/ppermute | solution.py:466
  57.2 0.5 collective-permute-start.16
  57.7 1.3 collective-permute-start.21
  59.1 4.0 %proj.3 = (bf16[256,512]{1,0:T(8,128)(2,1)S(1)}, bf16[256,256]{1,0:T(8,128)(2,1)S(1)}) custom-call(s32[8]{0:T(128)S(1)} %get-tuple-element.55.order_ref, bf16[256,1024]{1,0:T(8,128)(2,1)S(1)} %get-tuple-element.69.refs_0_, bf16[256,1024]{1,0:T(8,128)(2,1)S(1)} %collective-permute-done.9.refs_1_, bf16[256,1024]{1,0:T(8,128)(2,1)S(1)} %collective-permute-done.10.refs_2_, ...), custom_call_target="tpu_custom_call" | custom-call | flops 3221225472 | bytes 16777216 | tf_op jit(solution)/shard_map/proj/pallas_call | solution.py:204
  63.2 1.8 %collective-permute-done.21.refs_1_.refs_2_ = bf16[256,256]{1,0:T(8,128)(2,1)S(1)} collective-permute-done((bf16[256,256]{1,0:T(8,128)(2,1)S(1)}, bf16[256,256]{1,0:T(8,128)(2,1)S(1)}, u32[]{:S(2)}, u32[]{:S(2)}) %collective-permute-start.21) | collective-permute-done | bytes 131104 | tf_op jit(solution)/shard_map/ppermute | solution.py:471
  65.0 1.3 collective-permute-start.22
  66.3 5.6 %collective-permute-done.22.refs_2_.refs_3_ = bf16[256,256]{1,0:T(8,128)(2,1)S(1)} collective-permute-done((bf16[256,256]{1,0:T(8,128)(2,1)S(1)}, bf16[256,256]{1,0:T(8,128)(2,1)S(1)}, u32[]{:S(2)}, u32[]{:S(2)}) %collective-permute-start.22) | collective-permute-done | bytes 131104 | tf_op jit(solution)/shard_map/ppermute | solution.py:471
  71.9 1.3 collective-permute-start.23
  73.1 1.3 collective-permute-start.18
  74.4 1.3 collective-permute-start.19
  75.7 1.3 collective-permute-start.20
  77.0 3.4 %collective-permute-done.23.refs_3_.refs_4_ = bf16[256,256]{1,0:T(8,128)(2,1)S(1)} collective-permute-done((bf16[256,256]{1,0:T(8,128)(2,1)S(1)}, bf16[256,256]{1,0:T(8,128)(2,1)S(1)}, u32[]{:S(2)}, u32[]{:S(2)}) %collective-permute-start.23) | collective-permute-done | bytes 131104 | tf_op jit(solution)/shard_map/ppermute | solution.py:471
  80.5 2.6 %attend.4 = (f32[8,256]{1,0:T(8,128)S(1)}, f32[8,256]{1,0:T(8,128)S(1)}, f32[4,128,256]{2,1,0:T(8,128)S(1)}) custom-call(s32[1]{0:T(128)} %bitcast.1.me_ref, bf16[256,512]{1,0:T(8,128)(2,1)S(1)} %get-tuple-element.67.q_ref, bf16[256,256]{1,0:T(8,128)(2,1)S(1)} %get-tuple-element.78.refs_0_, bf16[256,256]{1,0:T(8,128)(2,1)S(1)} %collective-permute-done.21.refs_1_.refs_2_, ...), custom_call_target="tpu_custom_call" | custom-call | flops 536870912 | bytes 524288 | tf_op jit(solution)/shard_map/attend/pallas_call | solution.py:313
  83.0 0.2 collective-permute-done.18.refs_0_
  83.3 5.4 %collective-permute-done.19.refs_1_ = bf16[256,256]{1,0:T(8,128)(2,1)S(1)} collective-permute-done((bf16[256,256]{1,0:T(8,128)(2,1)S(1)}, bf16[256,256]{1,0:T(8,128)(2,1)S(1)}, u32[]{:S(2)}, u32[]{:S(2)}) %collective-permute-start.19) | collective-permute-done | bytes 131104 | tf_op jit(solution)/shard_map/ppermute | solution.py:471
  88.7 2.3 %attend.5.refs_0_ = bf16[256,512]{1,0:T(8,128)(2,1)S(1)} custom-call(s32[1]{0:T(128)} %bitcast.1.me_ref, bf16[256,512]{1,0:T(8,128)(2,1)S(1)} %get-tuple-element.67.q_ref, bf16[256,256]{1,0:T(8,128)(2,1)S(1)} %collective-permute-done.18.refs_0_, bf16[256,256]{1,0:T(8,128)(2,1)S(1)} %collective-permute-done.19.refs_1_, ...), custom_call_target="tpu_custom_call" | custom-call | flops 402653184 | bytes 393216 | tf_op jit(solution)/shard_map/attend/pallas_call | solution.py:313
  91.1 1.6 %collective-permute-start.25 = (bf16[256,512]{1,0:T(8,128)(2,1)S(1)}, bf16[256,512]{1,0:T(8,128)(2,1)S(1)}, u32[]{:S(2)}, u32[]{:S(2)}) collective-permute-start(bf16[256,512]{1,0:T(8,128)(2,1)S(1)} %attend.5.refs_0_), channel_id=1, source_target_pairs={{0,2},{1,3},{2,0},{3,1},{4,6},{5,7},{6,4},{7,5},{8,10},{9,11},{10,... | collective-permute-start | bytes 786440 | tf_op jit(solution)/shard_map/ppermute | solution.py:466
  92.6 0.5 collective-permute-start.28
  93.1 3.1 %attend.6 = (f32[8,256]{1,0:T(8,128)S(1)}, f32[8,256]{1,0:T(8,128)S(1)}, f32[4,128,256]{2,1,0:T(8,128)S(1)}) custom-call(s32[1]{0:T(128)} %bitcast.1.me_ref, bf16[256,512]{1,0:T(8,128)(2,1)S(1)} %get-tuple-element.79.q_ref, bf16[256,256]{1,0:T(8,128)(2,1)S(1)} %get-tuple-element.78.refs_0_, bf16[256,256]{1,0:T(8,128)(2,1)S(1)} %get-tuple-element.77.refs_1_, ...), custom_call_target="tpu_custom_call" | custom-call | flops 671088640 | bytes 655360 | tf_op jit(solution)/shard_map/attend/pallas_call | solution.py:313
  96.2 2.2 %attend.7.refs_0_ = bf16[256,512]{1,0:T(8,128)(2,1)S(1)} custom-call(s32[1]{0:T(128)} %bitcast.1.me_ref, bf16[256,512]{1,0:T(8,128)(2,1)S(1)} %get-tuple-element.79.q_ref, bf16[256,256]{1,0:T(8,128)(2,1)S(1)} %collective-permute-done.18.refs_0_, bf16[256,256]{1,0:T(8,128)(2,1)S(1)} %collective-permute-done.19.refs_1_, ...), custom_call_target="tpu_custom_call" | custom-call | flops 402653184 | bytes 393216 | tf_op jit(solution)/shard_map/attend/pallas_call | solution.py:313
  98.4 1.8 %collective-permute-done.25.refs_2_ = bf16[256,512]{1,0:T(8,128)(2,1)S(1)} collective-permute-done((bf16[256,512]{1,0:T(8,128)(2,1)S(1)}, bf16[256,512]{1,0:T(8,128)(2,1)S(1)}, u32[]{:S(2)}, u32[]{:S(2)}) %collective-permute-start.25) | collective-permute-done | bytes 262176 | tf_op jit(solution)/shard_map/ppermute | solution.py:466
  100.2 1.6 %collective-permute-done.28.refs_4_ = bf16[256,512]{1,0:T(8,128)(2,1)S(1)} collective-permute-done((bf16[256,512]{1,0:T(8,128)(2,1)S(1)}, bf16[256,512]{1,0:T(8,128)(2,1)S(1)}, u32[]{:S(2)}, u32[]{:S(2)}) %collective-permute-start.28) | collective-permute-done | bytes 262176 | tf_op jit(solution)/shard_map/ppermute | solution.py:466
  101.7 0.6 collective-permute-start.34
  102.3 0.8 collective-permute-start.26
  103.2 1.3 collective-permute-start.37
  104.5 1.5 %collective-permute-start.30 = (bf16[128,512]{1,0:T(8,128)(2,1)S(1)}, bf16[128,512]{1,0:T(8,128)(2,1)S(1)}, u32[]{:S(2)}, u32[]{:S(2)}) collective-permute-start(bf16[128,512]{1,0:T(8,128)(2,1)S(1)} %slice.35), channel_id=1, source_target_pairs={{0,2},{1,3},{2,0},{3,1},{4,6},{5,7},{6,4},{7,5},{8,10},{9,11},{10,... | collective-permute-start | bytes 393224 | tf_op jit(solution)/shard_map/ppermute | solution.py:466
  105.9 1.5 %collective-permute-done.26.refs_6_ = bf16[128,512]{1,0:T(8,128)(2,1)S(1)} collective-permute-done((bf16[128,512]{1,0:T(8,128)(2,1)S(1)}, bf16[128,512]{1,0:T(8,128)(2,1)S(1)}, u32[]{:S(2)}, u32[]{:S(2)}) %collective-permute-start.26) | collective-permute-done | bytes 131104 | tf_op jit(solution)/shard_map/ppermute | solution.py:466
  107.4 0.7 collective-permute-done.34.refs_2_
  108.1 0.6 collective-permute-start.35
  108.7 0.8 collective-permute-done.30.refs_7_
  109.5 0.7 collective-permute-done.37.refs_4_
  110.2 3.2 %collective-permute-done.35.refs_6_ = bf16[128,512]{1,0:T(8,128)(2,1)S(1)} collective-permute-done((bf16[128,512]{1,0:T(8,128)(2,1)S(1)}, bf16[128,512]{1,0:T(8,128)(2,1)S(1)}, u32[]{:S(2)}, u32[]{:S(2)}) %collective-permute-start.35) | collective-permute-done | bytes 131104 | tf_op jit(solution)/shard_map/ppermute | solution.py:466
  113.4 0.6 collective-permute-start.33
  114.0 1.4 %collective-permute-start.39 = (bf16[128,512]{1,0:T(8,128)(2,1)S(1)}, bf16[128,512]{1,0:T(8,128)(2,1)S(1)}, u32[]{:S(2)}, u32[]{:S(2)}) collective-permute-start(bf16[128,512]{1,0:T(8,128)(2,1)S(1)} %slice.37), channel_id=1, source_target_pairs={{0,2},{1,3},{2,0},{3,1},{4,6},{5,7},{6,4},{7,5},{8,10},{9,11},{10,... | collective-permute-start | bytes 393224 | tf_op jit(solution)/shard_map/ppermute | solution.py:466
  115.4 5.9 %project_out.2 = (f32[256,1024]{1,0:T(8,128)S(1)}, f32[8,256]{1,0:T(8,128)S(1)}) custom-call(f32[8]{0:T(128)S(1)} %get-tuple-element.53.sign_ref, bf16[512,1024]{1,0:T(8,128)(2,1)S(1)} %copy-done, bf16[256,512]{1,0:T(8,128)(2,1)S(1)} %attend.5.refs_0_, bf16[256,512]{1,0:T(8,128)(2,1)S(1)} %collective-permute-done.24.refs_1_, ...), custom_call_target="tpu_custom_call" | custom-call | flops 2147483648 | bytes 12058624 | tf_op jit(solution)/shard_map/project_out/pallas_call | solution.py:408
  121.4 0.5 collective-permute-start.36
  121.9 0.4 collective-permute-start.40
  122.4 1.1 collective-permute-done.41.refs_9_
  123.6 5.9 %project_out.3 = (f32[256,1024]{1,0:T(8,128)S(1)}, f32[8,256]{1,0:T(8,128)S(1)}) custom-call(f32[8]{0:T(128)S(1)} %get-tuple-element.53.sign_ref, bf16[512,1024]{1,0:T(8,128)(2,1)S(1)} %copy-done, bf16[256,512]{1,0:T(8,128)(2,1)S(1)} %attend.7.refs_0_, bf16[256,512]{1,0:T(8,128)(2,1)S(1)} %collective-permute-done.33.refs_1_, ...), custom_call_target="tpu_custom_call" | custom-call | flops 2147483648 | bytes 12058624 | tf_op jit(solution)/shard_map/project_out/pallas_call | solution.py:408
  129.7 1.0 collective-permute-done.42
  130.8 0.7 collective-permute-start.43
  131.5 3.0 %collective-permute-done.43 = f32[8,512]{1,0:T(8,128)S(1)} collective-permute-done((f32[8,512]{1,0:T(8,128)S(1)}, f32[8,512]{1,0:T(8,128)S(1)}, u32[]{:S(2)}, u32[]{:S(2)}) %collective-permute-start.43) | collective-permute-done | bytes 16416 | tf_op jit(solution)/shard_map/ppermute | solution.py:466
  134.5 0.6 collective-permute-start.44
  135.1 3.2 %collective-permute-done.44 = f32[8,512]{1,0:T(8,128)S(1)} collective-permute-done((f32[8,512]{1,0:T(8,128)S(1)}, f32[8,512]{1,0:T(8,128)S(1)}, u32[]{:S(2)}, u32[]{:S(2)}) %collective-permute-start.44) | collective-permute-done | bytes 16416 | tf_op jit(solution)/shard_map/ppermute | solution.py:466
  138.3 1.3 final.1
  (54 shorter events, 1.1 us)
Async XLA Ops:
  3.4 3.2 %collective-permute-start = (bf16[272,1024]{1,0:T(8,128)(2,1)S(1)}, bf16[272,1024]{1,0:T(8,128)(2,1)S(1)}, u32[]{:S(2)}, u32[]{:S(2)}) collective-permute-start(bf16[272,1024]{1,0:T(8,128)(2,1)S(1)} %get-tuple-element.57.refs_0_), channel_id=1, source_target_pairs={{0,1},{1,0},{2,3},{3,2},{4,5},{5,4},{6,7},{7,6},{8,9},{9,8},{10,11... | collective-permute-start | bytes 1671176 | tf_op jit(solution)/shard_map/ppermute | solution.py:466
  3.5 15.0 %collective-permute-start.1 = (bf16[272,1024]{1,0:T(8,128)(2,1)S(1)}, bf16[272,1024]{1,0:T(8,128)(2,1)S(1)}, u32[]{:S(2)}, u32[]{:S(2)}) collective-permute-start(bf16[272,1024]{1,0:T(8,128)(2,1)S(1)} %get-tuple-element.57.refs_0_), channel_id=1, source_target_pairs={{0,2},{1,3},{2,0},{3,1},{4,6},{5,7},{6,4},{7,5},{8,10},{9,11},{10,... | collective-permute-start | bytes 1671176 | tf_op jit(solution)/shard_map/ppermute | solution.py:466
  5.0 15.1 %collective-permute-start.4 = (bf16[272,1024]{1,0:T(8,128)(2,1)S(1)}, bf16[272,1024]{1,0:T(8,128)(2,1)S(1)}, u32[]{:S(2)}, u32[]{:S(2)}) collective-permute-start(bf16[272,1024]{1,0:T(8,128)(2,1)S(1)} %get-tuple-element.57.refs_0_), channel_id=1, source_target_pairs={{0,4},{1,5},{2,6},{3,7},{4,0},{5,1},{6,2},{7,3},{8,12},{9,13},{10,... | collective-permute-start | bytes 1671176 | tf_op jit(solution)/shard_map/ppermute | solution.py:466
  18.5 9.3 %collective-permute-start.2 = (bf16[128,1024]{1,0:T(8,128)(2,1)S(1)}, bf16[128,1024]{1,0:T(8,128)(2,1)S(1)}, u32[]{:S(2)}, u32[]{:S(2)}) collective-permute-start(bf16[128,1024]{1,0:T(8,128)(2,1)S(1)} %slice.24), channel_id=1, source_target_pairs={{0,4},{1,5},{2,6},{3,7},{4,0},{5,1},{6,2},{7,3},{8,12},{9,13},{10,... | collective-permute-start | bytes 786440 | tf_op jit(solution)/shard_map/ppermute | solution.py:466
  20.1 19.5 %collective-permute-start.10 = (bf16[256,1024]{1,0:T(8,128)(2,1)S(1)}, bf16[256,1024]{1,0:T(8,128)(2,1)S(1)}, u32[]{:S(2)}, u32[]{:S(2)}) collective-permute-start(bf16[256,1024]{1,0:T(8,128)(2,1)S(1)} %get-tuple-element.69.refs_0_), channel_id=1, source_target_pairs={{0,2},{1,3},{2,0},{3,1},{4,6},{5,7},{6,4},{7,5},{8,10},{9,11},{10,... | collective-permute-start | bytes 1572872 | tf_op jit(solution)/shard_map/ppermute | solution.py:466
  21.6 19.2 %collective-permute-start.13 = (bf16[256,1024]{1,0:T(8,128)(2,1)S(1)}, bf16[256,1024]{1,0:T(8,128)(2,1)S(1)}, u32[]{:S(2)}, u32[]{:S(2)}) collective-permute-start(bf16[256,1024]{1,0:T(8,128)(2,1)S(1)} %get-tuple-element.69.refs_0_), channel_id=1, source_target_pairs={{0,4},{1,5},{2,6},{3,7},{4,0},{5,1},{6,2},{7,3},{8,12},{9,13},{10,... | collective-permute-start | bytes 1572872 | tf_op jit(solution)/shard_map/ppermute | solution.py:466
  22.2 17.5 %collective-permute-start.6 = (bf16[144,1024]{1,0:T(8,128)(2,1)S(1)}, bf16[144,1024]{1,0:T(8,128)(2,1)S(1)}, u32[]{:S(2)}, u32[]{:S(2)}) collective-permute-start(bf16[144,1024]{1,0:T(8,128)(2,1)S(1)} %slice.25), channel_id=1, source_target_pairs={{0,2},{1,3},{2,0},{3,1},{4,6},{5,7},{6,4},{7,5},{8,10},{9,11},{10,... | collective-permute-start | bytes 884744 | tf_op jit(solution)/shard_map/ppermute | solution.py:466
  27.8 22.2 %collective-permute-start.5 = (bf16[272,1024]{1,0:T(8,128)(2,1)S(1)}, bf16[272,1024]{1,0:T(8,128)(2,1)S(1)}, u32[]{:S(2)}, u32[]{:S(2)}) collective-permute-start(bf16[272,1024]{1,0:T(8,128)(2,1)S(1)} %collective-permute-done.4.refs_4_), channel_id=1, source_target_pairs={{0,1},{1,0},{2,3},{3,2},{4,5},{5,4},{6,7},{7,6},{8,9},{9,8},{10,11... | collective-permute-start | bytes 1671176 | tf_op jit(solution)/shard_map/ppermute | solution.py:466
  27.8 22.2 %collective-permute-start.3 = (bf16[272,1024]{1,0:T(8,128)(2,1)S(1)}, bf16[272,1024]{1,0:T(8,128)(2,1)S(1)}, u32[]{:S(2)}, u32[]{:S(2)}) collective-permute-start(bf16[272,1024]{1,0:T(8,128)(2,1)S(1)} %collective-permute-done.1.refs_2_), channel_id=1, source_target_pairs={{0,1},{1,0},{2,3},{3,2},{4,5},{5,4},{6,7},{7,6},{8,9},{9,8},{10,11... | collective-permute-start | bytes 1671176 | tf_op jit(solution)/shard_map/ppermute | solution.py:466
  39.7 10.3 %collective-permute-start.8 = (bf16[144,1024]{1,0:T(8,128)(2,1)S(1)}, bf16[144,1024]{1,0:T(8,128)(2,1)S(1)}, u32[]{:S(2)}, u32[]{:S(2)}) collective-permute-start(bf16[144,1024]{1,0:T(8,128)(2,1)S(1)} %collective-permute-done.6.refs_7_), channel_id=1, source_target_pairs={{0,1},{1,0},{2,3},{3,2},{4,5},{5,4},{6,7},{7,6},{8,9},{9,8},{10,11... | collective-permute-start | bytes 884744 | tf_op jit(solution)/shard_map/ppermute | solution.py:466
  39.7 8.8 %collective-permute-start.11 = (bf16[128,1024]{1,0:T(8,128)(2,1)S(1)}, bf16[128,1024]{1,0:T(8,128)(2,1)S(1)}, u32[]{:S(2)}, u32[]{:S(2)}) collective-permute-start(bf16[128,1024]{1,0:T(8,128)(2,1)S(1)} %slice.32), channel_id=1, source_target_pairs={{0,4},{1,5},{2,6},{3,7},{4,0},{5,1},{6,2},{7,3},{8,12},{9,13},{10,... | collective-permute-start | bytes 786440 | tf_op jit(solution)/shard_map/ppermute | solution.py:466
  40.8 7.6 %collective-permute-start.7 = (bf16[128,1024]{1,0:T(8,128)(2,1)S(1)}, bf16[128,1024]{1,0:T(8,128)(2,1)S(1)}, u32[]{:S(2)}, u32[]{:S(2)}) collective-permute-start(bf16[128,1024]{1,0:T(8,128)(2,1)S(1)} %collective-permute-done.2.refs_6_), channel_id=1, source_target_pairs={{0,1},{1,0},{2,3},{3,2},{4,5},{5,4},{6,7},{7,6},{8,9},{9,8},{10,11... | collective-permute-start | bytes 786440 | tf_op jit(solution)/shard_map/ppermute | solution.py:466
  48.5 9.2 %collective-permute-start.9 = (bf16[256,1024]{1,0:T(8,128)(2,1)S(1)}, bf16[256,1024]{1,0:T(8,128)(2,1)S(1)}, u32[]{:S(2)}, u32[]{:S(2)}) collective-permute-start(bf16[256,1024]{1,0:T(8,128)(2,1)S(1)} %get-tuple-element.69.refs_0_), channel_id=1, source_target_pairs={{0,1},{1,0},{2,3},{3,2},{4,5},{5,4},{6,7},{7,6},{8,9},{9,8},{10,11... | collective-permute-start | bytes 1572872 | tf_op jit(solution)/shard_map/ppermute | solution.py:466
  48.5 8.7 %collective-permute-start.15 = (bf16[128,1024]{1,0:T(8,128)(2,1)S(1)}, bf16[128,1024]{1,0:T(8,128)(2,1)S(1)}, u32[]{:S(2)}, u32[]{:S(2)}) collective-permute-start(bf16[128,1024]{1,0:T(8,128)(2,1)S(1)} %slice.33), channel_id=1, source_target_pairs={{0,2},{1,3},{2,0},{3,1},{4,6},{5,7},{6,4},{7,5},{8,10},{9,11},{10,... | collective-permute-start | bytes 786440 | tf_op jit(solution)/shard_map/ppermute | solution.py:466
  54.0 5.1 %collective-permute-start.14 = (bf16[256,1024]{1,0:T(8,128)(2,1)S(1)}, bf16[256,1024]{1,0:T(8,128)(2,1)S(1)}, u32[]{:S(2)}, u32[]{:S(2)}) collective-permute-start(bf16[256,1024]{1,0:T(8,128)(2,1)S(1)} %collective-permute-done.13.refs_4_), channel_id=1, source_target_pairs={{0,1},{1,0},{2,3},{3,2},{4,5},{5,4},{6,7},{7,6},{8,9},{9,8},{10,11... | collective-permute-start | bytes 1572872 | tf_op jit(solution)/shard_map/ppermute | solution.py:466
  54.3 4.8 %collective-permute-start.12 = (bf16[256,1024]{1,0:T(8,128)(2,1)S(1)}, bf16[256,1024]{1,0:T(8,128)(2,1)S(1)}, u32[]{:S(2)}, u32[]{:S(2)}) collective-permute-start(bf16[256,1024]{1,0:T(8,128)(2,1)S(1)} %collective-permute-done.10.refs_2_), channel_id=1, source_target_pairs={{0,1},{1,0},{2,3},{3,2},{4,5},{5,4},{6,7},{7,6},{8,9},{9,8},{10,11... | collective-permute-start | bytes 1572872 | tf_op jit(solution)/shard_map/ppermute | solution.py:466
  57.2 1.8 %collective-permute-start.17 = (bf16[128,1024]{1,0:T(8,128)(2,1)S(1)}, bf16[128,1024]{1,0:T(8,128)(2,1)S(1)}, u32[]{:S(2)}, u32[]{:S(2)}) collective-permute-start(bf16[128,1024]{1,0:T(8,128)(2,1)S(1)} %collective-permute-done.15.refs_7_), channel_id=1, source_target_pairs={{0,1},{1,0},{2,3},{3,2},{4,5},{5,4},{6,7},{7,6},{8,9},{9,8},{10,11... | collective-permute-start | bytes 786440 | tf_op jit(solution)/shard_map/ppermute | solution.py:466
  57.2 1.9 %collective-permute-start.16 = (bf16[128,1024]{1,0:T(8,128)(2,1)S(1)}, bf16[128,1024]{1,0:T(8,128)(2,1)S(1)}, u32[]{:S(2)}, u32[]{:S(2)}) collective-permute-start(bf16[128,1024]{1,0:T(8,128)(2,1)S(1)} %collective-permute-done.11.refs_6_), channel_id=1, source_target_pairs={{0,1},{1,0},{2,3},{3,2},{4,5},{5,4},{6,7},{7,6},{8,9},{9,8},{10,11... | collective-permute-start | bytes 786440 | tf_op jit(solution)/shard_map/ppermute | solution.py:466
  57.7 7.3 %collective-permute-start.21 = (bf16[256,256]{1,0:T(8,128)(2,1)S(1)}, bf16[256,256]{1,0:T(8,128)(2,1)S(1)}, u32[]{:S(2)}, u32[]{:S(2)}) collective-permute-start(bf16[256,256]{1,0:T(8,128)(2,1)S(1)} %get-tuple-element.78.refs_0_), channel_id=1, source_target_pairs={{0,8},{8,16},{16,24},{1,9},{9,17},{17,25},{2,10},{10,18},{18,26},{... | collective-permute-start | bytes 393224 | tf_op jit(solution)/shard_map/ppermute | solution.py:471
  63.2 52.2 %copy-start = (bf16[512,1024]{1,0:T(8,128)(2,1)S(1)}, bf16[512,1024]{1,0:T(8,128)(2,1)}, u32[]{:S(2)}) copy-start(bf16[512,1024]{1,0:T(8,128)(2,1)} %t_ref.3) | copy-start | bytes 3145732
  65.0 6.8 %collective-permute-start.22 = (bf16[256,256]{1,0:T(8,128)(2,1)S(1)}, bf16[256,256]{1,0:T(8,128)(2,1)S(1)}, u32[]{:S(2)}, u32[]{:S(2)}) collective-permute-start(bf16[256,256]{1,0:T(8,128)(2,1)S(1)} %collective-permute-done.21.refs_1_.refs_2_), channel_id=1, source_target_pairs={{8,16},{16,24},{9,17},{17,25},{10,18},{18,26},{11,19},{19,27},{12,... | collective-permute-start | bytes 393224 | tf_op jit(solution)/shard_map/ppermute | solution.py:471
  71.9 8.6 %collective-permute-start.23 = (bf16[256,256]{1,0:T(8,128)(2,1)S(1)}, bf16[256,256]{1,0:T(8,128)(2,1)S(1)}, u32[]{:S(2)}, u32[]{:S(2)}) collective-permute-start(bf16[256,256]{1,0:T(8,128)(2,1)S(1)} %collective-permute-done.22.refs_2_.refs_3_), channel_id=1, source_target_pairs={{16,24},{17,25},{18,26},{19,27},{20,28},{21,29},{22,30},{23,31}} | collective-permute-start | bytes 393224 | tf_op jit(solution)/shard_map/ppermute | solution.py:471
  73.1 10.1 %collective-permute-start.18 = (bf16[256,256]{1,0:T(8,128)(2,1)S(1)}, bf16[256,256]{1,0:T(8,128)(2,1)S(1)}, u32[]{:S(2)}, u32[]{:S(2)}) collective-permute-start(bf16[256,256]{1,0:T(8,128)(2,1)S(1)} %get-tuple-element.77.refs_1_), channel_id=1, source_target_pairs={{0,8},{8,16},{16,24},{1,9},{9,17},{17,25},{2,10},{10,18},{18,26},{... | collective-permute-start | bytes 393224 | tf_op jit(solution)/shard_map/ppermute | solution.py:471
  74.4 14.3 %collective-permute-start.19 = (bf16[256,256]{1,0:T(8,128)(2,1)S(1)}, bf16[256,256]{1,0:T(8,128)(2,1)S(1)}, u32[]{:S(2)}, u32[]{:S(2)}) collective-permute-start(bf16[256,256]{1,0:T(8,128)(2,1)S(1)} %get-tuple-element.77.refs_1_), channel_id=1, source_target_pairs={{0,16},{8,24},{1,17},{9,25},{2,18},{10,26},{3,19},{11,27},{4,20},{... | collective-permute-start | bytes 393224 | tf_op jit(solution)/shard_map/ppermute | solution.py:471
  75.7 13.0 %collective-permute-start.20 = (bf16[256,256]{1,0:T(8,128)(2,1)S(1)}, bf16[256,256]{1,0:T(8,128)(2,1)S(1)}, u32[]{:S(2)}, u32[]{:S(2)}) collective-permute-start(bf16[256,256]{1,0:T(8,128)(2,1)S(1)} %get-tuple-element.77.refs_1_), channel_id=1, source_target_pairs={{0,24},{1,25},{2,26},{3,27},{4,28},{5,29},{6,30},{7,31}} | collective-permute-start | bytes 393224 | tf_op jit(solution)/shard_map/ppermute | solution.py:471
  91.1 9.1 %collective-permute-start.25 = (bf16[256,512]{1,0:T(8,128)(2,1)S(1)}, bf16[256,512]{1,0:T(8,128)(2,1)S(1)}, u32[]{:S(2)}, u32[]{:S(2)}) collective-permute-start(bf16[256,512]{1,0:T(8,128)(2,1)S(1)} %attend.5.refs_0_), channel_id=1, source_target_pairs={{0,2},{1,3},{2,0},{3,1},{4,6},{5,7},{6,4},{7,5},{8,10},{9,11},{10,... | collective-permute-start | bytes 786440 | tf_op jit(solution)/shard_map/ppermute | solution.py:466
  92.6 9.1 %collective-permute-start.28 = (bf16[256,512]{1,0:T(8,128)(2,1)S(1)}, bf16[256,512]{1,0:T(8,128)(2,1)S(1)}, u32[]{:S(2)}, u32[]{:S(2)}) collective-permute-start(bf16[256,512]{1,0:T(8,128)(2,1)S(1)} %attend.5.refs_0_), channel_id=1, source_target_pairs={{0,4},{1,5},{2,6},{3,7},{4,0},{5,1},{6,2},{7,3},{8,12},{9,13},{10,... | collective-permute-start | bytes 786440 | tf_op jit(solution)/shard_map/ppermute | solution.py:466
  101.7 6.4 %collective-permute-start.34 = (bf16[256,512]{1,0:T(8,128)(2,1)S(1)}, bf16[256,512]{1,0:T(8,128)(2,1)S(1)}, u32[]{:S(2)}, u32[]{:S(2)}) collective-permute-start(bf16[256,512]{1,0:T(8,128)(2,1)S(1)} %attend.7.refs_0_), channel_id=1, source_target_pairs={{0,2},{1,3},{2,0},{3,1},{4,6},{5,7},{6,4},{7,5},{8,10},{9,11},{10,... | collective-permute-start | bytes 786440 | tf_op jit(solution)/shard_map/ppermute | solution.py:466
  102.3 5.0 %collective-permute-start.26 = (bf16[128,512]{1,0:T(8,128)(2,1)S(1)}, bf16[128,512]{1,0:T(8,128)(2,1)S(1)}, u32[]{:S(2)}, u32[]{:S(2)}) collective-permute-start(bf16[128,512]{1,0:T(8,128)(2,1)S(1)} %slice.34), channel_id=1, source_target_pairs={{0,4},{1,5},{2,6},{3,7},{4,0},{5,1},{6,2},{7,3},{8,12},{9,13},{10,... | collective-permute-start | bytes 393224 | tf_op jit(solution)/shard_map/ppermute | solution.py:466
  103.2 7.0 %collective-permute-start.37 = (bf16[256,512]{1,0:T(8,128)(2,1)S(1)}, bf16[256,512]{1,0:T(8,128)(2,1)S(1)}, u32[]{:S(2)}, u32[]{:S(2)}) collective-permute-start(bf16[256,512]{1,0:T(8,128)(2,1)S(1)} %attend.7.refs_0_), channel_id=1, source_target_pairs={{0,4},{1,5},{2,6},{3,7},{4,0},{5,1},{6,2},{7,3},{8,12},{9,13},{10,... | collective-permute-start | bytes 786440 | tf_op jit(solution)/shard_map/ppermute | solution.py:466
  104.5 5.0 %collective-permute-start.30 = (bf16[128,512]{1,0:T(8,128)(2,1)S(1)}, bf16[128,512]{1,0:T(8,128)(2,1)S(1)}, u32[]{:S(2)}, u32[]{:S(2)}) collective-permute-start(bf16[128,512]{1,0:T(8,128)(2,1)S(1)} %slice.35), channel_id=1, source_target_pairs={{0,2},{1,3},{2,0},{3,1},{4,6},{5,7},{6,4},{7,5},{8,10},{9,11},{10,... | collective-permute-start | bytes 393224 | tf_op jit(solution)/shard_map/ppermute | solution.py:466
  105.9 7.5 %collective-permute-start.24 = (bf16[256,512]{1,0:T(8,128)(2,1)S(1)}, bf16[256,512]{1,0:T(8,128)(2,1)S(1)}, u32[]{:S(2)}, u32[]{:S(2)}) collective-permute-start(bf16[256,512]{1,0:T(8,128)(2,1)S(1)} %attend.5.refs_0_), channel_id=1, source_target_pairs={{0,1},{1,0},{2,3},{3,2},{4,5},{5,4},{6,7},{7,6},{8,9},{9,8},{10,11... | collective-permute-start | bytes 786440 | tf_op jit(solution)/shard_map/ppermute | solution.py:466
  107.4 8.0 %collective-permute-start.29 = (bf16[256,512]{1,0:T(8,128)(2,1)S(1)}, bf16[256,512]{1,0:T(8,128)(2,1)S(1)}, u32[]{:S(2)}, u32[]{:S(2)}) collective-permute-start(bf16[256,512]{1,0:T(8,128)(2,1)S(1)} %collective-permute-done.28.refs_4_), channel_id=1, source_target_pairs={{0,1},{1,0},{2,3},{3,2},{4,5},{5,4},{6,7},{7,6},{8,9},{9,8},{10,11... | collective-permute-start | bytes 786440 | tf_op jit(solution)/shard_map/ppermute | solution.py:466
  108.1 5.3 %collective-permute-start.35 = (bf16[128,512]{1,0:T(8,128)(2,1)S(1)}, bf16[128,512]{1,0:T(8,128)(2,1)S(1)}, u32[]{:S(2)}, u32[]{:S(2)}) collective-permute-start(bf16[128,512]{1,0:T(8,128)(2,1)S(1)} %slice.36), channel_id=1, source_target_pairs={{0,4},{1,5},{2,6},{3,7},{4,0},{5,1},{6,2},{7,3},{8,12},{9,13},{10,... | collective-permute-start | bytes 393224 | tf_op jit(solution)/shard_map/ppermute | solution.py:466
  109.5 5.9 %collective-permute-start.27 = (bf16[256,512]{1,0:T(8,128)(2,1)S(1)}, bf16[256,512]{1,0:T(8,128)(2,1)S(1)}, u32[]{:S(2)}, u32[]{:S(2)}) collective-permute-start(bf16[256,512]{1,0:T(8,128)(2,1)S(1)} %collective-permute-done.25.refs_2_), channel_id=1, source_target_pairs={{0,1},{1,0},{2,3},{3,2},{4,5},{5,4},{6,7},{7,6},{8,9},{9,8},{10,11... | collective-permute-start | bytes 786440 | tf_op jit(solution)/shard_map/ppermute | solution.py:466
  110.2 3.8 %collective-permute-start.31 = (bf16[128,512]{1,0:T(8,128)(2,1)S(1)}, bf16[128,512]{1,0:T(8,128)(2,1)S(1)}, u32[]{:S(2)}, u32[]{:S(2)}) collective-permute-start(bf16[128,512]{1,0:T(8,128)(2,1)S(1)} %collective-permute-done.26.refs_6_), channel_id=1, source_target_pairs={{0,1},{1,0},{2,3},{3,2},{4,5},{5,4},{6,7},{7,6},{8,9},{9,8},{10,11... | collective-permute-start | bytes 393224 | tf_op jit(solution)/shard_map/ppermute | solution.py:466
  113.4 2.0 %collective-permute-start.32 = (bf16[128,512]{1,0:T(8,128)(2,1)S(1)}, bf16[128,512]{1,0:T(8,128)(2,1)S(1)}, u32[]{:S(2)}, u32[]{:S(2)}) collective-permute-start(bf16[128,512]{1,0:T(8,128)(2,1)S(1)} %collective-permute-done.30.refs_7_), channel_id=1, source_target_pairs={{0,1},{1,0},{2,3},{3,2},{4,5},{5,4},{6,7},{7,6},{8,9},{9,8},{10,11... | collective-permute-start | bytes 393224 | tf_op jit(solution)/shard_map/ppermute | solution.py:466
  113.4 9.0 %collective-permute-start.33 = (bf16[256,512]{1,0:T(8,128)(2,1)S(1)}, bf16[256,512]{1,0:T(8,128)(2,1)S(1)}, u32[]{:S(2)}, u32[]{:S(2)}) collective-permute-start(bf16[256,512]{1,0:T(8,128)(2,1)S(1)} %attend.7.refs_0_), channel_id=1, source_target_pairs={{0,1},{1,0},{2,3},{3,2},{4,5},{5,4},{6,7},{7,6},{8,9},{9,8},{10,11... | collective-permute-start | bytes 786440 | tf_op jit(solution)/shard_map/ppermute | solution.py:466
  114.0 7.9 %collective-permute-start.39 = (bf16[128,512]{1,0:T(8,128)(2,1)S(1)}, bf16[128,512]{1,0:T(8,128)(2,1)S(1)}, u32[]{:S(2)}, u32[]{:S(2)}) collective-permute-start(bf16[128,512]{1,0:T(8,128)(2,1)S(1)} %slice.37), channel_id=1, source_target_pairs={{0,2},{1,3},{2,0},{3,1},{4,6},{5,7},{6,4},{7,5},{8,10},{9,11},{10,... | collective-permute-start | bytes 393224 | tf_op jit(solution)/shard_map/ppermute | solution.py:466
  121.3 2.3 %collective-permute-start.38 = (bf16[256,512]{1,0:T(8,128)(2,1)S(1)}, bf16[256,512]{1,0:T(8,128)(2,1)S(1)}, u32[]{:S(2)}, u32[]{:S(2)}) collective-permute-start(bf16[256,512]{1,0:T(8,128)(2,1)S(1)} %collective-permute-done.37.refs_4_), channel_id=1, source_target_pairs={{0,1},{1,0},{2,3},{3,2},{4,5},{5,4},{6,7},{7,6},{8,9},{9,8},{10,11... | collective-permute-start | bytes 786440 | tf_op jit(solution)/shard_map/ppermute | solution.py:466
  121.4 2.3 %collective-permute-start.36 = (bf16[256,512]{1,0:T(8,128)(2,1)S(1)}, bf16[256,512]{1,0:T(8,128)(2,1)S(1)}, u32[]{:S(2)}, u32[]{:S(2)}) collective-permute-start(bf16[256,512]{1,0:T(8,128)(2,1)S(1)} %collective-permute-done.34.refs_2_), channel_id=1, source_target_pairs={{0,1},{1,0},{2,3},{3,2},{4,5},{5,4},{6,7},{7,6},{8,9},{9,8},{10,11... | collective-permute-start | bytes 786440 | tf_op jit(solution)/shard_map/ppermute | solution.py:466
  121.9 1.6 %collective-permute-start.41 = (bf16[128,512]{1,0:T(8,128)(2,1)S(1)}, bf16[128,512]{1,0:T(8,128)(2,1)S(1)}, u32[]{:S(2)}, u32[]{:S(2)}) collective-permute-start(bf16[128,512]{1,0:T(8,128)(2,1)S(1)} %collective-permute-done.39.refs_7_), channel_id=1, source_target_pairs={{0,1},{1,0},{2,3},{3,2},{4,5},{5,4},{6,7},{7,6},{8,9},{9,8},{10,11... | collective-permute-start | bytes 393224 | tf_op jit(solution)/shard_map/ppermute | solution.py:466
  121.9 1.7 %collective-permute-start.40 = (bf16[128,512]{1,0:T(8,128)(2,1)S(1)}, bf16[128,512]{1,0:T(8,128)(2,1)S(1)}, u32[]{:S(2)}, u32[]{:S(2)}) collective-permute-start(bf16[128,512]{1,0:T(8,128)(2,1)S(1)} %collective-permute-done.35.refs_6_), channel_id=1, source_target_pairs={{0,1},{1,0},{2,3},{3,2},{4,5},{5,4},{6,7},{7,6},{8,9},{9,8},{10,11... | collective-permute-start | bytes 393224 | tf_op jit(solution)/shard_map/ppermute | solution.py:466
  129.6 1.2 collective-permute-start.42
  130.8 3.7 %collective-permute-start.43 = (f32[8,512]{1,0:T(8,128)S(1)}, f32[8,512]{1,0:T(8,128)S(1)}, u32[]{:S(2)}, u32[]{:S(2)}) collective-permute-start(f32[8,512]{1,0:T(8,128)S(1)} %add.10), channel_id=1, source_target_pairs={{0,2},{1,3},{2,0},{3,1},{4,6},{5,7},{6,4},{7,5},{8,10},{9,11},{10,... | collective-permute-start | bytes 49160 | tf_op jit(solution)/shard_map/ppermute | solution.py:466
  134.5 3.7 %collective-permute-start.44 = (f32[8,512]{1,0:T(8,128)S(1)}, f32[8,512]{1,0:T(8,128)S(1)}, u32[]{:S(2)}, u32[]{:S(2)}) collective-permute-start(f32[8,512]{1,0:T(8,128)S(1)} %add.11), channel_id=1, source_target_pairs={{0,4},{1,5},{2,6},{3,7},{4,0},{5,1},{6,2},{7,3},{8,12},{9,13},{10,... | collective-permute-start | bytes 49160 | tf_op jit(solution)/shard_map/ppermute | solution.py:466

commit v5 on v3

--- a/solution.py
+++ b/solution.py
@@ -19,7 +19,7 @@
 EXTRA = 16
 LOAD_PARTS = 4
 LOAD_MIB = 38
-PROJ_MIB = 12
+PROJ_MIB = 14
 ATT_MIB = 12
 OUT_MIB = 12
 MIB = 1024 * 1024
@@ -50,7 +50,7 @@
 
 
 def pre_kernel(h_hbm, g_hbm, *refs):
-    outs, (h_all, g_ref, sem) = refs[:HALVES], refs[HALVES:]
+    c_ref, h_all, g_ref, sem = refs
     rows, width = h_all.shape
     steps = sem.shape[0] - 1
     part = rows // steps
@@ -64,8 +64,7 @@
     for i in range(steps):
         copies[i + 1].wait()
         total = jnp.zeros((part, GROUP), jnp.float32)
-        row = i * part % (rows // HALVES)
-        c_ref = outs[i * part // (rows // HALVES)]
+        row = i * part
         for at in range(0, width, GROUP):
             h = h_all[i * part : (i + 1) * part, at : at + GROUP].astype(jnp.float32)
             total = total + h * h
@@ -79,20 +78,17 @@
             piece = left.astype(jnp.bfloat16).astype(jnp.float32)
             left = left - piece
             sums = jnp.where(row == place, piece, sums)
-        outs[0][rows // HALVES :, i * part : (i + 1) * part] = sums.astype(jnp.bfloat16)
+        c_ref[rows:, i * part : (i + 1) * part] = sums.astype(jnp.bfloat16)
 
 
 def pre(hidden, gain):
     rows, width = hidden.shape
-    steps = HALVES * 2
+    steps = 4
     return pl.pallas_call(
         pre_kernel,
         in_specs=[IN_HBM] * 2,
-        out_specs=[IN_VMEM] * HALVES,
-        out_shape=[
-            pltpu.VMEM((rows // HALVES + (0 if i else EXTRA), width), jnp.bfloat16)
-            for i in range(HALVES)
-        ],
+        out_specs=IN_VMEM,
+        out_shape=pltpu.VMEM((rows + EXTRA, width), jnp.bfloat16),
         scratch_shapes=[
             pltpu.VMEM((rows, width), jnp.bfloat16),
             pltpu.VMEM(gain.shape, jnp.bfloat16),
@@ -134,29 +130,32 @@
     )(*weights)
 
 
-def proj_kernel(counts, chunk, order_ref, *refs):
+def proj_kernel(counts, masks, begins, ends, order_ref, *refs):
     depth = len(counts)
-    blocks = refs[: sum(counts)]
-    refs = refs[sum(counts) :]
-    if chunk:
-        wq_ref, wk_ref, wv_ref, ss_ref, q_ref, kv_ref, accq, acck, accv = refs
-        squares = ss_ref[...]
+    blocks, refs = refs[: sum(counts)], refs[sum(counts) :]
+    wq_ref, wk_ref, wv_ref, *refs = refs
+    if not begins:
+        *before, ss_in = refs[:4]
+        refs = refs[4:]
+        squares = ss_in[0:1, :]
     else:
-        wq_ref, wk_ref, wv_ref, q_ref, kv_ref, ss_ref, accq, acck, accv = refs
-        squares = jnp.zeros((1, ss_ref.shape[1]), jnp.float32)
-    rows = q_ref.shape[0]
+        before = [None] * 3
+        squares = jnp.zeros((1, ss_rows(blocks)), jnp.float32)
+    if ends:
+        q_ref, kv_ref, *accs = refs
+    else:
+        *accs, ss_ref = refs
     nk = wk_ref.shape[1]
     k_rows = blocks[0].shape[1]
     at_block = 0
     for k in range(depth):
-        at = pl.ds(pl.multiple_of(order_ref[k] * k_rows, k_rows), k_rows)
+        at = pl.ds(pl.multiple_of(order_ref[masks[k]] * k_rows, k_rows), k_rows)
         mine = [b[...] for b in blocks[at_block : at_block + counts[k]]]
         at_block += counts[k]
-        if not chunk:
-            body_rows = mine[-1].shape[0] - EXTRA
-            tail = mine[-1][body_rows:, : ss_ref.shape[1]].astype(jnp.float32)
-            squares = squares + (tail[0:1] + tail[1:2] + tail[2:3])
-            mine[-1] = mine[-1][:body_rows]
+        body_rows = mine[-1].shape[0] - EXTRA
+        tail = mine[-1][body_rows:, : squares.shape[1]].astype(jnp.float32)
+        squares = squares + (tail[0:1] + tail[1:2] + tail[2:3])
+        mine[-1] = mine[-1][:body_rows]
         left = mine[0] if len(mine) == 1 else jnp.concatenate(mine, axis=0)
         wq, wk, wv = wq_ref[at, :], wk_ref[at, :], wv_ref[at, :]
         if nk % 128 == 0:
@@ -167,46 +166,57 @@
         else:
             parts = [jnp.dot(left, w, preferred_element_type=jnp.float32) for w in (wk, wv)]
         first = jnp.dot(left, wq, preferred_element_type=jnp.float32)
-        for part, acc in zip((first, *parts), (accq, acck, accv)):
-            if k == 0:
+        for part, acc, old in zip((first, *parts), accs, before):
+            if k:
+                acc[...] += part
+            elif not begins:
+                acc[...] = old[...] + part
+            else:
                 acc[...] = part
-            else:
-                acc[...] += part
-
-    features = k_rows * depth
-    if not chunk:
-        squares = jnp.broadcast_to(squares, ss_ref.shape)
-        ss_ref[...] = squares
-    squares = squares[:, chunk * rows : (chunk + 1) * rows]
-    inverse = lax.rsqrt(squares * (1.0 / features) + EPS_IN)
-    scale = jnp.transpose(inverse)[:, :1]
-    q_ref[...] = (accq[...] * scale).astype(jnp.bfloat16)
-    kv_ref[:, :nk] = (acck[...] * scale).astype(jnp.bfloat16)
-    kv_ref[:, nk:] = (accv[...] * scale).astype(jnp.bfloat16)
-
-
-def proj(order, blocks, chunk, rows, squares, wq, wk, wv):
+
+    if not ends:
+        ss_ref[...] = jnp.broadcast_to(squares, ss_ref.shape)
+    else:
+        accq, acck, accv = accs
+        features = wq_ref.shape[0]
+        squares = jnp.broadcast_to(squares, (8, squares.shape[1]))
+        inverse = lax.rsqrt(squares * (1.0 / features) + EPS_IN)
+        scale = jnp.transpose(inverse)[:, :1]
+        q_ref[...] = (accq[...] * scale).astype(jnp.bfloat16)
+        kv_ref[:, :nk] = (acck[...] * scale).astype(jnp.bfloat16)
+        kv_ref[:, nk:] = (accv[...] * scale).astype(jnp.bfloat16)
+
+
+def ss_rows(blocks):
+    return blocks[0].shape[0] - EXTRA
+
+
+def proj(order, blocks, rows, state, ends, wq, wk, wv):
+    masks = sorted(blocks)
+    blocks = [blocks[m] for m in masks]
     depth = len(blocks)
     counts = [len(b) for b in blocks]
     part_cols = blocks[0][0].shape[1]
-    nq, nk, nv = wq.shape[1], wk.shape[1], wv.shape[1]
-    n = nq + nk + nv
+    sizes = wq.shape[1], wk.shape[1], wv.shape[1]
+    n = sum(sizes)
     flat = [p for b in blocks for p in b]
-    args = [order, *flat, wq, wk, wv]
-    out_shape = [
-        jax.ShapeDtypeStruct((rows, nq), jnp.bfloat16),
-        jax.ShapeDtypeStruct((rows, nk + nv), jnp.bfloat16),
-    ]
-    if chunk:
-        args.append(squares)
+    args = [order, *flat, wq, wk, wv, *state]
+    if ends:
+        out_shape = [
+            jax.ShapeDtypeStruct((rows, sizes[0]), jnp.bfloat16),
+            jax.ShapeDtypeStruct((rows, sizes[1] + sizes[2]), jnp.bfloat16),
+        ]
+        scratch = [pltpu.VMEM((rows, m), jnp.float32) for m in sizes]
     else:
-        out_shape.append(jax.ShapeDtypeStruct((8, rows * HALVES), jnp.float32))
+        out_shape = [pltpu.VMEM((rows, m), jnp.float32) for m in sizes]
+        out_shape.append(jax.ShapeDtypeStruct((8, rows), jnp.float32))
+        scratch = []
     return pl.pallas_call(
-        functools.partial(proj_kernel, counts, chunk),
+        functools.partial(proj_kernel, counts, masks, not state, ends),
         in_specs=[IN_SMEM] + [IN_VMEM] * (len(args) - 1),
         out_specs=[IN_VMEM] * len(out_shape),
         out_shape=out_shape,
-        scratch_shapes=[pltpu.VMEM((rows, m), jnp.float32) for m in (nq, nk, nv)],
+        scratch_shapes=scratch,
         compiler_params=params(PROJ_MIB),
         cost_estimate=cost(
             2 * rows * part_cols * depth * n, 2 * part_cols * depth * (rows + n)
@@ -216,7 +226,7 @@
 
 
 def att_kernel(first, kv_heads, near, far, begins, ends, me_ref, q_ref, *refs):
-    count = len(near) + len(far)
+    count = near + len(far)
     kvs, refs = refs[:count], refs[count:]
     if not begins:
         high_in, total_in, accum_in, *refs = refs
@@ -224,9 +234,9 @@
         sign_ref, o_ref, high, total, accum = refs
     else:
         high, total, accum = refs
-    rows = q_ref.shape[0]
+    rows = accum.shape[2]
     heads = q_ref.shape[1] // HD
-    part = kvs[0].shape[0]
+    part = rows
     group = heads // kv_heads
     scale = HD ** (-0.5) * LOG2E
 
@@ -235,16 +245,17 @@
         total[...] = total_in[...]
         accum[...] = accum_in[...]
 
-    def visit(kv_ref, start, fresh):
+    def visit(kv_ref, sub, start, fresh):
+        keys = slice(sub * part, (sub + 1) * part)
         masked = start is not None and start + part > first
         scores, turned = [], []
         for kv in range(kv_heads):
             at = (kv_heads + kv) * HD
-            turned.append(jnp.transpose(kv_ref[:, at : at + HD]))
+            turned.append(jnp.transpose(kv_ref[keys, at : at + HD]))
         for head in range(heads):
             kv = head // group
-            q = q_ref[:, head * HD : (head + 1) * HD]
-            k = kv_ref[:, kv * HD : (kv + 1) * HD]
+            q = q_ref[first : first + rows, head * HD : (head + 1) * HD]
+            k = kv_ref[keys, kv * HD : (kv + 1) * HD]
             s = lax.dot_general(
                 k, q, (((1,), (1,)), ((), ())), preferred_element_type=jnp.float32
             )
@@ -273,13 +284,15 @@
                 accum[head] = accum[head] * decay + mixed
             high[head : head + 1] = best
 
-    for at, start in enumerate(near):
-        visit(kvs[at], start, begins and at == 0)
+    for at in range(near):
+        for sub in range((first + rows) // part):
+            visit(kvs[at], sub, sub * part, begins and at == 0 and sub == 0)
     for at, hop in enumerate(far):
 
         @pl.when(me_ref[0] >= hop)
         def _():
-            visit(kvs[len(near) + at], None, False)
+            for sub in range(kvs[near + at].shape[0] // part):
+                visit(kvs[near + at], sub, None, False)
 
     if ends:
         for head in range(heads):
@@ -290,10 +303,9 @@
             )
 
 
-def attend(me, q, first, kv_heads, near, far, state, signs):
-    rows = q.shape[0]
+def attend(me, q, first, rows, kv_heads, near, far, state, signs):
     heads = q.shape[1] // HD
-    kvs = [kv for _, kv in near + far]
+    kvs = near + [kv for _, kv in far]
     keys = sum(kv.shape[0] for kv in kvs)
     shapes = [(max(heads, 8), rows), (max(heads, 8), rows), (heads, HD, rows)]
     args = [me, q, *kvs]
@@ -306,9 +318,9 @@
         args.append(signs)
         out_shape = jax.ShapeDtypeStruct((rows, heads * HD), jnp.bfloat16)
         scratch = [pltpu.VMEM(shape, jnp.float32) for shape in shapes]
-    near_at, far_at = [n for n, _ in near], [n for n, _ in far]
+    far_at = [n for n, _ in far]
     kernel = functools.partial(
-        att_kernel, first, kv_heads, near_at, far_at, state is None, signs is not None
+        att_kernel, first, kv_heads, len(near), far_at, state is None, signs is not None
     )
     return pl.pallas_call(
         kernel,
@@ -466,39 +478,41 @@
     return lax.ppermute(x, "tp", [(i, i ^ mask) for i in range(count)])
 
 
-def send_up(x, distance):
+def send_up(x, first):
     count = lax.axis_size("ctx")
-    return lax.ppermute(x, "ctx", [(i, i + distance) for i in range(count - distance)])
+    return lax.ppermute(x, "ctx", [(i, i + 1) for i in range(first, count - 1)])
 
 
 def after(x, *others):
     return lax.optimization_barrier((x,) + others)[0]
 
 
-def gather(own, core_after=None, beside=None):
+def gather(own, core_after=None, beside=None, middle=None):
     count = lax.axis_size("tp")
     got = {0: [own]}
     masks = [1 << b for b in range(1, count.bit_length() - 1)]
     if len(masks) >= 2:
         a, b = masks[0], masks[1]
         half = own.shape[0] // (2 * EXTRA) * EXTRA
-        got[a] = [swap(own, a)]
-        got[b] = [swap(own, b)]
-        via_a, via_b = got[a][0], got[b][0]
+        via_a, via_b = swap(own, a), swap(own, b)
         got[1] = [swap(own, 1)]
         if beside is not None:
-            first = beside(got[1][0])
-            via_a, via_b = after(via_a, first), after(via_b, first)
-        got[a | b] = [swap(via_a[:half], b), swap(via_b[half:], a)]
+            token = beside(got[1][0])
+            via_a, via_b = after(via_a, token), after(via_b, token)
+        got[a], got[b] = [via_a], [via_b]
+        diagonal = [swap(via_a[:half], b), swap(via_b[half:], a)]
+        if core_after is not None:
+            diagonal = [after(p, core_after) for p in diagonal]
+            via_a, via_b = after(via_a, core_after), after(via_b, core_after)
+        got[a | 1], got[b | 1] = [swap(via_a, 1)], [swap(via_b, 1)]
+        got[a | b] = diagonal
+        if middle is not None:
+            token = middle(got)
+            diagonal = [after(p, token) for p in diagonal]
+        got[a | b | 1] = [swap(p, 1) for p in diagonal]
         masks = masks[2:]
-    if core_after is not None:
-        for m in got:
-            if m > 1:
-                got[m] = [after(p, core_after) for p in got[m]]
-    if count > 1:
-        for m in list(got):
-            if m | 1 not in got:
-                got[m | 1] = [swap(p, 1) for p in got[m]]
+    elif count > 1:
+        got[1] = [swap(own, 1)]
     for mask in masks:
         for m in list(got):
             got[m | mask] = [swap(p, mask) for p in got[m]]
@@ -527,64 +541,57 @@
         (gain, order, ctx_at, flips, signs)
     )
     clipped = pre(hidden_in, gain)
-    squares = None
 
     kv_cols = w_key.shape[1]
     sharing = HD // kv_cols if kv_cols < HD else 1
     kv_heads = kv_cols * sharing // HD
-    queries, kvs = [], []
-    for at in range(HALVES):
-        own = clipped[at]
-        if at:
-            own = after(own, *[b[0] for b in blocks[2:6:2]], loaded[1])
-        if at:
-            blocks = gather(own, core_after=queries[-1])
-        else:
-            loaded = []
-
-            def bring(token):
-                first = after(w_query, token, order, ctx_at, flips, signs)
-                loaded.extend(load(first, w_key, w_value, w_out))
-                return loaded[1]
-
-            blocks = gather(own, beside=bring)
-            if not loaded:
-                bring(own)
-        part = squares
-        if at and ctx_count > 1:
-            part = after(part, kvs[0][1])
-        q, kv, *rest = proj(order, blocks, at, half, part, *loaded[:3])
-        if rest:
-            squares = rest[0]
-        if sharing > 1:
-            k, v = kv[:, :kv_cols], kv[:, kv_cols:]
-            for bit in range(sharing.bit_length() - 1):
-                upper = tp_at >> bit & 1 == 1
-                k2, v2 = swap(k, 1 << bit), swap(v, 1 << bit)
-                k, v = (
-                    jnp.where(
-                        upper,
-                        jnp.concatenate([far, near], axis=1),
-                        jnp.concatenate([near, far], axis=1),
-                    )
-                    for near, far in ((k, k2), (v, v2))
+    loaded = []
+
+    def bring(token):
+        first = after(w_query, token, order, ctx_at, flips, signs)
+        loaded.extend(load(first, w_key, w_value, w_out))
+        return loaded[1]
+
+    early, state = [], []
+
+    def begin(got):
+        early.extend(sorted(got)[:-1])
+        part = {m: got[m] for m in early}
+        state.extend(proj(order, part, rows, (), False, *loaded[:3]))
+        return state[-1]
+
+    blocks = gather(clipped, beside=bring, middle=begin)
+    if not loaded:
+        bring(clipped)
+    late = {m: block for m, block in enumerate(blocks) if m not in early}
+    q, kv = proj(order, late, rows, state, True, *loaded[:3])
+    if sharing > 1:
+        k, v = kv[:, :kv_cols], kv[:, kv_cols:]
+        for bit in range(sharing.bit_length() - 1):
+            upper = tp_at >> bit & 1 == 1
+            k2, v2 = swap(k, 1 << bit), swap(v, 1 << bit)
+            k, v = (
+                jnp.where(
+                    upper,
+                    jnp.concatenate([far, near], axis=1),
+                    jnp.concatenate([near, far], axis=1),
                 )
-            kv = jnp.concatenate([k, v], axis=1)
-        queries.append(q)
-        kvs.append([kv] + [send_up(kv, hop) for hop in range(1, ctx_count)])
-
-    states = []
-    for at in range(HALVES):
-        near = [(p * half, kvs[p][0]) for p in range(at + 1)]
-        far = [(hop, kvs[p][hop]) for p in range(HALVES - 1) for hop in range(1, ctx_count)]
-        states.append(
-            attend(ctx_at, queries[at], at * half, kv_heads, near, far, None, None)
-        )
+                for near, far in ((k, k2), (v, v2))
+            )
+        kv = jnp.concatenate([k, v], axis=1)
+    kvs = [kv]
+    for hop in range(1, ctx_count):
+        kvs.append(send_up(kvs[-1], hop - 1))
+    far = list(enumerate(kvs))[1:]
+
+    states = [
+        attend(ctx_at, q, at * half, half, kv_heads, [kv], far[:-1], None, None)
+        for at in range(HALVES)
+    ]
     branches, stats = [], []
     for at in range(HALVES):
-        far = [(hop, kvs[HALVES - 1][hop]) for hop in range(1, ctx_count)]
         signed = attend(
-            ctx_at, queries[at], at * half, kv_heads, [], far, states[at], signs
+            ctx_at, q, at * half, half, kv_heads, [], far[-1:], states[at], signs
         )
         if at:
             signed = after(signed, *[b[0] for b in blocks[2:6:2]])

time: 131 us -> 126 us (0.962); the launches traced: 129 us -> 126 us
  starting transfers between devices: 33.1 us -> 22.3 us
  waiting for transfers between devices: 53.3 us -> 62.7 us
    ppermute x39 -> x30, starting transfers between devices: 25.2 us -> 18.4 us  [swap(): return lax.ppermute(x, 'tp', [(i, i ^ mask) for i in range(count)])]
    ppermute x6 -> x3, waiting for transfers between devices: 16 us -> 21.3 us  [send_up(): return lax.ppermute(x, 'ctx', [(i, i + 1) for i in range(first, count - 1)])]
    ppermute x39 -> x30, waiting for transfers between devices: 37.3 us -> 41.4 us  [swap(): return lax.ppermute(x, 'tp', [(i, i ^ mask) for i in range(count)])]
    ppermute x6 -> x3, starting transfers between devices: 7.86 us -> 3.85 us  [send_up(): return lax.ppermute(x, 'ctx', [(i, i + 1) for i in range(first, count - 1)])]
  transfers between devices with their start and end apart: 45 -> 33, of which waited for: 18 -> 18; matrix products, arithmetic and copies ran while one was open for 0% -> 0% of each run, Pallas kernels for 22% -> 21%
where the time goes in v5:
time: 126 us
  waiting for transfers between devices  62.7 us (50%)
  Pallas kernels  39.5 us (31%)
  starting transfers between devices  22.3 us (18%)
    ppermute x30, waiting for transfers between devices, swap(): return lax.ppermute(x, 'tp', [(i, i ^ mask) for i in range(count)])  41.4 us
    ppermute x3, waiting for transfers between devices, send_up(): return lax.ppermute(x, 'ctx', [(i, i + 1) for i in range(first, count - 1)])  21.3 us
    ppermute x30, starting transfers between devices, swap(): return lax.ppermute(x, 'tp', [(i, i ^ mask) for i in range(count)])  18.4 us
    pallas_call x2, Pallas kernels, project_out(): pl.pallas_call(functools.partial(out_kernel, counts, steps, chunk), in_sp...  11.8 us
    pallas_call x4, Pallas kernels, attend(): pl.pallas_call(kernel, in_specs=[IN_SMEM] + [IN_VMEM] * (len(args) - 1),...  9.23 us
    pallas_call x2, Pallas kernels, proj(): pl.pallas_call(functools.partial(proj_kernel, counts, masks, not state, e...  8 us
    pallas_call x1, Pallas kernels, load(): pl.pallas_call(functools.partial(load_kernel, count), in_specs=[IN_HBM] *...  7.19 us
    ppermute x3, starting transfers between devices, send_up(): return lax.ppermute(x, 'ctx', [(i, i + 1) for i in range(first, count - 1)])  3.85 us
  transfers between devices with their start and end apart: 33, of which 18 were waited for; matrix products, arithmetic and copies ran while one was open for 0% of the time, Pallas kernels for 21%

profile of v5, /device:TPU:24, one launch (start us, length us, event | category | flops | bytes accessed | tf_op | source)
XLA Modules:
  0.0 126.2 jit_solution(4583503116669728735)
XLA Ops:
  0.7 0.7 add_convert_fusion.refs_4_
  1.3 2.1 %pre.1.refs_0_ = bf16[528,1024]{1,0:T(8,128)(2,1)S(1)} custom-call(bf16[512,1024]{1,0:T(8,128)(2,1)} %h_hbm.1, bf16[8,128]{1,0:T(8,128)(2,1)} %bitcast.3), custom_call_target="tpu_custom_call" | custom-call | flops 4194304 | bytes 2097152 | tf_op jit(solution)/shard_map/pre/pallas_call | solution.py:87
  3.4 0.1 collective-permute-start.1
  3.5 1.6 %collective-permute-start.3 = (bf16[528,1024]{1,0:T(8,128)(2,1)S(1)}, bf16[528,1024]{1,0:T(8,128)(2,1)S(1)}, u32[]{:S(2)}, u32[]{:S(2)}) collective-permute-start(bf16[528,1024]{1,0:T(8,128)(2,1)S(1)} %pre.1.refs_0_), channel_id=1, source_target_pairs={{0,4},{1,5},{2,6},{3,7},{4,0},{5,1},{6,2},{7,3},{8,12},{9,13},{10,... | collective-permute-start | bytes 3244040 | tf_op jit(solution)/shard_map/ppermute | solution.py:478
  5.1 1.5 %collective-permute-start = (bf16[528,1024]{1,0:T(8,128)(2,1)S(1)}, bf16[528,1024]{1,0:T(8,128)(2,1)S(1)}, u32[]{:S(2)}, u32[]{:S(2)}) collective-permute-start(bf16[528,1024]{1,0:T(8,128)(2,1)S(1)} %pre.1.refs_0_), channel_id=1, source_target_pairs={{0,2},{1,3},{2,0},{3,1},{4,6},{5,7},{6,4},{7,5},{8,10},{9,11},{10,... | collective-permute-start | bytes 3244040 | tf_op jit(solution)/shard_map/ppermute | solution.py:478
  6.6 0.0 collective-permute-done.1.refs_1_
  6.6 7.2 %load.1 = (bf16[8192,512]{1,0:T(8,128)(2,1)S(1)}, bf16[8192,128]{1,0:T(8,128)(2,1)S(1)}, bf16[8192,128]{1,0:T(8,128)(2,1)S(1)}, bf16[4096,1024]{1,0:T(8,128)(2,1)S(1)}) custom-call(bf16[8192,512]{1,0:T(8,128)(2,1)} %refs_0_, bf16[8192,128]{1,0:T(8,128)(2,1)} %refs_1_.1, bf16[8192,128]{1,0:T(8,128)(2,1)} %refs_2_.1, bf16[4096,1024]{1,0:T(8,128)(2,1)} %refs_3_.1), custom_call_target="tpu_custom_call" | custom-call | bytes 41943040 | tf_op jit(solution)/shard_map/load/pallas_call | solution.py:121
  13.8 16.0 %collective-permute-done.3.refs_4_ = bf16[528,1024]{1,0:T(8,128)(2,1)S(1)} collective-permute-done((bf16[528,1024]{1,0:T(8,128)(2,1)S(1)}, bf16[528,1024]{1,0:T(8,128)(2,1)S(1)}, u32[]{:S(2)}, u32[]{:S(2)}) %collective-permute-start.3) | collective-permute-done | bytes 1081376 | tf_op jit(solution)/shard_map/ppermute | solution.py:478
  29.8 1.2 collective-permute-done.refs_2_
  31.0 1.6 %collective-permute-start.4 = (bf16[272,1024]{1,0:T(8,128)(2,1)S(1)}, bf16[272,1024]{1,0:T(8,128)(2,1)S(1)}, u32[]{:S(2)}, u32[]{:S(2)}) collective-permute-start(bf16[272,1024]{1,0:T(8,128)(2,1)S(1)} %slice.19), channel_id=1, source_target_pairs={{0,2},{1,3},{2,0},{3,1},{4,6},{5,7},{6,4},{7,5},{8,10},{9,11},{10,... | collective-permute-start | bytes 1671176 | tf_op jit(solution)/shard_map/ppermute | solution.py:478
  32.6 0.9 collective-permute-start.2
  33.5 0.5 collective-permute-done.5.refs_3_
  34.0 5.6 %proj.2 = (f32[512,512]{1,0:T(8,128)S(1)}, f32[512,128]{1,0:T(8,128)S(1)}, f32[512,128]{1,0:T(8,128)S(1)}, f32[8,512]{1,0:T(8,128)S(1)}) custom-call(s32[8]{0:T(128)S(1)} %get-tuple-element.41.order_ref, bf16[528,1024]{1,0:T(8,128)(2,1)S(1)} %pre.1.refs_0_, bf16[528,1024]{1,0:T(8,128)(2,1)S(1)} %collective-permute-done.1.refs_1_, ...), custom_call_target="tpu_custom_call" | custom-call | flops 4831838208 | bytes 15728640 | tf_op jit(solution)/shard_map/proj/pallas_call | solution.py:214
  39.6 6.5 %collective-permute-done.4.refs_1_ = bf16[272,1024]{1,0:T(8,128)(2,1)S(1)} collective-permute-done((bf16[272,1024]{1,0:T(8,128)(2,1)S(1)}, bf16[272,1024]{1,0:T(8,128)(2,1)S(1)}, u32[]{:S(2)}, u32[]{:S(2)}) %collective-permute-start.4) | collective-permute-done | bytes 557088 | tf_op jit(solution)/shard_map/ppermute | solution.py:478
  46.1 0.0 collective-permute-start.8
  46.1 0.6 collective-permute-done.2.refs_0_
  46.8 2.1 %collective-permute-done.7.refs_2_ = bf16[256,1024]{1,0:T(8,128)(2,1)S(1)} collective-permute-done((bf16[256,1024]{1,0:T(8,128)(2,1)S(1)}, bf16[256,1024]{1,0:T(8,128)(2,1)S(1)}, u32[]{:S(2)}, u32[]{:S(2)}) %collective-permute-start.7) | collective-permute-done | bytes 524320 | tf_op jit(solution)/shard_map/ppermute | solution.py:478
  48.9 0.0 collective-permute-done.8.refs_3_
  48.9 2.4 %proj.3 = (bf16[512,512]{1,0:T(8,128)(2,1)S(1)}, bf16[512,256]{1,0:T(8,128)(2,1)S(1)}) custom-call(s32[8]{0:T(128)S(1)} %get-tuple-element.41.order_ref, bf16[256,1024]{1,0:T(8,128)(2,1)S(1)} %collective-permute-done.2.refs_0_, bf16[272,1024]{1,0:T(8,128)(2,1)S(1)} %collective-permute-done.4.refs_1_, bf16[256,1024]{1,0:T(8,128)(2,1)S(1)} %collective-permute-done.7.refs_2_, ...), custom_call_target="tpu_custom_call" | custom-call | flops 1610612736 | bytes 5242880 | tf_op jit(solution)/shard_map/proj/pallas_call | solution.py:214
  51.3 1.3 %collective-permute-start.9 = (bf16[512,256]{1,0:T(8,128)(2,1)S(1)}, bf16[512,256]{1,0:T(8,128)(2,1)S(1)}, u32[]{:S(2)}, u32[]{:S(2)}) collective-permute-start(bf16[512,256]{1,0:T(8,128)(2,1)S(1)} %get-tuple-element.57.refs_0_), channel_id=1, source_target_pairs={{0,8},{8,16},{16,24},{1,9},{9,17},{17,25},{2,10},{10,18},{18,26},{... | collective-permute-start | bytes 786440 | tf_op jit(solution)/shard_map/ppermute | solution.py:483
  52.6 8.9 %collective-permute-done.9.refs_1_ = bf16[512,256]{1,0:T(8,128)(2,1)S(1)} collective-permute-done((bf16[512,256]{1,0:T(8,128)(2,1)S(1)}, bf16[512,256]{1,0:T(8,128)(2,1)S(1)}, u32[]{:S(2)}, u32[]{:S(2)}) %collective-permute-start.9) | collective-permute-done | bytes 262176 | tf_op jit(solution)/shard_map/ppermute | solution.py:483
  61.5 1.3 %collective-permute-start.10 = (bf16[512,256]{1,0:T(8,128)(2,1)S(1)}, bf16[512,256]{1,0:T(8,128)(2,1)S(1)}, u32[]{:S(2)}, u32[]{:S(2)}) collective-permute-start(bf16[512,256]{1,0:T(8,128)(2,1)S(1)} %collective-permute-done.9.refs_1_), channel_id=1, source_target_pairs={{8,16},{16,24},{9,17},{17,25},{10,18},{18,26},{11,19},{19,27},{12,... | collective-permute-start | bytes 786440 | tf_op jit(solution)/shard_map/ppermute | solution.py:483
  62.8 8.1 %collective-permute-done.10.refs_2_ = bf16[512,256]{1,0:T(8,128)(2,1)S(1)} collective-permute-done((bf16[512,256]{1,0:T(8,128)(2,1)S(1)}, bf16[512,256]{1,0:T(8,128)(2,1)S(1)}, u32[]{:S(2)}, u32[]{:S(2)}) %collective-permute-start.10) | collective-permute-done | bytes 262176 | tf_op jit(solution)/shard_map/ppermute | solution.py:483
  70.9 1.3 %collective-permute-start.11 = (bf16[512,256]{1,0:T(8,128)(2,1)S(1)}, bf16[512,256]{1,0:T(8,128)(2,1)S(1)}, u32[]{:S(2)}, u32[]{:S(2)}) collective-permute-start(bf16[512,256]{1,0:T(8,128)(2,1)S(1)} %collective-permute-done.10.refs_2_), channel_id=1, source_target_pairs={{16,24},{17,25},{18,26},{19,27},{20,28},{21,29},{22,30},{23,31}} | collective-permute-start | bytes 786440 | tf_op jit(solution)/shard_map/ppermute | solution.py:483
  72.2 2.9 %attend.4 = (f32[8,256]{1,0:T(8,128)S(1)}, f32[8,256]{1,0:T(8,128)S(1)}, f32[4,128,256]{2,1,0:T(8,128)S(1)}) custom-call(s32[1]{0:T(128)} %bitcast.1.me_ref, bf16[512,512]{1,0:T(8,128)(2,1)S(1)} %get-tuple-element.56.q_ref, bf16[512,256]{1,0:T(8,128)(2,1)S(1)} %get-tuple-element.57.refs_0_, bf16[512,256]{1,0:T(8,128)(2,1)S(1)} %collective-permute-done.9.refs_1_, ...), custom_call_target="tpu_custom_call" | custom-call | flops 805306368 | bytes 786432 | tf_op jit(solution)/shard_map/attend/pallas_call | solution.py:325
  75.1 4.3 %collective-permute-done.11.refs_0_ = bf16[512,256]{1,0:T(8,128)(2,1)S(1)} collective-permute-done((bf16[512,256]{1,0:T(8,128)(2,1)S(1)}, bf16[512,256]{1,0:T(8,128)(2,1)S(1)}, u32[]{:S(2)}, u32[]{:S(2)}) %collective-permute-start.11) | collective-permute-done | bytes 262176 | tf_op jit(solution)/shard_map/ppermute | solution.py:483
  79.4 1.4 %attend.5.refs_0_ = bf16[256,512]{1,0:T(8,128)(2,1)S(1)} custom-call(s32[1]{0:T(128)} %bitcast.1.me_ref, bf16[512,512]{1,0:T(8,128)(2,1)S(1)} %get-tuple-element.56.q_ref, bf16[512,256]{1,0:T(8,128)(2,1)S(1)} %collective-permute-done.11.refs_0_, f32[8,256]{1,0:T(8,128)S(1)} %get-tuple-element.58.refs_1_, f32[8,256]{1,0:T(8,128)S(1)} %get-tuple-element.59.refs_2_, ...), custom_call_target="tpu_custom_call" | custom-call | flops 268435456 | bytes 262144 | tf_op jit(solution)/shard_map/attend/pallas_call | solution.py:325
  80.8 0.0 copy-start
  80.8 1.6 %collective-permute-start.13 = (bf16[256,512]{1,0:T(8,128)(2,1)S(1)}, bf16[256,512]{1,0:T(8,128)(2,1)S(1)}, u32[]{:S(2)}, u32[]{:S(2)}) collective-permute-start(bf16[256,512]{1,0:T(8,128)(2,1)S(1)} %attend.5.refs_0_), channel_id=1, source_target_pairs={{0,2},{1,3},{2,0},{3,1},{4,6},{5,7},{6,4},{7,5},{8,10},{9,11},{10,... | collective-permute-start | bytes 786440 | tf_op jit(solution)/shard_map/ppermute | solution.py:478
  82.3 0.5 collective-permute-start.15
  82.8 3.6 %attend.6 = (f32[8,256]{1,0:T(8,128)S(1)}, f32[8,256]{1,0:T(8,128)S(1)}, f32[4,128,256]{2,1,0:T(8,128)S(1)}) custom-call(s32[1]{0:T(128)} %bitcast.1.me_ref, bf16[512,512]{1,0:T(8,128)(2,1)S(1)} %get-tuple-element.56.q_ref, bf16[512,256]{1,0:T(8,128)(2,1)S(1)} %get-tuple-element.57.refs_0_, bf16[512,256]{1,0:T(8,128)(2,1)S(1)} %collective-permute-done.9.refs_1_, ...), custom_call_target="tpu_custom_call" | custom-call | flops 805306368 | bytes 786432 | tf_op jit(solution)/shard_map/attend/pallas_call | solution.py:325
  86.4 1.4 %attend.7.refs_0_ = bf16[256,512]{1,0:T(8,128)(2,1)S(1)} custom-call(s32[1]{0:T(128)} %bitcast.1.me_ref, bf16[512,512]{1,0:T(8,128)(2,1)S(1)} %get-tuple-element.56.q_ref, bf16[512,256]{1,0:T(8,128)(2,1)S(1)} %collective-permute-done.11.refs_0_, f32[8,256]{1,0:T(8,128)S(1)} %get-tuple-element.63.refs_1_, f32[8,256]{1,0:T(8,128)S(1)} %get-tuple-element.64.refs_2_, ...), custom_call_target="tpu_custom_call" | custom-call | flops 268435456 | bytes 262144 | tf_op jit(solution)/shard_map/attend/pallas_call | solution.py:325
  87.8 1.9 %collective-permute-done.15.refs_4_ = bf16[256,512]{1,0:T(8,128)(2,1)S(1)} collective-permute-done((bf16[256,512]{1,0:T(8,128)(2,1)S(1)}, bf16[256,512]{1,0:T(8,128)(2,1)S(1)}, u32[]{:S(2)}, u32[]{:S(2)}) %collective-permute-start.15) | collective-permute-done | bytes 262176 | tf_op jit(solution)/shard_map/ppermute | solution.py:478
  89.7 0.0 collective-permute-start.24
  89.7 0.8 collective-permute-start.22
  90.5 2.1 %collective-permute-start.17 = (bf16[128,512]{1,0:T(8,128)(2,1)S(1)}, bf16[128,512]{1,0:T(8,128)(2,1)S(1)}, u32[]{:S(2)}, u32[]{:S(2)}) collective-permute-start(bf16[128,512]{1,0:T(8,128)(2,1)S(1)} %slice.24), channel_id=1, source_target_pairs={{0,4},{1,5},{2,6},{3,7},{4,0},{5,1},{6,2},{7,3},{8,12},{9,13},{10,... | collective-permute-start | bytes 393224 | tf_op jit(solution)/shard_map/ppermute | solution.py:478
  92.6 1.3 %collective-permute-start.18 = (bf16[128,512]{1,0:T(8,128)(2,1)S(1)}, bf16[128,512]{1,0:T(8,128)(2,1)S(1)}, u32[]{:S(2)}, u32[]{:S(2)}) collective-permute-start(bf16[128,512]{1,0:T(8,128)(2,1)S(1)} %slice.25), channel_id=1, source_target_pairs={{0,2},{1,3},{2,0},{3,1},{4,6},{5,7},{6,4},{7,5},{8,10},{9,11},{10,... | collective-permute-start | bytes 393224 | tf_op jit(solution)/shard_map/ppermute | solution.py:478
  93.9 0.0 collective-permute-start.12
  93.9 3.6 %collective-permute-done.17.refs_6_ = bf16[128,512]{1,0:T(8,128)(2,1)S(1)} collective-permute-done((bf16[128,512]{1,0:T(8,128)(2,1)S(1)}, bf16[128,512]{1,0:T(8,128)(2,1)S(1)}, u32[]{:S(2)}, u32[]{:S(2)}) %collective-permute-start.17) | collective-permute-done | bytes 131104 | tf_op jit(solution)/shard_map/ppermute | solution.py:478
  97.5 0.1 collective-permute-done.18.refs_7_
  97.6 0.4 collective-permute-start.16
  98.0 0.1 collective-permute-start.19
  98.1 0.4 collective-permute-start.20
  98.6 0.0 collective-permute-done.12.refs_1_
  98.6 0.2 collective-permute-start.21
  98.8 0.8 collective-permute-done.19.refs_8_
  99.6 1.0 collective-permute-start.27
  100.6 0.0 collective-permute-done.20.refs_9_
  100.6 1.4 %collective-permute-start.26 = (bf16[128,512]{1,0:T(8,128)(2,1)S(1)}, bf16[128,512]{1,0:T(8,128)(2,1)S(1)}, u32[]{:S(2)}, u32[]{:S(2)}) collective-permute-start(bf16[128,512]{1,0:T(8,128)(2,1)S(1)} %slice.26), channel_id=1, source_target_pairs={{0,4},{1,5},{2,6},{3,7},{4,0},{5,1},{6,2},{7,3},{8,12},{9,13},{10,... | collective-permute-start | bytes 393224 | tf_op jit(solution)/shard_map/ppermute | solution.py:478
  102.0 5.9 %project_out.2 = (f32[256,1024]{1,0:T(8,128)S(1)}, f32[8,256]{1,0:T(8,128)S(1)}) custom-call(f32[8]{0:T(128)S(1)} %get-tuple-element.39.sign_ref, bf16[512,1024]{1,0:T(8,128)(2,1)S(1)} %copy-done, bf16[256,512]{1,0:T(8,128)(2,1)S(1)} %attend.5.refs_0_, bf16[256,512]{1,0:T(8,128)(2,1)S(1)} %collective-permute-done.12.refs_1_, ...), custom_call_target="tpu_custom_call" | custom-call | flops 2147483648 | bytes 12058624 | tf_op jit(solution)/shard_map/project_out/pallas_call | solution.py:420
  107.9 0.0 collective-permute-start.25
  108.0 0.5 collective-permute-start.23
  108.5 0.1 collective-permute-start.29
  108.6 0.4 collective-permute-start.28
  109.0 1.1 collective-permute-done.29.refs_9_
  110.1 0.2 collective-permute-done.28.refs_8_
  110.3 5.9 %project_out.3 = (f32[256,1024]{1,0:T(8,128)S(1)}, f32[8,256]{1,0:T(8,128)S(1)}) custom-call(f32[8]{0:T(128)S(1)} %get-tuple-element.39.sign_ref, bf16[512,1024]{1,0:T(8,128)(2,1)S(1)} %copy-done, bf16[256,512]{1,0:T(8,128)(2,1)S(1)} %attend.7.refs_0_, bf16[256,512]{1,0:T(8,128)(2,1)S(1)} %collective-permute-done.21.refs_1_, ...), custom_call_target="tpu_custom_call" | custom-call | flops 2147483648 | bytes 12058624 | tf_op jit(solution)/shard_map/project_out/pallas_call | solution.py:420
  116.2 0.2 collective-permute-start.30
  116.4 1.0 collective-permute-done.30
  117.4 1.3 collective-permute-start.31
  118.7 2.5 %collective-permute-done.31 = f32[8,512]{1,0:T(8,128)S(1)} collective-permute-done((f32[8,512]{1,0:T(8,128)S(1)}, f32[8,512]{1,0:T(8,128)S(1)}, u32[]{:S(2)}, u32[]{:S(2)}) %collective-permute-start.31) | collective-permute-done | bytes 16416 | tf_op jit(solution)/shard_map/ppermute | solution.py:478
  121.1 0.6 collective-permute-start.32
  121.8 3.1 %collective-permute-done.32 = f32[8,512]{1,0:T(8,128)S(1)} collective-permute-done((f32[8,512]{1,0:T(8,128)S(1)}, f32[8,512]{1,0:T(8,128)S(1)}, u32[]{:S(2)}, u32[]{:S(2)}) %collective-permute-start.32) | collective-permute-done | bytes 16416 | tf_op jit(solution)/shard_map/ppermute | solution.py:478
  124.9 1.3 %final.1 = (bf16[512,1024]{1,0:T(8,128)(2,1)}, f32[1,512]{1,0:T(1,128)}) custom-call(f32[256,1024]{1,0:T(8,128)S(1)} %get-tuple-element.62.refs_0_, f32[256,1024]{1,0:T(8,128)S(1)} %get-tuple-element.71.refs_1_, f32[8,512]{1,0:T(8,128)S(1)} %add.12.refs_2_), custom_call_target="tpu_custom_call" | custom-call | flops 1048576 | bytes 3145728 | tf_op jit(solution)/shard_map/final/pallas_call | solution.py:461
  (28 shorter events, 0.2 us)
Async XLA Ops:
  3.4 3.2 %collective-permute-start.1 = (bf16[528,1024]{1,0:T(8,128)(2,1)S(1)}, bf16[528,1024]{1,0:T(8,128)(2,1)S(1)}, u32[]{:S(2)}, u32[]{:S(2)}) collective-permute-start(bf16[528,1024]{1,0:T(8,128)(2,1)S(1)} %pre.1.refs_0_), channel_id=1, source_target_pairs={{0,1},{1,0},{2,3},{3,2},{4,5},{5,4},{6,7},{7,6},{8,9},{9,8},{10,11... | collective-permute-start | bytes 3244040 | tf_op jit(solution)/shard_map/ppermute | solution.py:478
  3.5 26.3 %collective-permute-start.3 = (bf16[528,1024]{1,0:T(8,128)(2,1)S(1)}, bf16[528,1024]{1,0:T(8,128)(2,1)S(1)}, u32[]{:S(2)}, u32[]{:S(2)}) collective-permute-start(bf16[528,1024]{1,0:T(8,128)(2,1)S(1)} %pre.1.refs_0_), channel_id=1, source_target_pairs={{0,4},{1,5},{2,6},{3,7},{4,0},{5,1},{6,2},{7,3},{8,12},{9,13},{10,... | collective-permute-start | bytes 3244040 | tf_op jit(solution)/shard_map/ppermute | solution.py:478
  5.1 25.9 %collective-permute-start = (bf16[528,1024]{1,0:T(8,128)(2,1)S(1)}, bf16[528,1024]{1,0:T(8,128)(2,1)S(1)}, u32[]{:S(2)}, u32[]{:S(2)}) collective-permute-start(bf16[528,1024]{1,0:T(8,128)(2,1)S(1)} %pre.1.refs_0_), channel_id=1, source_target_pairs={{0,2},{1,3},{2,0},{3,1},{4,6},{5,7},{6,4},{7,5},{8,10},{9,11},{10,... | collective-permute-start | bytes 3244040 | tf_op jit(solution)/shard_map/ppermute | solution.py:478
  29.8 3.7 %collective-permute-start.6 = (bf16[528,1024]{1,0:T(8,128)(2,1)S(1)}, bf16[528,1024]{1,0:T(8,128)(2,1)S(1)}, u32[]{:S(2)}, u32[]{:S(2)}) collective-permute-start(bf16[528,1024]{1,0:T(8,128)(2,1)S(1)} %collective-permute-done.3.refs_4_), channel_id=1, source_target_pairs={{0,1},{1,0},{2,3},{3,2},{4,5},{5,4},{6,7},{7,6},{8,9},{9,8},{10,11... | collective-permute-start | bytes 3244040 | tf_op jit(solution)/shard_map/ppermute | solution.py:478
  31.0 3.0 %collective-permute-start.5 = (bf16[528,1024]{1,0:T(8,128)(2,1)S(1)}, bf16[528,1024]{1,0:T(8,128)(2,1)S(1)}, u32[]{:S(2)}, u32[]{:S(2)}) collective-permute-start(bf16[528,1024]{1,0:T(8,128)(2,1)S(1)} %collective-permute-done.refs_2_), channel_id=1, source_target_pairs={{0,1},{1,0},{2,3},{3,2},{4,5},{5,4},{6,7},{7,6},{8,9},{9,8},{10,11... | collective-permute-start | bytes 3244040 | tf_op jit(solution)/shard_map/ppermute | solution.py:478
  31.0 15.1 %collective-permute-start.4 = (bf16[272,1024]{1,0:T(8,128)(2,1)S(1)}, bf16[272,1024]{1,0:T(8,128)(2,1)S(1)}, u32[]{:S(2)}, u32[]{:S(2)}) collective-permute-start(bf16[272,1024]{1,0:T(8,128)(2,1)S(1)} %slice.19), channel_id=1, source_target_pairs={{0,2},{1,3},{2,0},{3,1},{4,6},{5,7},{6,4},{7,5},{8,10},{9,11},{10,... | collective-permute-start | bytes 1671176 | tf_op jit(solution)/shard_map/ppermute | solution.py:478
  32.6 14.1 %collective-permute-start.2 = (bf16[256,1024]{1,0:T(8,128)(2,1)S(1)}, bf16[256,1024]{1,0:T(8,128)(2,1)S(1)}, u32[]{:S(2)}, u32[]{:S(2)}) collective-permute-start(bf16[256,1024]{1,0:T(8,128)(2,1)S(1)} %slice.18), channel_id=1, source_target_pairs={{0,4},{1,5},{2,6},{3,7},{4,0},{5,1},{6,2},{7,3},{8,12},{9,13},{10,... | collective-permute-start | bytes 1572872 | tf_op jit(solution)/shard_map/ppermute | solution.py:478
  46.1 2.7 %collective-permute-start.8 = (bf16[272,1024]{1,0:T(8,128)(2,1)S(1)}, bf16[272,1024]{1,0:T(8,128)(2,1)S(1)}, u32[]{:S(2)}, u32[]{:S(2)}) collective-permute-start(bf16[272,1024]{1,0:T(8,128)(2,1)S(1)} %collective-permute-done.4.refs_1_), channel_id=1, source_target_pairs={{0,1},{1,0},{2,3},{3,2},{4,5},{5,4},{6,7},{7,6},{8,9},{9,8},{10,11... | collective-permute-start | bytes 1671176 | tf_op jit(solution)/shard_map/ppermute | solution.py:478
  46.8 2.1 %collective-permute-start.7 = (bf16[256,1024]{1,0:T(8,128)(2,1)S(1)}, bf16[256,1024]{1,0:T(8,128)(2,1)S(1)}, u32[]{:S(2)}, u32[]{:S(2)}) collective-permute-start(bf16[256,1024]{1,0:T(8,128)(2,1)S(1)} %collective-permute-done.2.refs_0_), channel_id=1, source_target_pairs={{0,1},{1,0},{2,3},{3,2},{4,5},{5,4},{6,7},{7,6},{8,9},{9,8},{10,11... | collective-permute-start | bytes 1572872 | tf_op jit(solution)/shard_map/ppermute | solution.py:478
  51.3 10.2 %collective-permute-start.9 = (bf16[512,256]{1,0:T(8,128)(2,1)S(1)}, bf16[512,256]{1,0:T(8,128)(2,1)S(1)}, u32[]{:S(2)}, u32[]{:S(2)}) collective-permute-start(bf16[512,256]{1,0:T(8,128)(2,1)S(1)} %get-tuple-element.57.refs_0_), channel_id=1, source_target_pairs={{0,8},{8,16},{16,24},{1,9},{9,17},{17,25},{2,10},{10,18},{18,26},{... | collective-permute-start | bytes 786440 | tf_op jit(solution)/shard_map/ppermute | solution.py:483
  61.5 9.4 %collective-permute-start.10 = (bf16[512,256]{1,0:T(8,128)(2,1)S(1)}, bf16[512,256]{1,0:T(8,128)(2,1)S(1)}, u32[]{:S(2)}, u32[]{:S(2)}) collective-permute-start(bf16[512,256]{1,0:T(8,128)(2,1)S(1)} %collective-permute-done.9.refs_1_), channel_id=1, source_target_pairs={{8,16},{16,24},{9,17},{17,25},{10,18},{18,26},{11,19},{19,27},{12,... | collective-permute-start | bytes 786440 | tf_op jit(solution)/shard_map/ppermute | solution.py:483
  70.9 8.5 %collective-permute-start.11 = (bf16[512,256]{1,0:T(8,128)(2,1)S(1)}, bf16[512,256]{1,0:T(8,128)(2,1)S(1)}, u32[]{:S(2)}, u32[]{:S(2)}) collective-permute-start(bf16[512,256]{1,0:T(8,128)(2,1)S(1)} %collective-permute-done.10.refs_2_), channel_id=1, source_target_pairs={{16,24},{17,25},{18,26},{19,27},{20,28},{21,29},{22,30},{23,31}} | collective-permute-start | bytes 786440 | tf_op jit(solution)/shard_map/ppermute | solution.py:483
  80.8 21.3 %copy-start = (bf16[512,1024]{1,0:T(8,128)(2,1)S(1)}, bf16[512,1024]{1,0:T(8,128)(2,1)}, u32[]{:S(2)}) copy-start(bf16[512,1024]{1,0:T(8,128)(2,1)} %t_ref.3) | copy-start | bytes 3145732
  80.8 7.0 %collective-permute-start.13 = (bf16[256,512]{1,0:T(8,128)(2,1)S(1)}, bf16[256,512]{1,0:T(8,128)(2,1)S(1)}, u32[]{:S(2)}, u32[]{:S(2)}) collective-permute-start(bf16[256,512]{1,0:T(8,128)(2,1)S(1)} %attend.5.refs_0_), channel_id=1, source_target_pairs={{0,2},{1,3},{2,0},{3,1},{4,6},{5,7},{6,4},{7,5},{8,10},{9,11},{10,... | collective-permute-start | bytes 786440 | tf_op jit(solution)/shard_map/ppermute | solution.py:478
  82.3 7.4 %collective-permute-start.15 = (bf16[256,512]{1,0:T(8,128)(2,1)S(1)}, bf16[256,512]{1,0:T(8,128)(2,1)S(1)}, u32[]{:S(2)}, u32[]{:S(2)}) collective-permute-start(bf16[256,512]{1,0:T(8,128)(2,1)S(1)} %attend.5.refs_0_), channel_id=1, source_target_pairs={{0,4},{1,5},{2,6},{3,7},{4,0},{5,1},{6,2},{7,3},{8,12},{9,13},{10,... | collective-permute-start | bytes 786440 | tf_op jit(solution)/shard_map/ppermute | solution.py:478
  89.7 8.3 %collective-permute-start.24 = (bf16[256,512]{1,0:T(8,128)(2,1)S(1)}, bf16[256,512]{1,0:T(8,128)(2,1)S(1)}, u32[]{:S(2)}, u32[]{:S(2)}) collective-permute-start(bf16[256,512]{1,0:T(8,128)(2,1)S(1)} %attend.7.refs_0_), channel_id=1, source_target_pairs={{0,4},{1,5},{2,6},{3,7},{4,0},{5,1},{6,2},{7,3},{8,12},{9,13},{10,... | collective-permute-start | bytes 786440 | tf_op jit(solution)/shard_map/ppermute | solution.py:478
  89.7 8.4 %collective-permute-start.22 = (bf16[256,512]{1,0:T(8,128)(2,1)S(1)}, bf16[256,512]{1,0:T(8,128)(2,1)S(1)}, u32[]{:S(2)}, u32[]{:S(2)}) collective-permute-start(bf16[256,512]{1,0:T(8,128)(2,1)S(1)} %attend.7.refs_0_), channel_id=1, source_target_pairs={{0,2},{1,3},{2,0},{3,1},{4,6},{5,7},{6,4},{7,5},{8,10},{9,11},{10,... | collective-permute-start | bytes 786440 | tf_op jit(solution)/shard_map/ppermute | solution.py:478
  90.5 7.0 %collective-permute-start.17 = (bf16[128,512]{1,0:T(8,128)(2,1)S(1)}, bf16[128,512]{1,0:T(8,128)(2,1)S(1)}, u32[]{:S(2)}, u32[]{:S(2)}) collective-permute-start(bf16[128,512]{1,0:T(8,128)(2,1)S(1)} %slice.24), channel_id=1, source_target_pairs={{0,4},{1,5},{2,6},{3,7},{4,0},{5,1},{6,2},{7,3},{8,12},{9,13},{10,... | collective-permute-start | bytes 393224 | tf_op jit(solution)/shard_map/ppermute | solution.py:478
  92.6 5.0 %collective-permute-start.18 = (bf16[128,512]{1,0:T(8,128)(2,1)S(1)}, bf16[128,512]{1,0:T(8,128)(2,1)S(1)}, u32[]{:S(2)}, u32[]{:S(2)}) collective-permute-start(bf16[128,512]{1,0:T(8,128)(2,1)S(1)} %slice.25), channel_id=1, source_target_pairs={{0,2},{1,3},{2,0},{3,1},{4,6},{5,7},{6,4},{7,5},{8,10},{9,11},{10,... | collective-permute-start | bytes 393224 | tf_op jit(solution)/shard_map/ppermute | solution.py:478
  93.9 4.6 %collective-permute-start.12 = (bf16[256,512]{1,0:T(8,128)(2,1)S(1)}, bf16[256,512]{1,0:T(8,128)(2,1)S(1)}, u32[]{:S(2)}, u32[]{:S(2)}) collective-permute-start(bf16[256,512]{1,0:T(8,128)(2,1)S(1)} %attend.5.refs_0_), channel_id=1, source_target_pairs={{0,1},{1,0},{2,3},{3,2},{4,5},{5,4},{6,7},{7,6},{8,9},{9,8},{10,11... | collective-permute-start | bytes 786440 | tf_op jit(solution)/shard_map/ppermute | solution.py:478
  97.5 4.5 %collective-permute-start.14 = (bf16[256,512]{1,0:T(8,128)(2,1)S(1)}, bf16[256,512]{1,0:T(8,128)(2,1)S(1)}, u32[]{:S(2)}, u32[]{:S(2)}) collective-permute-start(bf16[256,512]{1,0:T(8,128)(2,1)S(1)} %collective-permute-done.13.refs_2_), channel_id=1, source_target_pairs={{0,1},{1,0},{2,3},{3,2},{4,5},{5,4},{6,7},{7,6},{8,9},{9,8},{10,11... | collective-permute-start | bytes 786440 | tf_op jit(solution)/shard_map/ppermute | solution.py:478
  97.6 4.4 %collective-permute-start.16 = (bf16[256,512]{1,0:T(8,128)(2,1)S(1)}, bf16[256,512]{1,0:T(8,128)(2,1)S(1)}, u32[]{:S(2)}, u32[]{:S(2)}) collective-permute-start(bf16[256,512]{1,0:T(8,128)(2,1)S(1)} %collective-permute-done.15.refs_4_), channel_id=1, source_target_pairs={{0,1},{1,0},{2,3},{3,2},{4,5},{5,4},{6,7},{7,6},{8,9},{9,8},{10,11... | collective-permute-start | bytes 786440 | tf_op jit(solution)/shard_map/ppermute | solution.py:478
  98.0 1.6 %collective-permute-start.19 = (bf16[128,512]{1,0:T(8,128)(2,1)S(1)}, bf16[128,512]{1,0:T(8,128)(2,1)S(1)}, u32[]{:S(2)}, u32[]{:S(2)}) collective-permute-start(bf16[128,512]{1,0:T(8,128)(2,1)S(1)} %collective-permute-done.17.refs_6_), channel_id=1, source_target_pairs={{0,1},{1,0},{2,3},{3,2},{4,5},{5,4},{6,7},{7,6},{8,9},{9,8},{10,11... | collective-permute-start | bytes 393224 | tf_op jit(solution)/shard_map/ppermute | solution.py:478
  98.1 2.5 %collective-permute-start.20 = (bf16[128,512]{1,0:T(8,128)(2,1)S(1)}, bf16[128,512]{1,0:T(8,128)(2,1)S(1)}, u32[]{:S(2)}, u32[]{:S(2)}) collective-permute-start(bf16[128,512]{1,0:T(8,128)(2,1)S(1)} %collective-permute-done.18.refs_7_), channel_id=1, source_target_pairs={{0,1},{1,0},{2,3},{3,2},{4,5},{5,4},{6,7},{7,6},{8,9},{9,8},{10,11... | collective-permute-start | bytes 393224 | tf_op jit(solution)/shard_map/ppermute | solution.py:478
  98.6 10.4 %collective-permute-start.21 = (bf16[256,512]{1,0:T(8,128)(2,1)S(1)}, bf16[256,512]{1,0:T(8,128)(2,1)S(1)}, u32[]{:S(2)}, u32[]{:S(2)}) collective-permute-start(bf16[256,512]{1,0:T(8,128)(2,1)S(1)} %attend.7.refs_0_), channel_id=1, source_target_pairs={{0,1},{1,0},{2,3},{3,2},{4,5},{5,4},{6,7},{7,6},{8,9},{9,8},{10,11... | collective-permute-start | bytes 786440 | tf_op jit(solution)/shard_map/ppermute | solution.py:478
  99.6 8.9 %collective-permute-start.27 = (bf16[128,512]{1,0:T(8,128)(2,1)S(1)}, bf16[128,512]{1,0:T(8,128)(2,1)S(1)}, u32[]{:S(2)}, u32[]{:S(2)}) collective-permute-start(bf16[128,512]{1,0:T(8,128)(2,1)S(1)} %slice.27), channel_id=1, source_target_pairs={{0,2},{1,3},{2,0},{3,1},{4,6},{5,7},{6,4},{7,5},{8,10},{9,11},{10,... | collective-permute-start | bytes 393224 | tf_op jit(solution)/shard_map/ppermute | solution.py:478
  100.6 7.9 %collective-permute-start.26 = (bf16[128,512]{1,0:T(8,128)(2,1)S(1)}, bf16[128,512]{1,0:T(8,128)(2,1)S(1)}, u32[]{:S(2)}, u32[]{:S(2)}) collective-permute-start(bf16[128,512]{1,0:T(8,128)(2,1)S(1)} %slice.26), channel_id=1, source_target_pairs={{0,4},{1,5},{2,6},{3,7},{4,0},{5,1},{6,2},{7,3},{8,12},{9,13},{10,... | collective-permute-start | bytes 393224 | tf_op jit(solution)/shard_map/ppermute | solution.py:478
  107.9 2.3 %collective-permute-start.25 = (bf16[256,512]{1,0:T(8,128)(2,1)S(1)}, bf16[256,512]{1,0:T(8,128)(2,1)S(1)}, u32[]{:S(2)}, u32[]{:S(2)}) collective-permute-start(bf16[256,512]{1,0:T(8,128)(2,1)S(1)} %collective-permute-done.24.refs_4_), channel_id=1, source_target_pairs={{0,1},{1,0},{2,3},{3,2},{4,5},{5,4},{6,7},{7,6},{8,9},{9,8},{10,11... | collective-permute-start | bytes 786440 | tf_op jit(solution)/shard_map/ppermute | solution.py:478
  108.0 2.3 %collective-permute-start.23 = (bf16[256,512]{1,0:T(8,128)(2,1)S(1)}, bf16[256,512]{1,0:T(8,128)(2,1)S(1)}, u32[]{:S(2)}, u32[]{:S(2)}) collective-permute-start(bf16[256,512]{1,0:T(8,128)(2,1)S(1)} %collective-permute-done.22.refs_2_), channel_id=1, source_target_pairs={{0,1},{1,0},{2,3},{3,2},{4,5},{5,4},{6,7},{7,6},{8,9},{9,8},{10,11... | collective-permute-start | bytes 786440 | tf_op jit(solution)/shard_map/ppermute | solution.py:478
  108.5 1.6 %collective-permute-start.29 = (bf16[128,512]{1,0:T(8,128)(2,1)S(1)}, bf16[128,512]{1,0:T(8,128)(2,1)S(1)}, u32[]{:S(2)}, u32[]{:S(2)}) collective-permute-start(bf16[128,512]{1,0:T(8,128)(2,1)S(1)} %collective-permute-done.27.refs_7_), channel_id=1, source_target_pairs={{0,1},{1,0},{2,3},{3,2},{4,5},{5,4},{6,7},{7,6},{8,9},{9,8},{10,11... | collective-permute-start | bytes 393224 | tf_op jit(solution)/shard_map/ppermute | solution.py:478
  108.6 1.7 %collective-permute-start.28 = (bf16[128,512]{1,0:T(8,128)(2,1)S(1)}, bf16[128,512]{1,0:T(8,128)(2,1)S(1)}, u32[]{:S(2)}, u32[]{:S(2)}) collective-permute-start(bf16[128,512]{1,0:T(8,128)(2,1)S(1)} %collective-permute-done.26.refs_6_), channel_id=1, source_target_pairs={{0,1},{1,0},{2,3},{3,2},{4,5},{5,4},{6,7},{7,6},{8,9},{9,8},{10,11... | collective-permute-start | bytes 393224 | tf_op jit(solution)/shard_map/ppermute | solution.py:478
  116.2 1.2 collective-permute-start.30
  117.4 3.7 %collective-permute-start.31 = (f32[8,512]{1,0:T(8,128)S(1)}, f32[8,512]{1,0:T(8,128)S(1)}, u32[]{:S(2)}, u32[]{:S(2)}) collective-permute-start(f32[8,512]{1,0:T(8,128)S(1)} %add.10), channel_id=1, source_target_pairs={{0,2},{1,3},{2,0},{3,1},{4,6},{5,7},{6,4},{7,5},{8,10},{9,11},{10,... | collective-permute-start | bytes 49160 | tf_op jit(solution)/shard_map/ppermute | solution.py:478
  121.1 3.7 %collective-permute-start.32 = (f32[8,512]{1,0:T(8,128)S(1)}, f32[8,512]{1,0:T(8,128)S(1)}, u32[]{:S(2)}, u32[]{:S(2)}) collective-permute-start(f32[8,512]{1,0:T(8,128)S(1)} %add.11), channel_id=1, source_target_pairs={{0,4},{1,5},{2,6},{3,7},{4,0},{5,1},{6,2},{7,3},{8,12},{9,13},{10,... | collective-permute-start | bytes 49160 | tf_op jit(solution)/shard_map/ppermute | solution.py:478

commit v6 on v5

--- a/solution.py
+++ b/solution.py
@@ -142,7 +142,8 @@
         before = [None] * 3
         squares = jnp.zeros((1, ss_rows(blocks)), jnp.float32)
     if ends:
-        q_ref, kv_ref, *accs = refs
+        q_ref, *kv_refs = refs[: 1 + HALVES]
+        accs = refs[1 + HALVES :]
     else:
         *accs, ss_ref = refs
     nk = wk_ref.shape[1]
@@ -183,8 +184,11 @@
         inverse = lax.rsqrt(squares * (1.0 / features) + EPS_IN)
         scale = jnp.transpose(inverse)[:, :1]
         q_ref[...] = (accq[...] * scale).astype(jnp.bfloat16)
-        kv_ref[:, :nk] = (acck[...] * scale).astype(jnp.bfloat16)
-        kv_ref[:, nk:] = (accv[...] * scale).astype(jnp.bfloat16)
+        rows = kv_refs[0].shape[0]
+        for i, kv_ref in enumerate(kv_refs):
+            at = slice(i * rows, (i + 1) * rows)
+            kv_ref[:, :nk] = (acck[at, :] * scale[at]).astype(jnp.bfloat16)
+            kv_ref[:, nk:] = (accv[at, :] * scale[at]).astype(jnp.bfloat16)
 
 
 def ss_rows(blocks):
@@ -204,7 +208,9 @@
     if ends:
         out_shape = [
             jax.ShapeDtypeStruct((rows, sizes[0]), jnp.bfloat16),
-            jax.ShapeDtypeStruct((rows, sizes[1] + sizes[2]), jnp.bfloat16),
+        ] + [
+            jax.ShapeDtypeStruct((rows // HALVES, sizes[1] + sizes[2]), jnp.bfloat16)
+            for _ in range(HALVES)
         ]
         scratch = [pltpu.VMEM((rows, m), jnp.float32) for m in sizes]
     else:
@@ -236,7 +242,7 @@
         high, total, accum = refs
     rows = accum.shape[2]
     heads = q_ref.shape[1] // HD
-    part = rows
+    part = kvs[0].shape[0]
     group = heads // kv_heads
     scale = HD ** (-0.5) * LOG2E
 
@@ -285,14 +291,12 @@
             high[head : head + 1] = best
 
     for at in range(near):
-        for sub in range((first + rows) // part):
-            visit(kvs[at], sub, sub * part, begins and at == 0 and sub == 0)
+        visit(kvs[at], 0, at * part, begins and at == 0)
     for at, hop in enumerate(far):
 
         @pl.when(me_ref[0] >= hop)
         def _():
-            for sub in range(kvs[near + at].shape[0] // part):
-                visit(kvs[near + at], sub, None, False)
+            visit(kvs[near + at], 0, None, False)
 
     if ends:
         for head in range(heads):
@@ -439,9 +443,10 @@
 def final_kernel(features, chunks, parts, *refs):
     branches, stats = refs[:chunks], refs[chunks : chunks + parts]
     student_ref, loss_ref = refs[chunks + parts :]
-    total = stats[0][...]
-    for at in range(1, parts):
-        total = total + stats[at][...]
+    sums = [stat[...] for stat in stats]
+    while len(sums) > 1:
+        sums = [x + y for x, y in zip(sums[::2], sums[1::2])]
+    total = sums[0]
     inverse = lax.rsqrt(total[0:1] * (1.0 / features) + EPS_OUT)
     loss = inverse * inverse * total[0:1] - 2.0 * inverse * total[1:2] + total[2:3]
     loss_ref[...] = jnp.maximum(loss, 0.0) * (1.0 / features)
@@ -564,34 +569,36 @@
     if not loaded:
         bring(clipped)
     late = {m: block for m, block in enumerate(blocks) if m not in early}
-    q, kv = proj(order, late, rows, state, True, *loaded[:3])
-    if sharing > 1:
-        k, v = kv[:, :kv_cols], kv[:, kv_cols:]
-        for bit in range(sharing.bit_length() - 1):
-            upper = tp_at >> bit & 1 == 1
-            k2, v2 = swap(k, 1 << bit), swap(v, 1 << bit)
-            k, v = (
-                jnp.where(
-                    upper,
-                    jnp.concatenate([far, near], axis=1),
-                    jnp.concatenate([near, far], axis=1),
+    q, *kvs = proj(order, late, rows, state, True, *loaded[:3])
+    for i, kv in enumerate(kvs):
+        if sharing > 1:
+            k, v = kv[:, :kv_cols], kv[:, kv_cols:]
+            for bit in range(sharing.bit_length() - 1):
+                upper = tp_at >> bit & 1 == 1
+                k2, v2 = swap(k, 1 << bit), swap(v, 1 << bit)
+                k, v = (
+                    jnp.where(
+                        upper,
+                        jnp.concatenate([far, near], axis=1),
+                        jnp.concatenate([near, far], axis=1),
+                    )
+                    for near, far in ((k, k2), (v, v2))
                 )
-                for near, far in ((k, k2), (v, v2))
-            )
-        kv = jnp.concatenate([k, v], axis=1)
-    kvs = [kv]
+            kv = jnp.concatenate([k, v], axis=1)
+        kvs[i] = kv
+    far, sent = [], kvs
     for hop in range(1, ctx_count):
-        kvs.append(send_up(kvs[-1], hop - 1))
-    far = list(enumerate(kvs))[1:]
+        sent = [send_up(kv, hop - 1) for kv in sent]
+        far += [(hop, kv) for kv in sent]
 
     states = [
-        attend(ctx_at, q, at * half, half, kv_heads, [kv], far[:-1], None, None)
+        attend(ctx_at, q, at * half, half, kv_heads, kvs[: at + 1], far[:-HALVES], None, None)
         for at in range(HALVES)
     ]
     branches, stats = [], []
     for at in range(HALVES):
         signed = attend(
-            ctx_at, q, at * half, half, kv_heads, [], far[-1:], states[at], signs
+            ctx_at, q, at * half, half, kv_heads, [], far[-HALVES:], states[at], signs
         )
         if at:
             signed = after(signed, *[b[0] for b in blocks[2:6:2]])
@@ -600,9 +607,10 @@
         branches.append(b)
         stats.append(s)
     stat = jnp.concatenate(stats, axis=1)
-    for bit in range(tp_count.bit_length() - 1):
-        stat = stat + swap(stat, 1 << bit)
-    student, loss = final(features, branches, [stat])
+    if tp_count > 1:
+        stat = stat + swap(stat, 1)
+    totals = [stat] + [swap(stat, m) for m in range(2, tp_count, 2)]
+    student, loss = final(features, branches, totals)
     return student, loss.reshape(rows)
 
 

time: 126 us -> 123 us (0.976)
  waiting for transfers between devices: 62.7 us -> 54.4 us
  starting transfers between devices: 22.3 us -> 26.5 us
    ppermute x3 -> x6, waiting for transfers between devices: 21.3 us -> 14.7 us  [send_up(): return lax.ppermute(x, 'ctx', [(i, i + 1) for i in range(first, count - 1)])]
    ppermute x3 -> x6, starting transfers between devices: 3.85 us -> 7.71 us  [send_up(): return lax.ppermute(x, 'ctx', [(i, i + 1) for i in range(first, count - 1)])]
    ppermute x30 -> x31, waiting for transfers between devices: 41.4 us -> 39.7 us  [swap(): return lax.ppermute(x, 'tp', [(i, i ^ mask) for i in range(count)])]
    ppermute x30 -> x31, starting transfers between devices: 18.4 us -> 18.8 us  [swap(): return lax.ppermute(x, 'tp', [(i, i ^ mask) for i in range(count)])]
  transfers between devices with their start and end apart: 33 -> 37, of which waited for: 18 -> 22; matrix products, arithmetic and copies ran while one was open for 0% -> 0% of each run, Pallas kernels for 21% -> 22%
where the time goes in v6:
time: 123 us
  waiting for transfers between devices  54.4 us (44%)
  Pallas kernels  40.4 us (33%)
  starting transfers between devices  26.5 us (22%)
    ppermute x31, waiting for transfers between devices, swap(): return lax.ppermute(x, 'tp', [(i, i ^ mask) for i in range(count)])  39.7 us
    ppermute x31, starting transfers between devices, swap(): return lax.ppermute(x, 'tp', [(i, i ^ mask) for i in range(count)])  18.8 us
    ppermute x6, waiting for transfers between devices, send_up(): return lax.ppermute(x, 'ctx', [(i, i + 1) for i in range(first, count - 1)])  14.7 us
    pallas_call x2, Pallas kernels, project_out(): pl.pallas_call(functools.partial(out_kernel, counts, steps, chunk), in_sp...  11.8 us
    pallas_call x4, Pallas kernels, attend(): pl.pallas_call(kernel, in_specs=[IN_SMEM] + [IN_VMEM] * (len(args) - 1),...  10.1 us
    pallas_call x2, Pallas kernels, proj(): pl.pallas_call(functools.partial(proj_kernel, counts, masks, not state, e...  8 us
    ppermute x6, starting transfers between devices, send_up(): return lax.ppermute(x, 'ctx', [(i, i + 1) for i in range(first, count - 1)])  7.71 us
    pallas_call x1, Pallas kernels, load(): pl.pallas_call(functools.partial(load_kernel, count), in_specs=[IN_HBM] *...  7.19 us
  transfers between devices with their start and end apart: 37, of which 22 were waited for; matrix products, arithmetic and copies ran while one was open for 0% of the time, Pallas kernels for 22%

profile of v6, /device:TPU:24, one launch (start us, length us, event | category | flops | bytes accessed | tf_op | source)
XLA Modules:
  0.0 123.1 jit_solution(2284278345271254943)
XLA Ops:
  0.7 0.7 add_convert_fusion.refs_5_
  1.3 2.1 %pre.1.refs_0_ = bf16[528,1024]{1,0:T(8,128)(2,1)S(1)} custom-call(bf16[512,1024]{1,0:T(8,128)(2,1)} %h_hbm.1, bf16[8,128]{1,0:T(8,128)(2,1)} %bitcast.3), custom_call_target="tpu_custom_call" | custom-call | flops 4194304 | bytes 2097152 | tf_op jit(solution)/shard_map/pre/pallas_call | solution.py:87
  3.4 0.1 collective-permute-start.1
  3.5 1.6 %collective-permute-start.3 = (bf16[528,1024]{1,0:T(8,128)(2,1)S(1)}, bf16[528,1024]{1,0:T(8,128)(2,1)S(1)}, u32[]{:S(2)}, u32[]{:S(2)}) collective-permute-start(bf16[528,1024]{1,0:T(8,128)(2,1)S(1)} %pre.1.refs_0_), channel_id=1, source_target_pairs={{0,4},{1,5},{2,6},{3,7},{4,0},{5,1},{6,2},{7,3},{8,12},{9,13},{10,... | collective-permute-start | bytes 3244040 | tf_op jit(solution)/shard_map/ppermute | solution.py:483
  5.1 1.5 %collective-permute-start = (bf16[528,1024]{1,0:T(8,128)(2,1)S(1)}, bf16[528,1024]{1,0:T(8,128)(2,1)S(1)}, u32[]{:S(2)}, u32[]{:S(2)}) collective-permute-start(bf16[528,1024]{1,0:T(8,128)(2,1)S(1)} %pre.1.refs_0_), channel_id=1, source_target_pairs={{0,2},{1,3},{2,0},{3,1},{4,6},{5,7},{6,4},{7,5},{8,10},{9,11},{10,... | collective-permute-start | bytes 3244040 | tf_op jit(solution)/shard_map/ppermute | solution.py:483
  6.6 7.2 %load.1 = (bf16[8192,512]{1,0:T(8,128)(2,1)S(1)}, bf16[8192,128]{1,0:T(8,128)(2,1)S(1)}, bf16[8192,128]{1,0:T(8,128)(2,1)S(1)}, bf16[4096,1024]{1,0:T(8,128)(2,1)S(1)}) custom-call(bf16[8192,512]{1,0:T(8,128)(2,1)} %refs_0_, bf16[8192,128]{1,0:T(8,128)(2,1)} %refs_1_.1, bf16[8192,128]{1,0:T(8,128)(2,1)} %refs_2_.1, bf16[4096,1024]{1,0:T(8,128)(2,1)} %refs_3_.1), custom_call_target="tpu_custom_call" | custom-call | bytes 41943040 | tf_op jit(solution)/shard_map/load/pallas_call | solution.py:121
  13.8 16.0 %collective-permute-done.3.refs_4_ = bf16[528,1024]{1,0:T(8,128)(2,1)S(1)} collective-permute-done((bf16[528,1024]{1,0:T(8,128)(2,1)S(1)}, bf16[528,1024]{1,0:T(8,128)(2,1)S(1)}, u32[]{:S(2)}, u32[]{:S(2)}) %collective-permute-start.3) | collective-permute-done | bytes 1081376 | tf_op jit(solution)/shard_map/ppermute | solution.py:483
  29.8 1.2 %collective-permute-done.refs_2_ = bf16[528,1024]{1,0:T(8,128)(2,1)S(1)} collective-permute-done((bf16[528,1024]{1,0:T(8,128)(2,1)S(1)}, bf16[528,1024]{1,0:T(8,128)(2,1)S(1)}, u32[]{:S(2)}, u32[]{:S(2)}) %collective-permute-start) | collective-permute-done | bytes 1081376 | tf_op jit(solution)/shard_map/ppermute | solution.py:483
  31.0 1.6 %collective-permute-start.4 = (bf16[272,1024]{1,0:T(8,128)(2,1)S(1)}, bf16[272,1024]{1,0:T(8,128)(2,1)S(1)}, u32[]{:S(2)}, u32[]{:S(2)}) collective-permute-start(bf16[272,1024]{1,0:T(8,128)(2,1)S(1)} %slice.19), channel_id=1, source_target_pairs={{0,2},{1,3},{2,0},{3,1},{4,6},{5,7},{6,4},{7,5},{8,10},{9,11},{10,... | collective-permute-start | bytes 1671176 | tf_op jit(solution)/shard_map/ppermute | solution.py:483
  32.6 0.9 collective-permute-start.2
  33.5 0.5 collective-permute-done.5.refs_3_
  34.0 5.6 %proj.2 = (f32[512,512]{1,0:T(8,128)S(1)}, f32[512,128]{1,0:T(8,128)S(1)}, f32[512,128]{1,0:T(8,128)S(1)}, f32[8,512]{1,0:T(8,128)S(1)}) custom-call(s32[8]{0:T(128)S(1)} %get-tuple-element.42.order_ref, bf16[528,1024]{1,0:T(8,128)(2,1)S(1)} %pre.1.refs_0_, bf16[528,1024]{1,0:T(8,128)(2,1)S(1)} %collective-permute-done.1.refs_1_, ...), custom_call_target="tpu_custom_call" | custom-call | flops 4831838208 | bytes 15728640 | tf_op jit(solution)/shard_map/proj/pallas_call | solution.py:220
  39.6 6.5 %collective-permute-done.4.refs_1_ = bf16[272,1024]{1,0:T(8,128)(2,1)S(1)} collective-permute-done((bf16[272,1024]{1,0:T(8,128)(2,1)S(1)}, bf16[272,1024]{1,0:T(8,128)(2,1)S(1)}, u32[]{:S(2)}, u32[]{:S(2)}) %collective-permute-start.4) | collective-permute-done | bytes 557088 | tf_op jit(solution)/shard_map/ppermute | solution.py:483
  46.1 0.6 collective-permute-done.2.refs_0_
  46.8 2.1 %collective-permute-done.7.refs_2_ = bf16[256,1024]{1,0:T(8,128)(2,1)S(1)} collective-permute-done((bf16[256,1024]{1,0:T(8,128)(2,1)S(1)}, bf16[256,1024]{1,0:T(8,128)(2,1)S(1)}, u32[]{:S(2)}, u32[]{:S(2)}) %collective-permute-start.7) | collective-permute-done | bytes 524320 | tf_op jit(solution)/shard_map/ppermute | solution.py:483
  48.9 2.4 %proj.3 = (bf16[512,512]{1,0:T(8,128)(2,1)S(1)}, bf16[256,256]{1,0:T(8,128)(2,1)S(1)}, bf16[256,256]{1,0:T(8,128)(2,1)S(1)}) custom-call(s32[8]{0:T(128)S(1)} %get-tuple-element.42.order_ref, bf16[256,1024]{1,0:T(8,128)(2,1)S(1)} %collective-permute-done.2.refs_0_, bf16[272,1024]{1,0:T(8,128)(2,1)S(1)} %collective-permute-done.4.refs_1_, ...), custom_call_target="tpu_custom_call" | custom-call | flops 1610612736 | bytes 5242880 | tf_op jit(solution)/shard_map/proj/pallas_call | solution.py:220
  51.3 1.3 %collective-permute-start.9 = (bf16[256,256]{1,0:T(8,128)(2,1)S(1)}, bf16[256,256]{1,0:T(8,128)(2,1)S(1)}, u32[]{:S(2)}, u32[]{:S(2)}) collective-permute-start(bf16[256,256]{1,0:T(8,128)(2,1)S(1)} %get-tuple-element.58.refs_0_), channel_id=1, source_target_pairs={{0,8},{8,16},{16,24},{1,9},{9,17},{17,25},{2,10},{10,18},{18,26},{... | collective-permute-start | bytes 393224 | tf_op jit(solution)/shard_map/ppermute | solution.py:488
  52.6 1.3 %collective-permute-start.12 = (bf16[256,256]{1,0:T(8,128)(2,1)S(1)}, bf16[256,256]{1,0:T(8,128)(2,1)S(1)}, u32[]{:S(2)}, u32[]{:S(2)}) collective-permute-start(bf16[256,256]{1,0:T(8,128)(2,1)S(1)} %get-tuple-element.59.refs_1_), channel_id=1, source_target_pairs={{0,8},{8,16},{16,24},{1,9},{9,17},{17,25},{2,10},{10,18},{18,26},{... | collective-permute-start | bytes 393224 | tf_op jit(solution)/shard_map/ppermute | solution.py:488
  53.9 5.6 %collective-permute-done.9.refs_1_.refs_2_ = bf16[256,256]{1,0:T(8,128)(2,1)S(1)} collective-permute-done((bf16[256,256]{1,0:T(8,128)(2,1)S(1)}, bf16[256,256]{1,0:T(8,128)(2,1)S(1)}, u32[]{:S(2)}, u32[]{:S(2)}) %collective-permute-start.9) | collective-permute-done | bytes 131104 | tf_op jit(solution)/shard_map/ppermute | solution.py:488
  59.5 1.3 %collective-permute-start.10 = (bf16[256,256]{1,0:T(8,128)(2,1)S(1)}, bf16[256,256]{1,0:T(8,128)(2,1)S(1)}, u32[]{:S(2)}, u32[]{:S(2)}) collective-permute-start(bf16[256,256]{1,0:T(8,128)(2,1)S(1)} %collective-permute-done.9.refs_1_.refs_2_), channel_id=1, source_target_pairs={{8,16},{16,24},{9,17},{17,25},{10,18},{18,26},{11,19},{19,27},{12,... | collective-permute-start | bytes 393224 | tf_op jit(solution)/shard_map/ppermute | solution.py:488
  60.8 0.7 collective-permute-done.12.refs_2_.refs_3_
  61.5 1.3 %collective-permute-start.13 = (bf16[256,256]{1,0:T(8,128)(2,1)S(1)}, bf16[256,256]{1,0:T(8,128)(2,1)S(1)}, u32[]{:S(2)}, u32[]{:S(2)}) collective-permute-start(bf16[256,256]{1,0:T(8,128)(2,1)S(1)} %collective-permute-done.12.refs_2_.refs_3_), channel_id=1, source_target_pairs={{8,16},{16,24},{9,17},{17,25},{10,18},{18,26},{11,19},{19,27},{12,... | collective-permute-start | bytes 393224 | tf_op jit(solution)/shard_map/ppermute | solution.py:488
  62.8 4.7 %collective-permute-done.10.refs_3_.refs_4_ = bf16[256,256]{1,0:T(8,128)(2,1)S(1)} collective-permute-done((bf16[256,256]{1,0:T(8,128)(2,1)S(1)}, bf16[256,256]{1,0:T(8,128)(2,1)S(1)}, u32[]{:S(2)}, u32[]{:S(2)}) %collective-permute-start.10) | collective-permute-done | bytes 131104 | tf_op jit(solution)/shard_map/ppermute | solution.py:488
  67.5 1.3 %collective-permute-start.11 = (bf16[256,256]{1,0:T(8,128)(2,1)S(1)}, bf16[256,256]{1,0:T(8,128)(2,1)S(1)}, u32[]{:S(2)}, u32[]{:S(2)}) collective-permute-start(bf16[256,256]{1,0:T(8,128)(2,1)S(1)} %collective-permute-done.10.refs_3_.refs_4_), channel_id=1, source_target_pairs={{16,24},{17,25},{18,26},{19,27},{20,28},{21,29},{22,30},{23,31}} | collective-permute-start | bytes 393224 | tf_op jit(solution)/shard_map/ppermute | solution.py:488
  68.8 1.3 %collective-permute-done.13.refs_4_.refs_5_ = bf16[256,256]{1,0:T(8,128)(2,1)S(1)} collective-permute-done((bf16[256,256]{1,0:T(8,128)(2,1)S(1)}, bf16[256,256]{1,0:T(8,128)(2,1)S(1)}, u32[]{:S(2)}, u32[]{:S(2)}) %collective-permute-start.13) | collective-permute-done | bytes 131104 | tf_op jit(solution)/shard_map/ppermute | solution.py:488
  70.1 1.3 %collective-permute-start.14 = (bf16[256,256]{1,0:T(8,128)(2,1)S(1)}, bf16[256,256]{1,0:T(8,128)(2,1)S(1)}, u32[]{:S(2)}, u32[]{:S(2)}) collective-permute-start(bf16[256,256]{1,0:T(8,128)(2,1)S(1)} %collective-permute-done.13.refs_4_.refs_5_), channel_id=1, source_target_pairs={{16,24},{17,25},{18,26},{19,27},{20,28},{21,29},{22,30},{23,31}} | collective-permute-start | bytes 393224 | tf_op jit(solution)/shard_map/ppermute | solution.py:488
  71.4 3.2 %attend.4 = (f32[8,256]{1,0:T(8,128)S(1)}, f32[8,256]{1,0:T(8,128)S(1)}, f32[4,128,256]{2,1,0:T(8,128)S(1)}) custom-call(s32[1]{0:T(128)} %bitcast.1.me_ref, bf16[512,512]{1,0:T(8,128)(2,1)S(1)} %get-tuple-element.57.q_ref, bf16[256,256]{1,0:T(8,128)(2,1)S(1)} %get-tuple-element.58.refs_0_, bf16[256,256]{1,0:T(8,128)(2,1)S(1)} %collective-permute-done.9.refs_1_.refs_2_, ...), custom_call_target="tpu_custom_call" | custom-call | flops 671088640 | bytes 655360 | tf_op jit(solution)/shard_map/attend/pallas_call | solution.py:329
  74.6 0.8 collective-permute-done.11.refs_0_
  75.4 1.5 %collective-permute-done.14.refs_1_ = bf16[256,256]{1,0:T(8,128)(2,1)S(1)} collective-permute-done((bf16[256,256]{1,0:T(8,128)(2,1)S(1)}, bf16[256,256]{1,0:T(8,128)(2,1)S(1)}, u32[]{:S(2)}, u32[]{:S(2)}) %collective-permute-start.14) | collective-permute-done | bytes 131104 | tf_op jit(solution)/shard_map/ppermute | solution.py:488
  76.9 1.5 %attend.5.refs_0_ = bf16[256,512]{1,0:T(8,128)(2,1)S(1)} custom-call(s32[1]{0:T(128)} %bitcast.1.me_ref, bf16[512,512]{1,0:T(8,128)(2,1)S(1)} %get-tuple-element.57.q_ref, bf16[256,256]{1,0:T(8,128)(2,1)S(1)} %collective-permute-done.11.refs_0_, bf16[256,256]{1,0:T(8,128)(2,1)S(1)} %collective-permute-done.14.refs_1_, ...), custom_call_target="tpu_custom_call" | custom-call | flops 268435456 | bytes 262144 | tf_op jit(solution)/shard_map/attend/pallas_call | solution.py:329
  78.4 1.6 %collective-permute-start.16 = (bf16[256,512]{1,0:T(8,128)(2,1)S(1)}, bf16[256,512]{1,0:T(8,128)(2,1)S(1)}, u32[]{:S(2)}, u32[]{:S(2)}) collective-permute-start(bf16[256,512]{1,0:T(8,128)(2,1)S(1)} %attend.5.refs_0_), channel_id=1, source_target_pairs={{0,2},{1,3},{2,0},{3,1},{4,6},{5,7},{6,4},{7,5},{8,10},{9,11},{10,... | collective-permute-start | bytes 786440 | tf_op jit(solution)/shard_map/ppermute | solution.py:483
  80.0 0.5 collective-permute-start.18
  80.5 3.9 %attend.6 = (f32[8,256]{1,0:T(8,128)S(1)}, f32[8,256]{1,0:T(8,128)S(1)}, f32[4,128,256]{2,1,0:T(8,128)S(1)}) custom-call(s32[1]{0:T(128)} %bitcast.1.me_ref, bf16[512,512]{1,0:T(8,128)(2,1)S(1)} %get-tuple-element.57.q_ref, bf16[256,256]{1,0:T(8,128)(2,1)S(1)} %get-tuple-element.58.refs_0_, bf16[256,256]{1,0:T(8,128)(2,1)S(1)} %get-tuple-element.59.refs_1_, ...), custom_call_target="tpu_custom_call" | custom-call | flops 805306368 | bytes 786432 | tf_op jit(solution)/shard_map/attend/pallas_call | solution.py:329
  84.4 1.5 %attend.7.refs_0_ = bf16[256,512]{1,0:T(8,128)(2,1)S(1)} custom-call(s32[1]{0:T(128)} %bitcast.1.me_ref, bf16[512,512]{1,0:T(8,128)(2,1)S(1)} %get-tuple-element.57.q_ref, bf16[256,256]{1,0:T(8,128)(2,1)S(1)} %collective-permute-done.11.refs_0_, bf16[256,256]{1,0:T(8,128)(2,1)S(1)} %collective-permute-done.14.refs_1_, ...), custom_call_target="tpu_custom_call" | custom-call | flops 268435456 | bytes 262144 | tf_op jit(solution)/shard_map/attend/pallas_call | solution.py:329
  86.0 0.4 collective-permute-done.18.refs_4_
  86.4 1.2 collective-permute-start.27
  87.5 0.5 collective-permute-start.25
  88.1 0.9 collective-permute-start.20
  89.0 1.6 %collective-permute-start.21 = (bf16[128,512]{1,0:T(8,128)(2,1)S(1)}, bf16[128,512]{1,0:T(8,128)(2,1)S(1)}, u32[]{:S(2)}, u32[]{:S(2)}) collective-permute-start(bf16[128,512]{1,0:T(8,128)(2,1)S(1)} %slice.25), channel_id=1, source_target_pairs={{0,2},{1,3},{2,0},{3,1},{4,6},{5,7},{6,4},{7,5},{8,10},{9,11},{10,... | collective-permute-start | bytes 393224 | tf_op jit(solution)/shard_map/ppermute | solution.py:483
  90.6 4.4 %collective-permute-done.20.refs_6_ = bf16[128,512]{1,0:T(8,128)(2,1)S(1)} collective-permute-done((bf16[128,512]{1,0:T(8,128)(2,1)S(1)}, bf16[128,512]{1,0:T(8,128)(2,1)S(1)}, u32[]{:S(2)}, u32[]{:S(2)}) %collective-permute-start.20) | collective-permute-done | bytes 131104 | tf_op jit(solution)/shard_map/ppermute | solution.py:483
  95.0 1.0 collective-permute-done.21.refs_7_
  96.0 0.5 collective-permute-start.22
  96.5 0.1 collective-permute-start.23
  96.6 0.5 collective-permute-start.24
  97.1 0.6 collective-permute-done.22.refs_8_
  97.7 0.5 collective-permute-start.30
  98.3 0.7 collective-permute-start.29
  98.9 5.9 %project_out.2 = (f32[256,1024]{1,0:T(8,128)S(1)}, f32[8,256]{1,0:T(8,128)S(1)}) custom-call(f32[8]{0:T(128)S(1)} %get-tuple-element.40.sign_ref, bf16[512,1024]{1,0:T(8,128)(2,1)S(1)} %copy-done, bf16[256,512]{1,0:T(8,128)(2,1)S(1)} %attend.5.refs_0_, bf16[256,512]{1,0:T(8,128)(2,1)S(1)} %collective-permute-done.15.refs_1_, ...), custom_call_target="tpu_custom_call" | custom-call | flops 2147483648 | bytes 12058624 | tf_op jit(solution)/shard_map/project_out/pallas_call | solution.py:424
  104.8 0.0 collective-permute-start.28
  104.9 0.5 collective-permute-start.26
  105.4 0.1 collective-permute-start.32
  105.5 0.4 collective-permute-start.31
  105.9 1.1 collective-permute-done.32.refs_9_
  107.0 0.2 collective-permute-done.31.refs_8_
  107.2 5.9 %project_out.3 = (f32[256,1024]{1,0:T(8,128)S(1)}, f32[8,256]{1,0:T(8,128)S(1)}) custom-call(f32[8]{0:T(128)S(1)} %get-tuple-element.40.sign_ref, bf16[512,1024]{1,0:T(8,128)(2,1)S(1)} %copy-done, bf16[256,512]{1,0:T(8,128)(2,1)S(1)} %attend.7.refs_0_, bf16[256,512]{1,0:T(8,128)(2,1)S(1)} %collective-permute-done.24.refs_1_, ...), custom_call_target="tpu_custom_call" | custom-call | flops 2147483648 | bytes 12058624 | tf_op jit(solution)/shard_map/project_out/pallas_call | solution.py:424
  113.1 0.2 collective-permute-start.33
  113.3 1.0 collective-permute-done.33
  114.3 1.6 %collective-permute-start.34 = (f32[8,512]{1,0:T(8,128)S(1)}, f32[8,512]{1,0:T(8,128)S(1)}, u32[]{:S(2)}, u32[]{:S(2)}) collective-permute-start(f32[8,512]{1,0:T(8,128)S(1)} %add.4.refs_2_), channel_id=1, source_target_pairs={{0,2},{1,3},{2,0},{3,1},{4,6},{5,7},{6,4},{7,5},{8,10},{9,11},{10,... | collective-permute-start | bytes 49160 | tf_op jit(solution)/shard_map/ppermute | solution.py:483
  115.9 1.3 %collective-permute-start.35 = (f32[8,512]{1,0:T(8,128)S(1)}, f32[8,512]{1,0:T(8,128)S(1)}, u32[]{:S(2)}, u32[]{:S(2)}) collective-permute-start(f32[8,512]{1,0:T(8,128)S(1)} %add.4.refs_2_), channel_id=1, source_target_pairs={{0,4},{1,5},{2,6},{3,7},{4,0},{5,1},{6,2},{7,3},{8,12},{9,13},{10,... | collective-permute-start | bytes 49160 | tf_op jit(solution)/shard_map/ppermute | solution.py:483
  117.2 0.6 collective-permute-start.36
  117.8 0.2 collective-permute-done.34.refs_3_
  118.1 1.6 %collective-permute-done.35.refs_4_ = f32[8,512]{1,0:T(8,128)S(1)} collective-permute-done((f32[8,512]{1,0:T(8,128)S(1)}, f32[8,512]{1,0:T(8,128)S(1)}, u32[]{:S(2)}, u32[]{:S(2)}) %collective-permute-start.35) | collective-permute-done | bytes 16416 | tf_op jit(solution)/shard_map/ppermute | solution.py:483
  119.6 2.2 %collective-permute-done.36.refs_5_ = f32[8,512]{1,0:T(8,128)S(1)} collective-permute-done((f32[8,512]{1,0:T(8,128)S(1)}, f32[8,512]{1,0:T(8,128)S(1)}, u32[]{:S(2)}, u32[]{:S(2)}) %collective-permute-start.36) | collective-permute-done | bytes 16416 | tf_op jit(solution)/shard_map/ppermute | solution.py:483
  121.8 1.3 %final.1 = (bf16[512,1024]{1,0:T(8,128)(2,1)}, f32[1,512]{1,0:T(1,128)}) custom-call(f32[256,1024]{1,0:T(8,128)S(1)} %get-tuple-element.64.refs_0_, f32[256,1024]{1,0:T(8,128)S(1)} %get-tuple-element.73.refs_1_, f32[8,512]{1,0:T(8,128)S(1)} %add.4.refs_2_, f32[8,512]{1,0:T(8,128)S(1)} %collective-permute-done.34.refs_3_, ...), custom_call_target="tpu_custom_call" | custom-call | flops 1048576 | bytes 3145728 | tf_op jit(solution)/shard_map/final/pallas_call | solution.py:466
  (34 shorter events, 0.2 us)
Async XLA Ops:
  3.4 3.2 %collective-permute-start.1 = (bf16[528,1024]{1,0:T(8,128)(2,1)S(1)}, bf16[528,1024]{1,0:T(8,128)(2,1)S(1)}, u32[]{:S(2)}, u32[]{:S(2)}) collective-permute-start(bf16[528,1024]{1,0:T(8,128)(2,1)S(1)} %pre.1.refs_0_), channel_id=1, source_target_pairs={{0,1},{1,0},{2,3},{3,2},{4,5},{5,4},{6,7},{7,6},{8,9},{9,8},{10,11... | collective-permute-start | bytes 3244040 | tf_op jit(solution)/shard_map/ppermute | solution.py:483
  3.5 26.3 %collective-permute-start.3 = (bf16[528,1024]{1,0:T(8,128)(2,1)S(1)}, bf16[528,1024]{1,0:T(8,128)(2,1)S(1)}, u32[]{:S(2)}, u32[]{:S(2)}) collective-permute-start(bf16[528,1024]{1,0:T(8,128)(2,1)S(1)} %pre.1.refs_0_), channel_id=1, source_target_pairs={{0,4},{1,5},{2,6},{3,7},{4,0},{5,1},{6,2},{7,3},{8,12},{9,13},{10,... | collective-permute-start | bytes 3244040 | tf_op jit(solution)/shard_map/ppermute | solution.py:483
  5.1 25.9 %collective-permute-start = (bf16[528,1024]{1,0:T(8,128)(2,1)S(1)}, bf16[528,1024]{1,0:T(8,128)(2,1)S(1)}, u32[]{:S(2)}, u32[]{:S(2)}) collective-permute-start(bf16[528,1024]{1,0:T(8,128)(2,1)S(1)} %pre.1.refs_0_), channel_id=1, source_target_pairs={{0,2},{1,3},{2,0},{3,1},{4,6},{5,7},{6,4},{7,5},{8,10},{9,11},{10,... | collective-permute-start | bytes 3244040 | tf_op jit(solution)/shard_map/ppermute | solution.py:483
  29.8 3.7 %collective-permute-start.6 = (bf16[528,1024]{1,0:T(8,128)(2,1)S(1)}, bf16[528,1024]{1,0:T(8,128)(2,1)S(1)}, u32[]{:S(2)}, u32[]{:S(2)}) collective-permute-start(bf16[528,1024]{1,0:T(8,128)(2,1)S(1)} %collective-permute-done.3.refs_4_), channel_id=1, source_target_pairs={{0,1},{1,0},{2,3},{3,2},{4,5},{5,4},{6,7},{7,6},{8,9},{9,8},{10,11... | collective-permute-start | bytes 3244040 | tf_op jit(solution)/shard_map/ppermute | solution.py:483
  31.0 3.0 %collective-permute-start.5 = (bf16[528,1024]{1,0:T(8,128)(2,1)S(1)}, bf16[528,1024]{1,0:T(8,128)(2,1)S(1)}, u32[]{:S(2)}, u32[]{:S(2)}) collective-permute-start(bf16[528,1024]{1,0:T(8,128)(2,1)S(1)} %collective-permute-done.refs_2_), channel_id=1, source_target_pairs={{0,1},{1,0},{2,3},{3,2},{4,5},{5,4},{6,7},{7,6},{8,9},{9,8},{10,11... | collective-permute-start | bytes 3244040 | tf_op jit(solution)/shard_map/ppermute | solution.py:483
  31.0 15.1 %collective-permute-start.4 = (bf16[272,1024]{1,0:T(8,128)(2,1)S(1)}, bf16[272,1024]{1,0:T(8,128)(2,1)S(1)}, u32[]{:S(2)}, u32[]{:S(2)}) collective-permute-start(bf16[272,1024]{1,0:T(8,128)(2,1)S(1)} %slice.19), channel_id=1, source_target_pairs={{0,2},{1,3},{2,0},{3,1},{4,6},{5,7},{6,4},{7,5},{8,10},{9,11},{10,... | collective-permute-start | bytes 1671176 | tf_op jit(solution)/shard_map/ppermute | solution.py:483
  32.6 14.1 %collective-permute-start.2 = (bf16[256,1024]{1,0:T(8,128)(2,1)S(1)}, bf16[256,1024]{1,0:T(8,128)(2,1)S(1)}, u32[]{:S(2)}, u32[]{:S(2)}) collective-permute-start(bf16[256,1024]{1,0:T(8,128)(2,1)S(1)} %slice.18), channel_id=1, source_target_pairs={{0,4},{1,5},{2,6},{3,7},{4,0},{5,1},{6,2},{7,3},{8,12},{9,13},{10,... | collective-permute-start | bytes 1572872 | tf_op jit(solution)/shard_map/ppermute | solution.py:483
  46.1 2.7 %collective-permute-start.8 = (bf16[272,1024]{1,0:T(8,128)(2,1)S(1)}, bf16[272,1024]{1,0:T(8,128)(2,1)S(1)}, u32[]{:S(2)}, u32[]{:S(2)}) collective-permute-start(bf16[272,1024]{1,0:T(8,128)(2,1)S(1)} %collective-permute-done.4.refs_1_), channel_id=1, source_target_pairs={{0,1},{1,0},{2,3},{3,2},{4,5},{5,4},{6,7},{7,6},{8,9},{9,8},{10,11... | collective-permute-start | bytes 1671176 | tf_op jit(solution)/shard_map/ppermute | solution.py:483
  46.8 2.1 %collective-permute-start.7 = (bf16[256,1024]{1,0:T(8,128)(2,1)S(1)}, bf16[256,1024]{1,0:T(8,128)(2,1)S(1)}, u32[]{:S(2)}, u32[]{:S(2)}) collective-permute-start(bf16[256,1024]{1,0:T(8,128)(2,1)S(1)} %collective-permute-done.2.refs_0_), channel_id=1, source_target_pairs={{0,1},{1,0},{2,3},{3,2},{4,5},{5,4},{6,7},{7,6},{8,9},{9,8},{10,11... | collective-permute-start | bytes 1572872 | tf_op jit(solution)/shard_map/ppermute | solution.py:483
  51.3 8.2 %collective-permute-start.9 = (bf16[256,256]{1,0:T(8,128)(2,1)S(1)}, bf16[256,256]{1,0:T(8,128)(2,1)S(1)}, u32[]{:S(2)}, u32[]{:S(2)}) collective-permute-start(bf16[256,256]{1,0:T(8,128)(2,1)S(1)} %get-tuple-element.58.refs_0_), channel_id=1, source_target_pairs={{0,8},{8,16},{16,24},{1,9},{9,17},{17,25},{2,10},{10,18},{18,26},{... | collective-permute-start | bytes 393224 | tf_op jit(solution)/shard_map/ppermute | solution.py:488
  52.6 8.9 %collective-permute-start.12 = (bf16[256,256]{1,0:T(8,128)(2,1)S(1)}, bf16[256,256]{1,0:T(8,128)(2,1)S(1)}, u32[]{:S(2)}, u32[]{:S(2)}) collective-permute-start(bf16[256,256]{1,0:T(8,128)(2,1)S(1)} %get-tuple-element.59.refs_1_), channel_id=1, source_target_pairs={{0,8},{8,16},{16,24},{1,9},{9,17},{17,25},{2,10},{10,18},{18,26},{... | collective-permute-start | bytes 393224 | tf_op jit(solution)/shard_map/ppermute | solution.py:488
  59.5 8.0 %collective-permute-start.10 = (bf16[256,256]{1,0:T(8,128)(2,1)S(1)}, bf16[256,256]{1,0:T(8,128)(2,1)S(1)}, u32[]{:S(2)}, u32[]{:S(2)}) collective-permute-start(bf16[256,256]{1,0:T(8,128)(2,1)S(1)} %collective-permute-done.9.refs_1_.refs_2_), channel_id=1, source_target_pairs={{8,16},{16,24},{9,17},{17,25},{10,18},{18,26},{11,19},{19,27},{12,... | collective-permute-start | bytes 393224 | tf_op jit(solution)/shard_map/ppermute | solution.py:488
  61.5 8.6 %collective-permute-start.13 = (bf16[256,256]{1,0:T(8,128)(2,1)S(1)}, bf16[256,256]{1,0:T(8,128)(2,1)S(1)}, u32[]{:S(2)}, u32[]{:S(2)}) collective-permute-start(bf16[256,256]{1,0:T(8,128)(2,1)S(1)} %collective-permute-done.12.refs_2_.refs_3_), channel_id=1, source_target_pairs={{8,16},{16,24},{9,17},{17,25},{10,18},{18,26},{11,19},{19,27},{12,... | collective-permute-start | bytes 393224 | tf_op jit(solution)/shard_map/ppermute | solution.py:488
  67.5 7.9 %collective-permute-start.11 = (bf16[256,256]{1,0:T(8,128)(2,1)S(1)}, bf16[256,256]{1,0:T(8,128)(2,1)S(1)}, u32[]{:S(2)}, u32[]{:S(2)}) collective-permute-start(bf16[256,256]{1,0:T(8,128)(2,1)S(1)} %collective-permute-done.10.refs_3_.refs_4_), channel_id=1, source_target_pairs={{16,24},{17,25},{18,26},{19,27},{20,28},{21,29},{22,30},{23,31}} | collective-permute-start | bytes 393224 | tf_op jit(solution)/shard_map/ppermute | solution.py:488
  70.1 6.8 %collective-permute-start.14 = (bf16[256,256]{1,0:T(8,128)(2,1)S(1)}, bf16[256,256]{1,0:T(8,128)(2,1)S(1)}, u32[]{:S(2)}, u32[]{:S(2)}) collective-permute-start(bf16[256,256]{1,0:T(8,128)(2,1)S(1)} %collective-permute-done.13.refs_4_.refs_5_), channel_id=1, source_target_pairs={{16,24},{17,25},{18,26},{19,27},{20,28},{21,29},{22,30},{23,31}} | collective-permute-start | bytes 393224 | tf_op jit(solution)/shard_map/ppermute | solution.py:488
  78.4 20.5 %copy-start = (bf16[512,1024]{1,0:T(8,128)(2,1)S(1)}, bf16[512,1024]{1,0:T(8,128)(2,1)}, u32[]{:S(2)}) copy-start(bf16[512,1024]{1,0:T(8,128)(2,1)} %t_ref.3) | copy-start | bytes 3145732
  78.4 7.5 %collective-permute-start.16 = (bf16[256,512]{1,0:T(8,128)(2,1)S(1)}, bf16[256,512]{1,0:T(8,128)(2,1)S(1)}, u32[]{:S(2)}, u32[]{:S(2)}) collective-permute-start(bf16[256,512]{1,0:T(8,128)(2,1)S(1)} %attend.5.refs_0_), channel_id=1, source_target_pairs={{0,2},{1,3},{2,0},{3,1},{4,6},{5,7},{6,4},{7,5},{8,10},{9,11},{10,... | collective-permute-start | bytes 786440 | tf_op jit(solution)/shard_map/ppermute | solution.py:483
  80.0 6.4 %collective-permute-start.18 = (bf16[256,512]{1,0:T(8,128)(2,1)S(1)}, bf16[256,512]{1,0:T(8,128)(2,1)S(1)}, u32[]{:S(2)}, u32[]{:S(2)}) collective-permute-start(bf16[256,512]{1,0:T(8,128)(2,1)S(1)} %attend.5.refs_0_), channel_id=1, source_target_pairs={{0,4},{1,5},{2,6},{3,7},{4,0},{5,1},{6,2},{7,3},{8,12},{9,13},{10,... | collective-permute-start | bytes 786440 | tf_op jit(solution)/shard_map/ppermute | solution.py:483
  86.4 9.6 %collective-permute-start.27 = (bf16[256,512]{1,0:T(8,128)(2,1)S(1)}, bf16[256,512]{1,0:T(8,128)(2,1)S(1)}, u32[]{:S(2)}, u32[]{:S(2)}) collective-permute-start(bf16[256,512]{1,0:T(8,128)(2,1)S(1)} %attend.7.refs_0_), channel_id=1, source_target_pairs={{0,4},{1,5},{2,6},{3,7},{4,0},{5,1},{6,2},{7,3},{8,12},{9,13},{10,... | collective-permute-start | bytes 786440 | tf_op jit(solution)/shard_map/ppermute | solution.py:483
  87.5 9.0 %collective-permute-start.25 = (bf16[256,512]{1,0:T(8,128)(2,1)S(1)}, bf16[256,512]{1,0:T(8,128)(2,1)S(1)}, u32[]{:S(2)}, u32[]{:S(2)}) collective-permute-start(bf16[256,512]{1,0:T(8,128)(2,1)S(1)} %attend.7.refs_0_), channel_id=1, source_target_pairs={{0,2},{1,3},{2,0},{3,1},{4,6},{5,7},{6,4},{7,5},{8,10},{9,11},{10,... | collective-permute-start | bytes 786440 | tf_op jit(solution)/shard_map/ppermute | solution.py:483
  88.1 6.9 %collective-permute-start.20 = (bf16[128,512]{1,0:T(8,128)(2,1)S(1)}, bf16[128,512]{1,0:T(8,128)(2,1)S(1)}, u32[]{:S(2)}, u32[]{:S(2)}) collective-permute-start(bf16[128,512]{1,0:T(8,128)(2,1)S(1)} %slice.24), channel_id=1, source_target_pairs={{0,4},{1,5},{2,6},{3,7},{4,0},{5,1},{6,2},{7,3},{8,12},{9,13},{10,... | collective-permute-start | bytes 393224 | tf_op jit(solution)/shard_map/ppermute | solution.py:483
  89.0 7.0 %collective-permute-start.21 = (bf16[128,512]{1,0:T(8,128)(2,1)S(1)}, bf16[128,512]{1,0:T(8,128)(2,1)S(1)}, u32[]{:S(2)}, u32[]{:S(2)}) collective-permute-start(bf16[128,512]{1,0:T(8,128)(2,1)S(1)} %slice.25), channel_id=1, source_target_pairs={{0,2},{1,3},{2,0},{3,1},{4,6},{5,7},{6,4},{7,5},{8,10},{9,11},{10,... | collective-permute-start | bytes 393224 | tf_op jit(solution)/shard_map/ppermute | solution.py:483
  90.6 6.0 %collective-permute-start.15 = (bf16[256,512]{1,0:T(8,128)(2,1)S(1)}, bf16[256,512]{1,0:T(8,128)(2,1)S(1)}, u32[]{:S(2)}, u32[]{:S(2)}) collective-permute-start(bf16[256,512]{1,0:T(8,128)(2,1)S(1)} %attend.5.refs_0_), channel_id=1, source_target_pairs={{0,1},{1,0},{2,3},{3,2},{4,5},{5,4},{6,7},{7,6},{8,9},{9,8},{10,11... | collective-permute-start | bytes 786440 | tf_op jit(solution)/shard_map/ppermute | solution.py:483
  95.0 3.9 %collective-permute-start.17 = (bf16[256,512]{1,0:T(8,128)(2,1)S(1)}, bf16[256,512]{1,0:T(8,128)(2,1)S(1)}, u32[]{:S(2)}, u32[]{:S(2)}) collective-permute-start(bf16[256,512]{1,0:T(8,128)(2,1)S(1)} %collective-permute-done.16.refs_2_), channel_id=1, source_target_pairs={{0,1},{1,0},{2,3},{3,2},{4,5},{5,4},{6,7},{7,6},{8,9},{9,8},{10,11... | collective-permute-start | bytes 786440 | tf_op jit(solution)/shard_map/ppermute | solution.py:483
  96.0 2.9 %collective-permute-start.19 = (bf16[256,512]{1,0:T(8,128)(2,1)S(1)}, bf16[256,512]{1,0:T(8,128)(2,1)S(1)}, u32[]{:S(2)}, u32[]{:S(2)}) collective-permute-start(bf16[256,512]{1,0:T(8,128)(2,1)S(1)} %collective-permute-done.18.refs_4_), channel_id=1, source_target_pairs={{0,1},{1,0},{2,3},{3,2},{4,5},{5,4},{6,7},{7,6},{8,9},{9,8},{10,11... | collective-permute-start | bytes 786440 | tf_op jit(solution)/shard_map/ppermute | solution.py:483
  96.0 1.7 %collective-permute-start.22 = (bf16[128,512]{1,0:T(8,128)(2,1)S(1)}, bf16[128,512]{1,0:T(8,128)(2,1)S(1)}, u32[]{:S(2)}, u32[]{:S(2)}) collective-permute-start(bf16[128,512]{1,0:T(8,128)(2,1)S(1)} %collective-permute-done.20.refs_6_), channel_id=1, source_target_pairs={{0,1},{1,0},{2,3},{3,2},{4,5},{5,4},{6,7},{7,6},{8,9},{9,8},{10,11... | collective-permute-start | bytes 393224 | tf_op jit(solution)/shard_map/ppermute | solution.py:483
  96.5 1.7 %collective-permute-start.23 = (bf16[128,512]{1,0:T(8,128)(2,1)S(1)}, bf16[128,512]{1,0:T(8,128)(2,1)S(1)}, u32[]{:S(2)}, u32[]{:S(2)}) collective-permute-start(bf16[128,512]{1,0:T(8,128)(2,1)S(1)} %collective-permute-done.21.refs_7_), channel_id=1, source_target_pairs={{0,1},{1,0},{2,3},{3,2},{4,5},{5,4},{6,7},{7,6},{8,9},{9,8},{10,11... | collective-permute-start | bytes 393224 | tf_op jit(solution)/shard_map/ppermute | solution.py:483
  96.6 9.3 %collective-permute-start.24 = (bf16[256,512]{1,0:T(8,128)(2,1)S(1)}, bf16[256,512]{1,0:T(8,128)(2,1)S(1)}, u32[]{:S(2)}, u32[]{:S(2)}) collective-permute-start(bf16[256,512]{1,0:T(8,128)(2,1)S(1)} %attend.7.refs_0_), channel_id=1, source_target_pairs={{0,1},{1,0},{2,3},{3,2},{4,5},{5,4},{6,7},{7,6},{8,9},{9,8},{10,11... | collective-permute-start | bytes 786440 | tf_op jit(solution)/shard_map/ppermute | solution.py:483
  97.7 7.7 %collective-permute-start.30 = (bf16[128,512]{1,0:T(8,128)(2,1)S(1)}, bf16[128,512]{1,0:T(8,128)(2,1)S(1)}, u32[]{:S(2)}, u32[]{:S(2)}) collective-permute-start(bf16[128,512]{1,0:T(8,128)(2,1)S(1)} %slice.27), channel_id=1, source_target_pairs={{0,2},{1,3},{2,0},{3,1},{4,6},{5,7},{6,4},{7,5},{8,10},{9,11},{10,... | collective-permute-start | bytes 393224 | tf_op jit(solution)/shard_map/ppermute | solution.py:483
  98.3 7.2 %collective-permute-start.29 = (bf16[128,512]{1,0:T(8,128)(2,1)S(1)}, bf16[128,512]{1,0:T(8,128)(2,1)S(1)}, u32[]{:S(2)}, u32[]{:S(2)}) collective-permute-start(bf16[128,512]{1,0:T(8,128)(2,1)S(1)} %slice.26), channel_id=1, source_target_pairs={{0,4},{1,5},{2,6},{3,7},{4,0},{5,1},{6,2},{7,3},{8,12},{9,13},{10,... | collective-permute-start | bytes 393224 | tf_op jit(solution)/shard_map/ppermute | solution.py:483
  104.8 2.3 %collective-permute-start.28 = (bf16[256,512]{1,0:T(8,128)(2,1)S(1)}, bf16[256,512]{1,0:T(8,128)(2,1)S(1)}, u32[]{:S(2)}, u32[]{:S(2)}) collective-permute-start(bf16[256,512]{1,0:T(8,128)(2,1)S(1)} %collective-permute-done.27.refs_4_), channel_id=1, source_target_pairs={{0,1},{1,0},{2,3},{3,2},{4,5},{5,4},{6,7},{7,6},{8,9},{9,8},{10,11... | collective-permute-start | bytes 786440 | tf_op jit(solution)/shard_map/ppermute | solution.py:483
  104.9 2.3 %collective-permute-start.26 = (bf16[256,512]{1,0:T(8,128)(2,1)S(1)}, bf16[256,512]{1,0:T(8,128)(2,1)S(1)}, u32[]{:S(2)}, u32[]{:S(2)}) collective-permute-start(bf16[256,512]{1,0:T(8,128)(2,1)S(1)} %collective-permute-done.25.refs_2_), channel_id=1, source_target_pairs={{0,1},{1,0},{2,3},{3,2},{4,5},{5,4},{6,7},{7,6},{8,9},{9,8},{10,11... | collective-permute-start | bytes 786440 | tf_op jit(solution)/shard_map/ppermute | solution.py:483
  105.4 1.6 %collective-permute-start.32 = (bf16[128,512]{1,0:T(8,128)(2,1)S(1)}, bf16[128,512]{1,0:T(8,128)(2,1)S(1)}, u32[]{:S(2)}, u32[]{:S(2)}) collective-permute-start(bf16[128,512]{1,0:T(8,128)(2,1)S(1)} %collective-permute-done.30.refs_7_), channel_id=1, source_target_pairs={{0,1},{1,0},{2,3},{3,2},{4,5},{5,4},{6,7},{7,6},{8,9},{9,8},{10,11... | collective-permute-start | bytes 393224 | tf_op jit(solution)/shard_map/ppermute | solution.py:483
  105.5 1.7 %collective-permute-start.31 = (bf16[128,512]{1,0:T(8,128)(2,1)S(1)}, bf16[128,512]{1,0:T(8,128)(2,1)S(1)}, u32[]{:S(2)}, u32[]{:S(2)}) collective-permute-start(bf16[128,512]{1,0:T(8,128)(2,1)S(1)} %collective-permute-done.29.refs_6_), channel_id=1, source_target_pairs={{0,1},{1,0},{2,3},{3,2},{4,5},{5,4},{6,7},{7,6},{8,9},{9,8},{10,11... | collective-permute-start | bytes 393224 | tf_op jit(solution)/shard_map/ppermute | solution.py:483
  113.1 1.2 collective-permute-start.33
  114.3 3.7 %collective-permute-start.34 = (f32[8,512]{1,0:T(8,128)S(1)}, f32[8,512]{1,0:T(8,128)S(1)}, u32[]{:S(2)}, u32[]{:S(2)}) collective-permute-start(f32[8,512]{1,0:T(8,128)S(1)} %add.4.refs_2_), channel_id=1, source_target_pairs={{0,2},{1,3},{2,0},{3,1},{4,6},{5,7},{6,4},{7,5},{8,10},{9,11},{10,... | collective-permute-start | bytes 49160 | tf_op jit(solution)/shard_map/ppermute | solution.py:483
  115.9 3.7 %collective-permute-start.35 = (f32[8,512]{1,0:T(8,128)S(1)}, f32[8,512]{1,0:T(8,128)S(1)}, u32[]{:S(2)}, u32[]{:S(2)}) collective-permute-start(f32[8,512]{1,0:T(8,128)S(1)} %add.4.refs_2_), channel_id=1, source_target_pairs={{0,4},{1,5},{2,6},{3,7},{4,0},{5,1},{6,2},{7,3},{8,12},{9,13},{10,... | collective-permute-start | bytes 49160 | tf_op jit(solution)/shard_map/ppermute | solution.py:483
  117.2 4.6 %collective-permute-start.36 = (f32[8,512]{1,0:T(8,128)S(1)}, f32[8,512]{1,0:T(8,128)S(1)}, u32[]{:S(2)}, u32[]{:S(2)}) collective-permute-start(f32[8,512]{1,0:T(8,128)S(1)} %add.4.refs_2_), channel_id=1, source_target_pairs={{0,6},{1,7},{2,4},{3,5},{4,2},{5,3},{6,0},{7,1},{8,14},{9,15},{10,... | collective-permute-start | bytes 49160 | tf_op jit(solution)/shard_map/ppermute | solution.py:483

commit v7 on v6

--- a/solution.py
+++ b/solution.py
@@ -508,7 +508,6 @@
         diagonal = [swap(via_a[:half], b), swap(via_b[half:], a)]
         if core_after is not None:
             diagonal = [after(p, core_after) for p in diagonal]
-            via_a, via_b = after(via_a, core_after), after(via_b, core_after)
         got[a | 1], got[b | 1] = [swap(via_a, 1)], [swap(via_b, 1)]
         got[a | b] = diagonal
         if middle is not None:
@@ -595,13 +594,12 @@
         attend(ctx_at, q, at * half, half, kv_heads, kvs[: at + 1], far[:-HALVES], None, None)
         for at in range(HALVES)
     ]
+    q = after(q, *[state[0] for state in states])
     branches, stats = [], []
     for at in range(HALVES):
         signed = attend(
             ctx_at, q, at * half, half, kv_heads, [], far[-HALVES:], states[at], signs
         )
-        if at:
-            signed = after(signed, *[b[0] for b in blocks[2:6:2]])
         blocks = gather(signed, branches[-1] if at else None)
         b, s = project_out(flips, blocks, loaded[3], teacher, at)
         branches.append(b)

time: 123 us -> 123 us (level)
    ppermute x31, waiting for transfers between devices: 39.7 us -> 42.3 us  [swap(): return lax.ppermute(x, 'tp', [(i, i ^ mask) for i in range(count)])]
    ppermute x6, waiting for transfers between devices: 14.7 us -> 12.3 us  [send_up(): return lax.ppermute(x, 'ctx', [(i, i + 1) for i in range(first, count - 1)])]
  transfers between devices with their start and end apart: 37 -> 37, of which waited for: 22 -> 21; matrix products, arithmetic and copies ran while one was open for 0% -> 0% of each run, Pallas kernels for 22% -> 22%
where the time goes in v7:
time: 123 us; the launch traced here: 122 us
  waiting for transfers between devices  54.6 us (44%)
  Pallas kernels  40.4 us (33%)
  starting transfers between devices  25.7 us (21%)
    ppermute x31, waiting for transfers between devices, swap(): return lax.ppermute(x, 'tp', [(i, i ^ mask) for i in range(count)])  42.3 us
    ppermute x31, starting transfers between devices, swap(): return lax.ppermute(x, 'tp', [(i, i ^ mask) for i in range(count)])  18 us
    ppermute x6, waiting for transfers between devices, send_up(): return lax.ppermute(x, 'ctx', [(i, i + 1) for i in range(first, count - 1)])  12.3 us
    pallas_call x2, Pallas kernels, project_out(): pl.pallas_call(functools.partial(out_kernel, counts, steps, chunk), in_sp...  11.8 us
    pallas_call x4, Pallas kernels, attend(): pl.pallas_call(kernel, in_specs=[IN_SMEM] + [IN_VMEM] * (len(args) - 1),...  10.1 us
    pallas_call x2, Pallas kernels, proj(): pl.pallas_call(functools.partial(proj_kernel, counts, masks, not state, e...  8 us
    ppermute x6, starting transfers between devices, send_up(): return lax.ppermute(x, 'ctx', [(i, i + 1) for i in range(first, count - 1)])  7.71 us
    pallas_call x1, Pallas kernels, load(): pl.pallas_call(functools.partial(load_kernel, count), in_specs=[IN_HBM] *...  7.19 us
  transfers between devices with their start and end apart: 37, of which 21 were waited for; matrix products, arithmetic and copies ran while one was open for 0% of the time, Pallas kernels for 22%

profile of v7, /device:TPU:24, one launch (start us, length us, event | category | flops | bytes accessed | tf_op | source)
XLA Modules:
  0.0 122.5 jit_solution(12181939284047653377)
XLA Ops:
  0.7 0.7 add_convert_fusion.refs_5_
  1.3 2.1 %pre.1.refs_0_ = bf16[528,1024]{1,0:T(8,128)(2,1)S(1)} custom-call(bf16[512,1024]{1,0:T(8,128)(2,1)} %h_hbm.1, bf16[8,128]{1,0:T(8,128)(2,1)} %bitcast.3), custom_call_target="tpu_custom_call" | custom-call | flops 4194304 | bytes 2097152 | tf_op jit(solution)/shard_map/pre/pallas_call | solution.py:87
  3.4 0.1 collective-permute-start.1
  3.5 1.6 %collective-permute-start.3 = (bf16[528,1024]{1,0:T(8,128)(2,1)S(1)}, bf16[528,1024]{1,0:T(8,128)(2,1)S(1)}, u32[]{:S(2)}, u32[]{:S(2)}) collective-permute-start(bf16[528,1024]{1,0:T(8,128)(2,1)S(1)} %pre.1.refs_0_), channel_id=1, source_target_pairs={{0,4},{1,5},{2,6},{3,7},{4,0},{5,1},{6,2},{7,3},{8,12},{9,13},{10,... | collective-permute-start | bytes 3244040 | tf_op jit(solution)/shard_map/ppermute | solution.py:483
  5.1 1.5 %collective-permute-start = (bf16[528,1024]{1,0:T(8,128)(2,1)S(1)}, bf16[528,1024]{1,0:T(8,128)(2,1)S(1)}, u32[]{:S(2)}, u32[]{:S(2)}) collective-permute-start(bf16[528,1024]{1,0:T(8,128)(2,1)S(1)} %pre.1.refs_0_), channel_id=1, source_target_pairs={{0,2},{1,3},{2,0},{3,1},{4,6},{5,7},{6,4},{7,5},{8,10},{9,11},{10,... | collective-permute-start | bytes 3244040 | tf_op jit(solution)/shard_map/ppermute | solution.py:483
  6.6 0.0 collective-permute-done.1.refs_1_
  6.6 7.2 %load.1 = (bf16[8192,512]{1,0:T(8,128)(2,1)S(1)}, bf16[8192,128]{1,0:T(8,128)(2,1)S(1)}, bf16[8192,128]{1,0:T(8,128)(2,1)S(1)}, bf16[4096,1024]{1,0:T(8,128)(2,1)S(1)}) custom-call(bf16[8192,512]{1,0:T(8,128)(2,1)} %refs_0_, bf16[8192,128]{1,0:T(8,128)(2,1)} %refs_1_.1, bf16[8192,128]{1,0:T(8,128)(2,1)} %refs_2_.1, bf16[4096,1024]{1,0:T(8,128)(2,1)} %refs_3_.1), custom_call_target="tpu_custom_call" | custom-call | bytes 41943040 | tf_op jit(solution)/shard_map/load/pallas_call | solution.py:121
  13.8 16.0 %collective-permute-done.3.refs_4_ = bf16[528,1024]{1,0:T(8,128)(2,1)S(1)} collective-permute-done((bf16[528,1024]{1,0:T(8,128)(2,1)S(1)}, bf16[528,1024]{1,0:T(8,128)(2,1)S(1)}, u32[]{:S(2)}, u32[]{:S(2)}) %collective-permute-start.3) | collective-permute-done | bytes 1081376 | tf_op jit(solution)/shard_map/ppermute | solution.py:483
  29.8 1.2 %collective-permute-done.refs_2_ = bf16[528,1024]{1,0:T(8,128)(2,1)S(1)} collective-permute-done((bf16[528,1024]{1,0:T(8,128)(2,1)S(1)}, bf16[528,1024]{1,0:T(8,128)(2,1)S(1)}, u32[]{:S(2)}, u32[]{:S(2)}) %collective-permute-start) | collective-permute-done | bytes 1081376 | tf_op jit(solution)/shard_map/ppermute | solution.py:483
  31.0 1.6 %collective-permute-start.4 = (bf16[272,1024]{1,0:T(8,128)(2,1)S(1)}, bf16[272,1024]{1,0:T(8,128)(2,1)S(1)}, u32[]{:S(2)}, u32[]{:S(2)}) collective-permute-start(bf16[272,1024]{1,0:T(8,128)(2,1)S(1)} %slice.19), channel_id=1, source_target_pairs={{0,2},{1,3},{2,0},{3,1},{4,6},{5,7},{6,4},{7,5},{8,10},{9,11},{10,... | collective-permute-start | bytes 1671176 | tf_op jit(solution)/shard_map/ppermute | solution.py:483
  32.6 0.9 collective-permute-start.2
  33.5 0.5 collective-permute-done.5.refs_3_
  34.0 5.6 %proj.2 = (f32[512,512]{1,0:T(8,128)S(1)}, f32[512,128]{1,0:T(8,128)S(1)}, f32[512,128]{1,0:T(8,128)S(1)}, f32[8,512]{1,0:T(8,128)S(1)}) custom-call(s32[8]{0:T(128)S(1)} %get-tuple-element.40.order_ref, bf16[528,1024]{1,0:T(8,128)(2,1)S(1)} %pre.1.refs_0_, bf16[528,1024]{1,0:T(8,128)(2,1)S(1)} %collective-permute-done.1.refs_1_, ...), custom_call_target="tpu_custom_call" | custom-call | flops 4831838208 | bytes 15728640 | tf_op jit(solution)/shard_map/proj/pallas_call | solution.py:220
  39.6 6.5 %collective-permute-done.4.refs_1_ = bf16[272,1024]{1,0:T(8,128)(2,1)S(1)} collective-permute-done((bf16[272,1024]{1,0:T(8,128)(2,1)S(1)}, bf16[272,1024]{1,0:T(8,128)(2,1)S(1)}, u32[]{:S(2)}, u32[]{:S(2)}) %collective-permute-start.4) | collective-permute-done | bytes 557088 | tf_op jit(solution)/shard_map/ppermute | solution.py:483
  46.1 0.6 collective-permute-done.2.refs_0_
  46.8 2.1 %collective-permute-done.7.refs_2_ = bf16[256,1024]{1,0:T(8,128)(2,1)S(1)} collective-permute-done((bf16[256,1024]{1,0:T(8,128)(2,1)S(1)}, bf16[256,1024]{1,0:T(8,128)(2,1)S(1)}, u32[]{:S(2)}, u32[]{:S(2)}) %collective-permute-start.7) | collective-permute-done | bytes 524320 | tf_op jit(solution)/shard_map/ppermute | solution.py:483
  48.9 2.4 %proj.3 = (bf16[512,512]{1,0:T(8,128)(2,1)S(1)}, bf16[256,256]{1,0:T(8,128)(2,1)S(1)}, bf16[256,256]{1,0:T(8,128)(2,1)S(1)}) custom-call(s32[8]{0:T(128)S(1)} %get-tuple-element.40.order_ref, bf16[256,1024]{1,0:T(8,128)(2,1)S(1)} %collective-permute-done.2.refs_0_, bf16[272,1024]{1,0:T(8,128)(2,1)S(1)} %collective-permute-done.4.refs_1_, ...), custom_call_target="tpu_custom_call" | custom-call | flops 1610612736 | bytes 5242880 | tf_op jit(solution)/shard_map/proj/pallas_call | solution.py:220
  51.3 1.3 %collective-permute-start.9 = (bf16[256,256]{1,0:T(8,128)(2,1)S(1)}, bf16[256,256]{1,0:T(8,128)(2,1)S(1)}, u32[]{:S(2)}, u32[]{:S(2)}) collective-permute-start(bf16[256,256]{1,0:T(8,128)(2,1)S(1)} %get-tuple-element.56.refs_0_), channel_id=1, source_target_pairs={{0,8},{8,16},{16,24},{1,9},{9,17},{17,25},{2,10},{10,18},{18,26},{... | collective-permute-start | bytes 393224 | tf_op jit(solution)/shard_map/ppermute | solution.py:488
  52.6 1.3 %collective-permute-start.10 = (bf16[256,256]{1,0:T(8,128)(2,1)S(1)}, bf16[256,256]{1,0:T(8,128)(2,1)S(1)}, u32[]{:S(2)}, u32[]{:S(2)}) collective-permute-start(bf16[256,256]{1,0:T(8,128)(2,1)S(1)} %get-tuple-element.57.refs_1_), channel_id=1, source_target_pairs={{0,8},{8,16},{16,24},{1,9},{9,17},{17,25},{2,10},{10,18},{18,26},{... | collective-permute-start | bytes 393224 | tf_op jit(solution)/shard_map/ppermute | solution.py:488
  53.9 5.6 %collective-permute-done.9.refs_1_.refs_2_ = bf16[256,256]{1,0:T(8,128)(2,1)S(1)} collective-permute-done((bf16[256,256]{1,0:T(8,128)(2,1)S(1)}, bf16[256,256]{1,0:T(8,128)(2,1)S(1)}, u32[]{:S(2)}, u32[]{:S(2)}) %collective-permute-start.9) | collective-permute-done | bytes 131104 | tf_op jit(solution)/shard_map/ppermute | solution.py:488
  59.5 1.3 %collective-permute-start.11 = (bf16[256,256]{1,0:T(8,128)(2,1)S(1)}, bf16[256,256]{1,0:T(8,128)(2,1)S(1)}, u32[]{:S(2)}, u32[]{:S(2)}) collective-permute-start(bf16[256,256]{1,0:T(8,128)(2,1)S(1)} %collective-permute-done.9.refs_1_.refs_2_), channel_id=1, source_target_pairs={{8,16},{16,24},{9,17},{17,25},{10,18},{18,26},{11,19},{19,27},{12,... | collective-permute-start | bytes 393224 | tf_op jit(solution)/shard_map/ppermute | solution.py:488
  60.8 0.7 collective-permute-done.10.refs_2_.refs_3_
  61.5 1.3 %collective-permute-start.12 = (bf16[256,256]{1,0:T(8,128)(2,1)S(1)}, bf16[256,256]{1,0:T(8,128)(2,1)S(1)}, u32[]{:S(2)}, u32[]{:S(2)}) collective-permute-start(bf16[256,256]{1,0:T(8,128)(2,1)S(1)} %collective-permute-done.10.refs_2_.refs_3_), channel_id=1, source_target_pairs={{8,16},{16,24},{9,17},{17,25},{10,18},{18,26},{11,19},{19,27},{12,... | collective-permute-start | bytes 393224 | tf_op jit(solution)/shard_map/ppermute | solution.py:488
  62.8 4.7 %collective-permute-done.11.refs_3_.refs_4_ = bf16[256,256]{1,0:T(8,128)(2,1)S(1)} collective-permute-done((bf16[256,256]{1,0:T(8,128)(2,1)S(1)}, bf16[256,256]{1,0:T(8,128)(2,1)S(1)}, u32[]{:S(2)}, u32[]{:S(2)}) %collective-permute-start.11) | collective-permute-done | bytes 131104 | tf_op jit(solution)/shard_map/ppermute | solution.py:488
  67.5 1.3 %collective-permute-start.13 = (bf16[256,256]{1,0:T(8,128)(2,1)S(1)}, bf16[256,256]{1,0:T(8,128)(2,1)S(1)}, u32[]{:S(2)}, u32[]{:S(2)}) collective-permute-start(bf16[256,256]{1,0:T(8,128)(2,1)S(1)} %collective-permute-done.11.refs_3_.refs_4_), channel_id=1, source_target_pairs={{16,24},{17,25},{18,26},{19,27},{20,28},{21,29},{22,30},{23,31}} | collective-permute-start | bytes 393224 | tf_op jit(solution)/shard_map/ppermute | solution.py:488
  68.8 1.3 %collective-permute-done.12.refs_4_.refs_5_ = bf16[256,256]{1,0:T(8,128)(2,1)S(1)} collective-permute-done((bf16[256,256]{1,0:T(8,128)(2,1)S(1)}, bf16[256,256]{1,0:T(8,128)(2,1)S(1)}, u32[]{:S(2)}, u32[]{:S(2)}) %collective-permute-start.12) | collective-permute-done | bytes 131104 | tf_op jit(solution)/shard_map/ppermute | solution.py:488
  70.1 1.3 %collective-permute-start.14 = (bf16[256,256]{1,0:T(8,128)(2,1)S(1)}, bf16[256,256]{1,0:T(8,128)(2,1)S(1)}, u32[]{:S(2)}, u32[]{:S(2)}) collective-permute-start(bf16[256,256]{1,0:T(8,128)(2,1)S(1)} %collective-permute-done.12.refs_4_.refs_5_), channel_id=1, source_target_pairs={{16,24},{17,25},{18,26},{19,27},{20,28},{21,29},{22,30},{23,31}} | collective-permute-start | bytes 393224 | tf_op jit(solution)/shard_map/ppermute | solution.py:488
  71.4 3.2 %attend.4 = (f32[8,256]{1,0:T(8,128)S(1)}, f32[8,256]{1,0:T(8,128)S(1)}, f32[4,128,256]{2,1,0:T(8,128)S(1)}) custom-call(s32[1]{0:T(128)} %bitcast.1.me_ref, bf16[512,512]{1,0:T(8,128)(2,1)S(1)} %get-tuple-element.60.q_ref, bf16[256,256]{1,0:T(8,128)(2,1)S(1)} %get-tuple-element.56.refs_0_, bf16[256,256]{1,0:T(8,128)(2,1)S(1)} %collective-permute-done.9.refs_1_.refs_2_, ...), custom_call_target="tpu_custom_call" | custom-call | flops 671088640 | bytes 655360 | tf_op jit(solution)/shard_map/attend/pallas_call | solution.py:329
  74.6 3.9 %attend.5 = (f32[8,256]{1,0:T(8,128)S(1)}, f32[8,256]{1,0:T(8,128)S(1)}, f32[4,128,256]{2,1,0:T(8,128)S(1)}) custom-call(s32[1]{0:T(128)} %bitcast.1.me_ref, bf16[512,512]{1,0:T(8,128)(2,1)S(1)} %get-tuple-element.60.q_ref, bf16[256,256]{1,0:T(8,128)(2,1)S(1)} %get-tuple-element.56.refs_0_, bf16[256,256]{1,0:T(8,128)(2,1)S(1)} %get-tuple-element.57.refs_1_, ...), custom_call_target="tpu_custom_call" | custom-call | flops 805306368 | bytes 786432 | tf_op jit(solution)/shard_map/attend/pallas_call | solution.py:329
  78.5 0.0 copy-start
  78.5 1.5 %attend.6.refs_0_ = bf16[256,512]{1,0:T(8,128)(2,1)S(1)} custom-call(s32[1]{0:T(128)} %bitcast.1.me_ref, bf16[512,512]{1,0:T(8,128)(2,1)S(1)} %get-tuple-element.60.q_ref, bf16[256,256]{1,0:T(8,128)(2,1)S(1)} %collective-permute-done.13.refs_0_, bf16[256,256]{1,0:T(8,128)(2,1)S(1)} %collective-permute-done.14.refs_1_, ...), custom_call_target="tpu_custom_call" | custom-call | flops 268435456 | bytes 262144 | tf_op jit(solution)/shard_map/attend/pallas_call | solution.py:329
  80.0 1.6 %collective-permute-start.16 = (bf16[256,512]{1,0:T(8,128)(2,1)S(1)}, bf16[256,512]{1,0:T(8,128)(2,1)S(1)}, u32[]{:S(2)}, u32[]{:S(2)}) collective-permute-start(bf16[256,512]{1,0:T(8,128)(2,1)S(1)} %attend.6.refs_0_), channel_id=1, source_target_pairs={{0,2},{1,3},{2,0},{3,1},{4,6},{5,7},{6,4},{7,5},{8,10},{9,11},{10,... | collective-permute-start | bytes 786440 | tf_op jit(solution)/shard_map/ppermute | solution.py:483
  81.6 0.5 collective-permute-start.18
  82.1 1.5 %attend.7.refs_0_ = bf16[256,512]{1,0:T(8,128)(2,1)S(1)} custom-call(s32[1]{0:T(128)} %bitcast.1.me_ref, bf16[512,512]{1,0:T(8,128)(2,1)S(1)} %get-tuple-element.60.q_ref, bf16[256,256]{1,0:T(8,128)(2,1)S(1)} %collective-permute-done.13.refs_0_, bf16[256,256]{1,0:T(8,128)(2,1)S(1)} %collective-permute-done.14.refs_1_, ...), custom_call_target="tpu_custom_call" | custom-call | flops 268435456 | bytes 262144 | tf_op jit(solution)/shard_map/attend/pallas_call | solution.py:329
  83.6 1.6 %collective-permute-start.27 = (bf16[256,512]{1,0:T(8,128)(2,1)S(1)}, bf16[256,512]{1,0:T(8,128)(2,1)S(1)}, u32[]{:S(2)}, u32[]{:S(2)}) collective-permute-start(bf16[256,512]{1,0:T(8,128)(2,1)S(1)} %attend.7.refs_0_), channel_id=1, source_target_pairs={{0,4},{1,5},{2,6},{3,7},{4,0},{5,1},{6,2},{7,3},{8,12},{9,13},{10,... | collective-permute-start | bytes 786440 | tf_op jit(solution)/shard_map/ppermute | solution.py:483
  85.2 0.5 collective-permute-start.25
  85.7 2.3 %collective-permute-done.16.refs_2_ = bf16[256,512]{1,0:T(8,128)(2,1)S(1)} collective-permute-done((bf16[256,512]{1,0:T(8,128)(2,1)S(1)}, bf16[256,512]{1,0:T(8,128)(2,1)S(1)}, u32[]{:S(2)}, u32[]{:S(2)}) %collective-permute-start.16) | collective-permute-done | bytes 262176 | tf_op jit(solution)/shard_map/ppermute | solution.py:483
  88.0 0.6 collective-permute-start.20
  88.6 2.2 %collective-permute-done.18.refs_4_ = bf16[256,512]{1,0:T(8,128)(2,1)S(1)} collective-permute-done((bf16[256,512]{1,0:T(8,128)(2,1)S(1)}, bf16[256,512]{1,0:T(8,128)(2,1)S(1)}, u32[]{:S(2)}, u32[]{:S(2)}) %collective-permute-start.18) | collective-permute-done | bytes 262176 | tf_op jit(solution)/shard_map/ppermute | solution.py:483
  90.8 0.6 collective-permute-start.21
  91.4 3.2 %collective-permute-done.27.refs_4_ = bf16[256,512]{1,0:T(8,128)(2,1)S(1)} collective-permute-done((bf16[256,512]{1,0:T(8,128)(2,1)S(1)}, bf16[256,512]{1,0:T(8,128)(2,1)S(1)}, u32[]{:S(2)}, u32[]{:S(2)}) %collective-permute-start.27) | collective-permute-done | bytes 262176 | tf_op jit(solution)/shard_map/ppermute | solution.py:483
  94.6 0.5 collective-permute-start.19
  95.1 0.9 collective-permute-done.20.refs_6_
  96.0 0.5 collective-permute-start.23
  96.6 0.1 collective-permute-start.24
  96.6 0.7 collective-permute-done.22.refs_8_
  97.3 0.5 collective-permute-start.30
  97.9 0.5 collective-permute-start.29
  98.4 0.5 collective-permute-start.28
  98.9 5.9 %project_out.2 = (f32[256,1024]{1,0:T(8,128)S(1)}, f32[8,256]{1,0:T(8,128)S(1)}) custom-call(f32[8]{0:T(128)S(1)} %get-tuple-element.38.sign_ref, bf16[512,1024]{1,0:T(8,128)(2,1)S(1)} %copy-done, bf16[256,512]{1,0:T(8,128)(2,1)S(1)} %attend.6.refs_0_, bf16[256,512]{1,0:T(8,128)(2,1)S(1)} %collective-permute-done.15.refs_1_, ...), custom_call_target="tpu_custom_call" | custom-call | flops 2147483648 | bytes 12058624 | tf_op jit(solution)/shard_map/project_out/pallas_call | solution.py:424
  104.8 0.1 collective-permute-start.32
  105.0 0.4 collective-permute-start.31
  105.4 0.8 collective-permute-done.32.refs_9_
  106.2 0.2 collective-permute-done.31.refs_8_
  106.4 5.9 %project_out.3 = (f32[256,1024]{1,0:T(8,128)S(1)}, f32[8,256]{1,0:T(8,128)S(1)}) custom-call(f32[8]{0:T(128)S(1)} %get-tuple-element.38.sign_ref, bf16[512,1024]{1,0:T(8,128)(2,1)S(1)} %copy-done, bf16[256,512]{1,0:T(8,128)(2,1)S(1)} %attend.7.refs_0_, bf16[256,512]{1,0:T(8,128)(2,1)S(1)} %collective-permute-done.24.refs_1_, ...), custom_call_target="tpu_custom_call" | custom-call | flops 2147483648 | bytes 12058624 | tf_op jit(solution)/shard_map/project_out/pallas_call | solution.py:424
  112.3 0.4 collective-permute-start.33
  112.7 0.9 collective-permute-done.33
  113.6 1.6 %collective-permute-start.34 = (f32[8,512]{1,0:T(8,128)S(1)}, f32[8,512]{1,0:T(8,128)S(1)}, u32[]{:S(2)}, u32[]{:S(2)}) collective-permute-start(f32[8,512]{1,0:T(8,128)S(1)} %add.4.refs_2_), channel_id=1, source_target_pairs={{0,2},{1,3},{2,0},{3,1},{4,6},{5,7},{6,4},{7,5},{8,10},{9,11},{10,... | collective-permute-start | bytes 49160 | tf_op jit(solution)/shard_map/ppermute | solution.py:483
  115.1 1.4 %collective-permute-start.35 = (f32[8,512]{1,0:T(8,128)S(1)}, f32[8,512]{1,0:T(8,128)S(1)}, u32[]{:S(2)}, u32[]{:S(2)}) collective-permute-start(f32[8,512]{1,0:T(8,128)S(1)} %add.4.refs_2_), channel_id=1, source_target_pairs={{0,4},{1,5},{2,6},{3,7},{4,0},{5,1},{6,2},{7,3},{8,12},{9,13},{10,... | collective-permute-start | bytes 49160 | tf_op jit(solution)/shard_map/ppermute | solution.py:483
  116.6 0.5 collective-permute-start.36
  117.1 0.2 collective-permute-done.34.refs_3_
  117.3 1.6 %collective-permute-done.35.refs_4_ = f32[8,512]{1,0:T(8,128)S(1)} collective-permute-done((f32[8,512]{1,0:T(8,128)S(1)}, f32[8,512]{1,0:T(8,128)S(1)}, u32[]{:S(2)}, u32[]{:S(2)}) %collective-permute-start.35) | collective-permute-done | bytes 16416 | tf_op jit(solution)/shard_map/ppermute | solution.py:483
  118.9 2.3 %collective-permute-done.36.refs_5_ = f32[8,512]{1,0:T(8,128)S(1)} collective-permute-done((f32[8,512]{1,0:T(8,128)S(1)}, f32[8,512]{1,0:T(8,128)S(1)}, u32[]{:S(2)}, u32[]{:S(2)}) %collective-permute-start.36) | collective-permute-done | bytes 16416 | tf_op jit(solution)/shard_map/ppermute | solution.py:483
  121.2 1.3 %final.1 = (bf16[512,1024]{1,0:T(8,128)(2,1)}, f32[1,512]{1,0:T(1,128)}) custom-call(f32[256,1024]{1,0:T(8,128)S(1)} %get-tuple-element.64.refs_0_, f32[256,1024]{1,0:T(8,128)S(1)} %get-tuple-element.69.refs_1_, f32[8,512]{1,0:T(8,128)S(1)} %add.4.refs_2_, f32[8,512]{1,0:T(8,128)S(1)} %collective-permute-done.34.refs_3_, ...), custom_call_target="tpu_custom_call" | custom-call | flops 1048576 | bytes 3145728 | tf_op jit(solution)/shard_map/final/pallas_call | solution.py:466
  (34 shorter events, 0.2 us)
Async XLA Ops:
  3.4 3.2 %collective-permute-start.1 = (bf16[528,1024]{1,0:T(8,128)(2,1)S(1)}, bf16[528,1024]{1,0:T(8,128)(2,1)S(1)}, u32[]{:S(2)}, u32[]{:S(2)}) collective-permute-start(bf16[528,1024]{1,0:T(8,128)(2,1)S(1)} %pre.1.refs_0_), channel_id=1, source_target_pairs={{0,1},{1,0},{2,3},{3,2},{4,5},{5,4},{6,7},{7,6},{8,9},{9,8},{10,11... | collective-permute-start | bytes 3244040 | tf_op jit(solution)/shard_map/ppermute | solution.py:483
  3.5 26.3 %collective-permute-start.3 = (bf16[528,1024]{1,0:T(8,128)(2,1)S(1)}, bf16[528,1024]{1,0:T(8,128)(2,1)S(1)}, u32[]{:S(2)}, u32[]{:S(2)}) collective-permute-start(bf16[528,1024]{1,0:T(8,128)(2,1)S(1)} %pre.1.refs_0_), channel_id=1, source_target_pairs={{0,4},{1,5},{2,6},{3,7},{4,0},{5,1},{6,2},{7,3},{8,12},{9,13},{10,... | collective-permute-start | bytes 3244040 | tf_op jit(solution)/shard_map/ppermute | solution.py:483
  5.1 25.9 %collective-permute-start = (bf16[528,1024]{1,0:T(8,128)(2,1)S(1)}, bf16[528,1024]{1,0:T(8,128)(2,1)S(1)}, u32[]{:S(2)}, u32[]{:S(2)}) collective-permute-start(bf16[528,1024]{1,0:T(8,128)(2,1)S(1)} %pre.1.refs_0_), channel_id=1, source_target_pairs={{0,2},{1,3},{2,0},{3,1},{4,6},{5,7},{6,4},{7,5},{8,10},{9,11},{10,... | collective-permute-start | bytes 3244040 | tf_op jit(solution)/shard_map/ppermute | solution.py:483
  29.8 3.7 %collective-permute-start.6 = (bf16[528,1024]{1,0:T(8,128)(2,1)S(1)}, bf16[528,1024]{1,0:T(8,128)(2,1)S(1)}, u32[]{:S(2)}, u32[]{:S(2)}) collective-permute-start(bf16[528,1024]{1,0:T(8,128)(2,1)S(1)} %collective-permute-done.3.refs_4_), channel_id=1, source_target_pairs={{0,1},{1,0},{2,3},{3,2},{4,5},{5,4},{6,7},{7,6},{8,9},{9,8},{10,11... | collective-permute-start | bytes 3244040 | tf_op jit(solution)/shard_map/ppermute | solution.py:483
  31.0 3.0 %collective-permute-start.5 = (bf16[528,1024]{1,0:T(8,128)(2,1)S(1)}, bf16[528,1024]{1,0:T(8,128)(2,1)S(1)}, u32[]{:S(2)}, u32[]{:S(2)}) collective-permute-start(bf16[528,1024]{1,0:T(8,128)(2,1)S(1)} %collective-permute-done.refs_2_), channel_id=1, source_target_pairs={{0,1},{1,0},{2,3},{3,2},{4,5},{5,4},{6,7},{7,6},{8,9},{9,8},{10,11... | collective-permute-start | bytes 3244040 | tf_op jit(solution)/shard_map/ppermute | solution.py:483
  31.0 15.1 %collective-permute-start.4 = (bf16[272,1024]{1,0:T(8,128)(2,1)S(1)}, bf16[272,1024]{1,0:T(8,128)(2,1)S(1)}, u32[]{:S(2)}, u32[]{:S(2)}) collective-permute-start(bf16[272,1024]{1,0:T(8,128)(2,1)S(1)} %slice.19), channel_id=1, source_target_pairs={{0,2},{1,3},{2,0},{3,1},{4,6},{5,7},{6,4},{7,5},{8,10},{9,11},{10,... | collective-permute-start | bytes 1671176 | tf_op jit(solution)/shard_map/ppermute | solution.py:483
  32.6 14.1 %collective-permute-start.2 = (bf16[256,1024]{1,0:T(8,128)(2,1)S(1)}, bf16[256,1024]{1,0:T(8,128)(2,1)S(1)}, u32[]{:S(2)}, u32[]{:S(2)}) collective-permute-start(bf16[256,1024]{1,0:T(8,128)(2,1)S(1)} %slice.18), channel_id=1, source_target_pairs={{0,4},{1,5},{2,6},{3,7},{4,0},{5,1},{6,2},{7,3},{8,12},{9,13},{10,... | collective-permute-start | bytes 1572872 | tf_op jit(solution)/shard_map/ppermute | solution.py:483
  46.1 2.7 %collective-permute-start.8 = (bf16[272,1024]{1,0:T(8,128)(2,1)S(1)}, bf16[272,1024]{1,0:T(8,128)(2,1)S(1)}, u32[]{:S(2)}, u32[]{:S(2)}) collective-permute-start(bf16[272,1024]{1,0:T(8,128)(2,1)S(1)} %collective-permute-done.4.refs_1_), channel_id=1, source_target_pairs={{0,1},{1,0},{2,3},{3,2},{4,5},{5,4},{6,7},{7,6},{8,9},{9,8},{10,11... | collective-permute-start | bytes 1671176 | tf_op jit(solution)/shard_map/ppermute | solution.py:483
  46.8 2.1 %collective-permute-start.7 = (bf16[256,1024]{1,0:T(8,128)(2,1)S(1)}, bf16[256,1024]{1,0:T(8,128)(2,1)S(1)}, u32[]{:S(2)}, u32[]{:S(2)}) collective-permute-start(bf16[256,1024]{1,0:T(8,128)(2,1)S(1)} %collective-permute-done.2.refs_0_), channel_id=1, source_target_pairs={{0,1},{1,0},{2,3},{3,2},{4,5},{5,4},{6,7},{7,6},{8,9},{9,8},{10,11... | collective-permute-start | bytes 1572872 | tf_op jit(solution)/shard_map/ppermute | solution.py:483
  51.3 8.2 %collective-permute-start.9 = (bf16[256,256]{1,0:T(8,128)(2,1)S(1)}, bf16[256,256]{1,0:T(8,128)(2,1)S(1)}, u32[]{:S(2)}, u32[]{:S(2)}) collective-permute-start(bf16[256,256]{1,0:T(8,128)(2,1)S(1)} %get-tuple-element.56.refs_0_), channel_id=1, source_target_pairs={{0,8},{8,16},{16,24},{1,9},{9,17},{17,25},{2,10},{10,18},{18,26},{... | collective-permute-start | bytes 393224 | tf_op jit(solution)/shard_map/ppermute | solution.py:488
  52.6 8.9 %collective-permute-start.10 = (bf16[256,256]{1,0:T(8,128)(2,1)S(1)}, bf16[256,256]{1,0:T(8,128)(2,1)S(1)}, u32[]{:S(2)}, u32[]{:S(2)}) collective-permute-start(bf16[256,256]{1,0:T(8,128)(2,1)S(1)} %get-tuple-element.57.refs_1_), channel_id=1, source_target_pairs={{0,8},{8,16},{16,24},{1,9},{9,17},{17,25},{2,10},{10,18},{18,26},{... | collective-permute-start | bytes 393224 | tf_op jit(solution)/shard_map/ppermute | solution.py:488
  59.5 8.0 %collective-permute-start.11 = (bf16[256,256]{1,0:T(8,128)(2,1)S(1)}, bf16[256,256]{1,0:T(8,128)(2,1)S(1)}, u32[]{:S(2)}, u32[]{:S(2)}) collective-permute-start(bf16[256,256]{1,0:T(8,128)(2,1)S(1)} %collective-permute-done.9.refs_1_.refs_2_), channel_id=1, source_target_pairs={{8,16},{16,24},{9,17},{17,25},{10,18},{18,26},{11,19},{19,27},{12,... | collective-permute-start | bytes 393224 | tf_op jit(solution)/shard_map/ppermute | solution.py:488
  61.5 8.6 %collective-permute-start.12 = (bf16[256,256]{1,0:T(8,128)(2,1)S(1)}, bf16[256,256]{1,0:T(8,128)(2,1)S(1)}, u32[]{:S(2)}, u32[]{:S(2)}) collective-permute-start(bf16[256,256]{1,0:T(8,128)(2,1)S(1)} %collective-permute-done.10.refs_2_.refs_3_), channel_id=1, source_target_pairs={{8,16},{16,24},{9,17},{17,25},{10,18},{18,26},{11,19},{19,27},{12,... | collective-permute-start | bytes 393224 | tf_op jit(solution)/shard_map/ppermute | solution.py:488
  67.5 11.0 %collective-permute-start.13 = (bf16[256,256]{1,0:T(8,128)(2,1)S(1)}, bf16[256,256]{1,0:T(8,128)(2,1)S(1)}, u32[]{:S(2)}, u32[]{:S(2)}) collective-permute-start(bf16[256,256]{1,0:T(8,128)(2,1)S(1)} %collective-permute-done.11.refs_3_.refs_4_), channel_id=1, source_target_pairs={{16,24},{17,25},{18,26},{19,27},{20,28},{21,29},{22,30},{23,31}} | collective-permute-start | bytes 393224 | tf_op jit(solution)/shard_map/ppermute | solution.py:488
  70.1 8.4 %collective-permute-start.14 = (bf16[256,256]{1,0:T(8,128)(2,1)S(1)}, bf16[256,256]{1,0:T(8,128)(2,1)S(1)}, u32[]{:S(2)}, u32[]{:S(2)}) collective-permute-start(bf16[256,256]{1,0:T(8,128)(2,1)S(1)} %collective-permute-done.12.refs_4_.refs_5_), channel_id=1, source_target_pairs={{16,24},{17,25},{18,26},{19,27},{20,28},{21,29},{22,30},{23,31}} | collective-permute-start | bytes 393224 | tf_op jit(solution)/shard_map/ppermute | solution.py:488
  78.5 20.4 %copy-start = (bf16[512,1024]{1,0:T(8,128)(2,1)S(1)}, bf16[512,1024]{1,0:T(8,128)(2,1)}, u32[]{:S(2)}) copy-start(bf16[512,1024]{1,0:T(8,128)(2,1)} %t_ref.3) | copy-start | bytes 3145732
  80.0 7.9 %collective-permute-start.16 = (bf16[256,512]{1,0:T(8,128)(2,1)S(1)}, bf16[256,512]{1,0:T(8,128)(2,1)S(1)}, u32[]{:S(2)}, u32[]{:S(2)}) collective-permute-start(bf16[256,512]{1,0:T(8,128)(2,1)S(1)} %attend.6.refs_0_), channel_id=1, source_target_pairs={{0,2},{1,3},{2,0},{3,1},{4,6},{5,7},{6,4},{7,5},{8,10},{9,11},{10,... | collective-permute-start | bytes 786440 | tf_op jit(solution)/shard_map/ppermute | solution.py:483
  81.6 9.2 %collective-permute-start.18 = (bf16[256,512]{1,0:T(8,128)(2,1)S(1)}, bf16[256,512]{1,0:T(8,128)(2,1)S(1)}, u32[]{:S(2)}, u32[]{:S(2)}) collective-permute-start(bf16[256,512]{1,0:T(8,128)(2,1)S(1)} %attend.6.refs_0_), channel_id=1, source_target_pairs={{0,4},{1,5},{2,6},{3,7},{4,0},{5,1},{6,2},{7,3},{8,12},{9,13},{10,... | collective-permute-start | bytes 786440 | tf_op jit(solution)/shard_map/ppermute | solution.py:483
  83.6 11.0 %collective-permute-start.27 = (bf16[256,512]{1,0:T(8,128)(2,1)S(1)}, bf16[256,512]{1,0:T(8,128)(2,1)S(1)}, u32[]{:S(2)}, u32[]{:S(2)}) collective-permute-start(bf16[256,512]{1,0:T(8,128)(2,1)S(1)} %attend.7.refs_0_), channel_id=1, source_target_pairs={{0,4},{1,5},{2,6},{3,7},{4,0},{5,1},{6,2},{7,3},{8,12},{9,13},{10,... | collective-permute-start | bytes 786440 | tf_op jit(solution)/shard_map/ppermute | solution.py:483
  85.2 9.4 %collective-permute-start.25 = (bf16[256,512]{1,0:T(8,128)(2,1)S(1)}, bf16[256,512]{1,0:T(8,128)(2,1)S(1)}, u32[]{:S(2)}, u32[]{:S(2)}) collective-permute-start(bf16[256,512]{1,0:T(8,128)(2,1)S(1)} %attend.7.refs_0_), channel_id=1, source_target_pairs={{0,2},{1,3},{2,0},{3,1},{4,6},{5,7},{6,4},{7,5},{8,10},{9,11},{10,... | collective-permute-start | bytes 786440 | tf_op jit(solution)/shard_map/ppermute | solution.py:483
  85.7 10.8 %collective-permute-start.15 = (bf16[256,512]{1,0:T(8,128)(2,1)S(1)}, bf16[256,512]{1,0:T(8,128)(2,1)S(1)}, u32[]{:S(2)}, u32[]{:S(2)}) collective-permute-start(bf16[256,512]{1,0:T(8,128)(2,1)S(1)} %attend.6.refs_0_), channel_id=1, source_target_pairs={{0,1},{1,0},{2,3},{3,2},{4,5},{5,4},{6,7},{7,6},{8,9},{9,8},{10,11... | collective-permute-start | bytes 786440 | tf_op jit(solution)/shard_map/ppermute | solution.py:483
  88.0 8.0 %collective-permute-start.20 = (bf16[128,512]{1,0:T(8,128)(2,1)S(1)}, bf16[128,512]{1,0:T(8,128)(2,1)S(1)}, u32[]{:S(2)}, u32[]{:S(2)}) collective-permute-start(bf16[128,512]{1,0:T(8,128)(2,1)S(1)} %slice.24), channel_id=1, source_target_pairs={{0,4},{1,5},{2,6},{3,7},{4,0},{5,1},{6,2},{7,3},{8,12},{9,13},{10,... | collective-permute-start | bytes 393224 | tf_op jit(solution)/shard_map/ppermute | solution.py:483
  90.8 5.2 %collective-permute-start.21 = (bf16[128,512]{1,0:T(8,128)(2,1)S(1)}, bf16[128,512]{1,0:T(8,128)(2,1)S(1)}, u32[]{:S(2)}, u32[]{:S(2)}) collective-permute-start(bf16[128,512]{1,0:T(8,128)(2,1)S(1)} %slice.25), channel_id=1, source_target_pairs={{0,2},{1,3},{2,0},{3,1},{4,6},{5,7},{6,4},{7,5},{8,10},{9,11},{10,... | collective-permute-start | bytes 393224 | tf_op jit(solution)/shard_map/ppermute | solution.py:483
  94.6 3.8 %collective-permute-start.17 = (bf16[256,512]{1,0:T(8,128)(2,1)S(1)}, bf16[256,512]{1,0:T(8,128)(2,1)S(1)}, u32[]{:S(2)}, u32[]{:S(2)}) collective-permute-start(bf16[256,512]{1,0:T(8,128)(2,1)S(1)} %collective-permute-done.16.refs_2_), channel_id=1, source_target_pairs={{0,1},{1,0},{2,3},{3,2},{4,5},{5,4},{6,7},{7,6},{8,9},{9,8},{10,11... | collective-permute-start | bytes 786440 | tf_op jit(solution)/shard_map/ppermute | solution.py:483
  94.6 3.8 %collective-permute-start.19 = (bf16[256,512]{1,0:T(8,128)(2,1)S(1)}, bf16[256,512]{1,0:T(8,128)(2,1)S(1)}, u32[]{:S(2)}, u32[]{:S(2)}) collective-permute-start(bf16[256,512]{1,0:T(8,128)(2,1)S(1)} %collective-permute-done.18.refs_4_), channel_id=1, source_target_pairs={{0,1},{1,0},{2,3},{3,2},{4,5},{5,4},{6,7},{7,6},{8,9},{9,8},{10,11... | collective-permute-start | bytes 786440 | tf_op jit(solution)/shard_map/ppermute | solution.py:483
  96.0 1.3 %collective-permute-start.22 = (bf16[128,512]{1,0:T(8,128)(2,1)S(1)}, bf16[128,512]{1,0:T(8,128)(2,1)S(1)}, u32[]{:S(2)}, u32[]{:S(2)}) collective-permute-start(bf16[128,512]{1,0:T(8,128)(2,1)S(1)} %collective-permute-done.20.refs_6_), channel_id=1, source_target_pairs={{0,1},{1,0},{2,3},{3,2},{4,5},{5,4},{6,7},{7,6},{8,9},{9,8},{10,11... | collective-permute-start | bytes 393224 | tf_op jit(solution)/shard_map/ppermute | solution.py:483
  96.0 1.9 %collective-permute-start.23 = (bf16[128,512]{1,0:T(8,128)(2,1)S(1)}, bf16[128,512]{1,0:T(8,128)(2,1)S(1)}, u32[]{:S(2)}, u32[]{:S(2)}) collective-permute-start(bf16[128,512]{1,0:T(8,128)(2,1)S(1)} %collective-permute-done.21.refs_7_), channel_id=1, source_target_pairs={{0,1},{1,0},{2,3},{3,2},{4,5},{5,4},{6,7},{7,6},{8,9},{9,8},{10,11... | collective-permute-start | bytes 393224 | tf_op jit(solution)/shard_map/ppermute | solution.py:483
  96.6 8.8 %collective-permute-start.24 = (bf16[256,512]{1,0:T(8,128)(2,1)S(1)}, bf16[256,512]{1,0:T(8,128)(2,1)S(1)}, u32[]{:S(2)}, u32[]{:S(2)}) collective-permute-start(bf16[256,512]{1,0:T(8,128)(2,1)S(1)} %attend.7.refs_0_), channel_id=1, source_target_pairs={{0,1},{1,0},{2,3},{3,2},{4,5},{5,4},{6,7},{7,6},{8,9},{9,8},{10,11... | collective-permute-start | bytes 786440 | tf_op jit(solution)/shard_map/ppermute | solution.py:483
  97.3 7.5 %collective-permute-start.30 = (bf16[128,512]{1,0:T(8,128)(2,1)S(1)}, bf16[128,512]{1,0:T(8,128)(2,1)S(1)}, u32[]{:S(2)}, u32[]{:S(2)}) collective-permute-start(bf16[128,512]{1,0:T(8,128)(2,1)S(1)} %slice.27), channel_id=1, source_target_pairs={{0,2},{1,3},{2,0},{3,1},{4,6},{5,7},{6,4},{7,5},{8,10},{9,11},{10,... | collective-permute-start | bytes 393224 | tf_op jit(solution)/shard_map/ppermute | solution.py:483
  97.9 7.1 %collective-permute-start.29 = (bf16[128,512]{1,0:T(8,128)(2,1)S(1)}, bf16[128,512]{1,0:T(8,128)(2,1)S(1)}, u32[]{:S(2)}, u32[]{:S(2)}) collective-permute-start(bf16[128,512]{1,0:T(8,128)(2,1)S(1)} %slice.26), channel_id=1, source_target_pairs={{0,4},{1,5},{2,6},{3,7},{4,0},{5,1},{6,2},{7,3},{8,12},{9,13},{10,... | collective-permute-start | bytes 393224 | tf_op jit(solution)/shard_map/ppermute | solution.py:483
  98.4 7.0 %collective-permute-start.26 = (bf16[256,512]{1,0:T(8,128)(2,1)S(1)}, bf16[256,512]{1,0:T(8,128)(2,1)S(1)}, u32[]{:S(2)}, u32[]{:S(2)}) collective-permute-start(bf16[256,512]{1,0:T(8,128)(2,1)S(1)} %collective-permute-done.25.refs_2_), channel_id=1, source_target_pairs={{0,1},{1,0},{2,3},{3,2},{4,5},{5,4},{6,7},{7,6},{8,9},{9,8},{10,11... | collective-permute-start | bytes 786440 | tf_op jit(solution)/shard_map/ppermute | solution.py:483
  98.4 7.0 %collective-permute-start.28 = (bf16[256,512]{1,0:T(8,128)(2,1)S(1)}, bf16[256,512]{1,0:T(8,128)(2,1)S(1)}, u32[]{:S(2)}, u32[]{:S(2)}) collective-permute-start(bf16[256,512]{1,0:T(8,128)(2,1)S(1)} %collective-permute-done.27.refs_4_), channel_id=1, source_target_pairs={{0,1},{1,0},{2,3},{3,2},{4,5},{5,4},{6,7},{7,6},{8,9},{9,8},{10,11... | collective-permute-start | bytes 786440 | tf_op jit(solution)/shard_map/ppermute | solution.py:483
  104.8 1.4 %collective-permute-start.32 = (bf16[128,512]{1,0:T(8,128)(2,1)S(1)}, bf16[128,512]{1,0:T(8,128)(2,1)S(1)}, u32[]{:S(2)}, u32[]{:S(2)}) collective-permute-start(bf16[128,512]{1,0:T(8,128)(2,1)S(1)} %collective-permute-done.30.refs_7_), channel_id=1, source_target_pairs={{0,1},{1,0},{2,3},{3,2},{4,5},{5,4},{6,7},{7,6},{8,9},{9,8},{10,11... | collective-permute-start | bytes 393224 | tf_op jit(solution)/shard_map/ppermute | solution.py:483
  105.0 1.5 %collective-permute-start.31 = (bf16[128,512]{1,0:T(8,128)(2,1)S(1)}, bf16[128,512]{1,0:T(8,128)(2,1)S(1)}, u32[]{:S(2)}, u32[]{:S(2)}) collective-permute-start(bf16[128,512]{1,0:T(8,128)(2,1)S(1)} %collective-permute-done.29.refs_6_), channel_id=1, source_target_pairs={{0,1},{1,0},{2,3},{3,2},{4,5},{5,4},{6,7},{7,6},{8,9},{9,8},{10,11... | collective-permute-start | bytes 393224 | tf_op jit(solution)/shard_map/ppermute | solution.py:483
  112.3 1.2 %collective-permute-start.33 = (f32[8,512]{1,0:T(8,128)S(1)}, f32[8,512]{1,0:T(8,128)S(1)}, u32[]{:S(2)}, u32[]{:S(2)}) collective-permute-start(f32[8,512]{1,0:T(8,128)S(1)} %constant_dynamic-update-slice_fusion), channel_id=1, source_target_pairs={{0,1},{1,0},{2,3},{3,2},{4,5},{5,4},{6,7},{7,6},{8,9},{9,8},{10,11... | collective-permute-start | bytes 49160 | tf_op jit(solution)/shard_map/ppermute | solution.py:483
  113.6 3.7 %collective-permute-start.34 = (f32[8,512]{1,0:T(8,128)S(1)}, f32[8,512]{1,0:T(8,128)S(1)}, u32[]{:S(2)}, u32[]{:S(2)}) collective-permute-start(f32[8,512]{1,0:T(8,128)S(1)} %add.4.refs_2_), channel_id=1, source_target_pairs={{0,2},{1,3},{2,0},{3,1},{4,6},{5,7},{6,4},{7,5},{8,10},{9,11},{10,... | collective-permute-start | bytes 49160 | tf_op jit(solution)/shard_map/ppermute | solution.py:483
  115.1 3.7 %collective-permute-start.35 = (f32[8,512]{1,0:T(8,128)S(1)}, f32[8,512]{1,0:T(8,128)S(1)}, u32[]{:S(2)}, u32[]{:S(2)}) collective-permute-start(f32[8,512]{1,0:T(8,128)S(1)} %add.4.refs_2_), channel_id=1, source_target_pairs={{0,4},{1,5},{2,6},{3,7},{4,0},{5,1},{6,2},{7,3},{8,12},{9,13},{10,... | collective-permute-start | bytes 49160 | tf_op jit(solution)/shard_map/ppermute | solution.py:483
  116.6 4.6 %collective-permute-start.36 = (f32[8,512]{1,0:T(8,128)S(1)}, f32[8,512]{1,0:T(8,128)S(1)}, u32[]{:S(2)}, u32[]{:S(2)}) collective-permute-start(f32[8,512]{1,0:T(8,128)S(1)} %add.4.refs_2_), channel_id=1, source_target_pairs={{0,6},{1,7},{2,4},{3,5},{4,2},{5,3},{6,0},{7,1},{8,14},{9,15},{10,... | collective-permute-start | bytes 49160 | tf_op jit(solution)/shard_map/ppermute | solution.py:483

commit v8 on v7

--- a/solution.py
+++ b/solution.py
@@ -541,9 +541,6 @@
     signs = (2 * sign_bits - 1).astype(jnp.float32)
     gain = norm_gain.reshape(-1, GROUP)
 
-    gain, order, ctx_at, flips, signs = lax.optimization_barrier(
-        (gain, order, ctx_at, flips, signs)
-    )
     clipped = pre(hidden_in, gain)
 
     kv_cols = w_key.shape[1]
@@ -585,15 +582,24 @@
                 )
             kv = jnp.concatenate([k, v], axis=1)
         kvs[i] = kv
-    far, sent = [], kvs
+    far, sent, states = [], kvs, []
     for hop in range(1, ctx_count):
+        if hop == 3:
+            sent = [after(kv, *[state[0] for state in states]) for kv in sent]
         sent = [send_up(kv, hop - 1) for kv in sent]
         far += [(hop, kv) for kv in sent]
-
-    states = [
-        attend(ctx_at, q, at * half, half, kv_heads, kvs[: at + 1], far[:-HALVES], None, None)
-        for at in range(HALVES)
-    ]
+        begun = far if ctx_count > 2 else []
+        if hop == 1:
+            states = [
+                attend(ctx_at, q, at * half, half, kv_heads, kvs[: at + 1], begun, None, None)
+                for at in range(HALVES)
+            ]
+    middle = far[HALVES:-HALVES]
+    if middle:
+        states = [
+            attend(ctx_at, q, at * half, half, kv_heads, [], middle, states[at], None)
+            for at in range(HALVES)
+        ]
     q = after(q, *[state[0] for state in states])
     branches, stats = [], []
     for at in range(HALVES):

time: 123 us -> 121 us (0.984)
  waiting for transfers between devices: 54.6 us -> 49.9 us
  starting transfers between devices: 25.7 us -> 27 us
    ppermute x31, waiting for transfers between devices: 42.3 us -> 39.2 us  [swap(): return lax.ppermute(x, 'tp', [(i, i ^ mask) for i in range(count)])]
    ppermute x6, waiting for transfers between devices: 12.3 us -> 10.7 us  [send_up(): return lax.ppermute(x, 'ctx', [(i, i + 1) for i in range(first, count - 1)])]
    pallas_call x4 -> x6, Pallas kernels: 10.1 us -> 10.2 us  [attend(): pl.pallas_call(kernel, in_specs=[IN_SMEM] + [IN_VMEM] * (len(args) - 1),...]
  transfers between devices with their start and end apart: 37 -> 37, of which waited for: 21 -> 22; matrix products, arithmetic and copies ran while one was open for 0% -> 1% of each run, Pallas kernels for 22% -> 24%
where the time goes in v8:
time: 121 us; the launch traced here: 120 us
  waiting for transfers between devices  49.9 us (41%)
  Pallas kernels  41.5 us (34%)
  starting transfers between devices  27 us (22%)
    ppermute x31, waiting for transfers between devices, swap(): return lax.ppermute(x, 'tp', [(i, i ^ mask) for i in range(count)])  39.2 us
    ppermute x31, starting transfers between devices, swap(): return lax.ppermute(x, 'tp', [(i, i ^ mask) for i in range(count)])  19.3 us
    pallas_call x2, Pallas kernels, project_out(): pl.pallas_call(functools.partial(out_kernel, counts, steps, chunk), in_sp...  11.8 us
    ppermute x6, waiting for transfers between devices, send_up(): return lax.ppermute(x, 'ctx', [(i, i + 1) for i in range(first, count - 1)])  10.7 us
    pallas_call x6, Pallas kernels, attend(): pl.pallas_call(kernel, in_specs=[IN_SMEM] + [IN_VMEM] * (len(args) - 1),...  10.2 us
    pallas_call x2, Pallas kernels, proj(): pl.pallas_call(functools.partial(proj_kernel, counts, masks, not state, e...  9.03 us
    ppermute x6, starting transfers between devices, send_up(): return lax.ppermute(x, 'ctx', [(i, i + 1) for i in range(first, count - 1)])  7.71 us
    pallas_call x1, Pallas kernels, load(): pl.pallas_call(functools.partial(load_kernel, count), in_specs=[IN_HBM] *...  7.19 us
  transfers between devices with their start and end apart: 37, of which 22 were waited for; matrix products, arithmetic and copies ran while one was open for 1% of the time, Pallas kernels for 24%

profile of v8, /device:TPU:24, one launch (start us, length us, event | category | flops | bytes accessed | tf_op | source)
XLA Modules:
  0.0 120.5 jit_solution(7473586845118316373)
XLA Ops:
  0.6 2.1 %pre.1.refs_0_ = bf16[528,1024]{1,0:T(8,128)(2,1)S(1)} custom-call(bf16[512,1024]{1,0:T(8,128)(2,1)} %h_hbm.1, bf16[8,128]{1,0:T(8,128)(2,1)} %bitcast.3), custom_call_target="tpu_custom_call" | custom-call | flops 4194304 | bytes 2097152 | tf_op jit(solution)/shard_map/pre/pallas_call | solution.py:87
  2.7 0.1 collective-permute-start.1
  2.8 1.6 %collective-permute-start.3 = (bf16[528,1024]{1,0:T(8,128)(2,1)S(1)}, bf16[528,1024]{1,0:T(8,128)(2,1)S(1)}, u32[]{:S(2)}, u32[]{:S(2)}) collective-permute-start(bf16[528,1024]{1,0:T(8,128)(2,1)S(1)} %pre.1.refs_0_), channel_id=1, source_target_pairs={{0,4},{1,5},{2,6},{3,7},{4,0},{5,1},{6,2},{7,3},{8,12},{9,13},{10,... | collective-permute-start | bytes 3244040 | tf_op jit(solution)/shard_map/ppermute | solution.py:483
  4.4 1.5 %collective-permute-start = (bf16[528,1024]{1,0:T(8,128)(2,1)S(1)}, bf16[528,1024]{1,0:T(8,128)(2,1)}, u32[]{:S(2)}, u32[]{:S(2)}) collective-permute-start(bf16[528,1024]{1,0:T(8,128)(2,1)S(1)} %pre.1.refs_0_), channel_id=1, source_target_pairs={{0,2},{1,3},{2,0},{3,1},{4,6},{5,7},{6,4},{7,5},{8,10},{9,11},{10,... | collective-permute-start | bytes 3244040 | tf_op jit(solution)/shard_map/ppermute | solution.py:483
  5.9 7.2 %load.1 = (bf16[8192,512]{1,0:T(8,128)(2,1)S(1)}, bf16[8192,128]{1,0:T(8,128)(2,1)S(1)}, bf16[8192,128]{1,0:T(8,128)(2,1)S(1)}, bf16[4096,1024]{1,0:T(8,128)(2,1)S(1)}) custom-call(bf16[8192,512]{1,0:T(8,128)(2,1)} %refs_0_, bf16[8192,128]{1,0:T(8,128)(2,1)} %refs_1_.1, bf16[8192,128]{1,0:T(8,128)(2,1)} %refs_2_.1, bf16[4096,1024]{1,0:T(8,128)(2,1)} %refs_3_.1), custom_call_target="tpu_custom_call" | custom-call | bytes 41943040 | tf_op jit(solution)/shard_map/load/pallas_call | solution.py:121
  13.1 16.0 %collective-permute-done.3.refs_4_ = bf16[528,1024]{1,0:T(8,128)(2,1)S(1)} collective-permute-done((bf16[528,1024]{1,0:T(8,128)(2,1)S(1)}, bf16[528,1024]{1,0:T(8,128)(2,1)S(1)}, u32[]{:S(2)}, u32[]{:S(2)}) %collective-permute-start.3) | collective-permute-done | bytes 1081376 | tf_op jit(solution)/shard_map/ppermute | solution.py:483
  29.1 1.3 %collective-permute-done.refs_2_ = bf16[528,1024]{1,0:T(8,128)(2,1)} collective-permute-done((bf16[528,1024]{1,0:T(8,128)(2,1)S(1)}, bf16[528,1024]{1,0:T(8,128)(2,1)}, u32[]{:S(2)}, u32[]{:S(2)}) %collective-permute-start) | collective-permute-done | bytes 1081376 | tf_op jit(solution)/shard_map/ppermute | solution.py:483
  30.5 1.6 %collective-permute-start.4 = (bf16[272,1024]{1,0:T(8,128)(2,1)S(1)}, bf16[272,1024]{1,0:T(8,128)(2,1)S(1)}, u32[]{:S(2)}, u32[]{:S(2)}) collective-permute-start(bf16[272,1024]{1,0:T(8,128)(2,1)S(1)} %slice.19), channel_id=1, source_target_pairs={{0,2},{1,3},{2,0},{3,1},{4,6},{5,7},{6,4},{7,5},{8,10},{9,11},{10,... | collective-permute-start | bytes 1671176 | tf_op jit(solution)/shard_map/ppermute | solution.py:483
  32.0 1.1 slice.18
  33.1 0.8 collective-permute-start.2
  33.8 6.6 %proj.2 = (f32[512,512]{1,0:T(8,128)S(1)}, f32[512,128]{1,0:T(8,128)S(1)}, f32[512,128]{1,0:T(8,128)S(1)}, f32[8,512]{1,0:T(8,128)S(1)}) custom-call(s32[8]{0:T(128)S(1)} %get-tuple-element.80.order_ref, bf16[528,1024]{1,0:T(8,128)(2,1)S(1)} %pre.1.refs_0_, bf16[528,1024]{1,0:T(8,128)(2,1)} %collective-permute-done.1.refs_1_, ...), custom_call_target="tpu_custom_call" | custom-call | flops 4831838208 | bytes 15728640 | tf_op jit(solution)/shard_map/proj/pallas_call | solution.py:220
  40.5 5.1 %collective-permute-done.4.refs_1_ = bf16[272,1024]{1,0:T(8,128)(2,1)S(1)} collective-permute-done((bf16[272,1024]{1,0:T(8,128)(2,1)S(1)}, bf16[272,1024]{1,0:T(8,128)(2,1)S(1)}, u32[]{:S(2)}, u32[]{:S(2)}) %collective-permute-start.4) | collective-permute-done | bytes 557088 | tf_op jit(solution)/shard_map/ppermute | solution.py:483
  45.6 1.6 %collective-permute-done.2.refs_0_ = bf16[256,1024]{1,0:T(8,128)(2,1)S(1)} collective-permute-done((bf16[256,1024]{1,0:T(8,128)(2,1)S(1)}, bf16[256,1024]{1,0:T(8,128)(2,1)S(1)}, u32[]{:S(2)}, u32[]{:S(2)}) %collective-permute-start.2) | collective-permute-done | bytes 524320 | tf_op jit(solution)/shard_map/ppermute | solution.py:483
  47.2 1.9 %collective-permute-done.7.refs_2_ = bf16[256,1024]{1,0:T(8,128)(2,1)S(1)} collective-permute-done((bf16[256,1024]{1,0:T(8,128)(2,1)S(1)}, bf16[256,1024]{1,0:T(8,128)(2,1)S(1)}, u32[]{:S(2)}, u32[]{:S(2)}) %collective-permute-start.7) | collective-permute-done | bytes 524320 | tf_op jit(solution)/shard_map/ppermute | solution.py:483
  49.1 2.4 %proj.3 = (bf16[512,512]{1,0:T(8,128)(2,1)S(1)}, bf16[256,256]{1,0:T(8,128)(2,1)S(1)}, bf16[256,256]{1,0:T(8,128)(2,1)S(1)}) custom-call(s32[8]{0:T(128)S(1)} %get-tuple-element.80.order_ref, bf16[256,1024]{1,0:T(8,128)(2,1)S(1)} %collective-permute-done.2.refs_0_, bf16[272,1024]{1,0:T(8,128)(2,1)S(1)} %collective-permute-done.4.refs_1_, ...), custom_call_target="tpu_custom_call" | custom-call | flops 1610612736 | bytes 5242880 | tf_op jit(solution)/shard_map/proj/pallas_call | solution.py:220
  51.5 1.3 %collective-permute-start.11 = (bf16[256,256]{1,0:T(8,128)(2,1)S(1)}, bf16[256,256]{1,0:T(8,128)(2,1)S(1)}, u32[]{:S(2)}, u32[]{:S(2)}) collective-permute-start(bf16[256,256]{1,0:T(8,128)(2,1)S(1)} %get-tuple-element.55.refs_1_), channel_id=1, source_target_pairs={{0,8},{8,16},{16,24},{1,9},{9,17},{17,25},{2,10},{10,18},{18,26},{... | collective-permute-start | bytes 393224 | tf_op jit(solution)/shard_map/ppermute | solution.py:488
  52.8 1.3 %collective-permute-start.9 = (bf16[256,256]{1,0:T(8,128)(2,1)S(1)}, bf16[256,256]{1,0:T(8,128)(2,1)S(1)}, u32[]{:S(2)}, u32[]{:S(2)}) collective-permute-start(bf16[256,256]{1,0:T(8,128)(2,1)S(1)} %get-tuple-element.54.refs_0_), channel_id=1, source_target_pairs={{0,8},{8,16},{16,24},{1,9},{9,17},{17,25},{2,10},{10,18},{18,26},{... | collective-permute-start | bytes 393224 | tf_op jit(solution)/shard_map/ppermute | solution.py:488
  54.1 5.6 %collective-permute-done.11.refs_2_.refs_3_ = bf16[256,256]{1,0:T(8,128)(2,1)S(1)} collective-permute-done((bf16[256,256]{1,0:T(8,128)(2,1)S(1)}, bf16[256,256]{1,0:T(8,128)(2,1)S(1)}, u32[]{:S(2)}, u32[]{:S(2)}) %collective-permute-start.11) | collective-permute-done | bytes 131104 | tf_op jit(solution)/shard_map/ppermute | solution.py:488
  59.8 1.3 %collective-permute-start.12 = (bf16[256,256]{1,0:T(8,128)(2,1)S(1)}, bf16[256,256]{1,0:T(8,128)(2,1)S(1)}, u32[]{:S(2)}, u32[]{:S(2)}) collective-permute-start(bf16[256,256]{1,0:T(8,128)(2,1)S(1)} %collective-permute-done.11.refs_2_.refs_3_), channel_id=1, source_target_pairs={{8,16},{16,24},{9,17},{17,25},{10,18},{18,26},{11,19},{19,27},{12,... | collective-permute-start | bytes 393224 | tf_op jit(solution)/shard_map/ppermute | solution.py:488
  61.1 0.7 collective-permute-done.9.refs_1_.refs_2_
  61.8 1.3 %collective-permute-start.10 = (bf16[256,256]{1,0:T(8,128)(2,1)S(1)}, bf16[256,256]{1,0:T(8,128)(2,1)S(1)}, u32[]{:S(2)}, u32[]{:S(2)}) collective-permute-start(bf16[256,256]{1,0:T(8,128)(2,1)S(1)} %collective-permute-done.9.refs_1_.refs_2_), channel_id=1, source_target_pairs={{8,16},{16,24},{9,17},{17,25},{10,18},{18,26},{11,19},{19,27},{12,... | collective-permute-start | bytes 393224 | tf_op jit(solution)/shard_map/ppermute | solution.py:488
  63.1 1.9 %attend.6 = (f32[8,256]{1,0:T(8,128)S(1)}, f32[8,256]{1,0:T(8,128)S(1)}, f32[4,128,256]{2,1,0:T(8,128)S(1)}) custom-call(s32[1]{0:T(128)} %bitcast.me_ref, bf16[512,512]{1,0:T(8,128)(2,1)S(1)} %get-tuple-element.64.q_ref, bf16[256,256]{1,0:T(8,128)(2,1)S(1)} %get-tuple-element.54.refs_0_, bf16[256,256]{1,0:T(8,128)(2,1)S(1)} %collective-permute-done.9.refs_1_.refs_2_, ...), custom_call_target="tpu_custom_call" | custom-call | flops 402653184 | bytes 393216 | tf_op jit(solution)/shard_map/attend/pallas_call | solution.py:329
  65.0 2.4 %attend.8 = (f32[8,256]{1,0:T(8,128)S(1)}, f32[8,256]{1,0:T(8,128)S(1)}, f32[4,128,256]{2,1,0:T(8,128)S(1)}) custom-call(s32[1]{0:T(128)} %bitcast.me_ref, bf16[512,512]{1,0:T(8,128)(2,1)S(1)} %get-tuple-element.64.q_ref, bf16[256,256]{1,0:T(8,128)(2,1)S(1)} %get-tuple-element.54.refs_0_, bf16[256,256]{1,0:T(8,128)(2,1)S(1)} %get-tuple-element.55.refs_1_, ...), custom_call_target="tpu_custom_call" | custom-call | flops 536870912 | bytes 524288 | tf_op jit(solution)/shard_map/attend/pallas_call | solution.py:329
  67.4 0.3 collective-permute-done.12.refs_1_
  67.7 1.3 %collective-permute-start.14 = (bf16[256,256]{1,0:T(8,128)(2,1)S(1)}, bf16[256,256]{1,0:T(8,128)(2,1)S(1)}, u32[]{:S(2)}, u32[]{:S(2)}) collective-permute-start(bf16[256,256]{1,0:T(8,128)(2,1)S(1)} %collective-permute-done.12.refs_1_), channel_id=1, source_target_pairs={{16,24},{17,25},{18,26},{19,27},{20,28},{21,29},{22,30},{23,31}} | collective-permute-start | bytes 393224 | tf_op jit(solution)/shard_map/ppermute | solution.py:488
  69.0 0.5 collective-permute-done.10.refs_0_
  69.4 1.3 %collective-permute-start.13 = (bf16[256,256]{1,0:T(8,128)(2,1)S(1)}, bf16[256,256]{1,0:T(8,128)(2,1)S(1)}, u32[]{:S(2)}, u32[]{:S(2)}) collective-permute-start(bf16[256,256]{1,0:T(8,128)(2,1)S(1)} %collective-permute-done.10.refs_0_), channel_id=1, source_target_pairs={{16,24},{17,25},{18,26},{19,27},{20,28},{21,29},{22,30},{23,31}} | collective-permute-start | bytes 393224 | tf_op jit(solution)/shard_map/ppermute | solution.py:488
  70.7 1.4 %attend.9 = (f32[8,256]{1,0:T(8,128)S(1)}, f32[8,256]{1,0:T(8,128)S(1)}, f32[4,128,256]{2,1,0:T(8,128)S(1)}) custom-call(s32[1]{0:T(128)} %bitcast.me_ref, bf16[512,512]{1,0:T(8,128)(2,1)S(1)} %get-tuple-element.64.q_ref, bf16[256,256]{1,0:T(8,128)(2,1)S(1)} %collective-permute-done.10.refs_0_, bf16[256,256]{1,0:T(8,128)(2,1)S(1)} %collective-permute-done.12.refs_1_, ...), custom_call_target="tpu_custom_call" | custom-call | flops 268435456 | bytes 262144 | tf_op jit(solution)/shard_map/attend/pallas_call | solution.py:329
  72.1 1.5 %attend.7 = (f32[8,256]{1,0:T(8,128)S(1)}, f32[8,256]{1,0:T(8,128)S(1)}, f32[4,128,256]{2,1,0:T(8,128)S(1)}) custom-call(s32[1]{0:T(128)} %bitcast.me_ref, bf16[512,512]{1,0:T(8,128)(2,1)S(1)} %get-tuple-element.64.q_ref, bf16[256,256]{1,0:T(8,128)(2,1)S(1)} %collective-permute-done.10.refs_0_, bf16[256,256]{1,0:T(8,128)(2,1)S(1)} %collective-permute-done.12.refs_1_, ...), custom_call_target="tpu_custom_call" | custom-call | flops 268435456 | bytes 262144 | tf_op jit(solution)/shard_map/attend/pallas_call | solution.py:329
  73.6 2.1 %collective-permute-done.14.refs_1_ = bf16[256,256]{1,0:T(8,128)(2,1)S(1)} collective-permute-done((bf16[256,256]{1,0:T(8,128)(2,1)S(1)}, bf16[256,256]{1,0:T(8,128)(2,1)S(1)}, u32[]{:S(2)}, u32[]{:S(2)}) %collective-permute-start.14) | collective-permute-done | bytes 131104 | tf_op jit(solution)/shard_map/ppermute | solution.py:488
  75.8 1.4 %collective-permute-done.13.refs_0_ = bf16[256,256]{1,0:T(8,128)(2,1)S(1)} collective-permute-done((bf16[256,256]{1,0:T(8,128)(2,1)S(1)}, bf16[256,256]{1,0:T(8,128)(2,1)S(1)}, u32[]{:S(2)}, u32[]{:S(2)}) %collective-permute-start.13) | collective-permute-done | bytes 131104 | tf_op jit(solution)/shard_map/ppermute | solution.py:488
  77.2 1.5 %attend.10.refs_0_ = bf16[256,512]{1,0:T(8,128)(2,1)S(1)} custom-call(s32[1]{0:T(128)} %bitcast.me_ref, bf16[512,512]{1,0:T(8,128)(2,1)S(1)} %get-tuple-element.64.q_ref, bf16[256,256]{1,0:T(8,128)(2,1)S(1)} %collective-permute-done.13.refs_0_, bf16[256,256]{1,0:T(8,128)(2,1)S(1)} %collective-permute-done.14.refs_1_, ...), custom_call_target="tpu_custom_call" | custom-call | flops 268435456 | bytes 262144 | tf_op jit(solution)/shard_map/attend/pallas_call | solution.py:329
  78.7 0.6 collective-permute-start.16
  79.3 0.6 collective-permute-start.18
  79.9 1.5 %attend.11.refs_0_ = bf16[256,512]{1,0:T(8,128)(2,1)S(1)} custom-call(s32[1]{0:T(128)} %bitcast.me_ref, bf16[512,512]{1,0:T(8,128)(2,1)S(1)} %get-tuple-element.64.q_ref, bf16[256,256]{1,0:T(8,128)(2,1)S(1)} %collective-permute-done.13.refs_0_, bf16[256,256]{1,0:T(8,128)(2,1)S(1)} %collective-permute-done.14.refs_1_, ...), custom_call_target="tpu_custom_call" | custom-call | flops 268435456 | bytes 262144 | tf_op jit(solution)/shard_map/attend/pallas_call | solution.py:329
  81.4 1.5 %collective-permute-start.27 = (bf16[256,512]{1,0:T(8,128)(2,1)S(1)}, bf16[256,512]{1,0:T(8,128)(2,1)S(1)}, u32[]{:S(2)}, u32[]{:S(2)}) collective-permute-start(bf16[256,512]{1,0:T(8,128)(2,1)S(1)} %attend.11.refs_0_), channel_id=1, source_target_pairs={{0,4},{1,5},{2,6},{3,7},{4,0},{5,1},{6,2},{7,3},{8,12},{9,13},{10,... | collective-permute-start | bytes 786440 | tf_op jit(solution)/shard_map/ppermute | solution.py:483
  82.9 1.5 %collective-permute-start.25 = (bf16[256,512]{1,0:T(8,128)(2,1)S(1)}, bf16[256,512]{1,0:T(8,128)(2,1)S(1)}, u32[]{:S(2)}, u32[]{:S(2)}) collective-permute-start(bf16[256,512]{1,0:T(8,128)(2,1)S(1)} %attend.11.refs_0_), channel_id=1, source_target_pairs={{0,2},{1,3},{2,0},{3,1},{4,6},{5,7},{6,4},{7,5},{8,10},{9,11},{10,... | collective-permute-start | bytes 786440 | tf_op jit(solution)/shard_map/ppermute | solution.py:483
  84.4 3.6 %collective-permute-done.16.refs_2_ = bf16[256,512]{1,0:T(8,128)(2,1)S(1)} collective-permute-done((bf16[256,512]{1,0:T(8,128)(2,1)S(1)}, bf16[256,512]{1,0:T(8,128)(2,1)S(1)}, u32[]{:S(2)}, u32[]{:S(2)}) %collective-permute-start.16) | collective-permute-done | bytes 262176 | tf_op jit(solution)/shard_map/ppermute | solution.py:483
  88.0 0.1 collective-permute-start.20
  88.0 0.5 collective-permute-done.18.refs_4_
  88.5 1.5 %collective-permute-start.21 = (bf16[128,512]{1,0:T(8,128)(2,1)S(1)}, bf16[128,512]{1,0:T(8,128)(2,1)S(1)}, u32[]{:S(2)}, u32[]{:S(2)}) collective-permute-start(bf16[128,512]{1,0:T(8,128)(2,1)S(1)} %slice.25), channel_id=1, source_target_pairs={{0,2},{1,3},{2,0},{3,1},{4,6},{5,7},{6,4},{7,5},{8,10},{9,11},{10,... | collective-permute-start | bytes 393224 | tf_op jit(solution)/shard_map/ppermute | solution.py:483
  90.1 2.5 %collective-permute-done.27.refs_4_ = bf16[256,512]{1,0:T(8,128)(2,1)S(1)} collective-permute-done((bf16[256,512]{1,0:T(8,128)(2,1)S(1)}, bf16[256,512]{1,0:T(8,128)(2,1)S(1)}, u32[]{:S(2)}, u32[]{:S(2)}) %collective-permute-start.27) | collective-permute-done | bytes 262176 | tf_op jit(solution)/shard_map/ppermute | solution.py:483
  92.6 0.5 collective-permute-start.19
  93.1 0.9 collective-permute-done.20.refs_6_
  94.0 0.5 collective-permute-start.23
  94.6 0.7 collective-permute-done.22.refs_8_
  95.4 1.6 %collective-permute-start.30 = (bf16[128,512]{1,0:T(8,128)(2,1)S(1)}, bf16[128,512]{1,0:T(8,128)(2,1)S(1)}, u32[]{:S(2)}, u32[]{:S(2)}) collective-permute-start(bf16[128,512]{1,0:T(8,128)(2,1)S(1)} %slice.27), channel_id=1, source_target_pairs={{0,2},{1,3},{2,0},{3,1},{4,6},{5,7},{6,4},{7,5},{8,10},{9,11},{10,... | collective-permute-start | bytes 393224 | tf_op jit(solution)/shard_map/ppermute | solution.py:483
  97.0 0.3 collective-permute-start.29
  97.4 0.5 collective-permute-start.28
  97.9 5.9 %project_out.2 = (f32[256,1024]{1,0:T(8,128)S(1)}, f32[8,256]{1,0:T(8,128)S(1)}) custom-call(f32[8]{0:T(128)S(1)} %get-tuple-element.81.sign_ref, bf16[512,1024]{1,0:T(8,128)(2,1)S(1)} %copy-done, bf16[256,512]{1,0:T(8,128)(2,1)S(1)} %attend.10.refs_0_, bf16[256,512]{1,0:T(8,128)(2,1)S(1)} %collective-permute-done.15.refs_1_, ...), custom_call_target="tpu_custom_call" | custom-call | flops 2147483648 | bytes 12058624 | tf_op jit(solution)/shard_map/project_out/pallas_call | solution.py:424
  103.8 0.1 collective-permute-start.32
  103.9 0.4 collective-permute-start.31
  104.3 0.8 collective-permute-done.32.refs_9_
  105.2 0.2 collective-permute-done.31.refs_8_
  105.3 5.9 %project_out.3 = (f32[256,1024]{1,0:T(8,128)S(1)}, f32[8,256]{1,0:T(8,128)S(1)}) custom-call(f32[8]{0:T(128)S(1)} %get-tuple-element.81.sign_ref, bf16[512,1024]{1,0:T(8,128)(2,1)S(1)} %copy-done, bf16[256,512]{1,0:T(8,128)(2,1)S(1)} %attend.11.refs_0_, bf16[256,512]{1,0:T(8,128)(2,1)S(1)} %collective-permute-done.24.refs_1_, ...), custom_call_target="tpu_custom_call" | custom-call | flops 2147483648 | bytes 12058624 | tf_op jit(solution)/shard_map/project_out/pallas_call | solution.py:424
  111.3 0.4 collective-permute-start.33
  111.6 0.9 collective-permute-done.33
  112.5 0.8 collective-permute-start.34
  113.3 1.3 %collective-permute-start.35 = (f32[8,512]{1,0:T(8,128)S(1)}, f32[8,512]{1,0:T(8,128)S(1)}, u32[]{:S(2)}, u32[]{:S(2)}) collective-permute-start(f32[8,512]{1,0:T(8,128)S(1)} %add.4.refs_2_), channel_id=1, source_target_pairs={{0,4},{1,5},{2,6},{3,7},{4,0},{5,1},{6,2},{7,3},{8,12},{9,13},{10,... | collective-permute-start | bytes 49160 | tf_op jit(solution)/shard_map/ppermute | solution.py:483
  114.6 1.4 %collective-permute-start.36 = (f32[8,512]{1,0:T(8,128)S(1)}, f32[8,512]{1,0:T(8,128)S(1)}, u32[]{:S(2)}, u32[]{:S(2)}) collective-permute-start(f32[8,512]{1,0:T(8,128)S(1)} %add.4.refs_2_), channel_id=1, source_target_pairs={{0,6},{1,7},{2,4},{3,5},{4,2},{5,3},{6,0},{7,1},{8,14},{9,15},{10,... | collective-permute-start | bytes 49160 | tf_op jit(solution)/shard_map/ppermute | solution.py:483
  116.0 0.2 collective-permute-done.34.refs_3_
  116.2 0.8 collective-permute-done.35.refs_4_
  117.0 2.2 %collective-permute-done.36.refs_5_ = f32[8,512]{1,0:T(8,128)S(1)} collective-permute-done((f32[8,512]{1,0:T(8,128)S(1)}, f32[8,512]{1,0:T(8,128)S(1)}, u32[]{:S(2)}, u32[]{:S(2)}) %collective-permute-start.36) | collective-permute-done | bytes 16416 | tf_op jit(solution)/shard_map/ppermute | solution.py:483
  119.2 1.3 %final.1 = (bf16[512,1024]{1,0:T(8,128)(2,1)}, f32[1,512]{1,0:T(1,128)}) custom-call(f32[256,1024]{1,0:T(8,128)S(1)} %get-tuple-element.70.refs_0_, f32[256,1024]{1,0:T(8,128)S(1)} %get-tuple-element.75.refs_1_, f32[8,512]{1,0:T(8,128)S(1)} %add.4.refs_2_, f32[8,512]{1,0:T(8,128)S(1)} %collective-permute-done.34.refs_3_, ...), custom_call_target="tpu_custom_call" | custom-call | flops 1048576 | bytes 3145728 | tf_op jit(solution)/shard_map/final/pallas_call | solution.py:466
  (38 shorter events, 0.2 us)
Async XLA Ops:
  0.6 5.2 %copy-start.1 = (s32[4,128]{1,0:T(4,128)S(1)}, s32[4,128]{1,0:T(4,128)}, u32[]{:S(2)}) copy-start(s32[4,128]{1,0:T(4,128)} %param.13) | copy-start | bytes 6148
  2.7 3.2 %collective-permute-start.1 = (bf16[528,1024]{1,0:T(8,128)(2,1)S(1)}, bf16[528,1024]{1,0:T(8,128)(2,1)}, u32[]{:S(2)}, u32[]{:S(2)}) collective-permute-start(bf16[528,1024]{1,0:T(8,128)(2,1)S(1)} %pre.1.refs_0_), channel_id=1, source_target_pairs={{0,1},{1,0},{2,3},{3,2},{4,5},{5,4},{6,7},{7,6},{8,9},{9,8},{10,11... | collective-permute-start | bytes 3244040 | tf_op jit(solution)/shard_map/ppermute | solution.py:483
  2.8 26.3 %collective-permute-start.3 = (bf16[528,1024]{1,0:T(8,128)(2,1)S(1)}, bf16[528,1024]{1,0:T(8,128)(2,1)S(1)}, u32[]{:S(2)}, u32[]{:S(2)}) collective-permute-start(bf16[528,1024]{1,0:T(8,128)(2,1)S(1)} %pre.1.refs_0_), channel_id=1, source_target_pairs={{0,4},{1,5},{2,6},{3,7},{4,0},{5,1},{6,2},{7,3},{8,12},{9,13},{10,... | collective-permute-start | bytes 3244040 | tf_op jit(solution)/shard_map/ppermute | solution.py:483
  4.4 26.0 %collective-permute-start = (bf16[528,1024]{1,0:T(8,128)(2,1)S(1)}, bf16[528,1024]{1,0:T(8,128)(2,1)}, u32[]{:S(2)}, u32[]{:S(2)}) collective-permute-start(bf16[528,1024]{1,0:T(8,128)(2,1)S(1)} %pre.1.refs_0_), channel_id=1, source_target_pairs={{0,2},{1,3},{2,0},{3,1},{4,6},{5,7},{6,4},{7,5},{8,10},{9,11},{10,... | collective-permute-start | bytes 3244040 | tf_op jit(solution)/shard_map/ppermute | solution.py:483
  29.1 4.8 %collective-permute-start.6 = (bf16[528,1024]{1,0:T(8,128)(2,1)S(1)}, bf16[528,1024]{1,0:T(8,128)(2,1)S(1)}, u32[]{:S(2)}, u32[]{:S(2)}) collective-permute-start(bf16[528,1024]{1,0:T(8,128)(2,1)S(1)} %collective-permute-done.3.refs_4_), channel_id=1, source_target_pairs={{0,1},{1,0},{2,3},{3,2},{4,5},{5,4},{6,7},{7,6},{8,9},{9,8},{10,11... | collective-permute-start | bytes 3244040 | tf_op jit(solution)/shard_map/ppermute | solution.py:483
  30.4 3.4 %collective-permute-start.5 = (bf16[528,1024]{1,0:T(8,128)(2,1)}, bf16[528,1024]{1,0:T(8,128)(2,1)S(1)}, u32[]{:S(2)}, u32[]{:S(2)}) collective-permute-start(bf16[528,1024]{1,0:T(8,128)(2,1)} %collective-permute-done.refs_2_), channel_id=1, source_target_pairs={{0,1},{1,0},{2,3},{3,2},{4,5},{5,4},{6,7},{7,6},{8,9},{9,8},{10,11... | collective-permute-start | bytes 3244040 | tf_op jit(solution)/shard_map/ppermute | solution.py:483
  30.5 15.1 %collective-permute-start.4 = (bf16[272,1024]{1,0:T(8,128)(2,1)S(1)}, bf16[272,1024]{1,0:T(8,128)(2,1)S(1)}, u32[]{:S(2)}, u32[]{:S(2)}) collective-permute-start(bf16[272,1024]{1,0:T(8,128)(2,1)S(1)} %slice.19), channel_id=1, source_target_pairs={{0,2},{1,3},{2,0},{3,1},{4,6},{5,7},{6,4},{7,5},{8,10},{9,11},{10,... | collective-permute-start | bytes 1671176 | tf_op jit(solution)/shard_map/ppermute | solution.py:483
  33.1 14.1 %collective-permute-start.2 = (bf16[256,1024]{1,0:T(8,128)(2,1)S(1)}, bf16[256,1024]{1,0:T(8,128)(2,1)S(1)}, u32[]{:S(2)}, u32[]{:S(2)}) collective-permute-start(bf16[256,1024]{1,0:T(8,128)(2,1)S(1)} %slice.18), channel_id=1, source_target_pairs={{0,4},{1,5},{2,6},{3,7},{4,0},{5,1},{6,2},{7,3},{8,12},{9,13},{10,... | collective-permute-start | bytes 1572872 | tf_op jit(solution)/shard_map/ppermute | solution.py:483
  45.6 3.6 %collective-permute-start.8 = (bf16[272,1024]{1,0:T(8,128)(2,1)S(1)}, bf16[272,1024]{1,0:T(8,128)(2,1)S(1)}, u32[]{:S(2)}, u32[]{:S(2)}) collective-permute-start(bf16[272,1024]{1,0:T(8,128)(2,1)S(1)} %collective-permute-done.4.refs_1_), channel_id=1, source_target_pairs={{0,1},{1,0},{2,3},{3,2},{4,5},{5,4},{6,7},{7,6},{8,9},{9,8},{10,11... | collective-permute-start | bytes 1671176 | tf_op jit(solution)/shard_map/ppermute | solution.py:483
  47.2 1.9 %collective-permute-start.7 = (bf16[256,1024]{1,0:T(8,128)(2,1)S(1)}, bf16[256,1024]{1,0:T(8,128)(2,1)S(1)}, u32[]{:S(2)}, u32[]{:S(2)}) collective-permute-start(bf16[256,1024]{1,0:T(8,128)(2,1)S(1)} %collective-permute-done.2.refs_0_), channel_id=1, source_target_pairs={{0,1},{1,0},{2,3},{3,2},{4,5},{5,4},{6,7},{7,6},{8,9},{9,8},{10,11... | collective-permute-start | bytes 1572872 | tf_op jit(solution)/shard_map/ppermute | solution.py:483
  51.5 8.2 %collective-permute-start.11 = (bf16[256,256]{1,0:T(8,128)(2,1)S(1)}, bf16[256,256]{1,0:T(8,128)(2,1)S(1)}, u32[]{:S(2)}, u32[]{:S(2)}) collective-permute-start(bf16[256,256]{1,0:T(8,128)(2,1)S(1)} %get-tuple-element.55.refs_1_), channel_id=1, source_target_pairs={{0,8},{8,16},{16,24},{1,9},{9,17},{17,25},{2,10},{10,18},{18,26},{... | collective-permute-start | bytes 393224 | tf_op jit(solution)/shard_map/ppermute | solution.py:488
  52.8 8.9 %collective-permute-start.9 = (bf16[256,256]{1,0:T(8,128)(2,1)S(1)}, bf16[256,256]{1,0:T(8,128)(2,1)S(1)}, u32[]{:S(2)}, u32[]{:S(2)}) collective-permute-start(bf16[256,256]{1,0:T(8,128)(2,1)S(1)} %get-tuple-element.54.refs_0_), channel_id=1, source_target_pairs={{0,8},{8,16},{16,24},{1,9},{9,17},{17,25},{2,10},{10,18},{18,26},{... | collective-permute-start | bytes 393224 | tf_op jit(solution)/shard_map/ppermute | solution.py:488
  59.8 7.9 %collective-permute-start.12 = (bf16[256,256]{1,0:T(8,128)(2,1)S(1)}, bf16[256,256]{1,0:T(8,128)(2,1)S(1)}, u32[]{:S(2)}, u32[]{:S(2)}) collective-permute-start(bf16[256,256]{1,0:T(8,128)(2,1)S(1)} %collective-permute-done.11.refs_2_.refs_3_), channel_id=1, source_target_pairs={{8,16},{16,24},{9,17},{17,25},{10,18},{18,26},{11,19},{19,27},{12,... | collective-permute-start | bytes 393224 | tf_op jit(solution)/shard_map/ppermute | solution.py:488
  61.8 7.7 %collective-permute-start.10 = (bf16[256,256]{1,0:T(8,128)(2,1)S(1)}, bf16[256,256]{1,0:T(8,128)(2,1)S(1)}, u32[]{:S(2)}, u32[]{:S(2)}) collective-permute-start(bf16[256,256]{1,0:T(8,128)(2,1)S(1)} %collective-permute-done.9.refs_1_.refs_2_), channel_id=1, source_target_pairs={{8,16},{16,24},{9,17},{17,25},{10,18},{18,26},{11,19},{19,27},{12,... | collective-permute-start | bytes 393224 | tf_op jit(solution)/shard_map/ppermute | solution.py:488
  67.7 8.1 %collective-permute-start.14 = (bf16[256,256]{1,0:T(8,128)(2,1)S(1)}, bf16[256,256]{1,0:T(8,128)(2,1)S(1)}, u32[]{:S(2)}, u32[]{:S(2)}) collective-permute-start(bf16[256,256]{1,0:T(8,128)(2,1)S(1)} %collective-permute-done.12.refs_1_), channel_id=1, source_target_pairs={{16,24},{17,25},{18,26},{19,27},{20,28},{21,29},{22,30},{23,31}} | collective-permute-start | bytes 393224 | tf_op jit(solution)/shard_map/ppermute | solution.py:488
  69.4 7.7 %collective-permute-start.13 = (bf16[256,256]{1,0:T(8,128)(2,1)S(1)}, bf16[256,256]{1,0:T(8,128)(2,1)S(1)}, u32[]{:S(2)}, u32[]{:S(2)}) collective-permute-start(bf16[256,256]{1,0:T(8,128)(2,1)S(1)} %collective-permute-done.10.refs_0_), channel_id=1, source_target_pairs={{16,24},{17,25},{18,26},{19,27},{20,28},{21,29},{22,30},{23,31}} | collective-permute-start | bytes 393224 | tf_op jit(solution)/shard_map/ppermute | solution.py:488
  77.2 20.7 %copy-start = (bf16[512,1024]{1,0:T(8,128)(2,1)S(1)}, bf16[512,1024]{1,0:T(8,128)(2,1)}, u32[]{:S(2)}) copy-start(bf16[512,1024]{1,0:T(8,128)(2,1)} %t_ref.3) | copy-start | bytes 3145732
  78.7 9.3 %collective-permute-start.16 = (bf16[256,512]{1,0:T(8,128)(2,1)S(1)}, bf16[256,512]{1,0:T(8,128)(2,1)S(1)}, u32[]{:S(2)}, u32[]{:S(2)}) collective-permute-start(bf16[256,512]{1,0:T(8,128)(2,1)S(1)} %attend.10.refs_0_), channel_id=1, source_target_pairs={{0,2},{1,3},{2,0},{3,1},{4,6},{5,7},{6,4},{7,5},{8,10},{9,11},{10,... | collective-permute-start | bytes 786440 | tf_op jit(solution)/shard_map/ppermute | solution.py:483
  79.3 9.2 %collective-permute-start.18 = (bf16[256,512]{1,0:T(8,128)(2,1)S(1)}, bf16[256,512]{1,0:T(8,128)(2,1)S(1)}, u32[]{:S(2)}, u32[]{:S(2)}) collective-permute-start(bf16[256,512]{1,0:T(8,128)(2,1)S(1)} %attend.10.refs_0_), channel_id=1, source_target_pairs={{0,4},{1,5},{2,6},{3,7},{4,0},{5,1},{6,2},{7,3},{8,12},{9,13},{10,... | collective-permute-start | bytes 786440 | tf_op jit(solution)/shard_map/ppermute | solution.py:483
  81.4 11.2 %collective-permute-start.27 = (bf16[256,512]{1,0:T(8,128)(2,1)S(1)}, bf16[256,512]{1,0:T(8,128)(2,1)S(1)}, u32[]{:S(2)}, u32[]{:S(2)}) collective-permute-start(bf16[256,512]{1,0:T(8,128)(2,1)S(1)} %attend.11.refs_0_), channel_id=1, source_target_pairs={{0,4},{1,5},{2,6},{3,7},{4,0},{5,1},{6,2},{7,3},{8,12},{9,13},{10,... | collective-permute-start | bytes 786440 | tf_op jit(solution)/shard_map/ppermute | solution.py:483
  82.9 9.7 %collective-permute-start.25 = (bf16[256,512]{1,0:T(8,128)(2,1)S(1)}, bf16[256,512]{1,0:T(8,128)(2,1)S(1)}, u32[]{:S(2)}, u32[]{:S(2)}) collective-permute-start(bf16[256,512]{1,0:T(8,128)(2,1)S(1)} %attend.11.refs_0_), channel_id=1, source_target_pairs={{0,2},{1,3},{2,0},{3,1},{4,6},{5,7},{6,4},{7,5},{8,10},{9,11},{10,... | collective-permute-start | bytes 786440 | tf_op jit(solution)/shard_map/ppermute | solution.py:483
  84.4 10.2 %collective-permute-start.15 = (bf16[256,512]{1,0:T(8,128)(2,1)S(1)}, bf16[256,512]{1,0:T(8,128)(2,1)S(1)}, u32[]{:S(2)}, u32[]{:S(2)}) collective-permute-start(bf16[256,512]{1,0:T(8,128)(2,1)S(1)} %attend.10.refs_0_), channel_id=1, source_target_pairs={{0,1},{1,0},{2,3},{3,2},{4,5},{5,4},{6,7},{7,6},{8,9},{9,8},{10,11... | collective-permute-start | bytes 786440 | tf_op jit(solution)/shard_map/ppermute | solution.py:483
  88.0 6.0 %collective-permute-start.20 = (bf16[128,512]{1,0:T(8,128)(2,1)S(1)}, bf16[128,512]{1,0:T(8,128)(2,1)S(1)}, u32[]{:S(2)}, u32[]{:S(2)}) collective-permute-start(bf16[128,512]{1,0:T(8,128)(2,1)S(1)} %slice.24), channel_id=1, source_target_pairs={{0,4},{1,5},{2,6},{3,7},{4,0},{5,1},{6,2},{7,3},{8,12},{9,13},{10,... | collective-permute-start | bytes 393224 | tf_op jit(solution)/shard_map/ppermute | solution.py:483
  88.5 5.5 %collective-permute-start.21 = (bf16[128,512]{1,0:T(8,128)(2,1)S(1)}, bf16[128,512]{1,0:T(8,128)(2,1)S(1)}, u32[]{:S(2)}, u32[]{:S(2)}) collective-permute-start(bf16[128,512]{1,0:T(8,128)(2,1)S(1)} %slice.25), channel_id=1, source_target_pairs={{0,2},{1,3},{2,0},{3,1},{4,6},{5,7},{6,4},{7,5},{8,10},{9,11},{10,... | collective-permute-start | bytes 393224 | tf_op jit(solution)/shard_map/ppermute | solution.py:483
  92.6 4.7 %collective-permute-start.17 = (bf16[256,512]{1,0:T(8,128)(2,1)S(1)}, bf16[256,512]{1,0:T(8,128)(2,1)S(1)}, u32[]{:S(2)}, u32[]{:S(2)}) collective-permute-start(bf16[256,512]{1,0:T(8,128)(2,1)S(1)} %collective-permute-done.16.refs_2_), channel_id=1, source_target_pairs={{0,1},{1,0},{2,3},{3,2},{4,5},{5,4},{6,7},{7,6},{8,9},{9,8},{10,11... | collective-permute-start | bytes 786440 | tf_op jit(solution)/shard_map/ppermute | solution.py:483
  92.6 4.7 %collective-permute-start.19 = (bf16[256,512]{1,0:T(8,128)(2,1)S(1)}, bf16[256,512]{1,0:T(8,128)(2,1)S(1)}, u32[]{:S(2)}, u32[]{:S(2)}) collective-permute-start(bf16[256,512]{1,0:T(8,128)(2,1)S(1)} %collective-permute-done.18.refs_4_), channel_id=1, source_target_pairs={{0,1},{1,0},{2,3},{3,2},{4,5},{5,4},{6,7},{7,6},{8,9},{9,8},{10,11... | collective-permute-start | bytes 786440 | tf_op jit(solution)/shard_map/ppermute | solution.py:483
  94.0 1.3 %collective-permute-start.22 = (bf16[128,512]{1,0:T(8,128)(2,1)S(1)}, bf16[128,512]{1,0:T(8,128)(2,1)S(1)}, u32[]{:S(2)}, u32[]{:S(2)}) collective-permute-start(bf16[128,512]{1,0:T(8,128)(2,1)S(1)} %collective-permute-done.20.refs_6_), channel_id=1, source_target_pairs={{0,1},{1,0},{2,3},{3,2},{4,5},{5,4},{6,7},{7,6},{8,9},{9,8},{10,11... | collective-permute-start | bytes 393224 | tf_op jit(solution)/shard_map/ppermute | solution.py:483
  94.0 3.0 %collective-permute-start.23 = (bf16[128,512]{1,0:T(8,128)(2,1)S(1)}, bf16[128,512]{1,0:T(8,128)(2,1)S(1)}, u32[]{:S(2)}, u32[]{:S(2)}) collective-permute-start(bf16[128,512]{1,0:T(8,128)(2,1)S(1)} %collective-permute-done.21.refs_7_), channel_id=1, source_target_pairs={{0,1},{1,0},{2,3},{3,2},{4,5},{5,4},{6,7},{7,6},{8,9},{9,8},{10,11... | collective-permute-start | bytes 393224 | tf_op jit(solution)/shard_map/ppermute | solution.py:483
  94.6 9.8 %collective-permute-start.24 = (bf16[256,512]{1,0:T(8,128)(2,1)S(1)}, bf16[256,512]{1,0:T(8,128)(2,1)S(1)}, u32[]{:S(2)}, u32[]{:S(2)}) collective-permute-start(bf16[256,512]{1,0:T(8,128)(2,1)S(1)} %attend.11.refs_0_), channel_id=1, source_target_pairs={{0,1},{1,0},{2,3},{3,2},{4,5},{5,4},{6,7},{7,6},{8,9},{9,8},{10,11... | collective-permute-start | bytes 786440 | tf_op jit(solution)/shard_map/ppermute | solution.py:483
  95.4 8.4 %collective-permute-start.30 = (bf16[128,512]{1,0:T(8,128)(2,1)S(1)}, bf16[128,512]{1,0:T(8,128)(2,1)S(1)}, u32[]{:S(2)}, u32[]{:S(2)}) collective-permute-start(bf16[128,512]{1,0:T(8,128)(2,1)S(1)} %slice.27), channel_id=1, source_target_pairs={{0,2},{1,3},{2,0},{3,1},{4,6},{5,7},{6,4},{7,5},{8,10},{9,11},{10,... | collective-permute-start | bytes 393224 | tf_op jit(solution)/shard_map/ppermute | solution.py:483
  97.0 6.9 %collective-permute-start.29 = (bf16[128,512]{1,0:T(8,128)(2,1)S(1)}, bf16[128,512]{1,0:T(8,128)(2,1)S(1)}, u32[]{:S(2)}, u32[]{:S(2)}) collective-permute-start(bf16[128,512]{1,0:T(8,128)(2,1)S(1)} %slice.26), channel_id=1, source_target_pairs={{0,4},{1,5},{2,6},{3,7},{4,0},{5,1},{6,2},{7,3},{8,12},{9,13},{10,... | collective-permute-start | bytes 393224 | tf_op jit(solution)/shard_map/ppermute | solution.py:483
  97.3 7.0 %collective-permute-start.26 = (bf16[256,512]{1,0:T(8,128)(2,1)S(1)}, bf16[256,512]{1,0:T(8,128)(2,1)S(1)}, u32[]{:S(2)}, u32[]{:S(2)}) collective-permute-start(bf16[256,512]{1,0:T(8,128)(2,1)S(1)} %collective-permute-done.25.refs_2_), channel_id=1, source_target_pairs={{0,1},{1,0},{2,3},{3,2},{4,5},{5,4},{6,7},{7,6},{8,9},{9,8},{10,11... | collective-permute-start | bytes 786440 | tf_op jit(solution)/shard_map/ppermute | solution.py:483
  97.4 7.0 %collective-permute-start.28 = (bf16[256,512]{1,0:T(8,128)(2,1)S(1)}, bf16[256,512]{1,0:T(8,128)(2,1)S(1)}, u32[]{:S(2)}, u32[]{:S(2)}) collective-permute-start(bf16[256,512]{1,0:T(8,128)(2,1)S(1)} %collective-permute-done.27.refs_4_), channel_id=1, source_target_pairs={{0,1},{1,0},{2,3},{3,2},{4,5},{5,4},{6,7},{7,6},{8,9},{9,8},{10,11... | collective-permute-start | bytes 786440 | tf_op jit(solution)/shard_map/ppermute | solution.py:483
  103.8 1.4 %collective-permute-start.32 = (bf16[128,512]{1,0:T(8,128)(2,1)S(1)}, bf16[128,512]{1,0:T(8,128)(2,1)S(1)}, u32[]{:S(2)}, u32[]{:S(2)}) collective-permute-start(bf16[128,512]{1,0:T(8,128)(2,1)S(1)} %collective-permute-done.30.refs_7_), channel_id=1, source_target_pairs={{0,1},{1,0},{2,3},{3,2},{4,5},{5,4},{6,7},{7,6},{8,9},{9,8},{10,11... | collective-permute-start | bytes 393224 | tf_op jit(solution)/shard_map/ppermute | solution.py:483
  103.9 1.5 %collective-permute-start.31 = (bf16[128,512]{1,0:T(8,128)(2,1)S(1)}, bf16[128,512]{1,0:T(8,128)(2,1)S(1)}, u32[]{:S(2)}, u32[]{:S(2)}) collective-permute-start(bf16[128,512]{1,0:T(8,128)(2,1)S(1)} %collective-permute-done.29.refs_6_), channel_id=1, source_target_pairs={{0,1},{1,0},{2,3},{3,2},{4,5},{5,4},{6,7},{7,6},{8,9},{9,8},{10,11... | collective-permute-start | bytes 393224 | tf_op jit(solution)/shard_map/ppermute | solution.py:483
  111.3 1.2 %collective-permute-start.33 = (f32[8,512]{1,0:T(8,128)S(1)}, f32[8,512]{1,0:T(8,128)S(1)}, u32[]{:S(2)}, u32[]{:S(2)}) collective-permute-start(f32[8,512]{1,0:T(8,128)S(1)} %constant_dynamic-update-slice_fusion), channel_id=1, source_target_pairs={{0,1},{1,0},{2,3},{3,2},{4,5},{5,4},{6,7},{7,6},{8,9},{9,8},{10,11... | collective-permute-start | bytes 49160 | tf_op jit(solution)/shard_map/ppermute | solution.py:483
  112.5 3.7 %collective-permute-start.34 = (f32[8,512]{1,0:T(8,128)S(1)}, f32[8,512]{1,0:T(8,128)S(1)}, u32[]{:S(2)}, u32[]{:S(2)}) collective-permute-start(f32[8,512]{1,0:T(8,128)S(1)} %add.4.refs_2_), channel_id=1, source_target_pairs={{0,2},{1,3},{2,0},{3,1},{4,6},{5,7},{6,4},{7,5},{8,10},{9,11},{10,... | collective-permute-start | bytes 49160 | tf_op jit(solution)/shard_map/ppermute | solution.py:483
  113.3 3.7 %collective-permute-start.35 = (f32[8,512]{1,0:T(8,128)S(1)}, f32[8,512]{1,0:T(8,128)S(1)}, u32[]{:S(2)}, u32[]{:S(2)}) collective-permute-start(f32[8,512]{1,0:T(8,128)S(1)} %add.4.refs_2_), channel_id=1, source_target_pairs={{0,4},{1,5},{2,6},{3,7},{4,0},{5,1},{6,2},{7,3},{8,12},{9,13},{10,... | collective-permute-start | bytes 49160 | tf_op jit(solution)/shard_map/ppermute | solution.py:483
  114.6 4.6 %collective-permute-start.36 = (f32[8,512]{1,0:T(8,128)S(1)}, f32[8,512]{1,0:T(8,128)S(1)}, u32[]{:S(2)}, u32[]{:S(2)}) collective-permute-start(f32[8,512]{1,0:T(8,128)S(1)} %add.4.refs_2_), channel_id=1, source_target_pairs={{0,6},{1,7},{2,4},{3,5},{4,2},{5,3},{6,0},{7,1},{8,14},{9,15},{10,... | collective-permute-start | bytes 49160 | tf_op jit(solution)/shard_map/ppermute | solution.py:483

commit v9 on v8

--- a/solution.py
+++ b/solution.py
@@ -18,7 +18,7 @@
 HALVES = 2
 EXTRA = 16
 LOAD_PARTS = 4
-LOAD_MIB = 38
+LOAD_MIB = 37
 PROJ_MIB = 14
 ATT_MIB = 12
 OUT_MIB = 12

time: 121 us -> 121 us (level)
  no operation moved by 1% of the time
where the time goes in v9:
time: 121 us
  waiting for transfers between devices  49.6 us (41%)
  Pallas kernels  41.6 us (34%)
  starting transfers between devices  27.5 us (23%)
    ppermute x31, waiting for transfers between devices, swap(): return lax.ppermute(x, 'tp', [(i, i ^ mask) for i in range(count)])  39 us
    ppermute x31, starting transfers between devices, swap(): return lax.ppermute(x, 'tp', [(i, i ^ mask) for i in range(count)])  19.8 us
    pallas_call x2, Pallas kernels, project_out(): pl.pallas_call(functools.partial(out_kernel, counts, steps, chunk), in_sp...  11.8 us
    ppermute x6, waiting for transfers between devices, send_up(): return lax.ppermute(x, 'ctx', [(i, i + 1) for i in range(first, count - 1)])  10.6 us
    pallas_call x6, Pallas kernels, attend(): pl.pallas_call(kernel, in_specs=[IN_SMEM] + [IN_VMEM] * (len(args) - 1),...  10.2 us
    pallas_call x2, Pallas kernels, proj(): pl.pallas_call(functools.partial(proj_kernel, counts, masks, not state, e...  9.04 us
    ppermute x6, starting transfers between devices, send_up(): return lax.ppermute(x, 'ctx', [(i, i + 1) for i in range(first, count - 1)])  7.71 us
    pallas_call x1, Pallas kernels, load(): pl.pallas_call(functools.partial(load_kernel, count), in_specs=[IN_HBM] *...  7.19 us
  transfers between devices with their start and end apart: 37, of which 22 were waited for; matrix products, arithmetic and copies ran while one was open for 1% of the time, Pallas kernels for 24%

profile of v9, /device:TPU:24, one launch (start us, length us, event | category | flops | bytes accessed | tf_op | source)
XLA Modules:
  0.0 120.7 jit_solution(4945463589904978794)
XLA Ops:
  0.6 2.1 %pre.1.refs_0_ = bf16[528,1024]{1,0:T(8,128)(2,1)S(1)} custom-call(bf16[512,1024]{1,0:T(8,128)(2,1)} %h_hbm.1, bf16[8,128]{1,0:T(8,128)(2,1)} %bitcast.3), custom_call_target="tpu_custom_call" | custom-call | flops 4194304 | bytes 2097152 | tf_op jit(solution)/shard_map/pre/pallas_call | solution.py:87
  2.7 0.1 collective-permute-start.1
  2.8 1.6 %collective-permute-start.3 = (bf16[528,1024]{1,0:T(8,128)(2,1)S(1)}, bf16[528,1024]{1,0:T(8,128)(2,1)S(1)}, u32[]{:S(2)}, u32[]{:S(2)}) collective-permute-start(bf16[528,1024]{1,0:T(8,128)(2,1)S(1)} %pre.1.refs_0_), channel_id=1, source_target_pairs={{0,4},{1,5},{2,6},{3,7},{4,0},{5,1},{6,2},{7,3},{8,12},{9,13},{10,... | collective-permute-start | bytes 3244040 | tf_op jit(solution)/shard_map/ppermute | solution.py:483
  4.4 1.5 %collective-permute-start = (bf16[528,1024]{1,0:T(8,128)(2,1)S(1)}, bf16[528,1024]{1,0:T(8,128)(2,1)}, u32[]{:S(2)}, u32[]{:S(2)}) collective-permute-start(bf16[528,1024]{1,0:T(8,128)(2,1)S(1)} %pre.1.refs_0_), channel_id=1, source_target_pairs={{0,2},{1,3},{2,0},{3,1},{4,6},{5,7},{6,4},{7,5},{8,10},{9,11},{10,... | collective-permute-start | bytes 3244040 | tf_op jit(solution)/shard_map/ppermute | solution.py:483
  5.9 7.2 %load.1 = (bf16[8192,512]{1,0:T(8,128)(2,1)S(1)}, bf16[8192,128]{1,0:T(8,128)(2,1)S(1)}, bf16[8192,128]{1,0:T(8,128)(2,1)S(1)}, bf16[4096,1024]{1,0:T(8,128)(2,1)S(1)}) custom-call(bf16[8192,512]{1,0:T(8,128)(2,1)} %refs_0_, bf16[8192,128]{1,0:T(8,128)(2,1)} %refs_1_.1, bf16[8192,128]{1,0:T(8,128)(2,1)} %refs_2_.1, bf16[4096,1024]{1,0:T(8,128)(2,1)} %refs_3_.1), custom_call_target="tpu_custom_call" | custom-call | bytes 41943040 | tf_op jit(solution)/shard_map/load/pallas_call | solution.py:121
  13.1 16.0 %collective-permute-done.3.refs_4_ = bf16[528,1024]{1,0:T(8,128)(2,1)S(1)} collective-permute-done((bf16[528,1024]{1,0:T(8,128)(2,1)S(1)}, bf16[528,1024]{1,0:T(8,128)(2,1)S(1)}, u32[]{:S(2)}, u32[]{:S(2)}) %collective-permute-start.3) | collective-permute-done | bytes 1081376 | tf_op jit(solution)/shard_map/ppermute | solution.py:483
  29.1 1.3 %collective-permute-done.refs_2_ = bf16[528,1024]{1,0:T(8,128)(2,1)} collective-permute-done((bf16[528,1024]{1,0:T(8,128)(2,1)S(1)}, bf16[528,1024]{1,0:T(8,128)(2,1)}, u32[]{:S(2)}, u32[]{:S(2)}) %collective-permute-start) | collective-permute-done | bytes 1081376 | tf_op jit(solution)/shard_map/ppermute | solution.py:483
  30.5 1.6 %collective-permute-start.4 = (bf16[272,1024]{1,0:T(8,128)(2,1)S(1)}, bf16[272,1024]{1,0:T(8,128)(2,1)S(1)}, u32[]{:S(2)}, u32[]{:S(2)}) collective-permute-start(bf16[272,1024]{1,0:T(8,128)(2,1)S(1)} %slice.19), channel_id=1, source_target_pairs={{0,2},{1,3},{2,0},{3,1},{4,6},{5,7},{6,4},{7,5},{8,10},{9,11},{10,... | collective-permute-start | bytes 1671176 | tf_op jit(solution)/shard_map/ppermute | solution.py:483
  32.0 1.1 slice.18
  33.1 0.8 collective-permute-start.2
  33.8 6.6 %proj.2 = (f32[512,512]{1,0:T(8,128)S(1)}, f32[512,128]{1,0:T(8,128)S(1)}, f32[512,128]{1,0:T(8,128)S(1)}, f32[8,512]{1,0:T(8,128)S(1)}) custom-call(s32[8]{0:T(128)S(1)} %get-tuple-element.80.order_ref, bf16[528,1024]{1,0:T(8,128)(2,1)S(1)} %pre.1.refs_0_, bf16[528,1024]{1,0:T(8,128)(2,1)} %collective-permute-done.1.refs_1_, ...), custom_call_target="tpu_custom_call" | custom-call | flops 4831838208 | bytes 15728640 | tf_op jit(solution)/shard_map/proj/pallas_call | solution.py:220
  40.5 5.1 %collective-permute-done.4.refs_1_ = bf16[272,1024]{1,0:T(8,128)(2,1)S(1)} collective-permute-done((bf16[272,1024]{1,0:T(8,128)(2,1)S(1)}, bf16[272,1024]{1,0:T(8,128)(2,1)S(1)}, u32[]{:S(2)}, u32[]{:S(2)}) %collective-permute-start.4) | collective-permute-done | bytes 557088 | tf_op jit(solution)/shard_map/ppermute | solution.py:483
  45.6 1.6 %collective-permute-done.2.refs_0_ = bf16[256,1024]{1,0:T(8,128)(2,1)S(1)} collective-permute-done((bf16[256,1024]{1,0:T(8,128)(2,1)S(1)}, bf16[256,1024]{1,0:T(8,128)(2,1)S(1)}, u32[]{:S(2)}, u32[]{:S(2)}) %collective-permute-start.2) | collective-permute-done | bytes 524320 | tf_op jit(solution)/shard_map/ppermute | solution.py:483
  47.2 1.9 %collective-permute-done.7.refs_2_ = bf16[256,1024]{1,0:T(8,128)(2,1)S(1)} collective-permute-done((bf16[256,1024]{1,0:T(8,128)(2,1)S(1)}, bf16[256,1024]{1,0:T(8,128)(2,1)S(1)}, u32[]{:S(2)}, u32[]{:S(2)}) %collective-permute-start.7) | collective-permute-done | bytes 524320 | tf_op jit(solution)/shard_map/ppermute | solution.py:483
  49.1 2.4 %proj.3 = (bf16[512,512]{1,0:T(8,128)(2,1)S(1)}, bf16[256,256]{1,0:T(8,128)(2,1)S(1)}, bf16[256,256]{1,0:T(8,128)(2,1)S(1)}) custom-call(s32[8]{0:T(128)S(1)} %get-tuple-element.80.order_ref, bf16[256,1024]{1,0:T(8,128)(2,1)S(1)} %collective-permute-done.2.refs_0_, bf16[272,1024]{1,0:T(8,128)(2,1)S(1)} %collective-permute-done.4.refs_1_, ...), custom_call_target="tpu_custom_call" | custom-call | flops 1610612736 | bytes 5242880 | tf_op jit(solution)/shard_map/proj/pallas_call | solution.py:220
  51.5 1.3 %collective-permute-start.11 = (bf16[256,256]{1,0:T(8,128)(2,1)S(1)}, bf16[256,256]{1,0:T(8,128)(2,1)S(1)}, u32[]{:S(2)}, u32[]{:S(2)}) collective-permute-start(bf16[256,256]{1,0:T(8,128)(2,1)S(1)} %get-tuple-element.55.refs_1_), channel_id=1, source_target_pairs={{0,8},{8,16},{16,24},{1,9},{9,17},{17,25},{2,10},{10,18},{18,26},{... | collective-permute-start | bytes 393224 | tf_op jit(solution)/shard_map/ppermute | solution.py:488
  52.8 1.3 %collective-permute-start.9 = (bf16[256,256]{1,0:T(8,128)(2,1)S(1)}, bf16[256,256]{1,0:T(8,128)(2,1)S(1)}, u32[]{:S(2)}, u32[]{:S(2)}) collective-permute-start(bf16[256,256]{1,0:T(8,128)(2,1)S(1)} %get-tuple-element.54.refs_0_), channel_id=1, source_target_pairs={{0,8},{8,16},{16,24},{1,9},{9,17},{17,25},{2,10},{10,18},{18,26},{... | collective-permute-start | bytes 393224 | tf_op jit(solution)/shard_map/ppermute | solution.py:488
  54.1 5.6 %collective-permute-done.11.refs_2_.refs_3_ = bf16[256,256]{1,0:T(8,128)(2,1)S(1)} collective-permute-done((bf16[256,256]{1,0:T(8,128)(2,1)S(1)}, bf16[256,256]{1,0:T(8,128)(2,1)S(1)}, u32[]{:S(2)}, u32[]{:S(2)}) %collective-permute-start.11) | collective-permute-done | bytes 131104 | tf_op jit(solution)/shard_map/ppermute | solution.py:488
  59.8 1.3 %collective-permute-start.12 = (bf16[256,256]{1,0:T(8,128)(2,1)S(1)}, bf16[256,256]{1,0:T(8,128)(2,1)S(1)}, u32[]{:S(2)}, u32[]{:S(2)}) collective-permute-start(bf16[256,256]{1,0:T(8,128)(2,1)S(1)} %collective-permute-done.11.refs_2_.refs_3_), channel_id=1, source_target_pairs={{8,16},{16,24},{9,17},{17,25},{10,18},{18,26},{11,19},{19,27},{12,... | collective-permute-start | bytes 393224 | tf_op jit(solution)/shard_map/ppermute | solution.py:488
  61.1 0.7 collective-permute-done.9.refs_1_.refs_2_
  61.8 1.3 %collective-permute-start.10 = (bf16[256,256]{1,0:T(8,128)(2,1)S(1)}, bf16[256,256]{1,0:T(8,128)(2,1)S(1)}, u32[]{:S(2)}, u32[]{:S(2)}) collective-permute-start(bf16[256,256]{1,0:T(8,128)(2,1)S(1)} %collective-permute-done.9.refs_1_.refs_2_), channel_id=1, source_target_pairs={{8,16},{16,24},{9,17},{17,25},{10,18},{18,26},{11,19},{19,27},{12,... | collective-permute-start | bytes 393224 | tf_op jit(solution)/shard_map/ppermute | solution.py:488
  63.1 1.9 %attend.6 = (f32[8,256]{1,0:T(8,128)S(1)}, f32[8,256]{1,0:T(8,128)S(1)}, f32[4,128,256]{2,1,0:T(8,128)S(1)}) custom-call(s32[1]{0:T(128)} %bitcast.me_ref, bf16[512,512]{1,0:T(8,128)(2,1)S(1)} %get-tuple-element.64.q_ref, bf16[256,256]{1,0:T(8,128)(2,1)S(1)} %get-tuple-element.54.refs_0_, bf16[256,256]{1,0:T(8,128)(2,1)S(1)} %collective-permute-done.9.refs_1_.refs_2_, ...), custom_call_target="tpu_custom_call" | custom-call | flops 402653184 | bytes 393216 | tf_op jit(solution)/shard_map/attend/pallas_call | solution.py:329
  65.0 2.4 %attend.8 = (f32[8,256]{1,0:T(8,128)S(1)}, f32[8,256]{1,0:T(8,128)S(1)}, f32[4,128,256]{2,1,0:T(8,128)S(1)}) custom-call(s32[1]{0:T(128)} %bitcast.me_ref, bf16[512,512]{1,0:T(8,128)(2,1)S(1)} %get-tuple-element.64.q_ref, bf16[256,256]{1,0:T(8,128)(2,1)S(1)} %get-tuple-element.54.refs_0_, bf16[256,256]{1,0:T(8,128)(2,1)S(1)} %get-tuple-element.55.refs_1_, ...), custom_call_target="tpu_custom_call" | custom-call | flops 536870912 | bytes 524288 | tf_op jit(solution)/shard_map/attend/pallas_call | solution.py:329
  67.4 0.4 collective-permute-done.12.refs_1_
  67.8 1.3 %collective-permute-start.14 = (bf16[256,256]{1,0:T(8,128)(2,1)S(1)}, bf16[256,256]{1,0:T(8,128)(2,1)S(1)}, u32[]{:S(2)}, u32[]{:S(2)}) collective-permute-start(bf16[256,256]{1,0:T(8,128)(2,1)S(1)} %collective-permute-done.12.refs_1_), channel_id=1, source_target_pairs={{16,24},{17,25},{18,26},{19,27},{20,28},{21,29},{22,30},{23,31}} | collective-permute-start | bytes 393224 | tf_op jit(solution)/shard_map/ppermute | solution.py:488
  69.1 0.4 collective-permute-done.10.refs_0_
  69.4 1.3 %collective-permute-start.13 = (bf16[256,256]{1,0:T(8,128)(2,1)S(1)}, bf16[256,256]{1,0:T(8,128)(2,1)S(1)}, u32[]{:S(2)}, u32[]{:S(2)}) collective-permute-start(bf16[256,256]{1,0:T(8,128)(2,1)S(1)} %collective-permute-done.10.refs_0_), channel_id=1, source_target_pairs={{16,24},{17,25},{18,26},{19,27},{20,28},{21,29},{22,30},{23,31}} | collective-permute-start | bytes 393224 | tf_op jit(solution)/shard_map/ppermute | solution.py:488
  70.7 1.4 %attend.9 = (f32[8,256]{1,0:T(8,128)S(1)}, f32[8,256]{1,0:T(8,128)S(1)}, f32[4,128,256]{2,1,0:T(8,128)S(1)}) custom-call(s32[1]{0:T(128)} %bitcast.me_ref, bf16[512,512]{1,0:T(8,128)(2,1)S(1)} %get-tuple-element.64.q_ref, bf16[256,256]{1,0:T(8,128)(2,1)S(1)} %collective-permute-done.10.refs_0_, bf16[256,256]{1,0:T(8,128)(2,1)S(1)} %collective-permute-done.12.refs_1_, ...), custom_call_target="tpu_custom_call" | custom-call | flops 268435456 | bytes 262144 | tf_op jit(solution)/shard_map/attend/pallas_call | solution.py:329
  72.1 1.5 %attend.7 = (f32[8,256]{1,0:T(8,128)S(1)}, f32[8,256]{1,0:T(8,128)S(1)}, f32[4,128,256]{2,1,0:T(8,128)S(1)}) custom-call(s32[1]{0:T(128)} %bitcast.me_ref, bf16[512,512]{1,0:T(8,128)(2,1)S(1)} %get-tuple-element.64.q_ref, bf16[256,256]{1,0:T(8,128)(2,1)S(1)} %collective-permute-done.10.refs_0_, bf16[256,256]{1,0:T(8,128)(2,1)S(1)} %collective-permute-done.12.refs_1_, ...), custom_call_target="tpu_custom_call" | custom-call | flops 268435456 | bytes 262144 | tf_op jit(solution)/shard_map/attend/pallas_call | solution.py:329
  73.6 2.1 %collective-permute-done.14.refs_1_ = bf16[256,256]{1,0:T(8,128)(2,1)S(1)} collective-permute-done((bf16[256,256]{1,0:T(8,128)(2,1)S(1)}, bf16[256,256]{1,0:T(8,128)(2,1)S(1)}, u32[]{:S(2)}, u32[]{:S(2)}) %collective-permute-start.14) | collective-permute-done | bytes 131104 | tf_op jit(solution)/shard_map/ppermute | solution.py:488
  75.7 1.4 %collective-permute-done.13.refs_0_ = bf16[256,256]{1,0:T(8,128)(2,1)S(1)} collective-permute-done((bf16[256,256]{1,0:T(8,128)(2,1)S(1)}, bf16[256,256]{1,0:T(8,128)(2,1)S(1)}, u32[]{:S(2)}, u32[]{:S(2)}) %collective-permute-start.13) | collective-permute-done | bytes 131104 | tf_op jit(solution)/shard_map/ppermute | solution.py:488
  77.1 1.5 %attend.10.refs_0_ = bf16[256,512]{1,0:T(8,128)(2,1)S(1)} custom-call(s32[1]{0:T(128)} %bitcast.me_ref, bf16[512,512]{1,0:T(8,128)(2,1)S(1)} %get-tuple-element.64.q_ref, bf16[256,256]{1,0:T(8,128)(2,1)S(1)} %collective-permute-done.13.refs_0_, bf16[256,256]{1,0:T(8,128)(2,1)S(1)} %collective-permute-done.14.refs_1_, ...), custom_call_target="tpu_custom_call" | custom-call | flops 268435456 | bytes 262144 | tf_op jit(solution)/shard_map/attend/pallas_call | solution.py:329
  78.6 0.8 collective-permute-start.16
  79.4 0.5 collective-permute-start.18
  79.9 1.5 %attend.11.refs_0_ = bf16[256,512]{1,0:T(8,128)(2,1)S(1)} custom-call(s32[1]{0:T(128)} %bitcast.me_ref, bf16[512,512]{1,0:T(8,128)(2,1)S(1)} %get-tuple-element.64.q_ref, bf16[256,256]{1,0:T(8,128)(2,1)S(1)} %collective-permute-done.13.refs_0_, bf16[256,256]{1,0:T(8,128)(2,1)S(1)} %collective-permute-done.14.refs_1_, ...), custom_call_target="tpu_custom_call" | custom-call | flops 268435456 | bytes 262144 | tf_op jit(solution)/shard_map/attend/pallas_call | solution.py:329
  81.4 1.6 %collective-permute-start.27 = (bf16[256,512]{1,0:T(8,128)(2,1)S(1)}, bf16[256,512]{1,0:T(8,128)(2,1)S(1)}, u32[]{:S(2)}, u32[]{:S(2)}) collective-permute-start(bf16[256,512]{1,0:T(8,128)(2,1)S(1)} %attend.11.refs_0_), channel_id=1, source_target_pairs={{0,4},{1,5},{2,6},{3,7},{4,0},{5,1},{6,2},{7,3},{8,12},{9,13},{10,... | collective-permute-start | bytes 786440 | tf_op jit(solution)/shard_map/ppermute | solution.py:483
  83.0 1.3 %collective-permute-start.25 = (bf16[256,512]{1,0:T(8,128)(2,1)S(1)}, bf16[256,512]{1,0:T(8,128)(2,1)S(1)}, u32[]{:S(2)}, u32[]{:S(2)}) collective-permute-start(bf16[256,512]{1,0:T(8,128)(2,1)S(1)} %attend.11.refs_0_), channel_id=1, source_target_pairs={{0,2},{1,3},{2,0},{3,1},{4,6},{5,7},{6,4},{7,5},{8,10},{9,11},{10,... | collective-permute-start | bytes 786440 | tf_op jit(solution)/shard_map/ppermute | solution.py:483
  84.3 3.0 %collective-permute-done.16.refs_2_ = bf16[256,512]{1,0:T(8,128)(2,1)S(1)} collective-permute-done((bf16[256,512]{1,0:T(8,128)(2,1)S(1)}, bf16[256,512]{1,0:T(8,128)(2,1)S(1)}, u32[]{:S(2)}, u32[]{:S(2)}) %collective-permute-start.16) | collective-permute-done | bytes 262176 | tf_op jit(solution)/shard_map/ppermute | solution.py:483
  87.3 0.9 collective-permute-start.20
  88.2 0.4 collective-permute-done.18.refs_4_
  88.6 1.4 %collective-permute-start.21 = (bf16[128,512]{1,0:T(8,128)(2,1)S(1)}, bf16[128,512]{1,0:T(8,128)(2,1)S(1)}, u32[]{:S(2)}, u32[]{:S(2)}) collective-permute-start(bf16[128,512]{1,0:T(8,128)(2,1)S(1)} %slice.25), channel_id=1, source_target_pairs={{0,2},{1,3},{2,0},{3,1},{4,6},{5,7},{6,4},{7,5},{8,10},{9,11},{10,... | collective-permute-start | bytes 393224 | tf_op jit(solution)/shard_map/ppermute | solution.py:483
  90.0 2.8 %collective-permute-done.27.refs_4_ = bf16[256,512]{1,0:T(8,128)(2,1)S(1)} collective-permute-done((bf16[256,512]{1,0:T(8,128)(2,1)S(1)}, bf16[256,512]{1,0:T(8,128)(2,1)S(1)}, u32[]{:S(2)}, u32[]{:S(2)}) %collective-permute-start.27) | collective-permute-done | bytes 262176 | tf_op jit(solution)/shard_map/ppermute | solution.py:483
  92.9 0.5 collective-permute-start.19
  93.4 0.9 collective-permute-done.20.refs_6_
  94.3 0.5 collective-permute-start.23
  94.9 0.7 collective-permute-done.22.refs_8_
  95.6 1.2 collective-permute-start.30
  96.8 0.7 collective-permute-start.29
  97.5 0.5 collective-permute-start.28
  98.0 5.9 %project_out.2 = (f32[256,1024]{1,0:T(8,128)S(1)}, f32[8,256]{1,0:T(8,128)S(1)}) custom-call(f32[8]{0:T(128)S(1)} %get-tuple-element.81.sign_ref, bf16[512,1024]{1,0:T(8,128)(2,1)S(1)} %copy-done, bf16[256,512]{1,0:T(8,128)(2,1)S(1)} %attend.10.refs_0_, bf16[256,512]{1,0:T(8,128)(2,1)S(1)} %collective-permute-done.15.refs_1_, ...), custom_call_target="tpu_custom_call" | custom-call | flops 2147483648 | bytes 12058624 | tf_op jit(solution)/shard_map/project_out/pallas_call | solution.py:424
  103.9 0.1 collective-permute-start.32
  104.0 0.4 collective-permute-start.31
  104.5 0.8 collective-permute-done.32.refs_9_
  105.3 0.2 collective-permute-done.31.refs_8_
  105.5 5.9 %project_out.3 = (f32[256,1024]{1,0:T(8,128)S(1)}, f32[8,256]{1,0:T(8,128)S(1)}) custom-call(f32[8]{0:T(128)S(1)} %get-tuple-element.81.sign_ref, bf16[512,1024]{1,0:T(8,128)(2,1)S(1)} %copy-done, bf16[256,512]{1,0:T(8,128)(2,1)S(1)} %attend.11.refs_0_, bf16[256,512]{1,0:T(8,128)(2,1)S(1)} %collective-permute-done.24.refs_1_, ...), custom_call_target="tpu_custom_call" | custom-call | flops 2147483648 | bytes 12058624 | tf_op jit(solution)/shard_map/project_out/pallas_call | solution.py:424
  111.4 0.4 collective-permute-start.33
  111.8 0.9 collective-permute-done.33
  112.6 0.7 collective-permute-start.34
  113.3 1.5 %collective-permute-start.35 = (f32[8,512]{1,0:T(8,128)S(1)}, f32[8,512]{1,0:T(8,128)S(1)}, u32[]{:S(2)}, u32[]{:S(2)}) collective-permute-start(f32[8,512]{1,0:T(8,128)S(1)} %add.4.refs_2_), channel_id=1, source_target_pairs={{0,4},{1,5},{2,6},{3,7},{4,0},{5,1},{6,2},{7,3},{8,12},{9,13},{10,... | collective-permute-start | bytes 49160 | tf_op jit(solution)/shard_map/ppermute | solution.py:483
  114.8 1.3 %collective-permute-start.36 = (f32[8,512]{1,0:T(8,128)S(1)}, f32[8,512]{1,0:T(8,128)S(1)}, u32[]{:S(2)}, u32[]{:S(2)}) collective-permute-start(f32[8,512]{1,0:T(8,128)S(1)} %add.4.refs_2_), channel_id=1, source_target_pairs={{0,6},{1,7},{2,4},{3,5},{4,2},{5,3},{6,0},{7,1},{8,14},{9,15},{10,... | collective-permute-start | bytes 49160 | tf_op jit(solution)/shard_map/ppermute | solution.py:483
  116.1 0.2 collective-permute-done.34.refs_3_
  116.4 0.7 collective-permute-done.35.refs_4_
  117.0 2.4 %collective-permute-done.36.refs_5_ = f32[8,512]{1,0:T(8,128)S(1)} collective-permute-done((f32[8,512]{1,0:T(8,128)S(1)}, f32[8,512]{1,0:T(8,128)S(1)}, u32[]{:S(2)}, u32[]{:S(2)}) %collective-permute-start.36) | collective-permute-done | bytes 16416 | tf_op jit(solution)/shard_map/ppermute | solution.py:483
  119.5 1.3 %final.1 = (bf16[512,1024]{1,0:T(8,128)(2,1)}, f32[1,512]{1,0:T(1,128)}) custom-call(f32[256,1024]{1,0:T(8,128)S(1)} %get-tuple-element.70.refs_0_, f32[256,1024]{1,0:T(8,128)S(1)} %get-tuple-element.75.refs_1_, f32[8,512]{1,0:T(8,128)S(1)} %add.4.refs_2_, f32[8,512]{1,0:T(8,128)S(1)} %collective-permute-done.34.refs_3_, ...), custom_call_target="tpu_custom_call" | custom-call | flops 1048576 | bytes 3145728 | tf_op jit(solution)/shard_map/final/pallas_call | solution.py:466
  (38 shorter events, 0.2 us)
Async XLA Ops:
  0.6 5.2 %copy-start.1 = (s32[4,128]{1,0:T(4,128)S(1)}, s32[4,128]{1,0:T(4,128)}, u32[]{:S(2)}) copy-start(s32[4,128]{1,0:T(4,128)} %param.13) | copy-start | bytes 6148
  2.7 3.2 %collective-permute-start.1 = (bf16[528,1024]{1,0:T(8,128)(2,1)S(1)}, bf16[528,1024]{1,0:T(8,128)(2,1)}, u32[]{:S(2)}, u32[]{:S(2)}) collective-permute-start(bf16[528,1024]{1,0:T(8,128)(2,1)S(1)} %pre.1.refs_0_), channel_id=1, source_target_pairs={{0,1},{1,0},{2,3},{3,2},{4,5},{5,4},{6,7},{7,6},{8,9},{9,8},{10,11... | collective-permute-start | bytes 3244040 | tf_op jit(solution)/shard_map/ppermute | solution.py:483
  2.8 26.3 %collective-permute-start.3 = (bf16[528,1024]{1,0:T(8,128)(2,1)S(1)}, bf16[528,1024]{1,0:T(8,128)(2,1)S(1)}, u32[]{:S(2)}, u32[]{:S(2)}) collective-permute-start(bf16[528,1024]{1,0:T(8,128)(2,1)S(1)} %pre.1.refs_0_), channel_id=1, source_target_pairs={{0,4},{1,5},{2,6},{3,7},{4,0},{5,1},{6,2},{7,3},{8,12},{9,13},{10,... | collective-permute-start | bytes 3244040 | tf_op jit(solution)/shard_map/ppermute | solution.py:483
  4.4 26.0 %collective-permute-start = (bf16[528,1024]{1,0:T(8,128)(2,1)S(1)}, bf16[528,1024]{1,0:T(8,128)(2,1)}, u32[]{:S(2)}, u32[]{:S(2)}) collective-permute-start(bf16[528,1024]{1,0:T(8,128)(2,1)S(1)} %pre.1.refs_0_), channel_id=1, source_target_pairs={{0,2},{1,3},{2,0},{3,1},{4,6},{5,7},{6,4},{7,5},{8,10},{9,11},{10,... | collective-permute-start | bytes 3244040 | tf_op jit(solution)/shard_map/ppermute | solution.py:483
  29.1 4.8 %collective-permute-start.6 = (bf16[528,1024]{1,0:T(8,128)(2,1)S(1)}, bf16[528,1024]{1,0:T(8,128)(2,1)S(1)}, u32[]{:S(2)}, u32[]{:S(2)}) collective-permute-start(bf16[528,1024]{1,0:T(8,128)(2,1)S(1)} %collective-permute-done.3.refs_4_), channel_id=1, source_target_pairs={{0,1},{1,0},{2,3},{3,2},{4,5},{5,4},{6,7},{7,6},{8,9},{9,8},{10,11... | collective-permute-start | bytes 3244040 | tf_op jit(solution)/shard_map/ppermute | solution.py:483
  30.4 3.4 %collective-permute-start.5 = (bf16[528,1024]{1,0:T(8,128)(2,1)}, bf16[528,1024]{1,0:T(8,128)(2,1)S(1)}, u32[]{:S(2)}, u32[]{:S(2)}) collective-permute-start(bf16[528,1024]{1,0:T(8,128)(2,1)} %collective-permute-done.refs_2_), channel_id=1, source_target_pairs={{0,1},{1,0},{2,3},{3,2},{4,5},{5,4},{6,7},{7,6},{8,9},{9,8},{10,11... | collective-permute-start | bytes 3244040 | tf_op jit(solution)/shard_map/ppermute | solution.py:483
  30.5 15.1 %collective-permute-start.4 = (bf16[272,1024]{1,0:T(8,128)(2,1)S(1)}, bf16[272,1024]{1,0:T(8,128)(2,1)S(1)}, u32[]{:S(2)}, u32[]{:S(2)}) collective-permute-start(bf16[272,1024]{1,0:T(8,128)(2,1)S(1)} %slice.19), channel_id=1, source_target_pairs={{0,2},{1,3},{2,0},{3,1},{4,6},{5,7},{6,4},{7,5},{8,10},{9,11},{10,... | collective-permute-start | bytes 1671176 | tf_op jit(solution)/shard_map/ppermute | solution.py:483
  33.1 14.1 %collective-permute-start.2 = (bf16[256,1024]{1,0:T(8,128)(2,1)S(1)}, bf16[256,1024]{1,0:T(8,128)(2,1)S(1)}, u32[]{:S(2)}, u32[]{:S(2)}) collective-permute-start(bf16[256,1024]{1,0:T(8,128)(2,1)S(1)} %slice.18), channel_id=1, source_target_pairs={{0,4},{1,5},{2,6},{3,7},{4,0},{5,1},{6,2},{7,3},{8,12},{9,13},{10,... | collective-permute-start | bytes 1572872 | tf_op jit(solution)/shard_map/ppermute | solution.py:483
  45.6 3.6 %collective-permute-start.8 = (bf16[272,1024]{1,0:T(8,128)(2,1)S(1)}, bf16[272,1024]{1,0:T(8,128)(2,1)S(1)}, u32[]{:S(2)}, u32[]{:S(2)}) collective-permute-start(bf16[272,1024]{1,0:T(8,128)(2,1)S(1)} %collective-permute-done.4.refs_1_), channel_id=1, source_target_pairs={{0,1},{1,0},{2,3},{3,2},{4,5},{5,4},{6,7},{7,6},{8,9},{9,8},{10,11... | collective-permute-start | bytes 1671176 | tf_op jit(solution)/shard_map/ppermute | solution.py:483
  47.2 1.9 %collective-permute-start.7 = (bf16[256,1024]{1,0:T(8,128)(2,1)S(1)}, bf16[256,1024]{1,0:T(8,128)(2,1)S(1)}, u32[]{:S(2)}, u32[]{:S(2)}) collective-permute-start(bf16[256,1024]{1,0:T(8,128)(2,1)S(1)} %collective-permute-done.2.refs_0_), channel_id=1, source_target_pairs={{0,1},{1,0},{2,3},{3,2},{4,5},{5,4},{6,7},{7,6},{8,9},{9,8},{10,11... | collective-permute-start | bytes 1572872 | tf_op jit(solution)/shard_map/ppermute | solution.py:483
  51.5 8.2 %collective-permute-start.11 = (bf16[256,256]{1,0:T(8,128)(2,1)S(1)}, bf16[256,256]{1,0:T(8,128)(2,1)S(1)}, u32[]{:S(2)}, u32[]{:S(2)}) collective-permute-start(bf16[256,256]{1,0:T(8,128)(2,1)S(1)} %get-tuple-element.55.refs_1_), channel_id=1, source_target_pairs={{0,8},{8,16},{16,24},{1,9},{9,17},{17,25},{2,10},{10,18},{18,26},{... | collective-permute-start | bytes 393224 | tf_op jit(solution)/shard_map/ppermute | solution.py:488
  52.8 8.9 %collective-permute-start.9 = (bf16[256,256]{1,0:T(8,128)(2,1)S(1)}, bf16[256,256]{1,0:T(8,128)(2,1)S(1)}, u32[]{:S(2)}, u32[]{:S(2)}) collective-permute-start(bf16[256,256]{1,0:T(8,128)(2,1)S(1)} %get-tuple-element.54.refs_0_), channel_id=1, source_target_pairs={{0,8},{8,16},{16,24},{1,9},{9,17},{17,25},{2,10},{10,18},{18,26},{... | collective-permute-start | bytes 393224 | tf_op jit(solution)/shard_map/ppermute | solution.py:488
  59.8 8.0 %collective-permute-start.12 = (bf16[256,256]{1,0:T(8,128)(2,1)S(1)}, bf16[256,256]{1,0:T(8,128)(2,1)S(1)}, u32[]{:S(2)}, u32[]{:S(2)}) collective-permute-start(bf16[256,256]{1,0:T(8,128)(2,1)S(1)} %collective-permute-done.11.refs_2_.refs_3_), channel_id=1, source_target_pairs={{8,16},{16,24},{9,17},{17,25},{10,18},{18,26},{11,19},{19,27},{12,... | collective-permute-start | bytes 393224 | tf_op jit(solution)/shard_map/ppermute | solution.py:488
  61.8 7.6 %collective-permute-start.10 = (bf16[256,256]{1,0:T(8,128)(2,1)S(1)}, bf16[256,256]{1,0:T(8,128)(2,1)S(1)}, u32[]{:S(2)}, u32[]{:S(2)}) collective-permute-start(bf16[256,256]{1,0:T(8,128)(2,1)S(1)} %collective-permute-done.9.refs_1_.refs_2_), channel_id=1, source_target_pairs={{8,16},{16,24},{9,17},{17,25},{10,18},{18,26},{11,19},{19,27},{12,... | collective-permute-start | bytes 393224 | tf_op jit(solution)/shard_map/ppermute | solution.py:488
  67.8 7.9 %collective-permute-start.14 = (bf16[256,256]{1,0:T(8,128)(2,1)S(1)}, bf16[256,256]{1,0:T(8,128)(2,1)S(1)}, u32[]{:S(2)}, u32[]{:S(2)}) collective-permute-start(bf16[256,256]{1,0:T(8,128)(2,1)S(1)} %collective-permute-done.12.refs_1_), channel_id=1, source_target_pairs={{16,24},{17,25},{18,26},{19,27},{20,28},{21,29},{22,30},{23,31}} | collective-permute-start | bytes 393224 | tf_op jit(solution)/shard_map/ppermute | solution.py:488
  69.4 7.7 %collective-permute-start.13 = (bf16[256,256]{1,0:T(8,128)(2,1)S(1)}, bf16[256,256]{1,0:T(8,128)(2,1)S(1)}, u32[]{:S(2)}, u32[]{:S(2)}) collective-permute-start(bf16[256,256]{1,0:T(8,128)(2,1)S(1)} %collective-permute-done.10.refs_0_), channel_id=1, source_target_pairs={{16,24},{17,25},{18,26},{19,27},{20,28},{21,29},{22,30},{23,31}} | collective-permute-start | bytes 393224 | tf_op jit(solution)/shard_map/ppermute | solution.py:488
  77.1 20.9 %copy-start = (bf16[512,1024]{1,0:T(8,128)(2,1)S(1)}, bf16[512,1024]{1,0:T(8,128)(2,1)}, u32[]{:S(2)}) copy-start(bf16[512,1024]{1,0:T(8,128)(2,1)} %t_ref.3) | copy-start | bytes 3145732
  78.6 8.7 %collective-permute-start.16 = (bf16[256,512]{1,0:T(8,128)(2,1)S(1)}, bf16[256,512]{1,0:T(8,128)(2,1)S(1)}, u32[]{:S(2)}, u32[]{:S(2)}) collective-permute-start(bf16[256,512]{1,0:T(8,128)(2,1)S(1)} %attend.10.refs_0_), channel_id=1, source_target_pairs={{0,2},{1,3},{2,0},{3,1},{4,6},{5,7},{6,4},{7,5},{8,10},{9,11},{10,... | collective-permute-start | bytes 786440 | tf_op jit(solution)/shard_map/ppermute | solution.py:483
  79.4 9.2 %collective-permute-start.18 = (bf16[256,512]{1,0:T(8,128)(2,1)S(1)}, bf16[256,512]{1,0:T(8,128)(2,1)S(1)}, u32[]{:S(2)}, u32[]{:S(2)}) collective-permute-start(bf16[256,512]{1,0:T(8,128)(2,1)S(1)} %attend.10.refs_0_), channel_id=1, source_target_pairs={{0,4},{1,5},{2,6},{3,7},{4,0},{5,1},{6,2},{7,3},{8,12},{9,13},{10,... | collective-permute-start | bytes 786440 | tf_op jit(solution)/shard_map/ppermute | solution.py:483
  81.4 11.5 %collective-permute-start.27 = (bf16[256,512]{1,0:T(8,128)(2,1)S(1)}, bf16[256,512]{1,0:T(8,128)(2,1)S(1)}, u32[]{:S(2)}, u32[]{:S(2)}) collective-permute-start(bf16[256,512]{1,0:T(8,128)(2,1)S(1)} %attend.11.refs_0_), channel_id=1, source_target_pairs={{0,4},{1,5},{2,6},{3,7},{4,0},{5,1},{6,2},{7,3},{8,12},{9,13},{10,... | collective-permute-start | bytes 786440 | tf_op jit(solution)/shard_map/ppermute | solution.py:483
  83.0 9.9 %collective-permute-start.25 = (bf16[256,512]{1,0:T(8,128)(2,1)S(1)}, bf16[256,512]{1,0:T(8,128)(2,1)S(1)}, u32[]{:S(2)}, u32[]{:S(2)}) collective-permute-start(bf16[256,512]{1,0:T(8,128)(2,1)S(1)} %attend.11.refs_0_), channel_id=1, source_target_pairs={{0,2},{1,3},{2,0},{3,1},{4,6},{5,7},{6,4},{7,5},{8,10},{9,11},{10,... | collective-permute-start | bytes 786440 | tf_op jit(solution)/shard_map/ppermute | solution.py:483
  84.3 10.5 %collective-permute-start.15 = (bf16[256,512]{1,0:T(8,128)(2,1)S(1)}, bf16[256,512]{1,0:T(8,128)(2,1)S(1)}, u32[]{:S(2)}, u32[]{:S(2)}) collective-permute-start(bf16[256,512]{1,0:T(8,128)(2,1)S(1)} %attend.10.refs_0_), channel_id=1, source_target_pairs={{0,1},{1,0},{2,3},{3,2},{4,5},{5,4},{6,7},{7,6},{8,9},{9,8},{10,11... | collective-permute-start | bytes 786440 | tf_op jit(solution)/shard_map/ppermute | solution.py:483
  87.3 7.0 %collective-permute-start.20 = (bf16[128,512]{1,0:T(8,128)(2,1)S(1)}, bf16[128,512]{1,0:T(8,128)(2,1)S(1)}, u32[]{:S(2)}, u32[]{:S(2)}) collective-permute-start(bf16[128,512]{1,0:T(8,128)(2,1)S(1)} %slice.24), channel_id=1, source_target_pairs={{0,4},{1,5},{2,6},{3,7},{4,0},{5,1},{6,2},{7,3},{8,12},{9,13},{10,... | collective-permute-start | bytes 393224 | tf_op jit(solution)/shard_map/ppermute | solution.py:483
  88.6 5.6 %collective-permute-start.21 = (bf16[128,512]{1,0:T(8,128)(2,1)S(1)}, bf16[128,512]{1,0:T(8,128)(2,1)S(1)}, u32[]{:S(2)}, u32[]{:S(2)}) collective-permute-start(bf16[128,512]{1,0:T(8,128)(2,1)S(1)} %slice.25), channel_id=1, source_target_pairs={{0,2},{1,3},{2,0},{3,1},{4,6},{5,7},{6,4},{7,5},{8,10},{9,11},{10,... | collective-permute-start | bytes 393224 | tf_op jit(solution)/shard_map/ppermute | solution.py:483
  92.9 4.6 %collective-permute-start.17 = (bf16[256,512]{1,0:T(8,128)(2,1)S(1)}, bf16[256,512]{1,0:T(8,128)(2,1)S(1)}, u32[]{:S(2)}, u32[]{:S(2)}) collective-permute-start(bf16[256,512]{1,0:T(8,128)(2,1)S(1)} %collective-permute-done.16.refs_2_), channel_id=1, source_target_pairs={{0,1},{1,0},{2,3},{3,2},{4,5},{5,4},{6,7},{7,6},{8,9},{9,8},{10,11... | collective-permute-start | bytes 786440 | tf_op jit(solution)/shard_map/ppermute | solution.py:483
  92.9 4.6 %collective-permute-start.19 = (bf16[256,512]{1,0:T(8,128)(2,1)S(1)}, bf16[256,512]{1,0:T(8,128)(2,1)S(1)}, u32[]{:S(2)}, u32[]{:S(2)}) collective-permute-start(bf16[256,512]{1,0:T(8,128)(2,1)S(1)} %collective-permute-done.18.refs_4_), channel_id=1, source_target_pairs={{0,1},{1,0},{2,3},{3,2},{4,5},{5,4},{6,7},{7,6},{8,9},{9,8},{10,11... | collective-permute-start | bytes 786440 | tf_op jit(solution)/shard_map/ppermute | solution.py:483
  94.3 1.3 %collective-permute-start.22 = (bf16[128,512]{1,0:T(8,128)(2,1)S(1)}, bf16[128,512]{1,0:T(8,128)(2,1)S(1)}, u32[]{:S(2)}, u32[]{:S(2)}) collective-permute-start(bf16[128,512]{1,0:T(8,128)(2,1)S(1)} %collective-permute-done.20.refs_6_), channel_id=1, source_target_pairs={{0,1},{1,0},{2,3},{3,2},{4,5},{5,4},{6,7},{7,6},{8,9},{9,8},{10,11... | collective-permute-start | bytes 393224 | tf_op jit(solution)/shard_map/ppermute | solution.py:483
  94.3 2.5 %collective-permute-start.23 = (bf16[128,512]{1,0:T(8,128)(2,1)S(1)}, bf16[128,512]{1,0:T(8,128)(2,1)S(1)}, u32[]{:S(2)}, u32[]{:S(2)}) collective-permute-start(bf16[128,512]{1,0:T(8,128)(2,1)S(1)} %collective-permute-done.21.refs_7_), channel_id=1, source_target_pairs={{0,1},{1,0},{2,3},{3,2},{4,5},{5,4},{6,7},{7,6},{8,9},{9,8},{10,11... | collective-permute-start | bytes 393224 | tf_op jit(solution)/shard_map/ppermute | solution.py:483
  94.8 9.6 %collective-permute-start.24 = (bf16[256,512]{1,0:T(8,128)(2,1)S(1)}, bf16[256,512]{1,0:T(8,128)(2,1)S(1)}, u32[]{:S(2)}, u32[]{:S(2)}) collective-permute-start(bf16[256,512]{1,0:T(8,128)(2,1)S(1)} %attend.11.refs_0_), channel_id=1, source_target_pairs={{0,1},{1,0},{2,3},{3,2},{4,5},{5,4},{6,7},{7,6},{8,9},{9,8},{10,11... | collective-permute-start | bytes 786440 | tf_op jit(solution)/shard_map/ppermute | solution.py:483
  95.6 8.3 %collective-permute-start.30 = (bf16[128,512]{1,0:T(8,128)(2,1)S(1)}, bf16[128,512]{1,0:T(8,128)(2,1)S(1)}, u32[]{:S(2)}, u32[]{:S(2)}) collective-permute-start(bf16[128,512]{1,0:T(8,128)(2,1)S(1)} %slice.27), channel_id=1, source_target_pairs={{0,2},{1,3},{2,0},{3,1},{4,6},{5,7},{6,4},{7,5},{8,10},{9,11},{10,... | collective-permute-start | bytes 393224 | tf_op jit(solution)/shard_map/ppermute | solution.py:483
  96.8 7.2 %collective-permute-start.29 = (bf16[128,512]{1,0:T(8,128)(2,1)S(1)}, bf16[128,512]{1,0:T(8,128)(2,1)S(1)}, u32[]{:S(2)}, u32[]{:S(2)}) collective-permute-start(bf16[128,512]{1,0:T(8,128)(2,1)S(1)} %slice.26), channel_id=1, source_target_pairs={{0,4},{1,5},{2,6},{3,7},{4,0},{5,1},{6,2},{7,3},{8,12},{9,13},{10,... | collective-permute-start | bytes 393224 | tf_op jit(solution)/shard_map/ppermute | solution.py:483
  97.5 7.0 %collective-permute-start.26 = (bf16[256,512]{1,0:T(8,128)(2,1)S(1)}, bf16[256,512]{1,0:T(8,128)(2,1)S(1)}, u32[]{:S(2)}, u32[]{:S(2)}) collective-permute-start(bf16[256,512]{1,0:T(8,128)(2,1)S(1)} %collective-permute-done.25.refs_2_), channel_id=1, source_target_pairs={{0,1},{1,0},{2,3},{3,2},{4,5},{5,4},{6,7},{7,6},{8,9},{9,8},{10,11... | collective-permute-start | bytes 786440 | tf_op jit(solution)/shard_map/ppermute | solution.py:483
  97.5 7.0 %collective-permute-start.28 = (bf16[256,512]{1,0:T(8,128)(2,1)S(1)}, bf16[256,512]{1,0:T(8,128)(2,1)S(1)}, u32[]{:S(2)}, u32[]{:S(2)}) collective-permute-start(bf16[256,512]{1,0:T(8,128)(2,1)S(1)} %collective-permute-done.27.refs_4_), channel_id=1, source_target_pairs={{0,1},{1,0},{2,3},{3,2},{4,5},{5,4},{6,7},{7,6},{8,9},{9,8},{10,11... | collective-permute-start | bytes 786440 | tf_op jit(solution)/shard_map/ppermute | solution.py:483
  103.9 1.4 %collective-permute-start.32 = (bf16[128,512]{1,0:T(8,128)(2,1)S(1)}, bf16[128,512]{1,0:T(8,128)(2,1)S(1)}, u32[]{:S(2)}, u32[]{:S(2)}) collective-permute-start(bf16[128,512]{1,0:T(8,128)(2,1)S(1)} %collective-permute-done.30.refs_7_), channel_id=1, source_target_pairs={{0,1},{1,0},{2,3},{3,2},{4,5},{5,4},{6,7},{7,6},{8,9},{9,8},{10,11... | collective-permute-start | bytes 393224 | tf_op jit(solution)/shard_map/ppermute | solution.py:483
  104.0 1.5 %collective-permute-start.31 = (bf16[128,512]{1,0:T(8,128)(2,1)S(1)}, bf16[128,512]{1,0:T(8,128)(2,1)S(1)}, u32[]{:S(2)}, u32[]{:S(2)}) collective-permute-start(bf16[128,512]{1,0:T(8,128)(2,1)S(1)} %collective-permute-done.29.refs_6_), channel_id=1, source_target_pairs={{0,1},{1,0},{2,3},{3,2},{4,5},{5,4},{6,7},{7,6},{8,9},{9,8},{10,11... | collective-permute-start | bytes 393224 | tf_op jit(solution)/shard_map/ppermute | solution.py:483
  111.4 1.2 %collective-permute-start.33 = (f32[8,512]{1,0:T(8,128)S(1)}, f32[8,512]{1,0:T(8,128)S(1)}, u32[]{:S(2)}, u32[]{:S(2)}) collective-permute-start(f32[8,512]{1,0:T(8,128)S(1)} %constant_dynamic-update-slice_fusion), channel_id=1, source_target_pairs={{0,1},{1,0},{2,3},{3,2},{4,5},{5,4},{6,7},{7,6},{8,9},{9,8},{10,11... | collective-permute-start | bytes 49160 | tf_op jit(solution)/shard_map/ppermute | solution.py:483
  112.6 3.7 %collective-permute-start.34 = (f32[8,512]{1,0:T(8,128)S(1)}, f32[8,512]{1,0:T(8,128)S(1)}, u32[]{:S(2)}, u32[]{:S(2)}) collective-permute-start(f32[8,512]{1,0:T(8,128)S(1)} %add.4.refs_2_), channel_id=1, source_target_pairs={{0,2},{1,3},{2,0},{3,1},{4,6},{5,7},{6,4},{7,5},{8,10},{9,11},{10,... | collective-permute-start | bytes 49160 | tf_op jit(solution)/shard_map/ppermute | solution.py:483
  113.3 3.7 %collective-permute-start.35 = (f32[8,512]{1,0:T(8,128)S(1)}, f32[8,512]{1,0:T(8,128)S(1)}, u32[]{:S(2)}, u32[]{:S(2)}) collective-permute-start(f32[8,512]{1,0:T(8,128)S(1)} %add.4.refs_2_), channel_id=1, source_target_pairs={{0,4},{1,5},{2,6},{3,7},{4,0},{5,1},{6,2},{7,3},{8,12},{9,13},{10,... | collective-permute-start | bytes 49160 | tf_op jit(solution)/shard_map/ppermute | solution.py:483
  114.8 4.6 %collective-permute-start.36 = (f32[8,512]{1,0:T(8,128)S(1)}, f32[8,512]{1,0:T(8,128)S(1)}, u32[]{:S(2)}, u32[]{:S(2)}) collective-permute-start(f32[8,512]{1,0:T(8,128)S(1)} %add.4.refs_2_), channel_id=1, source_target_pairs={{0,6},{1,7},{2,4},{3,5},{4,2},{5,3},{6,0},{7,1},{8,14},{9,15},{10,... | collective-permute-start | bytes 49160 | tf_op jit(solution)/shard_map/ppermute | solution.py:483

commit v10 on v9

--- a/solution.py
+++ b/solution.py
@@ -18,7 +18,7 @@
 HALVES = 2
 EXTRA = 16
 LOAD_PARTS = 4
-LOAD_MIB = 37
+LOAD_MIB = 34
 PROJ_MIB = 14
 ATT_MIB = 12
 OUT_MIB = 12

time: 121 us -> 121 us (level)
  no operation moved by 1% of the time
where the time goes in v10:
time: 121 us; the launch traced here: 120 us
  waiting for transfers between devices  49.9 us (41%)
  Pallas kernels  41.6 us (34%)
  starting transfers between devices  27 us (22%)
    ppermute x31, waiting for transfers between devices, swap(): return lax.ppermute(x, 'tp', [(i, i ^ mask) for i in range(count)])  39.2 us
    ppermute x31, starting transfers between devices, swap(): return lax.ppermute(x, 'tp', [(i, i ^ mask) for i in range(count)])  19.3 us
    pallas_call x2, Pallas kernels, project_out(): pl.pallas_call(functools.partial(out_kernel, counts, steps, chunk), in_sp...  11.8 us
    ppermute x6, waiting for transfers between devices, send_up(): return lax.ppermute(x, 'ctx', [(i, i + 1) for i in range(first, count - 1)])  10.6 us
    pallas_call x6, Pallas kernels, attend(): pl.pallas_call(kernel, in_specs=[IN_SMEM] + [IN_VMEM] * (len(args) - 1),...  10.2 us
    pallas_call x2, Pallas kernels, proj(): pl.pallas_call(functools.partial(proj_kernel, counts, masks, not state, e...  9.02 us
    ppermute x6, starting transfers between devices, send_up(): return lax.ppermute(x, 'ctx', [(i, i + 1) for i in range(first, count - 1)])  7.71 us
    pallas_call x1, Pallas kernels, load(): pl.pallas_call(functools.partial(load_kernel, count), in_specs=[IN_HBM] *...  7.19 us
  transfers between devices with their start and end apart: 37, of which 22 were waited for; matrix products, arithmetic and copies ran while one was open for 1% of the time, Pallas kernels for 24%

profile of v10, /device:TPU:24, one launch (start us, length us, event | category | flops | bytes accessed | tf_op | source)
XLA Modules:
  0.0 120.5 jit_solution(8920262432727729460)
XLA Ops:
  0.6 2.1 %pre.1.refs_0_ = bf16[528,1024]{1,0:T(8,128)(2,1)S(1)} custom-call(bf16[512,1024]{1,0:T(8,128)(2,1)} %h_hbm.1, bf16[8,128]{1,0:T(8,128)(2,1)} %bitcast.3), custom_call_target="tpu_custom_call" | custom-call | flops 4194304 | bytes 2097152 | tf_op jit(solution)/shard_map/pre/pallas_call | solution.py:87
  2.7 0.1 collective-permute-start.1
  2.8 1.6 %collective-permute-start.3 = (bf16[528,1024]{1,0:T(8,128)(2,1)S(1)}, bf16[528,1024]{1,0:T(8,128)(2,1)S(1)}, u32[]{:S(2)}, u32[]{:S(2)}) collective-permute-start(bf16[528,1024]{1,0:T(8,128)(2,1)S(1)} %pre.1.refs_0_), channel_id=1, source_target_pairs={{0,4},{1,5},{2,6},{3,7},{4,0},{5,1},{6,2},{7,3},{8,12},{9,13},{10,... | collective-permute-start | bytes 3244040 | tf_op jit(solution)/shard_map/ppermute | solution.py:483
  4.4 1.5 %collective-permute-start = (bf16[528,1024]{1,0:T(8,128)(2,1)S(1)}, bf16[528,1024]{1,0:T(8,128)(2,1)}, u32[]{:S(2)}, u32[]{:S(2)}) collective-permute-start(bf16[528,1024]{1,0:T(8,128)(2,1)S(1)} %pre.1.refs_0_), channel_id=1, source_target_pairs={{0,2},{1,3},{2,0},{3,1},{4,6},{5,7},{6,4},{7,5},{8,10},{9,11},{10,... | collective-permute-start | bytes 3244040 | tf_op jit(solution)/shard_map/ppermute | solution.py:483
  5.9 7.2 %load.1 = (bf16[8192,512]{1,0:T(8,128)(2,1)S(1)}, bf16[8192,128]{1,0:T(8,128)(2,1)S(1)}, bf16[8192,128]{1,0:T(8,128)(2,1)S(1)}, bf16[4096,1024]{1,0:T(8,128)(2,1)S(1)}) custom-call(bf16[8192,512]{1,0:T(8,128)(2,1)} %refs_0_, bf16[8192,128]{1,0:T(8,128)(2,1)} %refs_1_.1, bf16[8192,128]{1,0:T(8,128)(2,1)} %refs_2_.1, bf16[4096,1024]{1,0:T(8,128)(2,1)} %refs_3_.1), custom_call_target="tpu_custom_call" | custom-call | bytes 41943040 | tf_op jit(solution)/shard_map/load/pallas_call | solution.py:121
  13.1 16.0 %collective-permute-done.3.refs_4_ = bf16[528,1024]{1,0:T(8,128)(2,1)S(1)} collective-permute-done((bf16[528,1024]{1,0:T(8,128)(2,1)S(1)}, bf16[528,1024]{1,0:T(8,128)(2,1)S(1)}, u32[]{:S(2)}, u32[]{:S(2)}) %collective-permute-start.3) | collective-permute-done | bytes 1081376 | tf_op jit(solution)/shard_map/ppermute | solution.py:483
  29.1 1.3 %collective-permute-done.refs_2_ = bf16[528,1024]{1,0:T(8,128)(2,1)} collective-permute-done((bf16[528,1024]{1,0:T(8,128)(2,1)S(1)}, bf16[528,1024]{1,0:T(8,128)(2,1)}, u32[]{:S(2)}, u32[]{:S(2)}) %collective-permute-start) | collective-permute-done | bytes 1081376 | tf_op jit(solution)/shard_map/ppermute | solution.py:483
  30.5 1.6 %collective-permute-start.4 = (bf16[272,1024]{1,0:T(8,128)(2,1)S(1)}, bf16[272,1024]{1,0:T(8,128)(2,1)S(1)}, u32[]{:S(2)}, u32[]{:S(2)}) collective-permute-start(bf16[272,1024]{1,0:T(8,128)(2,1)S(1)} %slice.19), channel_id=1, source_target_pairs={{0,2},{1,3},{2,0},{3,1},{4,6},{5,7},{6,4},{7,5},{8,10},{9,11},{10,... | collective-permute-start | bytes 1671176 | tf_op jit(solution)/shard_map/ppermute | solution.py:483
  32.0 1.1 slice.18
  33.1 0.8 collective-permute-start.2
  33.8 6.6 %proj.2 = (f32[512,512]{1,0:T(8,128)S(1)}, f32[512,128]{1,0:T(8,128)S(1)}, f32[512,128]{1,0:T(8,128)S(1)}, f32[8,512]{1,0:T(8,128)S(1)}) custom-call(s32[8]{0:T(128)S(1)} %get-tuple-element.80.order_ref, bf16[528,1024]{1,0:T(8,128)(2,1)S(1)} %pre.1.refs_0_, bf16[528,1024]{1,0:T(8,128)(2,1)} %collective-permute-done.1.refs_1_, ...), custom_call_target="tpu_custom_call" | custom-call | flops 4831838208 | bytes 15728640 | tf_op jit(solution)/shard_map/proj/pallas_call | solution.py:220
  40.5 5.1 %collective-permute-done.4.refs_1_ = bf16[272,1024]{1,0:T(8,128)(2,1)S(1)} collective-permute-done((bf16[272,1024]{1,0:T(8,128)(2,1)S(1)}, bf16[272,1024]{1,0:T(8,128)(2,1)S(1)}, u32[]{:S(2)}, u32[]{:S(2)}) %collective-permute-start.4) | collective-permute-done | bytes 557088 | tf_op jit(solution)/shard_map/ppermute | solution.py:483
  45.6 1.6 %collective-permute-done.2.refs_0_ = bf16[256,1024]{1,0:T(8,128)(2,1)S(1)} collective-permute-done((bf16[256,1024]{1,0:T(8,128)(2,1)S(1)}, bf16[256,1024]{1,0:T(8,128)(2,1)S(1)}, u32[]{:S(2)}, u32[]{:S(2)}) %collective-permute-start.2) | collective-permute-done | bytes 524320 | tf_op jit(solution)/shard_map/ppermute | solution.py:483
  47.2 1.9 %collective-permute-done.7.refs_2_ = bf16[256,1024]{1,0:T(8,128)(2,1)S(1)} collective-permute-done((bf16[256,1024]{1,0:T(8,128)(2,1)S(1)}, bf16[256,1024]{1,0:T(8,128)(2,1)S(1)}, u32[]{:S(2)}, u32[]{:S(2)}) %collective-permute-start.7) | collective-permute-done | bytes 524320 | tf_op jit(solution)/shard_map/ppermute | solution.py:483
  49.1 2.4 %proj.3 = (bf16[512,512]{1,0:T(8,128)(2,1)S(1)}, bf16[256,256]{1,0:T(8,128)(2,1)S(1)}, bf16[256,256]{1,0:T(8,128)(2,1)S(1)}) custom-call(s32[8]{0:T(128)S(1)} %get-tuple-element.80.order_ref, bf16[256,1024]{1,0:T(8,128)(2,1)S(1)} %collective-permute-done.2.refs_0_, bf16[272,1024]{1,0:T(8,128)(2,1)S(1)} %collective-permute-done.4.refs_1_, ...), custom_call_target="tpu_custom_call" | custom-call | flops 1610612736 | bytes 5242880 | tf_op jit(solution)/shard_map/proj/pallas_call | solution.py:220
  51.5 1.3 %collective-permute-start.11 = (bf16[256,256]{1,0:T(8,128)(2,1)S(1)}, bf16[256,256]{1,0:T(8,128)(2,1)S(1)}, u32[]{:S(2)}, u32[]{:S(2)}) collective-permute-start(bf16[256,256]{1,0:T(8,128)(2,1)S(1)} %get-tuple-element.55.refs_1_), channel_id=1, source_target_pairs={{0,8},{8,16},{16,24},{1,9},{9,17},{17,25},{2,10},{10,18},{18,26},{... | collective-permute-start | bytes 393224 | tf_op jit(solution)/shard_map/ppermute | solution.py:488
  52.8 1.3 %collective-permute-start.9 = (bf16[256,256]{1,0:T(8,128)(2,1)S(1)}, bf16[256,256]{1,0:T(8,128)(2,1)S(1)}, u32[]{:S(2)}, u32[]{:S(2)}) collective-permute-start(bf16[256,256]{1,0:T(8,128)(2,1)S(1)} %get-tuple-element.54.refs_0_), channel_id=1, source_target_pairs={{0,8},{8,16},{16,24},{1,9},{9,17},{17,25},{2,10},{10,18},{18,26},{... | collective-permute-start | bytes 393224 | tf_op jit(solution)/shard_map/ppermute | solution.py:488
  54.1 5.6 %collective-permute-done.11.refs_2_.refs_3_ = bf16[256,256]{1,0:T(8,128)(2,1)S(1)} collective-permute-done((bf16[256,256]{1,0:T(8,128)(2,1)S(1)}, bf16[256,256]{1,0:T(8,128)(2,1)S(1)}, u32[]{:S(2)}, u32[]{:S(2)}) %collective-permute-start.11) | collective-permute-done | bytes 131104 | tf_op jit(solution)/shard_map/ppermute | solution.py:488
  59.8 1.3 %collective-permute-start.12 = (bf16[256,256]{1,0:T(8,128)(2,1)S(1)}, bf16[256,256]{1,0:T(8,128)(2,1)S(1)}, u32[]{:S(2)}, u32[]{:S(2)}) collective-permute-start(bf16[256,256]{1,0:T(8,128)(2,1)S(1)} %collective-permute-done.11.refs_2_.refs_3_), channel_id=1, source_target_pairs={{8,16},{16,24},{9,17},{17,25},{10,18},{18,26},{11,19},{19,27},{12,... | collective-permute-start | bytes 393224 | tf_op jit(solution)/shard_map/ppermute | solution.py:488
  61.1 0.7 collective-permute-done.9.refs_1_.refs_2_
  61.8 1.3 %collective-permute-start.10 = (bf16[256,256]{1,0:T(8,128)(2,1)S(1)}, bf16[256,256]{1,0:T(8,128)(2,1)S(1)}, u32[]{:S(2)}, u32[]{:S(2)}) collective-permute-start(bf16[256,256]{1,0:T(8,128)(2,1)S(1)} %collective-permute-done.9.refs_1_.refs_2_), channel_id=1, source_target_pairs={{8,16},{16,24},{9,17},{17,25},{10,18},{18,26},{11,19},{19,27},{12,... | collective-permute-start | bytes 393224 | tf_op jit(solution)/shard_map/ppermute | solution.py:488
  63.1 1.9 %attend.6 = (f32[8,256]{1,0:T(8,128)S(1)}, f32[8,256]{1,0:T(8,128)S(1)}, f32[4,128,256]{2,1,0:T(8,128)S(1)}) custom-call(s32[1]{0:T(128)} %bitcast.me_ref, bf16[512,512]{1,0:T(8,128)(2,1)S(1)} %get-tuple-element.64.q_ref, bf16[256,256]{1,0:T(8,128)(2,1)S(1)} %get-tuple-element.54.refs_0_, bf16[256,256]{1,0:T(8,128)(2,1)S(1)} %collective-permute-done.9.refs_1_.refs_2_, ...), custom_call_target="tpu_custom_call" | custom-call | flops 402653184 | bytes 393216 | tf_op jit(solution)/shard_map/attend/pallas_call | solution.py:329
  65.0 2.4 %attend.8 = (f32[8,256]{1,0:T(8,128)S(1)}, f32[8,256]{1,0:T(8,128)S(1)}, f32[4,128,256]{2,1,0:T(8,128)S(1)}) custom-call(s32[1]{0:T(128)} %bitcast.me_ref, bf16[512,512]{1,0:T(8,128)(2,1)S(1)} %get-tuple-element.64.q_ref, bf16[256,256]{1,0:T(8,128)(2,1)S(1)} %get-tuple-element.54.refs_0_, bf16[256,256]{1,0:T(8,128)(2,1)S(1)} %get-tuple-element.55.refs_1_, ...), custom_call_target="tpu_custom_call" | custom-call | flops 536870912 | bytes 524288 | tf_op jit(solution)/shard_map/attend/pallas_call | solution.py:329
  67.4 0.3 collective-permute-done.12.refs_1_
  67.7 1.3 %collective-permute-start.14 = (bf16[256,256]{1,0:T(8,128)(2,1)S(1)}, bf16[256,256]{1,0:T(8,128)(2,1)S(1)}, u32[]{:S(2)}, u32[]{:S(2)}) collective-permute-start(bf16[256,256]{1,0:T(8,128)(2,1)S(1)} %collective-permute-done.12.refs_1_), channel_id=1, source_target_pairs={{16,24},{17,25},{18,26},{19,27},{20,28},{21,29},{22,30},{23,31}} | collective-permute-start | bytes 393224 | tf_op jit(solution)/shard_map/ppermute | solution.py:488
  69.0 0.5 collective-permute-done.10.refs_0_
  69.4 1.3 %collective-permute-start.13 = (bf16[256,256]{1,0:T(8,128)(2,1)S(1)}, bf16[256,256]{1,0:T(8,128)(2,1)S(1)}, u32[]{:S(2)}, u32[]{:S(2)}) collective-permute-start(bf16[256,256]{1,0:T(8,128)(2,1)S(1)} %collective-permute-done.10.refs_0_), channel_id=1, source_target_pairs={{16,24},{17,25},{18,26},{19,27},{20,28},{21,29},{22,30},{23,31}} | collective-permute-start | bytes 393224 | tf_op jit(solution)/shard_map/ppermute | solution.py:488
  70.7 1.4 %attend.9 = (f32[8,256]{1,0:T(8,128)S(1)}, f32[8,256]{1,0:T(8,128)S(1)}, f32[4,128,256]{2,1,0:T(8,128)S(1)}) custom-call(s32[1]{0:T(128)} %bitcast.me_ref, bf16[512,512]{1,0:T(8,128)(2,1)S(1)} %get-tuple-element.64.q_ref, bf16[256,256]{1,0:T(8,128)(2,1)S(1)} %collective-permute-done.10.refs_0_, bf16[256,256]{1,0:T(8,128)(2,1)S(1)} %collective-permute-done.12.refs_1_, ...), custom_call_target="tpu_custom_call" | custom-call | flops 268435456 | bytes 262144 | tf_op jit(solution)/shard_map/attend/pallas_call | solution.py:329
  72.1 1.5 %attend.7 = (f32[8,256]{1,0:T(8,128)S(1)}, f32[8,256]{1,0:T(8,128)S(1)}, f32[4,128,256]{2,1,0:T(8,128)S(1)}) custom-call(s32[1]{0:T(128)} %bitcast.me_ref, bf16[512,512]{1,0:T(8,128)(2,1)S(1)} %get-tuple-element.64.q_ref, bf16[256,256]{1,0:T(8,128)(2,1)S(1)} %collective-permute-done.10.refs_0_, bf16[256,256]{1,0:T(8,128)(2,1)S(1)} %collective-permute-done.12.refs_1_, ...), custom_call_target="tpu_custom_call" | custom-call | flops 268435456 | bytes 262144 | tf_op jit(solution)/shard_map/attend/pallas_call | solution.py:329
  73.6 2.1 %collective-permute-done.14.refs_1_ = bf16[256,256]{1,0:T(8,128)(2,1)S(1)} collective-permute-done((bf16[256,256]{1,0:T(8,128)(2,1)S(1)}, bf16[256,256]{1,0:T(8,128)(2,1)S(1)}, u32[]{:S(2)}, u32[]{:S(2)}) %collective-permute-start.14) | collective-permute-done | bytes 131104 | tf_op jit(solution)/shard_map/ppermute | solution.py:488
  75.8 1.4 %collective-permute-done.13.refs_0_ = bf16[256,256]{1,0:T(8,128)(2,1)S(1)} collective-permute-done((bf16[256,256]{1,0:T(8,128)(2,1)S(1)}, bf16[256,256]{1,0:T(8,128)(2,1)S(1)}, u32[]{:S(2)}, u32[]{:S(2)}) %collective-permute-start.13) | collective-permute-done | bytes 131104 | tf_op jit(solution)/shard_map/ppermute | solution.py:488
  77.2 1.5 %attend.10.refs_0_ = bf16[256,512]{1,0:T(8,128)(2,1)S(1)} custom-call(s32[1]{0:T(128)} %bitcast.me_ref, bf16[512,512]{1,0:T(8,128)(2,1)S(1)} %get-tuple-element.64.q_ref, bf16[256,256]{1,0:T(8,128)(2,1)S(1)} %collective-permute-done.13.refs_0_, bf16[256,256]{1,0:T(8,128)(2,1)S(1)} %collective-permute-done.14.refs_1_, ...), custom_call_target="tpu_custom_call" | custom-call | flops 268435456 | bytes 262144 | tf_op jit(solution)/shard_map/attend/pallas_call | solution.py:329
  78.7 0.6 collective-permute-start.16
  79.3 0.6 collective-permute-start.18
  79.9 1.5 %attend.11.refs_0_ = bf16[256,512]{1,0:T(8,128)(2,1)S(1)} custom-call(s32[1]{0:T(128)} %bitcast.me_ref, bf16[512,512]{1,0:T(8,128)(2,1)S(1)} %get-tuple-element.64.q_ref, bf16[256,256]{1,0:T(8,128)(2,1)S(1)} %collective-permute-done.13.refs_0_, bf16[256,256]{1,0:T(8,128)(2,1)S(1)} %collective-permute-done.14.refs_1_, ...), custom_call_target="tpu_custom_call" | custom-call | flops 268435456 | bytes 262144 | tf_op jit(solution)/shard_map/attend/pallas_call | solution.py:329
  81.4 1.5 %collective-permute-start.27 = (bf16[256,512]{1,0:T(8,128)(2,1)S(1)}, bf16[256,512]{1,0:T(8,128)(2,1)S(1)}, u32[]{:S(2)}, u32[]{:S(2)}) collective-permute-start(bf16[256,512]{1,0:T(8,128)(2,1)S(1)} %attend.11.refs_0_), channel_id=1, source_target_pairs={{0,4},{1,5},{2,6},{3,7},{4,0},{5,1},{6,2},{7,3},{8,12},{9,13},{10,... | collective-permute-start | bytes 786440 | tf_op jit(solution)/shard_map/ppermute | solution.py:483
  82.9 1.5 %collective-permute-start.25 = (bf16[256,512]{1,0:T(8,128)(2,1)S(1)}, bf16[256,512]{1,0:T(8,128)(2,1)S(1)}, u32[]{:S(2)}, u32[]{:S(2)}) collective-permute-start(bf16[256,512]{1,0:T(8,128)(2,1)S(1)} %attend.11.refs_0_), channel_id=1, source_target_pairs={{0,2},{1,3},{2,0},{3,1},{4,6},{5,7},{6,4},{7,5},{8,10},{9,11},{10,... | collective-permute-start | bytes 786440 | tf_op jit(solution)/shard_map/ppermute | solution.py:483
  84.4 3.6 %collective-permute-done.16.refs_2_ = bf16[256,512]{1,0:T(8,128)(2,1)S(1)} collective-permute-done((bf16[256,512]{1,0:T(8,128)(2,1)S(1)}, bf16[256,512]{1,0:T(8,128)(2,1)S(1)}, u32[]{:S(2)}, u32[]{:S(2)}) %collective-permute-start.16) | collective-permute-done | bytes 262176 | tf_op jit(solution)/shard_map/ppermute | solution.py:483
  88.1 0.5 collective-permute-done.18.refs_4_
  88.5 1.6 %collective-permute-start.21 = (bf16[128,512]{1,0:T(8,128)(2,1)S(1)}, bf16[128,512]{1,0:T(8,128)(2,1)S(1)}, u32[]{:S(2)}, u32[]{:S(2)}) collective-permute-start(bf16[128,512]{1,0:T(8,128)(2,1)S(1)} %slice.25), channel_id=1, source_target_pairs={{0,2},{1,3},{2,0},{3,1},{4,6},{5,7},{6,4},{7,5},{8,10},{9,11},{10,... | collective-permute-start | bytes 393224 | tf_op jit(solution)/shard_map/ppermute | solution.py:483
  90.1 2.5 %collective-permute-done.27.refs_4_ = bf16[256,512]{1,0:T(8,128)(2,1)S(1)} collective-permute-done((bf16[256,512]{1,0:T(8,128)(2,1)S(1)}, bf16[256,512]{1,0:T(8,128)(2,1)S(1)}, u32[]{:S(2)}, u32[]{:S(2)}) %collective-permute-start.27) | collective-permute-done | bytes 262176 | tf_op jit(solution)/shard_map/ppermute | solution.py:483
  92.6 0.5 collective-permute-start.19
  93.1 0.9 collective-permute-done.20.refs_6_
  94.0 0.5 collective-permute-start.23
  94.6 0.1 collective-permute-start.24
  94.6 0.7 collective-permute-done.22.refs_8_
  95.4 1.7 %collective-permute-start.30 = (bf16[128,512]{1,0:T(8,128)(2,1)S(1)}, bf16[128,512]{1,0:T(8,128)(2,1)S(1)}, u32[]{:S(2)}, u32[]{:S(2)}) collective-permute-start(bf16[128,512]{1,0:T(8,128)(2,1)S(1)} %slice.27), channel_id=1, source_target_pairs={{0,2},{1,3},{2,0},{3,1},{4,6},{5,7},{6,4},{7,5},{8,10},{9,11},{10,... | collective-permute-start | bytes 393224 | tf_op jit(solution)/shard_map/ppermute | solution.py:483
  97.0 0.3 collective-permute-start.29
  97.3 0.5 collective-permute-start.28
  97.9 5.9 %project_out.2 = (f32[256,1024]{1,0:T(8,128)S(1)}, f32[8,256]{1,0:T(8,128)S(1)}) custom-call(f32[8]{0:T(128)S(1)} %get-tuple-element.81.sign_ref, bf16[512,1024]{1,0:T(8,128)(2,1)S(1)} %copy-done, bf16[256,512]{1,0:T(8,128)(2,1)S(1)} %attend.10.refs_0_, bf16[256,512]{1,0:T(8,128)(2,1)S(1)} %collective-permute-done.15.refs_1_, ...), custom_call_target="tpu_custom_call" | custom-call | flops 2147483648 | bytes 12058624 | tf_op jit(solution)/shard_map/project_out/pallas_call | solution.py:424
  103.8 0.1 collective-permute-start.32
  103.9 0.4 collective-permute-start.31
  104.3 0.8 collective-permute-done.32.refs_9_
  105.2 0.2 collective-permute-done.31.refs_8_
  105.3 5.9 %project_out.3 = (f32[256,1024]{1,0:T(8,128)S(1)}, f32[8,256]{1,0:T(8,128)S(1)}) custom-call(f32[8]{0:T(128)S(1)} %get-tuple-element.81.sign_ref, bf16[512,1024]{1,0:T(8,128)(2,1)S(1)} %copy-done, bf16[256,512]{1,0:T(8,128)(2,1)S(1)} %attend.11.refs_0_, bf16[256,512]{1,0:T(8,128)(2,1)S(1)} %collective-permute-done.24.refs_1_, ...), custom_call_target="tpu_custom_call" | custom-call | flops 2147483648 | bytes 12058624 | tf_op jit(solution)/shard_map/project_out/pallas_call | solution.py:424
  111.3 0.4 collective-permute-start.33
  111.6 0.9 collective-permute-done.33
  112.5 0.8 collective-permute-start.34
  113.3 1.3 %collective-permute-start.35 = (f32[8,512]{1,0:T(8,128)S(1)}, f32[8,512]{1,0:T(8,128)S(1)}, u32[]{:S(2)}, u32[]{:S(2)}) collective-permute-start(f32[8,512]{1,0:T(8,128)S(1)} %add.4.refs_2_), channel_id=1, source_target_pairs={{0,4},{1,5},{2,6},{3,7},{4,0},{5,1},{6,2},{7,3},{8,12},{9,13},{10,... | collective-permute-start | bytes 49160 | tf_op jit(solution)/shard_map/ppermute | solution.py:483
  114.6 1.4 %collective-permute-start.36 = (f32[8,512]{1,0:T(8,128)S(1)}, f32[8,512]{1,0:T(8,128)S(1)}, u32[]{:S(2)}, u32[]{:S(2)}) collective-permute-start(f32[8,512]{1,0:T(8,128)S(1)} %add.4.refs_2_), channel_id=1, source_target_pairs={{0,6},{1,7},{2,4},{3,5},{4,2},{5,3},{6,0},{7,1},{8,14},{9,15},{10,... | collective-permute-start | bytes 49160 | tf_op jit(solution)/shard_map/ppermute | solution.py:483
  116.0 0.2 collective-permute-done.34.refs_3_
  116.2 0.8 collective-permute-done.35.refs_4_
  117.0 2.2 %collective-permute-done.36.refs_5_ = f32[8,512]{1,0:T(8,128)S(1)} collective-permute-done((f32[8,512]{1,0:T(8,128)S(1)}, f32[8,512]{1,0:T(8,128)S(1)}, u32[]{:S(2)}, u32[]{:S(2)}) %collective-permute-start.36) | collective-permute-done | bytes 16416 | tf_op jit(solution)/shard_map/ppermute | solution.py:483
  119.2 1.3 %final.1 = (bf16[512,1024]{1,0:T(8,128)(2,1)}, f32[1,512]{1,0:T(1,128)}) custom-call(f32[256,1024]{1,0:T(8,128)S(1)} %get-tuple-element.70.refs_0_, f32[256,1024]{1,0:T(8,128)S(1)} %get-tuple-element.75.refs_1_, f32[8,512]{1,0:T(8,128)S(1)} %add.4.refs_2_, f32[8,512]{1,0:T(8,128)S(1)} %collective-permute-done.34.refs_3_, ...), custom_call_target="tpu_custom_call" | custom-call | flops 1048576 | bytes 3145728 | tf_op jit(solution)/shard_map/final/pallas_call | solution.py:466
  (38 shorter events, 0.2 us)
Async XLA Ops:
  0.6 5.2 %copy-start.1 = (s32[4,128]{1,0:T(4,128)S(1)}, s32[4,128]{1,0:T(4,128)}, u32[]{:S(2)}) copy-start(s32[4,128]{1,0:T(4,128)} %param.13) | copy-start | bytes 6148
  2.7 3.2 %collective-permute-start.1 = (bf16[528,1024]{1,0:T(8,128)(2,1)S(1)}, bf16[528,1024]{1,0:T(8,128)(2,1)}, u32[]{:S(2)}, u32[]{:S(2)}) collective-permute-start(bf16[528,1024]{1,0:T(8,128)(2,1)S(1)} %pre.1.refs_0_), channel_id=1, source_target_pairs={{0,1},{1,0},{2,3},{3,2},{4,5},{5,4},{6,7},{7,6},{8,9},{9,8},{10,11... | collective-permute-start | bytes 3244040 | tf_op jit(solution)/shard_map/ppermute | solution.py:483
  2.8 26.3 %collective-permute-start.3 = (bf16[528,1024]{1,0:T(8,128)(2,1)S(1)}, bf16[528,1024]{1,0:T(8,128)(2,1)S(1)}, u32[]{:S(2)}, u32[]{:S(2)}) collective-permute-start(bf16[528,1024]{1,0:T(8,128)(2,1)S(1)} %pre.1.refs_0_), channel_id=1, source_target_pairs={{0,4},{1,5},{2,6},{3,7},{4,0},{5,1},{6,2},{7,3},{8,12},{9,13},{10,... | collective-permute-start | bytes 3244040 | tf_op jit(solution)/shard_map/ppermute | solution.py:483
  4.4 26.0 %collective-permute-start = (bf16[528,1024]{1,0:T(8,128)(2,1)S(1)}, bf16[528,1024]{1,0:T(8,128)(2,1)}, u32[]{:S(2)}, u32[]{:S(2)}) collective-permute-start(bf16[528,1024]{1,0:T(8,128)(2,1)S(1)} %pre.1.refs_0_), channel_id=1, source_target_pairs={{0,2},{1,3},{2,0},{3,1},{4,6},{5,7},{6,4},{7,5},{8,10},{9,11},{10,... | collective-permute-start | bytes 3244040 | tf_op jit(solution)/shard_map/ppermute | solution.py:483
  29.1 4.8 %collective-permute-start.6 = (bf16[528,1024]{1,0:T(8,128)(2,1)S(1)}, bf16[528,1024]{1,0:T(8,128)(2,1)S(1)}, u32[]{:S(2)}, u32[]{:S(2)}) collective-permute-start(bf16[528,1024]{1,0:T(8,128)(2,1)S(1)} %collective-permute-done.3.refs_4_), channel_id=1, source_target_pairs={{0,1},{1,0},{2,3},{3,2},{4,5},{5,4},{6,7},{7,6},{8,9},{9,8},{10,11... | collective-permute-start | bytes 3244040 | tf_op jit(solution)/shard_map/ppermute | solution.py:483
  30.4 3.4 %collective-permute-start.5 = (bf16[528,1024]{1,0:T(8,128)(2,1)}, bf16[528,1024]{1,0:T(8,128)(2,1)S(1)}, u32[]{:S(2)}, u32[]{:S(2)}) collective-permute-start(bf16[528,1024]{1,0:T(8,128)(2,1)} %collective-permute-done.refs_2_), channel_id=1, source_target_pairs={{0,1},{1,0},{2,3},{3,2},{4,5},{5,4},{6,7},{7,6},{8,9},{9,8},{10,11... | collective-permute-start | bytes 3244040 | tf_op jit(solution)/shard_map/ppermute | solution.py:483
  30.5 15.1 %collective-permute-start.4 = (bf16[272,1024]{1,0:T(8,128)(2,1)S(1)}, bf16[272,1024]{1,0:T(8,128)(2,1)S(1)}, u32[]{:S(2)}, u32[]{:S(2)}) collective-permute-start(bf16[272,1024]{1,0:T(8,128)(2,1)S(1)} %slice.19), channel_id=1, source_target_pairs={{0,2},{1,3},{2,0},{3,1},{4,6},{5,7},{6,4},{7,5},{8,10},{9,11},{10,... | collective-permute-start | bytes 1671176 | tf_op jit(solution)/shard_map/ppermute | solution.py:483
  33.1 14.1 %collective-permute-start.2 = (bf16[256,1024]{1,0:T(8,128)(2,1)S(1)}, bf16[256,1024]{1,0:T(8,128)(2,1)S(1)}, u32[]{:S(2)}, u32[]{:S(2)}) collective-permute-start(bf16[256,1024]{1,0:T(8,128)(2,1)S(1)} %slice.18), channel_id=1, source_target_pairs={{0,4},{1,5},{2,6},{3,7},{4,0},{5,1},{6,2},{7,3},{8,12},{9,13},{10,... | collective-permute-start | bytes 1572872 | tf_op jit(solution)/shard_map/ppermute | solution.py:483
  45.6 3.6 %collective-permute-start.8 = (bf16[272,1024]{1,0:T(8,128)(2,1)S(1)}, bf16[272,1024]{1,0:T(8,128)(2,1)S(1)}, u32[]{:S(2)}, u32[]{:S(2)}) collective-permute-start(bf16[272,1024]{1,0:T(8,128)(2,1)S(1)} %collective-permute-done.4.refs_1_), channel_id=1, source_target_pairs={{0,1},{1,0},{2,3},{3,2},{4,5},{5,4},{6,7},{7,6},{8,9},{9,8},{10,11... | collective-permute-start | bytes 1671176 | tf_op jit(solution)/shard_map/ppermute | solution.py:483
  47.2 1.9 %collective-permute-start.7 = (bf16[256,1024]{1,0:T(8,128)(2,1)S(1)}, bf16[256,1024]{1,0:T(8,128)(2,1)S(1)}, u32[]{:S(2)}, u32[]{:S(2)}) collective-permute-start(bf16[256,1024]{1,0:T(8,128)(2,1)S(1)} %collective-permute-done.2.refs_0_), channel_id=1, source_target_pairs={{0,1},{1,0},{2,3},{3,2},{4,5},{5,4},{6,7},{7,6},{8,9},{9,8},{10,11... | collective-permute-start | bytes 1572872 | tf_op jit(solution)/shard_map/ppermute | solution.py:483
  51.5 8.2 %collective-permute-start.11 = (bf16[256,256]{1,0:T(8,128)(2,1)S(1)}, bf16[256,256]{1,0:T(8,128)(2,1)S(1)}, u32[]{:S(2)}, u32[]{:S(2)}) collective-permute-start(bf16[256,256]{1,0:T(8,128)(2,1)S(1)} %get-tuple-element.55.refs_1_), channel_id=1, source_target_pairs={{0,8},{8,16},{16,24},{1,9},{9,17},{17,25},{2,10},{10,18},{18,26},{... | collective-permute-start | bytes 393224 | tf_op jit(solution)/shard_map/ppermute | solution.py:488
  52.8 8.9 %collective-permute-start.9 = (bf16[256,256]{1,0:T(8,128)(2,1)S(1)}, bf16[256,256]{1,0:T(8,128)(2,1)S(1)}, u32[]{:S(2)}, u32[]{:S(2)}) collective-permute-start(bf16[256,256]{1,0:T(8,128)(2,1)S(1)} %get-tuple-element.54.refs_0_), channel_id=1, source_target_pairs={{0,8},{8,16},{16,24},{1,9},{9,17},{17,25},{2,10},{10,18},{18,26},{... | collective-permute-start | bytes 393224 | tf_op jit(solution)/shard_map/ppermute | solution.py:488
  59.8 7.9 %collective-permute-start.12 = (bf16[256,256]{1,0:T(8,128)(2,1)S(1)}, bf16[256,256]{1,0:T(8,128)(2,1)S(1)}, u32[]{:S(2)}, u32[]{:S(2)}) collective-permute-start(bf16[256,256]{1,0:T(8,128)(2,1)S(1)} %collective-permute-done.11.refs_2_.refs_3_), channel_id=1, source_target_pairs={{8,16},{16,24},{9,17},{17,25},{10,18},{18,26},{11,19},{19,27},{12,... | collective-permute-start | bytes 393224 | tf_op jit(solution)/shard_map/ppermute | solution.py:488
  61.8 7.7 %collective-permute-start.10 = (bf16[256,256]{1,0:T(8,128)(2,1)S(1)}, bf16[256,256]{1,0:T(8,128)(2,1)S(1)}, u32[]{:S(2)}, u32[]{:S(2)}) collective-permute-start(bf16[256,256]{1,0:T(8,128)(2,1)S(1)} %collective-permute-done.9.refs_1_.refs_2_), channel_id=1, source_target_pairs={{8,16},{16,24},{9,17},{17,25},{10,18},{18,26},{11,19},{19,27},{12,... | collective-permute-start | bytes 393224 | tf_op jit(solution)/shard_map/ppermute | solution.py:488
  67.7 8.1 %collective-permute-start.14 = (bf16[256,256]{1,0:T(8,128)(2,1)S(1)}, bf16[256,256]{1,0:T(8,128)(2,1)S(1)}, u32[]{:S(2)}, u32[]{:S(2)}) collective-permute-start(bf16[256,256]{1,0:T(8,128)(2,1)S(1)} %collective-permute-done.12.refs_1_), channel_id=1, source_target_pairs={{16,24},{17,25},{18,26},{19,27},{20,28},{21,29},{22,30},{23,31}} | collective-permute-start | bytes 393224 | tf_op jit(solution)/shard_map/ppermute | solution.py:488
  69.4 7.7 %collective-permute-start.13 = (bf16[256,256]{1,0:T(8,128)(2,1)S(1)}, bf16[256,256]{1,0:T(8,128)(2,1)S(1)}, u32[]{:S(2)}, u32[]{:S(2)}) collective-permute-start(bf16[256,256]{1,0:T(8,128)(2,1)S(1)} %collective-permute-done.10.refs_0_), channel_id=1, source_target_pairs={{16,24},{17,25},{18,26},{19,27},{20,28},{21,29},{22,30},{23,31}} | collective-permute-start | bytes 393224 | tf_op jit(solution)/shard_map/ppermute | solution.py:488
  77.2 20.7 %copy-start = (bf16[512,1024]{1,0:T(8,128)(2,1)S(1)}, bf16[512,1024]{1,0:T(8,128)(2,1)}, u32[]{:S(2)}) copy-start(bf16[512,1024]{1,0:T(8,128)(2,1)} %t_ref.3) | copy-start | bytes 3145732
  78.7 9.3 %collective-permute-start.16 = (bf16[256,512]{1,0:T(8,128)(2,1)S(1)}, bf16[256,512]{1,0:T(8,128)(2,1)S(1)}, u32[]{:S(2)}, u32[]{:S(2)}) collective-permute-start(bf16[256,512]{1,0:T(8,128)(2,1)S(1)} %attend.10.refs_0_), channel_id=1, source_target_pairs={{0,2},{1,3},{2,0},{3,1},{4,6},{5,7},{6,4},{7,5},{8,10},{9,11},{10,... | collective-permute-start | bytes 786440 | tf_op jit(solution)/shard_map/ppermute | solution.py:483
  79.3 9.2 %collective-permute-start.18 = (bf16[256,512]{1,0:T(8,128)(2,1)S(1)}, bf16[256,512]{1,0:T(8,128)(2,1)S(1)}, u32[]{:S(2)}, u32[]{:S(2)}) collective-permute-start(bf16[256,512]{1,0:T(8,128)(2,1)S(1)} %attend.10.refs_0_), channel_id=1, source_target_pairs={{0,4},{1,5},{2,6},{3,7},{4,0},{5,1},{6,2},{7,3},{8,12},{9,13},{10,... | collective-permute-start | bytes 786440 | tf_op jit(solution)/shard_map/ppermute | solution.py:483
  81.4 11.2 %collective-permute-start.27 = (bf16[256,512]{1,0:T(8,128)(2,1)S(1)}, bf16[256,512]{1,0:T(8,128)(2,1)S(1)}, u32[]{:S(2)}, u32[]{:S(2)}) collective-permute-start(bf16[256,512]{1,0:T(8,128)(2,1)S(1)} %attend.11.refs_0_), channel_id=1, source_target_pairs={{0,4},{1,5},{2,6},{3,7},{4,0},{5,1},{6,2},{7,3},{8,12},{9,13},{10,... | collective-permute-start | bytes 786440 | tf_op jit(solution)/shard_map/ppermute | solution.py:483
  82.9 9.7 %collective-permute-start.25 = (bf16[256,512]{1,0:T(8,128)(2,1)S(1)}, bf16[256,512]{1,0:T(8,128)(2,1)S(1)}, u32[]{:S(2)}, u32[]{:S(2)}) collective-permute-start(bf16[256,512]{1,0:T(8,128)(2,1)S(1)} %attend.11.refs_0_), channel_id=1, source_target_pairs={{0,2},{1,3},{2,0},{3,1},{4,6},{5,7},{6,4},{7,5},{8,10},{9,11},{10,... | collective-permute-start | bytes 786440 | tf_op jit(solution)/shard_map/ppermute | solution.py:483
  84.4 10.2 %collective-permute-start.15 = (bf16[256,512]{1,0:T(8,128)(2,1)S(1)}, bf16[256,512]{1,0:T(8,128)(2,1)S(1)}, u32[]{:S(2)}, u32[]{:S(2)}) collective-permute-start(bf16[256,512]{1,0:T(8,128)(2,1)S(1)} %attend.10.refs_0_), channel_id=1, source_target_pairs={{0,1},{1,0},{2,3},{3,2},{4,5},{5,4},{6,7},{7,6},{8,9},{9,8},{10,11... | collective-permute-start | bytes 786440 | tf_op jit(solution)/shard_map/ppermute | solution.py:483
  88.0 6.0 %collective-permute-start.20 = (bf16[128,512]{1,0:T(8,128)(2,1)S(1)}, bf16[128,512]{1,0:T(8,128)(2,1)S(1)}, u32[]{:S(2)}, u32[]{:S(2)}) collective-permute-start(bf16[128,512]{1,0:T(8,128)(2,1)S(1)} %slice.24), channel_id=1, source_target_pairs={{0,4},{1,5},{2,6},{3,7},{4,0},{5,1},{6,2},{7,3},{8,12},{9,13},{10,... | collective-permute-start | bytes 393224 | tf_op jit(solution)/shard_map/ppermute | solution.py:483
  88.5 5.5 %collective-permute-start.21 = (bf16[128,512]{1,0:T(8,128)(2,1)S(1)}, bf16[128,512]{1,0:T(8,128)(2,1)S(1)}, u32[]{:S(2)}, u32[]{:S(2)}) collective-permute-start(bf16[128,512]{1,0:T(8,128)(2,1)S(1)} %slice.25), channel_id=1, source_target_pairs={{0,2},{1,3},{2,0},{3,1},{4,6},{5,7},{6,4},{7,5},{8,10},{9,11},{10,... | collective-permute-start | bytes 393224 | tf_op jit(solution)/shard_map/ppermute | solution.py:483
  92.6 4.7 %collective-permute-start.17 = (bf16[256,512]{1,0:T(8,128)(2,1)S(1)}, bf16[256,512]{1,0:T(8,128)(2,1)S(1)}, u32[]{:S(2)}, u32[]{:S(2)}) collective-permute-start(bf16[256,512]{1,0:T(8,128)(2,1)S(1)} %collective-permute-done.16.refs_2_), channel_id=1, source_target_pairs={{0,1},{1,0},{2,3},{3,2},{4,5},{5,4},{6,7},{7,6},{8,9},{9,8},{10,11... | collective-permute-start | bytes 786440 | tf_op jit(solution)/shard_map/ppermute | solution.py:483
  92.6 4.7 %collective-permute-start.19 = (bf16[256,512]{1,0:T(8,128)(2,1)S(1)}, bf16[256,512]{1,0:T(8,128)(2,1)S(1)}, u32[]{:S(2)}, u32[]{:S(2)}) collective-permute-start(bf16[256,512]{1,0:T(8,128)(2,1)S(1)} %collective-permute-done.18.refs_4_), channel_id=1, source_target_pairs={{0,1},{1,0},{2,3},{3,2},{4,5},{5,4},{6,7},{7,6},{8,9},{9,8},{10,11... | collective-permute-start | bytes 786440 | tf_op jit(solution)/shard_map/ppermute | solution.py:483
  94.0 1.3 %collective-permute-start.22 = (bf16[128,512]{1,0:T(8,128)(2,1)S(1)}, bf16[128,512]{1,0:T(8,128)(2,1)S(1)}, u32[]{:S(2)}, u32[]{:S(2)}) collective-permute-start(bf16[128,512]{1,0:T(8,128)(2,1)S(1)} %collective-permute-done.20.refs_6_), channel_id=1, source_target_pairs={{0,1},{1,0},{2,3},{3,2},{4,5},{5,4},{6,7},{7,6},{8,9},{9,8},{10,11... | collective-permute-start | bytes 393224 | tf_op jit(solution)/shard_map/ppermute | solution.py:483
  94.0 3.0 %collective-permute-start.23 = (bf16[128,512]{1,0:T(8,128)(2,1)S(1)}, bf16[128,512]{1,0:T(8,128)(2,1)S(1)}, u32[]{:S(2)}, u32[]{:S(2)}) collective-permute-start(bf16[128,512]{1,0:T(8,128)(2,1)S(1)} %collective-permute-done.21.refs_7_), channel_id=1, source_target_pairs={{0,1},{1,0},{2,3},{3,2},{4,5},{5,4},{6,7},{7,6},{8,9},{9,8},{10,11... | collective-permute-start | bytes 393224 | tf_op jit(solution)/shard_map/ppermute | solution.py:483
  94.6 9.8 %collective-permute-start.24 = (bf16[256,512]{1,0:T(8,128)(2,1)S(1)}, bf16[256,512]{1,0:T(8,128)(2,1)S(1)}, u32[]{:S(2)}, u32[]{:S(2)}) collective-permute-start(bf16[256,512]{1,0:T(8,128)(2,1)S(1)} %attend.11.refs_0_), channel_id=1, source_target_pairs={{0,1},{1,0},{2,3},{3,2},{4,5},{5,4},{6,7},{7,6},{8,9},{9,8},{10,11... | collective-permute-start | bytes 786440 | tf_op jit(solution)/shard_map/ppermute | solution.py:483
  95.4 8.4 %collective-permute-start.30 = (bf16[128,512]{1,0:T(8,128)(2,1)S(1)}, bf16[128,512]{1,0:T(8,128)(2,1)S(1)}, u32[]{:S(2)}, u32[]{:S(2)}) collective-permute-start(bf16[128,512]{1,0:T(8,128)(2,1)S(1)} %slice.27), channel_id=1, source_target_pairs={{0,2},{1,3},{2,0},{3,1},{4,6},{5,7},{6,4},{7,5},{8,10},{9,11},{10,... | collective-permute-start | bytes 393224 | tf_op jit(solution)/shard_map/ppermute | solution.py:483
  97.0 6.9 %collective-permute-start.29 = (bf16[128,512]{1,0:T(8,128)(2,1)S(1)}, bf16[128,512]{1,0:T(8,128)(2,1)S(1)}, u32[]{:S(2)}, u32[]{:S(2)}) collective-permute-start(bf16[128,512]{1,0:T(8,128)(2,1)S(1)} %slice.26), channel_id=1, source_target_pairs={{0,4},{1,5},{2,6},{3,7},{4,0},{5,1},{6,2},{7,3},{8,12},{9,13},{10,... | collective-permute-start | bytes 393224 | tf_op jit(solution)/shard_map/ppermute | solution.py:483
  97.3 7.0 %collective-permute-start.26 = (bf16[256,512]{1,0:T(8,128)(2,1)S(1)}, bf16[256,512]{1,0:T(8,128)(2,1)S(1)}, u32[]{:S(2)}, u32[]{:S(2)}) collective-permute-start(bf16[256,512]{1,0:T(8,128)(2,1)S(1)} %collective-permute-done.25.refs_2_), channel_id=1, source_target_pairs={{0,1},{1,0},{2,3},{3,2},{4,5},{5,4},{6,7},{7,6},{8,9},{9,8},{10,11... | collective-permute-start | bytes 786440 | tf_op jit(solution)/shard_map/ppermute | solution.py:483
  97.3 7.0 %collective-permute-start.28 = (bf16[256,512]{1,0:T(8,128)(2,1)S(1)}, bf16[256,512]{1,0:T(8,128)(2,1)S(1)}, u32[]{:S(2)}, u32[]{:S(2)}) collective-permute-start(bf16[256,512]{1,0:T(8,128)(2,1)S(1)} %collective-permute-done.27.refs_4_), channel_id=1, source_target_pairs={{0,1},{1,0},{2,3},{3,2},{4,5},{5,4},{6,7},{7,6},{8,9},{9,8},{10,11... | collective-permute-start | bytes 786440 | tf_op jit(solution)/shard_map/ppermute | solution.py:483
  103.8 1.4 %collective-permute-start.32 = (bf16[128,512]{1,0:T(8,128)(2,1)S(1)}, bf16[128,512]{1,0:T(8,128)(2,1)S(1)}, u32[]{:S(2)}, u32[]{:S(2)}) collective-permute-start(bf16[128,512]{1,0:T(8,128)(2,1)S(1)} %collective-permute-done.30.refs_7_), channel_id=1, source_target_pairs={{0,1},{1,0},{2,3},{3,2},{4,5},{5,4},{6,7},{7,6},{8,9},{9,8},{10,11... | collective-permute-start | bytes 393224 | tf_op jit(solution)/shard_map/ppermute | solution.py:483
  103.9 1.5 %collective-permute-start.31 = (bf16[128,512]{1,0:T(8,128)(2,1)S(1)}, bf16[128,512]{1,0:T(8,128)(2,1)S(1)}, u32[]{:S(2)}, u32[]{:S(2)}) collective-permute-start(bf16[128,512]{1,0:T(8,128)(2,1)S(1)} %collective-permute-done.29.refs_6_), channel_id=1, source_target_pairs={{0,1},{1,0},{2,3},{3,2},{4,5},{5,4},{6,7},{7,6},{8,9},{9,8},{10,11... | collective-permute-start | bytes 393224 | tf_op jit(solution)/shard_map/ppermute | solution.py:483
  111.3 1.2 %collective-permute-start.33 = (f32[8,512]{1,0:T(8,128)S(1)}, f32[8,512]{1,0:T(8,128)S(1)}, u32[]{:S(2)}, u32[]{:S(2)}) collective-permute-start(f32[8,512]{1,0:T(8,128)S(1)} %constant_dynamic-update-slice_fusion), channel_id=1, source_target_pairs={{0,1},{1,0},{2,3},{3,2},{4,5},{5,4},{6,7},{7,6},{8,9},{9,8},{10,11... | collective-permute-start | bytes 49160 | tf_op jit(solution)/shard_map/ppermute | solution.py:483
  112.5 3.7 %collective-permute-start.34 = (f32[8,512]{1,0:T(8,128)S(1)}, f32[8,512]{1,0:T(8,128)S(1)}, u32[]{:S(2)}, u32[]{:S(2)}) collective-permute-start(f32[8,512]{1,0:T(8,128)S(1)} %add.4.refs_2_), channel_id=1, source_target_pairs={{0,2},{1,3},{2,0},{3,1},{4,6},{5,7},{6,4},{7,5},{8,10},{9,11},{10,... | collective-permute-start | bytes 49160 | tf_op jit(solution)/shard_map/ppermute | solution.py:483
  113.3 3.7 %collective-permute-start.35 = (f32[8,512]{1,0:T(8,128)S(1)}, f32[8,512]{1,0:T(8,128)S(1)}, u32[]{:S(2)}, u32[]{:S(2)}) collective-permute-start(f32[8,512]{1,0:T(8,128)S(1)} %add.4.refs_2_), channel_id=1, source_target_pairs={{0,4},{1,5},{2,6},{3,7},{4,0},{5,1},{6,2},{7,3},{8,12},{9,13},{10,... | collective-permute-start | bytes 49160 | tf_op jit(solution)/shard_map/ppermute | solution.py:483
  114.6 4.6 %collective-permute-start.36 = (f32[8,512]{1,0:T(8,128)S(1)}, f32[8,512]{1,0:T(8,128)S(1)}, u32[]{:S(2)}, u32[]{:S(2)}) collective-permute-start(f32[8,512]{1,0:T(8,128)S(1)} %add.4.refs_2_), channel_id=1, source_target_pairs={{0,6},{1,7},{2,4},{3,5},{4,2},{5,3},{6,0},{7,1},{8,14},{9,15},{10,... | collective-permute-start | bytes 49160 | tf_op jit(solution)/shard_map/ppermute | solution.py:483

commit v11 on v8

--- a/solution.py
+++ b/solution.py
@@ -541,6 +541,7 @@
     signs = (2 * sign_bits - 1).astype(jnp.float32)
     gain = norm_gain.reshape(-1, GROUP)
 
+    gain, order, ctx_at, flips = lax.optimization_barrier((gain, order, ctx_at, flips))
     clipped = pre(hidden_in, gain)
 
     kv_cols = w_key.shape[1]

time: 121 us -> 121 us (level)
  waiting for transfers between devices: 49.9 us -> 53.2 us
  starting transfers between devices: 27 us -> 25.7 us
    ppermute x31, waiting for transfers between devices: 39.2 us -> 42.6 us  [swap(): return lax.ppermute(x, 'tp', [(i, i ^ mask) for i in range(count)])]
    ppermute x31, starting transfers between devices: 19.3 us -> 18 us  [swap(): return lax.ppermute(x, 'tp', [(i, i ^ mask) for i in range(count)])]
  transfers between devices with their start and end apart: 37 -> 37, of which waited for: 22 -> 23; matrix products, arithmetic and copies ran while one was open for 1% -> 0% of each run, Pallas kernels for 24% -> 23%
where the time goes in v11:
time: 121 us; the launch traced here: 120 us
  waiting for transfers between devices  53.2 us (44%)
  Pallas kernels  40.5 us (33%)
  starting transfers between devices  25.7 us (21%)
    ppermute x31, waiting for transfers between devices, swap(): return lax.ppermute(x, 'tp', [(i, i ^ mask) for i in range(count)])  42.6 us
    ppermute x31, starting transfers between devices, swap(): return lax.ppermute(x, 'tp', [(i, i ^ mask) for i in range(count)])  18 us
    pallas_call x2, Pallas kernels, project_out(): pl.pallas_call(functools.partial(out_kernel, counts, steps, chunk), in_sp...  11.8 us
    ppermute x6, waiting for transfers between devices, send_up(): return lax.ppermute(x, 'ctx', [(i, i + 1) for i in range(first, count - 1)])  10.6 us
    pallas_call x6, Pallas kernels, attend(): pl.pallas_call(kernel, in_specs=[IN_SMEM] + [IN_VMEM] * (len(args) - 1),...  10.2 us
    pallas_call x2, Pallas kernels, proj(): pl.pallas_call(functools.partial(proj_kernel, counts, masks, not state, e...  8 us
    ppermute x6, starting transfers between devices, send_up(): return lax.ppermute(x, 'ctx', [(i, i + 1) for i in range(first, count - 1)])  7.71 us
    pallas_call x1, Pallas kernels, load(): pl.pallas_call(functools.partial(load_kernel, count), in_specs=[IN_HBM] *...  7.19 us
  transfers between devices with their start and end apart: 37, of which 23 were waited for; matrix products, arithmetic and copies ran while one was open for 0% of the time, Pallas kernels for 23%

profile of v11, /device:TPU:24, one launch (start us, length us, event | category | flops | bytes accessed | tf_op | source)
XLA Modules:
  0.0 120.4 jit_solution(18258615941487617401)
XLA Ops:
  0.7 2.1 %pre.1.refs_0_ = bf16[528,1024]{1,0:T(8,128)(2,1)S(1)} custom-call(bf16[512,1024]{1,0:T(8,128)(2,1)} %h_hbm.1, bf16[8,128]{1,0:T(8,128)(2,1)} %bitcast.3), custom_call_target="tpu_custom_call" | custom-call | flops 4194304 | bytes 2097152 | tf_op jit(solution)/shard_map/pre/pallas_call | solution.py:87
  2.7 0.1 collective-permute-start.1
  2.8 1.6 %collective-permute-start.3 = (bf16[528,1024]{1,0:T(8,128)(2,1)S(1)}, bf16[528,1024]{1,0:T(8,128)(2,1)S(1)}, u32[]{:S(2)}, u32[]{:S(2)}) collective-permute-start(bf16[528,1024]{1,0:T(8,128)(2,1)S(1)} %pre.1.refs_0_), channel_id=1, source_target_pairs={{0,4},{1,5},{2,6},{3,7},{4,0},{5,1},{6,2},{7,3},{8,12},{9,13},{10,... | collective-permute-start | bytes 3244040 | tf_op jit(solution)/shard_map/ppermute | solution.py:483
  4.4 1.5 %collective-permute-start = (bf16[528,1024]{1,0:T(8,128)(2,1)S(1)}, bf16[528,1024]{1,0:T(8,128)(2,1)S(1)}, u32[]{:S(2)}, u32[]{:S(2)}) collective-permute-start(bf16[528,1024]{1,0:T(8,128)(2,1)S(1)} %pre.1.refs_0_), channel_id=1, source_target_pairs={{0,2},{1,3},{2,0},{3,1},{4,6},{5,7},{6,4},{7,5},{8,10},{9,11},{10,... | collective-permute-start | bytes 3244040 | tf_op jit(solution)/shard_map/ppermute | solution.py:483
  5.9 7.2 %load.1 = (bf16[8192,512]{1,0:T(8,128)(2,1)S(1)}, bf16[8192,128]{1,0:T(8,128)(2,1)S(1)}, bf16[8192,128]{1,0:T(8,128)(2,1)S(1)}, bf16[4096,1024]{1,0:T(8,128)(2,1)S(1)}) custom-call(bf16[8192,512]{1,0:T(8,128)(2,1)} %refs_0_, bf16[8192,128]{1,0:T(8,128)(2,1)} %refs_1_.1, bf16[8192,128]{1,0:T(8,128)(2,1)} %refs_2_.1, bf16[4096,1024]{1,0:T(8,128)(2,1)} %refs_3_.1), custom_call_target="tpu_custom_call" | custom-call | bytes 41943040 | tf_op jit(solution)/shard_map/load/pallas_call | solution.py:121
  13.1 16.0 %collective-permute-done.3.refs_4_ = bf16[528,1024]{1,0:T(8,128)(2,1)S(1)} collective-permute-done((bf16[528,1024]{1,0:T(8,128)(2,1)S(1)}, bf16[528,1024]{1,0:T(8,128)(2,1)S(1)}, u32[]{:S(2)}, u32[]{:S(2)}) %collective-permute-start.3) | collective-permute-done | bytes 1081376 | tf_op jit(solution)/shard_map/ppermute | solution.py:483
  29.1 1.2 %collective-permute-done.refs_2_ = bf16[528,1024]{1,0:T(8,128)(2,1)S(1)} collective-permute-done((bf16[528,1024]{1,0:T(8,128)(2,1)S(1)}, bf16[528,1024]{1,0:T(8,128)(2,1)S(1)}, u32[]{:S(2)}, u32[]{:S(2)}) %collective-permute-start) | collective-permute-done | bytes 1081376 | tf_op jit(solution)/shard_map/ppermute | solution.py:483
  30.4 1.6 %collective-permute-start.4 = (bf16[272,1024]{1,0:T(8,128)(2,1)S(1)}, bf16[272,1024]{1,0:T(8,128)(2,1)S(1)}, u32[]{:S(2)}, u32[]{:S(2)}) collective-permute-start(bf16[272,1024]{1,0:T(8,128)(2,1)S(1)} %slice.19), channel_id=1, source_target_pairs={{0,2},{1,3},{2,0},{3,1},{4,6},{5,7},{6,4},{7,5},{8,10},{9,11},{10,... | collective-permute-start | bytes 1671176 | tf_op jit(solution)/shard_map/ppermute | solution.py:483
  32.0 0.9 collective-permute-start.2
  32.8 0.5 collective-permute-done.5.refs_3_
  33.3 5.6 %proj.2 = (f32[512,512]{1,0:T(8,128)S(1)}, f32[512,128]{1,0:T(8,128)S(1)}, f32[512,128]{1,0:T(8,128)S(1)}, f32[8,512]{1,0:T(8,128)S(1)}) custom-call(s32[8]{0:T(128)S(1)} %get-tuple-element.47.order_ref, bf16[528,1024]{1,0:T(8,128)(2,1)S(1)} %pre.1.refs_0_, bf16[528,1024]{1,0:T(8,128)(2,1)S(1)} %collective-permute-done.1.refs_1_, ...), custom_call_target="tpu_custom_call" | custom-call | flops 4831838208 | bytes 15728640 | tf_op jit(solution)/shard_map/proj/pallas_call | solution.py:220
  38.9 6.5 %collective-permute-done.4.refs_1_ = bf16[272,1024]{1,0:T(8,128)(2,1)S(1)} collective-permute-done((bf16[272,1024]{1,0:T(8,128)(2,1)S(1)}, bf16[272,1024]{1,0:T(8,128)(2,1)S(1)}, u32[]{:S(2)}, u32[]{:S(2)}) %collective-permute-start.4) | collective-permute-done | bytes 557088 | tf_op jit(solution)/shard_map/ppermute | solution.py:483
  45.5 0.6 collective-permute-done.2.refs_0_
  46.1 2.1 %collective-permute-done.7.refs_2_ = bf16[256,1024]{1,0:T(8,128)(2,1)S(1)} collective-permute-done((bf16[256,1024]{1,0:T(8,128)(2,1)S(1)}, bf16[256,1024]{1,0:T(8,128)(2,1)S(1)}, u32[]{:S(2)}, u32[]{:S(2)}) %collective-permute-start.7) | collective-permute-done | bytes 524320 | tf_op jit(solution)/shard_map/ppermute | solution.py:483
  48.2 2.4 %proj.3 = (bf16[512,512]{1,0:T(8,128)(2,1)S(1)}, bf16[256,256]{1,0:T(8,128)(2,1)S(1)}, bf16[256,256]{1,0:T(8,128)(2,1)S(1)}) custom-call(s32[8]{0:T(128)S(1)} %get-tuple-element.47.order_ref, bf16[256,1024]{1,0:T(8,128)(2,1)S(1)} %collective-permute-done.2.refs_0_, bf16[272,1024]{1,0:T(8,128)(2,1)S(1)} %collective-permute-done.4.refs_1_, ...), custom_call_target="tpu_custom_call" | custom-call | flops 1610612736 | bytes 5242880 | tf_op jit(solution)/shard_map/proj/pallas_call | solution.py:220
  50.6 1.3 %collective-permute-start.11 = (bf16[256,256]{1,0:T(8,128)(2,1)S(1)}, bf16[256,256]{1,0:T(8,128)(2,1)S(1)}, u32[]{:S(2)}, u32[]{:S(2)}) collective-permute-start(bf16[256,256]{1,0:T(8,128)(2,1)S(1)} %get-tuple-element.63.refs_1_), channel_id=1, source_target_pairs={{0,8},{8,16},{16,24},{1,9},{9,17},{17,25},{2,10},{10,18},{18,26},{... | collective-permute-start | bytes 393224 | tf_op jit(solution)/shard_map/ppermute | solution.py:488
  51.9 1.3 %collective-permute-start.9 = (bf16[256,256]{1,0:T(8,128)(2,1)S(1)}, bf16[256,256]{1,0:T(8,128)(2,1)S(1)}, u32[]{:S(2)}, u32[]{:S(2)}) collective-permute-start(bf16[256,256]{1,0:T(8,128)(2,1)S(1)} %get-tuple-element.62.refs_0_), channel_id=1, source_target_pairs={{0,8},{8,16},{16,24},{1,9},{9,17},{17,25},{2,10},{10,18},{18,26},{... | collective-permute-start | bytes 393224 | tf_op jit(solution)/shard_map/ppermute | solution.py:488
  53.2 5.6 %collective-permute-done.11.refs_2_.refs_3_ = bf16[256,256]{1,0:T(8,128)(2,1)S(1)} collective-permute-done((bf16[256,256]{1,0:T(8,128)(2,1)S(1)}, bf16[256,256]{1,0:T(8,128)(2,1)S(1)}, u32[]{:S(2)}, u32[]{:S(2)}) %collective-permute-start.11) | collective-permute-done | bytes 131104 | tf_op jit(solution)/shard_map/ppermute | solution.py:488
  58.8 1.3 %collective-permute-start.12 = (bf16[256,256]{1,0:T(8,128)(2,1)S(1)}, bf16[256,256]{1,0:T(8,128)(2,1)S(1)}, u32[]{:S(2)}, u32[]{:S(2)}) collective-permute-start(bf16[256,256]{1,0:T(8,128)(2,1)S(1)} %collective-permute-done.11.refs_2_.refs_3_), channel_id=1, source_target_pairs={{8,16},{16,24},{9,17},{17,25},{10,18},{18,26},{11,19},{19,27},{12,... | collective-permute-start | bytes 393224 | tf_op jit(solution)/shard_map/ppermute | solution.py:488
  60.1 0.7 collective-permute-done.9.refs_1_.refs_2_
  60.8 1.3 %collective-permute-start.10 = (bf16[256,256]{1,0:T(8,128)(2,1)S(1)}, bf16[256,256]{1,0:T(8,128)(2,1)S(1)}, u32[]{:S(2)}, u32[]{:S(2)}) collective-permute-start(bf16[256,256]{1,0:T(8,128)(2,1)S(1)} %collective-permute-done.9.refs_1_.refs_2_), channel_id=1, source_target_pairs={{8,16},{16,24},{9,17},{17,25},{10,18},{18,26},{11,19},{19,27},{12,... | collective-permute-start | bytes 393224 | tf_op jit(solution)/shard_map/ppermute | solution.py:488
  62.1 1.9 %attend.6 = (f32[8,256]{1,0:T(8,128)S(1)}, f32[8,256]{1,0:T(8,128)S(1)}, f32[4,128,256]{2,1,0:T(8,128)S(1)}) custom-call(s32[1]{0:T(128)} %bitcast.1.me_ref, bf16[512,512]{1,0:T(8,128)(2,1)S(1)} %get-tuple-element.72.q_ref, bf16[256,256]{1,0:T(8,128)(2,1)S(1)} %get-tuple-element.62.refs_0_, bf16[256,256]{1,0:T(8,128)(2,1)S(1)} %collective-permute-done.9.refs_1_.refs_2_, ...), custom_call_target="tpu_custom_call" | custom-call | flops 402653184 | bytes 393216 | tf_op jit(solution)/shard_map/attend/pallas_call | solution.py:329
  64.0 2.4 %attend.8 = (f32[8,256]{1,0:T(8,128)S(1)}, f32[8,256]{1,0:T(8,128)S(1)}, f32[4,128,256]{2,1,0:T(8,128)S(1)}) custom-call(s32[1]{0:T(128)} %bitcast.1.me_ref, bf16[512,512]{1,0:T(8,128)(2,1)S(1)} %get-tuple-element.72.q_ref, bf16[256,256]{1,0:T(8,128)(2,1)S(1)} %get-tuple-element.62.refs_0_, bf16[256,256]{1,0:T(8,128)(2,1)S(1)} %get-tuple-element.63.refs_1_, ...), custom_call_target="tpu_custom_call" | custom-call | flops 536870912 | bytes 524288 | tf_op jit(solution)/shard_map/attend/pallas_call | solution.py:329
  66.5 0.4 collective-permute-done.12.refs_1_
  66.8 1.3 %collective-permute-start.14 = (bf16[256,256]{1,0:T(8,128)(2,1)S(1)}, bf16[256,256]{1,0:T(8,128)(2,1)S(1)}, u32[]{:S(2)}, u32[]{:S(2)}) collective-permute-start(bf16[256,256]{1,0:T(8,128)(2,1)S(1)} %collective-permute-done.12.refs_1_), channel_id=1, source_target_pairs={{16,24},{17,25},{18,26},{19,27},{20,28},{21,29},{22,30},{23,31}} | collective-permute-start | bytes 393224 | tf_op jit(solution)/shard_map/ppermute | solution.py:488
  68.1 0.4 collective-permute-done.10.refs_0_
  68.5 1.3 %collective-permute-start.13 = (bf16[256,256]{1,0:T(8,128)(2,1)S(1)}, bf16[256,256]{1,0:T(8,128)(2,1)S(1)}, u32[]{:S(2)}, u32[]{:S(2)}) collective-permute-start(bf16[256,256]{1,0:T(8,128)(2,1)S(1)} %collective-permute-done.10.refs_0_), channel_id=1, source_target_pairs={{16,24},{17,25},{18,26},{19,27},{20,28},{21,29},{22,30},{23,31}} | collective-permute-start | bytes 393224 | tf_op jit(solution)/shard_map/ppermute | solution.py:488
  69.8 1.3 %attend.9 = (f32[8,256]{1,0:T(8,128)S(1)}, f32[8,256]{1,0:T(8,128)S(1)}, f32[4,128,256]{2,1,0:T(8,128)S(1)}) custom-call(s32[1]{0:T(128)} %bitcast.1.me_ref, bf16[512,512]{1,0:T(8,128)(2,1)S(1)} %get-tuple-element.72.q_ref, bf16[256,256]{1,0:T(8,128)(2,1)S(1)} %collective-permute-done.10.refs_0_, bf16[256,256]{1,0:T(8,128)(2,1)S(1)} %collective-permute-done.12.refs_1_, ...), custom_call_target="tpu_custom_call" | custom-call | flops 268435456 | bytes 262144 | tf_op jit(solution)/shard_map/attend/pallas_call | solution.py:329
  71.1 1.5 %attend.7 = (f32[8,256]{1,0:T(8,128)S(1)}, f32[8,256]{1,0:T(8,128)S(1)}, f32[4,128,256]{2,1,0:T(8,128)S(1)}) custom-call(s32[1]{0:T(128)} %bitcast.1.me_ref, bf16[512,512]{1,0:T(8,128)(2,1)S(1)} %get-tuple-element.72.q_ref, bf16[256,256]{1,0:T(8,128)(2,1)S(1)} %collective-permute-done.10.refs_0_, bf16[256,256]{1,0:T(8,128)(2,1)S(1)} %collective-permute-done.12.refs_1_, ...), custom_call_target="tpu_custom_call" | custom-call | flops 268435456 | bytes 262144 | tf_op jit(solution)/shard_map/attend/pallas_call | solution.py:329
  72.7 2.1 %collective-permute-done.14.refs_1_ = bf16[256,256]{1,0:T(8,128)(2,1)S(1)} collective-permute-done((bf16[256,256]{1,0:T(8,128)(2,1)S(1)}, bf16[256,256]{1,0:T(8,128)(2,1)S(1)}, u32[]{:S(2)}, u32[]{:S(2)}) %collective-permute-start.14) | collective-permute-done | bytes 131104 | tf_op jit(solution)/shard_map/ppermute | solution.py:488
  74.7 1.4 %collective-permute-done.13.refs_0_ = bf16[256,256]{1,0:T(8,128)(2,1)S(1)} collective-permute-done((bf16[256,256]{1,0:T(8,128)(2,1)S(1)}, bf16[256,256]{1,0:T(8,128)(2,1)S(1)}, u32[]{:S(2)}, u32[]{:S(2)}) %collective-permute-start.13) | collective-permute-done | bytes 131104 | tf_op jit(solution)/shard_map/ppermute | solution.py:488
  76.1 1.5 %attend.10.refs_0_ = bf16[256,512]{1,0:T(8,128)(2,1)S(1)} custom-call(s32[1]{0:T(128)} %bitcast.1.me_ref, bf16[512,512]{1,0:T(8,128)(2,1)S(1)} %get-tuple-element.72.q_ref, bf16[256,256]{1,0:T(8,128)(2,1)S(1)} %collective-permute-done.13.refs_0_, bf16[256,256]{1,0:T(8,128)(2,1)S(1)} %collective-permute-done.14.refs_1_, ...), custom_call_target="tpu_custom_call" | custom-call | flops 268435456 | bytes 262144 | tf_op jit(solution)/shard_map/attend/pallas_call | solution.py:329
  77.7 1.6 %collective-permute-start.16 = (bf16[256,512]{1,0:T(8,128)(2,1)S(1)}, bf16[256,512]{1,0:T(8,128)(2,1)S(1)}, u32[]{:S(2)}, u32[]{:S(2)}) collective-permute-start(bf16[256,512]{1,0:T(8,128)(2,1)S(1)} %attend.10.refs_0_), channel_id=1, source_target_pairs={{0,2},{1,3},{2,0},{3,1},{4,6},{5,7},{6,4},{7,5},{8,10},{9,11},{10,... | collective-permute-start | bytes 786440 | tf_op jit(solution)/shard_map/ppermute | solution.py:483
  79.2 0.5 collective-permute-start.18
  79.7 1.5 %attend.11.refs_0_ = bf16[256,512]{1,0:T(8,128)(2,1)S(1)} custom-call(s32[1]{0:T(128)} %bitcast.1.me_ref, bf16[512,512]{1,0:T(8,128)(2,1)S(1)} %get-tuple-element.72.q_ref, bf16[256,256]{1,0:T(8,128)(2,1)S(1)} %collective-permute-done.13.refs_0_, bf16[256,256]{1,0:T(8,128)(2,1)S(1)} %collective-permute-done.14.refs_1_, ...), custom_call_target="tpu_custom_call" | custom-call | flops 268435456 | bytes 262144 | tf_op jit(solution)/shard_map/attend/pallas_call | solution.py:329
  81.2 1.6 %collective-permute-start.27 = (bf16[256,512]{1,0:T(8,128)(2,1)S(1)}, bf16[256,512]{1,0:T(8,128)(2,1)S(1)}, u32[]{:S(2)}, u32[]{:S(2)}) collective-permute-start(bf16[256,512]{1,0:T(8,128)(2,1)S(1)} %attend.11.refs_0_), channel_id=1, source_target_pairs={{0,4},{1,5},{2,6},{3,7},{4,0},{5,1},{6,2},{7,3},{8,12},{9,13},{10,... | collective-permute-start | bytes 786440 | tf_op jit(solution)/shard_map/ppermute | solution.py:483
  82.8 0.5 collective-permute-start.25
  83.4 2.3 %collective-permute-done.16.refs_2_ = bf16[256,512]{1,0:T(8,128)(2,1)S(1)} collective-permute-done((bf16[256,512]{1,0:T(8,128)(2,1)S(1)}, bf16[256,512]{1,0:T(8,128)(2,1)S(1)}, u32[]{:S(2)}, u32[]{:S(2)}) %collective-permute-start.16) | collective-permute-done | bytes 262176 | tf_op jit(solution)/shard_map/ppermute | solution.py:483
  85.7 0.6 collective-permute-start.20
  86.2 2.2 %collective-permute-done.18.refs_4_ = bf16[256,512]{1,0:T(8,128)(2,1)S(1)} collective-permute-done((bf16[256,512]{1,0:T(8,128)(2,1)S(1)}, bf16[256,512]{1,0:T(8,128)(2,1)S(1)}, u32[]{:S(2)}, u32[]{:S(2)}) %collective-permute-start.18) | collective-permute-done | bytes 262176 | tf_op jit(solution)/shard_map/ppermute | solution.py:483
  88.5 0.6 collective-permute-start.21
  89.1 3.5 %collective-permute-done.27.refs_4_ = bf16[256,512]{1,0:T(8,128)(2,1)S(1)} collective-permute-done((bf16[256,512]{1,0:T(8,128)(2,1)S(1)}, bf16[256,512]{1,0:T(8,128)(2,1)S(1)}, u32[]{:S(2)}, u32[]{:S(2)}) %collective-permute-start.27) | collective-permute-done | bytes 262176 | tf_op jit(solution)/shard_map/ppermute | solution.py:483
  92.5 0.5 collective-permute-start.19
  93.0 0.9 collective-permute-done.20.refs_6_
  93.9 0.5 collective-permute-start.23
  94.6 0.7 collective-permute-done.22.refs_8_
  95.3 0.5 collective-permute-start.30
  95.8 0.5 collective-permute-start.29
  96.3 0.5 collective-permute-start.28
  96.9 5.9 %project_out.2 = (f32[256,1024]{1,0:T(8,128)S(1)}, f32[8,256]{1,0:T(8,128)S(1)}) custom-call(f32[8]{0:T(128)S(1)} %get-tuple-element.45.sign_ref, bf16[512,1024]{1,0:T(8,128)(2,1)S(1)} %copy-done, bf16[256,512]{1,0:T(8,128)(2,1)S(1)} %attend.10.refs_0_, bf16[256,512]{1,0:T(8,128)(2,1)S(1)} %collective-permute-done.15.refs_1_, ...), custom_call_target="tpu_custom_call" | custom-call | flops 2147483648 | bytes 12058624 | tf_op jit(solution)/shard_map/project_out/pallas_call | solution.py:424
  102.8 0.1 collective-permute-start.32
  102.9 0.4 collective-permute-start.31
  103.3 0.8 collective-permute-done.32.refs_9_
  104.2 0.2 collective-permute-done.31.refs_8_
  104.3 5.9 %project_out.3 = (f32[256,1024]{1,0:T(8,128)S(1)}, f32[8,256]{1,0:T(8,128)S(1)}) custom-call(f32[8]{0:T(128)S(1)} %get-tuple-element.45.sign_ref, bf16[512,1024]{1,0:T(8,128)(2,1)S(1)} %copy-done, bf16[256,512]{1,0:T(8,128)(2,1)S(1)} %attend.11.refs_0_, bf16[256,512]{1,0:T(8,128)(2,1)S(1)} %collective-permute-done.24.refs_1_, ...), custom_call_target="tpu_custom_call" | custom-call | flops 2147483648 | bytes 12058624 | tf_op jit(solution)/shard_map/project_out/pallas_call | solution.py:424
  110.2 0.4 collective-permute-start.33
  110.6 0.9 collective-permute-done.33
  111.5 1.5 %collective-permute-start.34 = (f32[8,512]{1,0:T(8,128)S(1)}, f32[8,512]{1,0:T(8,128)S(1)}, u32[]{:S(2)}, u32[]{:S(2)}) collective-permute-start(f32[8,512]{1,0:T(8,128)S(1)} %add.4.refs_2_), channel_id=1, source_target_pairs={{0,2},{1,3},{2,0},{3,1},{4,6},{5,7},{6,4},{7,5},{8,10},{9,11},{10,... | collective-permute-start | bytes 49160 | tf_op jit(solution)/shard_map/ppermute | solution.py:483
  113.0 1.5 %collective-permute-start.35 = (f32[8,512]{1,0:T(8,128)S(1)}, f32[8,512]{1,0:T(8,128)S(1)}, u32[]{:S(2)}, u32[]{:S(2)}) collective-permute-start(f32[8,512]{1,0:T(8,128)S(1)} %add.4.refs_2_), channel_id=1, source_target_pairs={{0,4},{1,5},{2,6},{3,7},{4,0},{5,1},{6,2},{7,3},{8,12},{9,13},{10,... | collective-permute-start | bytes 49160 | tf_op jit(solution)/shard_map/ppermute | solution.py:483
  114.5 0.5 collective-permute-start.36
  115.0 0.2 collective-permute-done.34.refs_3_
  115.2 1.5 %collective-permute-done.35.refs_4_ = f32[8,512]{1,0:T(8,128)S(1)} collective-permute-done((f32[8,512]{1,0:T(8,128)S(1)}, f32[8,512]{1,0:T(8,128)S(1)}, u32[]{:S(2)}, u32[]{:S(2)}) %collective-permute-start.35) | collective-permute-done | bytes 16416 | tf_op jit(solution)/shard_map/ppermute | solution.py:483
  116.7 2.4 %collective-permute-done.36.refs_5_ = f32[8,512]{1,0:T(8,128)S(1)} collective-permute-done((f32[8,512]{1,0:T(8,128)S(1)}, f32[8,512]{1,0:T(8,128)S(1)}, u32[]{:S(2)}, u32[]{:S(2)}) %collective-permute-start.36) | collective-permute-done | bytes 16416 | tf_op jit(solution)/shard_map/ppermute | solution.py:483
  119.1 1.3 %final.1 = (bf16[512,1024]{1,0:T(8,128)(2,1)}, f32[1,512]{1,0:T(1,128)}) custom-call(f32[256,1024]{1,0:T(8,128)S(1)} %get-tuple-element.78.refs_0_, f32[256,1024]{1,0:T(8,128)S(1)} %get-tuple-element.83.refs_1_, f32[8,512]{1,0:T(8,128)S(1)} %add.4.refs_2_, f32[8,512]{1,0:T(8,128)S(1)} %collective-permute-done.34.refs_3_, ...), custom_call_target="tpu_custom_call" | custom-call | flops 1048576 | bytes 3145728 | tf_op jit(solution)/shard_map/final/pallas_call | solution.py:466
  (38 shorter events, 0.3 us)
Async XLA Ops:
  0.6 5.3 %copy-start.1 = (s32[4,128]{1,0:T(4,128)S(1)}, s32[4,128]{1,0:T(4,128)}, u32[]{:S(2)}) copy-start(s32[4,128]{1,0:T(4,128)} %param.13) | copy-start | bytes 6148
  2.7 3.2 %collective-permute-start.1 = (bf16[528,1024]{1,0:T(8,128)(2,1)S(1)}, bf16[528,1024]{1,0:T(8,128)(2,1)S(1)}, u32[]{:S(2)}, u32[]{:S(2)}) collective-permute-start(bf16[528,1024]{1,0:T(8,128)(2,1)S(1)} %pre.1.refs_0_), channel_id=1, source_target_pairs={{0,1},{1,0},{2,3},{3,2},{4,5},{5,4},{6,7},{7,6},{8,9},{9,8},{10,11... | collective-permute-start | bytes 3244040 | tf_op jit(solution)/shard_map/ppermute | solution.py:483
  2.8 26.3 %collective-permute-start.3 = (bf16[528,1024]{1,0:T(8,128)(2,1)S(1)}, bf16[528,1024]{1,0:T(8,128)(2,1)S(1)}, u32[]{:S(2)}, u32[]{:S(2)}) collective-permute-start(bf16[528,1024]{1,0:T(8,128)(2,1)S(1)} %pre.1.refs_0_), channel_id=1, source_target_pairs={{0,4},{1,5},{2,6},{3,7},{4,0},{5,1},{6,2},{7,3},{8,12},{9,13},{10,... | collective-permute-start | bytes 3244040 | tf_op jit(solution)/shard_map/ppermute | solution.py:483
  4.4 25.9 %collective-permute-start = (bf16[528,1024]{1,0:T(8,128)(2,1)S(1)}, bf16[528,1024]{1,0:T(8,128)(2,1)S(1)}, u32[]{:S(2)}, u32[]{:S(2)}) collective-permute-start(bf16[528,1024]{1,0:T(8,128)(2,1)S(1)} %pre.1.refs_0_), channel_id=1, source_target_pairs={{0,2},{1,3},{2,0},{3,1},{4,6},{5,7},{6,4},{7,5},{8,10},{9,11},{10,... | collective-permute-start | bytes 3244040 | tf_op jit(solution)/shard_map/ppermute | solution.py:483
  29.1 3.7 %collective-permute-start.6 = (bf16[528,1024]{1,0:T(8,128)(2,1)S(1)}, bf16[528,1024]{1,0:T(8,128)(2,1)S(1)}, u32[]{:S(2)}, u32[]{:S(2)}) collective-permute-start(bf16[528,1024]{1,0:T(8,128)(2,1)S(1)} %collective-permute-done.3.refs_4_), channel_id=1, source_target_pairs={{0,1},{1,0},{2,3},{3,2},{4,5},{5,4},{6,7},{7,6},{8,9},{9,8},{10,11... | collective-permute-start | bytes 3244040 | tf_op jit(solution)/shard_map/ppermute | solution.py:483
  30.3 3.0 %collective-permute-start.5 = (bf16[528,1024]{1,0:T(8,128)(2,1)S(1)}, bf16[528,1024]{1,0:T(8,128)(2,1)S(1)}, u32[]{:S(2)}, u32[]{:S(2)}) collective-permute-start(bf16[528,1024]{1,0:T(8,128)(2,1)S(1)} %collective-permute-done.refs_2_), channel_id=1, source_target_pairs={{0,1},{1,0},{2,3},{3,2},{4,5},{5,4},{6,7},{7,6},{8,9},{9,8},{10,11... | collective-permute-start | bytes 3244040 | tf_op jit(solution)/shard_map/ppermute | solution.py:483
  30.4 15.1 %collective-permute-start.4 = (bf16[272,1024]{1,0:T(8,128)(2,1)S(1)}, bf16[272,1024]{1,0:T(8,128)(2,1)S(1)}, u32[]{:S(2)}, u32[]{:S(2)}) collective-permute-start(bf16[272,1024]{1,0:T(8,128)(2,1)S(1)} %slice.19), channel_id=1, source_target_pairs={{0,2},{1,3},{2,0},{3,1},{4,6},{5,7},{6,4},{7,5},{8,10},{9,11},{10,... | collective-permute-start | bytes 1671176 | tf_op jit(solution)/shard_map/ppermute | solution.py:483
  32.0 14.1 %collective-permute-start.2 = (bf16[256,1024]{1,0:T(8,128)(2,1)S(1)}, bf16[256,1024]{1,0:T(8,128)(2,1)S(1)}, u32[]{:S(2)}, u32[]{:S(2)}) collective-permute-start(bf16[256,1024]{1,0:T(8,128)(2,1)S(1)} %slice.18), channel_id=1, source_target_pairs={{0,4},{1,5},{2,6},{3,7},{4,0},{5,1},{6,2},{7,3},{8,12},{9,13},{10,... | collective-permute-start | bytes 1572872 | tf_op jit(solution)/shard_map/ppermute | solution.py:483
  45.5 2.7 %collective-permute-start.8 = (bf16[272,1024]{1,0:T(8,128)(2,1)S(1)}, bf16[272,1024]{1,0:T(8,128)(2,1)S(1)}, u32[]{:S(2)}, u32[]{:S(2)}) collective-permute-start(bf16[272,1024]{1,0:T(8,128)(2,1)S(1)} %collective-permute-done.4.refs_1_), channel_id=1, source_target_pairs={{0,1},{1,0},{2,3},{3,2},{4,5},{5,4},{6,7},{7,6},{8,9},{9,8},{10,11... | collective-permute-start | bytes 1671176 | tf_op jit(solution)/shard_map/ppermute | solution.py:483
  46.1 2.1 %collective-permute-start.7 = (bf16[256,1024]{1,0:T(8,128)(2,1)S(1)}, bf16[256,1024]{1,0:T(8,128)(2,1)S(1)}, u32[]{:S(2)}, u32[]{:S(2)}) collective-permute-start(bf16[256,1024]{1,0:T(8,128)(2,1)S(1)} %collective-permute-done.2.refs_0_), channel_id=1, source_target_pairs={{0,1},{1,0},{2,3},{3,2},{4,5},{5,4},{6,7},{7,6},{8,9},{9,8},{10,11... | collective-permute-start | bytes 1572872 | tf_op jit(solution)/shard_map/ppermute | solution.py:483
  50.6 8.2 %collective-permute-start.11 = (bf16[256,256]{1,0:T(8,128)(2,1)S(1)}, bf16[256,256]{1,0:T(8,128)(2,1)S(1)}, u32[]{:S(2)}, u32[]{:S(2)}) collective-permute-start(bf16[256,256]{1,0:T(8,128)(2,1)S(1)} %get-tuple-element.63.refs_1_), channel_id=1, source_target_pairs={{0,8},{8,16},{16,24},{1,9},{9,17},{17,25},{2,10},{10,18},{18,26},{... | collective-permute-start | bytes 393224 | tf_op jit(solution)/shard_map/ppermute | solution.py:488
  51.9 8.9 %collective-permute-start.9 = (bf16[256,256]{1,0:T(8,128)(2,1)S(1)}, bf16[256,256]{1,0:T(8,128)(2,1)S(1)}, u32[]{:S(2)}, u32[]{:S(2)}) collective-permute-start(bf16[256,256]{1,0:T(8,128)(2,1)S(1)} %get-tuple-element.62.refs_0_), channel_id=1, source_target_pairs={{0,8},{8,16},{16,24},{1,9},{9,17},{17,25},{2,10},{10,18},{18,26},{... | collective-permute-start | bytes 393224 | tf_op jit(solution)/shard_map/ppermute | solution.py:488
  58.8 8.0 %collective-permute-start.12 = (bf16[256,256]{1,0:T(8,128)(2,1)S(1)}, bf16[256,256]{1,0:T(8,128)(2,1)S(1)}, u32[]{:S(2)}, u32[]{:S(2)}) collective-permute-start(bf16[256,256]{1,0:T(8,128)(2,1)S(1)} %collective-permute-done.11.refs_2_.refs_3_), channel_id=1, source_target_pairs={{8,16},{16,24},{9,17},{17,25},{10,18},{18,26},{11,19},{19,27},{12,... | collective-permute-start | bytes 393224 | tf_op jit(solution)/shard_map/ppermute | solution.py:488
  60.8 7.7 %collective-permute-start.10 = (bf16[256,256]{1,0:T(8,128)(2,1)S(1)}, bf16[256,256]{1,0:T(8,128)(2,1)S(1)}, u32[]{:S(2)}, u32[]{:S(2)}) collective-permute-start(bf16[256,256]{1,0:T(8,128)(2,1)S(1)} %collective-permute-done.9.refs_1_.refs_2_), channel_id=1, source_target_pairs={{8,16},{16,24},{9,17},{17,25},{10,18},{18,26},{11,19},{19,27},{12,... | collective-permute-start | bytes 393224 | tf_op jit(solution)/shard_map/ppermute | solution.py:488
  66.8 7.9 %collective-permute-start.14 = (bf16[256,256]{1,0:T(8,128)(2,1)S(1)}, bf16[256,256]{1,0:T(8,128)(2,1)S(1)}, u32[]{:S(2)}, u32[]{:S(2)}) collective-permute-start(bf16[256,256]{1,0:T(8,128)(2,1)S(1)} %collective-permute-done.12.refs_1_), channel_id=1, source_target_pairs={{16,24},{17,25},{18,26},{19,27},{20,28},{21,29},{22,30},{23,31}} | collective-permute-start | bytes 393224 | tf_op jit(solution)/shard_map/ppermute | solution.py:488
  68.5 7.7 %collective-permute-start.13 = (bf16[256,256]{1,0:T(8,128)(2,1)S(1)}, bf16[256,256]{1,0:T(8,128)(2,1)S(1)}, u32[]{:S(2)}, u32[]{:S(2)}) collective-permute-start(bf16[256,256]{1,0:T(8,128)(2,1)S(1)} %collective-permute-done.10.refs_0_), channel_id=1, source_target_pairs={{16,24},{17,25},{18,26},{19,27},{20,28},{21,29},{22,30},{23,31}} | collective-permute-start | bytes 393224 | tf_op jit(solution)/shard_map/ppermute | solution.py:488
  76.1 20.7 %copy-start = (bf16[512,1024]{1,0:T(8,128)(2,1)S(1)}, bf16[512,1024]{1,0:T(8,128)(2,1)}, u32[]{:S(2)}) copy-start(bf16[512,1024]{1,0:T(8,128)(2,1)} %t_ref.3) | copy-start | bytes 3145732
  77.7 8.0 %collective-permute-start.16 = (bf16[256,512]{1,0:T(8,128)(2,1)S(1)}, bf16[256,512]{1,0:T(8,128)(2,1)S(1)}, u32[]{:S(2)}, u32[]{:S(2)}) collective-permute-start(bf16[256,512]{1,0:T(8,128)(2,1)S(1)} %attend.10.refs_0_), channel_id=1, source_target_pairs={{0,2},{1,3},{2,0},{3,1},{4,6},{5,7},{6,4},{7,5},{8,10},{9,11},{10,... | collective-permute-start | bytes 786440 | tf_op jit(solution)/shard_map/ppermute | solution.py:483
  79.2 9.2 %collective-permute-start.18 = (bf16[256,512]{1,0:T(8,128)(2,1)S(1)}, bf16[256,512]{1,0:T(8,128)(2,1)S(1)}, u32[]{:S(2)}, u32[]{:S(2)}) collective-permute-start(bf16[256,512]{1,0:T(8,128)(2,1)S(1)} %attend.10.refs_0_), channel_id=1, source_target_pairs={{0,4},{1,5},{2,6},{3,7},{4,0},{5,1},{6,2},{7,3},{8,12},{9,13},{10,... | collective-permute-start | bytes 786440 | tf_op jit(solution)/shard_map/ppermute | solution.py:483
  81.2 11.3 %collective-permute-start.27 = (bf16[256,512]{1,0:T(8,128)(2,1)S(1)}, bf16[256,512]{1,0:T(8,128)(2,1)S(1)}, u32[]{:S(2)}, u32[]{:S(2)}) collective-permute-start(bf16[256,512]{1,0:T(8,128)(2,1)S(1)} %attend.11.refs_0_), channel_id=1, source_target_pairs={{0,4},{1,5},{2,6},{3,7},{4,0},{5,1},{6,2},{7,3},{8,12},{9,13},{10,... | collective-permute-start | bytes 786440 | tf_op jit(solution)/shard_map/ppermute | solution.py:483
  82.8 9.7 %collective-permute-start.25 = (bf16[256,512]{1,0:T(8,128)(2,1)S(1)}, bf16[256,512]{1,0:T(8,128)(2,1)S(1)}, u32[]{:S(2)}, u32[]{:S(2)}) collective-permute-start(bf16[256,512]{1,0:T(8,128)(2,1)S(1)} %attend.11.refs_0_), channel_id=1, source_target_pairs={{0,2},{1,3},{2,0},{3,1},{4,6},{5,7},{6,4},{7,5},{8,10},{9,11},{10,... | collective-permute-start | bytes 786440 | tf_op jit(solution)/shard_map/ppermute | solution.py:483
  83.4 11.1 %collective-permute-start.15 = (bf16[256,512]{1,0:T(8,128)(2,1)S(1)}, bf16[256,512]{1,0:T(8,128)(2,1)S(1)}, u32[]{:S(2)}, u32[]{:S(2)}) collective-permute-start(bf16[256,512]{1,0:T(8,128)(2,1)S(1)} %attend.10.refs_0_), channel_id=1, source_target_pairs={{0,1},{1,0},{2,3},{3,2},{4,5},{5,4},{6,7},{7,6},{8,9},{9,8},{10,11... | collective-permute-start | bytes 786440 | tf_op jit(solution)/shard_map/ppermute | solution.py:483
  85.7 8.2 %collective-permute-start.20 = (bf16[128,512]{1,0:T(8,128)(2,1)S(1)}, bf16[128,512]{1,0:T(8,128)(2,1)S(1)}, u32[]{:S(2)}, u32[]{:S(2)}) collective-permute-start(bf16[128,512]{1,0:T(8,128)(2,1)S(1)} %slice.24), channel_id=1, source_target_pairs={{0,4},{1,5},{2,6},{3,7},{4,0},{5,1},{6,2},{7,3},{8,12},{9,13},{10,... | collective-permute-start | bytes 393224 | tf_op jit(solution)/shard_map/ppermute | solution.py:483
  88.5 5.5 %collective-permute-start.21 = (bf16[128,512]{1,0:T(8,128)(2,1)S(1)}, bf16[128,512]{1,0:T(8,128)(2,1)S(1)}, u32[]{:S(2)}, u32[]{:S(2)}) collective-permute-start(bf16[128,512]{1,0:T(8,128)(2,1)S(1)} %slice.25), channel_id=1, source_target_pairs={{0,2},{1,3},{2,0},{3,1},{4,6},{5,7},{6,4},{7,5},{8,10},{9,11},{10,... | collective-permute-start | bytes 393224 | tf_op jit(solution)/shard_map/ppermute | solution.py:483
  92.5 3.8 %collective-permute-start.17 = (bf16[256,512]{1,0:T(8,128)(2,1)S(1)}, bf16[256,512]{1,0:T(8,128)(2,1)S(1)}, u32[]{:S(2)}, u32[]{:S(2)}) collective-permute-start(bf16[256,512]{1,0:T(8,128)(2,1)S(1)} %collective-permute-done.16.refs_2_), channel_id=1, source_target_pairs={{0,1},{1,0},{2,3},{3,2},{4,5},{5,4},{6,7},{7,6},{8,9},{9,8},{10,11... | collective-permute-start | bytes 786440 | tf_op jit(solution)/shard_map/ppermute | solution.py:483
  92.5 3.8 %collective-permute-start.19 = (bf16[256,512]{1,0:T(8,128)(2,1)S(1)}, bf16[256,512]{1,0:T(8,128)(2,1)S(1)}, u32[]{:S(2)}, u32[]{:S(2)}) collective-permute-start(bf16[256,512]{1,0:T(8,128)(2,1)S(1)} %collective-permute-done.18.refs_4_), channel_id=1, source_target_pairs={{0,1},{1,0},{2,3},{3,2},{4,5},{5,4},{6,7},{7,6},{8,9},{9,8},{10,11... | collective-permute-start | bytes 786440 | tf_op jit(solution)/shard_map/ppermute | solution.py:483
  93.9 1.3 %collective-permute-start.22 = (bf16[128,512]{1,0:T(8,128)(2,1)S(1)}, bf16[128,512]{1,0:T(8,128)(2,1)S(1)}, u32[]{:S(2)}, u32[]{:S(2)}) collective-permute-start(bf16[128,512]{1,0:T(8,128)(2,1)S(1)} %collective-permute-done.20.refs_6_), channel_id=1, source_target_pairs={{0,1},{1,0},{2,3},{3,2},{4,5},{5,4},{6,7},{7,6},{8,9},{9,8},{10,11... | collective-permute-start | bytes 393224 | tf_op jit(solution)/shard_map/ppermute | solution.py:483
  93.9 1.9 %collective-permute-start.23 = (bf16[128,512]{1,0:T(8,128)(2,1)S(1)}, bf16[128,512]{1,0:T(8,128)(2,1)S(1)}, u32[]{:S(2)}, u32[]{:S(2)}) collective-permute-start(bf16[128,512]{1,0:T(8,128)(2,1)S(1)} %collective-permute-done.21.refs_7_), channel_id=1, source_target_pairs={{0,1},{1,0},{2,3},{3,2},{4,5},{5,4},{6,7},{7,6},{8,9},{9,8},{10,11... | collective-permute-start | bytes 393224 | tf_op jit(solution)/shard_map/ppermute | solution.py:483
  94.5 8.8 %collective-permute-start.24 = (bf16[256,512]{1,0:T(8,128)(2,1)S(1)}, bf16[256,512]{1,0:T(8,128)(2,1)S(1)}, u32[]{:S(2)}, u32[]{:S(2)}) collective-permute-start(bf16[256,512]{1,0:T(8,128)(2,1)S(1)} %attend.11.refs_0_), channel_id=1, source_target_pairs={{0,1},{1,0},{2,3},{3,2},{4,5},{5,4},{6,7},{7,6},{8,9},{9,8},{10,11... | collective-permute-start | bytes 786440 | tf_op jit(solution)/shard_map/ppermute | solution.py:483
  95.3 7.5 %collective-permute-start.30 = (bf16[128,512]{1,0:T(8,128)(2,1)S(1)}, bf16[128,512]{1,0:T(8,128)(2,1)S(1)}, u32[]{:S(2)}, u32[]{:S(2)}) collective-permute-start(bf16[128,512]{1,0:T(8,128)(2,1)S(1)} %slice.27), channel_id=1, source_target_pairs={{0,2},{1,3},{2,0},{3,1},{4,6},{5,7},{6,4},{7,5},{8,10},{9,11},{10,... | collective-permute-start | bytes 393224 | tf_op jit(solution)/shard_map/ppermute | solution.py:483
  95.8 7.1 %collective-permute-start.29 = (bf16[128,512]{1,0:T(8,128)(2,1)S(1)}, bf16[128,512]{1,0:T(8,128)(2,1)S(1)}, u32[]{:S(2)}, u32[]{:S(2)}) collective-permute-start(bf16[128,512]{1,0:T(8,128)(2,1)S(1)} %slice.26), channel_id=1, source_target_pairs={{0,4},{1,5},{2,6},{3,7},{4,0},{5,1},{6,2},{7,3},{8,12},{9,13},{10,... | collective-permute-start | bytes 393224 | tf_op jit(solution)/shard_map/ppermute | solution.py:483
  96.3 7.0 %collective-permute-start.26 = (bf16[256,512]{1,0:T(8,128)(2,1)S(1)}, bf16[256,512]{1,0:T(8,128)(2,1)S(1)}, u32[]{:S(2)}, u32[]{:S(2)}) collective-permute-start(bf16[256,512]{1,0:T(8,128)(2,1)S(1)} %collective-permute-done.25.refs_2_), channel_id=1, source_target_pairs={{0,1},{1,0},{2,3},{3,2},{4,5},{5,4},{6,7},{7,6},{8,9},{9,8},{10,11... | collective-permute-start | bytes 786440 | tf_op jit(solution)/shard_map/ppermute | solution.py:483
  96.3 7.0 %collective-permute-start.28 = (bf16[256,512]{1,0:T(8,128)(2,1)S(1)}, bf16[256,512]{1,0:T(8,128)(2,1)S(1)}, u32[]{:S(2)}, u32[]{:S(2)}) collective-permute-start(bf16[256,512]{1,0:T(8,128)(2,1)S(1)} %collective-permute-done.27.refs_4_), channel_id=1, source_target_pairs={{0,1},{1,0},{2,3},{3,2},{4,5},{5,4},{6,7},{7,6},{8,9},{9,8},{10,11... | collective-permute-start | bytes 786440 | tf_op jit(solution)/shard_map/ppermute | solution.py:483
  102.8 1.4 %collective-permute-start.32 = (bf16[128,512]{1,0:T(8,128)(2,1)S(1)}, bf16[128,512]{1,0:T(8,128)(2,1)S(1)}, u32[]{:S(2)}, u32[]{:S(2)}) collective-permute-start(bf16[128,512]{1,0:T(8,128)(2,1)S(1)} %collective-permute-done.30.refs_7_), channel_id=1, source_target_pairs={{0,1},{1,0},{2,3},{3,2},{4,5},{5,4},{6,7},{7,6},{8,9},{9,8},{10,11... | collective-permute-start | bytes 393224 | tf_op jit(solution)/shard_map/ppermute | solution.py:483
  102.9 1.5 %collective-permute-start.31 = (bf16[128,512]{1,0:T(8,128)(2,1)S(1)}, bf16[128,512]{1,0:T(8,128)(2,1)S(1)}, u32[]{:S(2)}, u32[]{:S(2)}) collective-permute-start(bf16[128,512]{1,0:T(8,128)(2,1)S(1)} %collective-permute-done.29.refs_6_), channel_id=1, source_target_pairs={{0,1},{1,0},{2,3},{3,2},{4,5},{5,4},{6,7},{7,6},{8,9},{9,8},{10,11... | collective-permute-start | bytes 393224 | tf_op jit(solution)/shard_map/ppermute | solution.py:483
  110.2 1.2 %collective-permute-start.33 = (f32[8,512]{1,0:T(8,128)S(1)}, f32[8,512]{1,0:T(8,128)S(1)}, u32[]{:S(2)}, u32[]{:S(2)}) collective-permute-start(f32[8,512]{1,0:T(8,128)S(1)} %constant_dynamic-update-slice_fusion), channel_id=1, source_target_pairs={{0,1},{1,0},{2,3},{3,2},{4,5},{5,4},{6,7},{7,6},{8,9},{9,8},{10,11... | collective-permute-start | bytes 49160 | tf_op jit(solution)/shard_map/ppermute | solution.py:483
  111.5 3.7 %collective-permute-start.34 = (f32[8,512]{1,0:T(8,128)S(1)}, f32[8,512]{1,0:T(8,128)S(1)}, u32[]{:S(2)}, u32[]{:S(2)}) collective-permute-start(f32[8,512]{1,0:T(8,128)S(1)} %add.4.refs_2_), channel_id=1, source_target_pairs={{0,2},{1,3},{2,0},{3,1},{4,6},{5,7},{6,4},{7,5},{8,10},{9,11},{10,... | collective-permute-start | bytes 49160 | tf_op jit(solution)/shard_map/ppermute | solution.py:483
  113.0 3.7 %collective-permute-start.35 = (f32[8,512]{1,0:T(8,128)S(1)}, f32[8,512]{1,0:T(8,128)S(1)}, u32[]{:S(2)}, u32[]{:S(2)}) collective-permute-start(f32[8,512]{1,0:T(8,128)S(1)} %add.4.refs_2_), channel_id=1, source_target_pairs={{0,4},{1,5},{2,6},{3,7},{4,0},{5,1},{6,2},{7,3},{8,12},{9,13},{10,... | collective-permute-start | bytes 49160 | tf_op jit(solution)/shard_map/ppermute | solution.py:483
  114.5 4.6 %collective-permute-start.36 = (f32[8,512]{1,0:T(8,128)S(1)}, f32[8,512]{1,0:T(8,128)S(1)}, u32[]{:S(2)}, u32[]{:S(2)}) collective-permute-start(f32[8,512]{1,0:T(8,128)S(1)} %add.4.refs_2_), channel_id=1, source_target_pairs={{0,6},{1,7},{2,4},{3,5},{4,2},{5,3},{6,0},{7,1},{8,14},{9,15},{10,... | collective-permute-start | bytes 49160 | tf_op jit(solution)/shard_map/ppermute | solution.py:483
